TPU v7x, 32 devices: a whole 2x2x4 slice. The times are simulated.
32 devices in a mesh: req: 4 (over y, x), seq: 4 (over z), hid: 2 (over core).
Axes of the slice: x: 2, y: 2, z: 4, core: 2. Of those that a mesh axis runs over, the one named last changes fastest.
Arguments:
- tokens: bfloat16 [16384, 2048], P(('req', 'seq')), may hold values from -6 to 6
- attention_gain: bfloat16 [2048], replicated, may hold values from 0.099609375 to 1.8984375
- project_weight: bfloat16 [2048, 2048], P(None, 'hid'), may hold values from -0.125 to 0.125
- conv_weight: bfloat16 [4, 2048], P(None, 'hid'), may hold values from -3 to 3
- decay_down: bfloat16 [2048, 16], replicated, may hold values from -0.125 to 0.125
- decay_up: bfloat16 [16, 512], P(None, 'hid'), may hold values from -1.5 to 1.5
- decay_bias: float32 [512], P('hid'), may hold values from -2 to 10
- output_gate: bfloat16 [2048, 1024], P(None, 'hid'), may hold values from -0.125 to 0.125
- head_gain: bfloat16 [512], replicated, may hold values from 0.099609375 to 1.8984375
- output_weight: bfloat16 [1024, 2048], P('hid'), may hold values from -0.1875 to 0.1875
- mixer_gain: bfloat16 [2048], replicated, may hold values from 0.099609375 to 1.8984375
- gate_weight: bfloat16 [2048, 2816], P('req', 'hid'), may hold values from -0.125 to 0.125
- up_weight: bfloat16 [2048, 2816], P('req', 'hid'), may hold values from -0.125 to 0.125
- down_weight: bfloat16 [2816, 2048], P('hid', 'req'), may hold values from -0.109375 to 0.109375
- prompt_pages: int32 [4, 16], P('req'), may hold values from 0 to 64, as said below
- prompt_start: int32 [4, 16], P('req'), may hold values from 0 to 63, as said below
Outputs:
- hidden_out: bfloat16 [16384, 2048], P(('req', 'seq', 'hid'))
- page_states: bfloat16 [256, 2, 256, 512], P(('req', 'seq'), 'hid')
- conv_edges: bfloat16 [256, 3, 2048], P(('req', 'seq'), None, 'hid')
Inputs may be any that keep to these rules, and one draw needn't show every extreme that they name: `prompt_pages`: row r lists the page counts of the prompts of group r; 0 marks an unused slot; in every draw some group holds one prompt of all its 64 pages. `prompt_start`: the slots of a row that are used cover pages in increasing order without intersection and end by page 64; pages between prompts belong to none; an unused slot starts at page 64 - 1, and every draw has one.
All inputs are finite; a program needn't handle non-finite values.
Results may differ from a plain program's by a relative error of at most 0.014.
Values may be sent and summed in bfloat16 or wider, within the bound.
No kernel may reach another device: no remote copies, remote signals or barrier semaphores. Data moves between devices by JAX's collectives and lax.ppermute only.
A program may use at most 192 MiB of HBM per device.

v0:
```python
import jax
import jax.numpy as jnp
from jax import lax
from jax.sharding import PartitionSpec as P

HK = 256
HV = 512
KCONV = 4
PAGE = 64
CONVW = 1024


EPSILON = 1e-06
TOP_PRECISION = lax.Precision.HIGHEST


def shifted(value, axis, steps):
    count = lax.axis_size(axis)
    first, last = (max(0, -steps), min(count, count - steps))
    return lax.ppermute(value, axis, [(source, source + steps) for source in range(first, last)])


def prefix_2(array, axis, join, neutral):
    place = lax.axis_index(axis)
    gathered = jax.tree.map(
        lambda a, kind: lax.all_gather(a.astype(kind), axis), array, (jnp.bfloat16, jnp.bfloat16)
    )
    state = jax.tree.map(lambda a, e: jnp.zeros_like(a) + jnp.asarray(e, a.dtype), array, neutral)

    def one(lap, state):
        return join(
            state,
            jax.tree.map(
                lambda a, own: lax.dynamic_index_in_dim(a, lap, 0, False).astype(own.dtype),
                gathered,
                array,
            ),
        )

    return lax.fori_loop(0, place, one, state)


def rms_scaled(values, scale_gain):
    values = values.astype(jnp.float32)
    return (
        values
        * lax.rsqrt(jnp.mean(values * values, axis=-1, keepdims=True) + EPSILON)
        * scale_gain.astype(jnp.float32)
    )


def page_segments(page_counts, starts, total_pages):
    position = jnp.arange(total_pages, dtype=jnp.int32)
    inside = (position[None, :] >= starts[:, None]) & (
        position[None, :] < starts[:, None] + page_counts[:, None]
    )
    labels = jnp.arange(1, page_counts.shape[0] + 1, dtype=jnp.int32)
    segment = jnp.sum(jnp.where(inside, labels[:, None], 0), axis=0) - 1
    earlier = jnp.concatenate([jnp.full((1,), -1, jnp.int32), segment[:-1]])
    return ((segment == earlier) & (segment >= 0)).astype(jnp.float32)


def short_conv(by_page, before, carried, conv_taps):
    kept_rows = before.astype(jnp.float32) * carried[:, None, None]
    widened = jnp.concatenate([kept_rows, by_page.astype(jnp.float32)], axis=1)
    tap_count = conv_taps.shape[0]
    length = by_page.shape[1]
    result = jnp.zeros(by_page.shape, jnp.float32)
    for offset in range(tap_count):
        result = (
            result
            + conv_taps[offset].astype(jnp.float32)
            * widened[:, tap_count - 1 - offset : tap_count - 1 - offset + length]
        )
    return result


def split_features(mixed_rows, key_width):
    query_rows = jax.nn.silu(mixed_rows[..., :key_width])
    key_rows = jax.nn.silu(mixed_rows[..., key_width : 2 * key_width]) * key_width ** (-0.5)
    value_matrix = mixed_rows[..., 2 * key_width :]
    return (
        query_rows.transpose(0, 2, 1, 3),
        key_rows.transpose(0, 2, 1, 3),
        value_matrix.transpose(0, 2, 1, 3),
    )


def page_step(memory_state, inputs):
    query_rows, key_rows, value_matrix, decay_sum, carried = inputs
    memory_state = memory_state * carried
    length = query_rows.shape[1]
    raised_rows = query_rows * jnp.exp(decay_sum)
    lowered = key_rows * jnp.exp(-decay_sum)
    scores = jnp.einsum("hik,hjk->hij", raised_rows, lowered, precision=TOP_PRECISION)
    rows_index = jnp.arange(length)
    causal = rows_index[:, None] >= rows_index[None, :]
    scores = jnp.where(causal[None], scores, 0.0)
    layer_output = jnp.einsum("hij,hjv->hiv", scores, value_matrix, precision=TOP_PRECISION)
    layer_output = layer_output + jnp.einsum(
        "eow,ews->eos", raised_rows, memory_state, precision=TOP_PRECISION
    )
    closing_sum = decay_sum[:, -1:, :]
    weighted_rows = key_rows * jnp.exp(closing_sum - decay_sum)
    memory_state = jnp.exp(closing_sum[:, 0, :])[:, :, None] * memory_state + jnp.einsum(
        "lte,ltb->leb", weighted_rows, value_matrix, precision=TOP_PRECISION
    )
    return (memory_state, (layer_output, memory_state))


def on_device(
    tokens,
    attention_gain,
    project_weight,
    conv_weight,
    decay_down,
    decay_up,
    decay_bias,
    output_gate,
    head_gain,
    output_weight,
    mixer_gain,
    gate_weight,
    up_weight,
    down_weight,
    prompt_pages,
    prompt_start,
):
    token_count = tokens.shape[0]
    page_count = token_count // PAGE
    local_heads = project_weight.shape[1] // CONVW
    rim_rows = KCONV - 1
    seq_index = lax.axis_index("seq")
    group_pages = page_count * lax.axis_size("seq")
    page_flags = page_segments(prompt_pages[0], prompt_start[0], group_pages)
    carried = lax.dynamic_slice_in_dim(page_flags, seq_index * page_count, page_count)
    normed = rms_scaled(tokens, attention_gain).astype(jnp.bfloat16)
    projected = jnp.dot(normed, project_weight, preferred_element_type=jnp.float32).astype(
        jnp.bfloat16
    )
    by_page = projected.reshape(page_count, PAGE, local_heads * CONVW)
    incoming = shifted(by_page[-1, PAGE - rim_rows :], "seq", 1)
    before = jnp.concatenate([incoming[None], by_page[:-1, PAGE - rim_rows :]], axis=0)
    mixed_rows = short_conv(by_page, before, carried, conv_weight).reshape(
        page_count, PAGE, local_heads, CONVW
    )
    query_rows, key_rows, value_matrix = split_features(mixed_rows, HK)
    lowrank = jnp.dot(normed, decay_down, preferred_element_type=jnp.float32).astype(jnp.bfloat16)
    decay_log = (
        jax.nn.log_sigmoid(
            jnp.dot(lowrank, decay_up, preferred_element_type=jnp.float32) + decay_bias
        )
        / 16.0
    )
    decay_log = decay_log.reshape(page_count, PAGE, local_heads, HK).transpose(0, 2, 1, 3)
    decay_sum = jnp.cumsum(decay_log, axis=2)
    start_memory = jnp.zeros((local_heads, HK, HV), jnp.float32)
    local_memory, (outputs, memories) = lax.scan(
        page_step, start_memory, (query_rows, key_rows, value_matrix, decay_sum, carried)
    )
    totals = decay_sum[:, :, -1, :]
    through = jnp.cumsum(totals, axis=0)
    alive_mask = jnp.cumprod(carried)
    block_decay = alive_mask[-1] * jnp.exp(through[-1])

    def compose(earlier, latter):
        return (earlier[0] * latter[0], latter[0][..., None] * earlier[1] + latter[1])

    prefix = prefix_2(
        (block_decay, local_memory),
        "seq",
        compose,
        (jnp.ones_like(block_decay), jnp.zeros_like(local_memory)),
    )
    incoming_state = prefix[1]
    before_sum = through - totals
    extent_factor = alive_mask[:, None, None, None] * jnp.exp(decay_sum + before_sum[:, :, None, :])
    outputs = outputs + jnp.einsum(
        "dlof,lfg->dlog", query_rows * extent_factor, incoming_state, precision=TOP_PRECISION
    )
    memories = (
        memories + (alive_mask[:, None, None] * jnp.exp(through))[..., None] * incoming_state[None]
    )
    attended = outputs.transpose(0, 2, 1, 3).reshape(token_count, local_heads, HV)
    normed_heads = rms_scaled(attended, head_gain)
    opening = jax.nn.silu(jnp.dot(normed, output_gate, preferred_element_type=jnp.float32)).reshape(
        token_count, local_heads, HV
    )
    gated_rows = (
        (normed_heads * opening).astype(jnp.bfloat16).reshape(token_count, local_heads * HV)
    )
    partial_value = jnp.dot(gated_rows, output_weight, preferred_element_type=jnp.float32)
    half_rows = token_count // lax.axis_size("hid")
    row_start = lax.axis_index("hid") * half_rows
    mixed_sum = lax.psum(partial_value.astype(jnp.bfloat16), "hid").astype(jnp.float32)
    residual = (tokens.astype(jnp.float32) + mixed_sum).astype(jnp.bfloat16)
    feed_in = rms_scaled(residual, mixer_gain).astype(jnp.bfloat16)
    own_residual = lax.dynamic_slice_in_dim(residual, row_start, half_rows, 0)

    def widen(weight_rows):
        return jnp.dot(feed_in, weight_rows, preferred_element_type=jnp.float32)

    gate_part = widen(lax.all_gather(gate_weight, "req", axis=0, tiled=True))
    up_part = widen(lax.all_gather(up_weight, "req", axis=0, tiled=True))
    hidden = (jax.nn.silu(gate_part) * up_part).astype(jnp.bfloat16)
    partials = jnp.dot(
        hidden,
        lax.all_gather(down_weight, "req", axis=1, tiled=True),
        preferred_element_type=jnp.float32,
    )
    feed_sum = lax.psum_scatter(
        partials.astype(jnp.bfloat16), "hid", scatter_dimension=0, tiled=True
    ).astype(jnp.float32)
    result = (own_residual.astype(jnp.float32) + feed_sum).astype(jnp.bfloat16)
    return (result, memories.astype(jnp.bfloat16), by_page[:, PAGE - rim_rows :])


def solution(mesh):
    return jax.shard_map(
        on_device,
        mesh=mesh,
        in_specs=(
            P(("req", "seq"), None),
            P(),
            P(None, "hid"),
            P(None, "hid"),
            P(),
            P(None, "hid"),
            P("hid"),
            P(None, "hid"),
            P(),
            P("hid", None),
            P(),
            P("req", "hid"),
            P("req", "hid"),
            P("hid", "req"),
            P("req", None),
            P("req", None),
        ),
        out_specs=(
            P(("req", "seq", "hid"), None),
            P(("req", "seq"), "hid", None, None),
            P(("req", "seq"), None, "hid"),
        ),
        check_vma=False,
    )
```

profile of v0, /device:TPU:0, one launch (start us, length us, event | category | flops | bytes accessed | tf_op | source)
XLA Modules:
  0.0 485.7 jit_solution(1413439997962253311)
XLA Ops:
  8.1 3.2 fusion.29
  11.6 7.2 %convolution_convert_fusion.2 = bf16[1024,1024]{1,0:T(8,128)(2,1)S(1)} fusion(bf16[2048,1024]{1,0:T(8,128)(2,1)} %param.22, bf16[1024,2048]{1,0:T(8,128)(2,1)S(1)} %copy-done.2, f32[2048]{0:T(1024)S(1)} %convert_element_type.146, f32[1024]{0:T(1024)S(1)} %add_rsqrt_fusion.2), kind=kOutput, calls=%fused_computation.78 | convolution fusion | flops 4304404480 | bytes 10498048 | tf_op jit(solution)/shard_map/dot_general | solution.py:138
  18.9 5.1 %collective-permute-start = (bf16[3,1024]{1,0:T(4,128)(2,1)S(1)}, bf16[3,1024]{1,0:T(4,128)(2,1)S(1)}, u32[]{:S(2)}, u32[]{:S(2)}) collective-permute-start(bf16[3,1024]{1,0:T(4,128)(2,1)S(1)} %slice_bitcast_fusion.2), channel_id=1, source_target_pairs={{0,2},{2,4},{4,6},{1,3},{3,5},{5,7},{8,10},{10,12},{12,14},{9,11},... | collective-permute-start | bytes 18440 | tf_op jit(solution)/shard_map/ppermute | solution.py:20
  24.0 3.2 copy_convert_fusion
  27.4 4.2 fusion.50
  35.0 7.3 %fusion.37 = f32[16,64,1,1024]{3,0,1,2:T(8,128)S(1)} fusion(f32[16,64,1024]{2,0,1:T(8,128)} %copy_convert_fusion, f32[16,3,1024]{2,0,1:T(8,128)S(1)} %convert_multiply_fusion.4, f32[1024]{0:T(1024)S(1)} %bitcast.168, f32[1024]{0:T(1024)S(1)} %bitcast.169, f32[1024]{0:T(1024)S(1)} %bitcast.167, f32[1024]{0:T(1024)S(1)} %bitcast.166), kind=kLoop, calls=%fused_computation.61 | loop fusion | flops 10485760 | bytes 8601600 | tf_op jit(solution)/shard_map/reshape | solution.py:144
  46.0 143.3 %while.28 = (s32[]{:T(128)}, f32[1,256,512]{2,1,0:T(8,128)S(1)}, f32[16,1,64,512]{3,2,1,0:T(8,128)}, f32[16,1,256,512]{3,2,1,0:T(8,128)}, f32[16,1,64,256]{3,0,1...) while((s32[]{:T(128)}, f32[1,256,512]{2,1,0:T(8,128)S(1)}, ...), condition=%wide.region_4.5_spmd.clone, body=%wide.region_3.4_spmd.clone.sunk | while | flops 240001024 | bytes 4038800 | solution.py:158
  70.6 2.2 bitcast_dynamic-update-slice_fusion.2
  142.2 2.2 bitcast_dynamic-update-slice_fusion.2
  191.4 9.1 %all_gather.19 = bf16[4,1,256]{2,1,0:T(2,128)(2,1)S(1)} all-gather(bf16[1,1,256]{2,1,0:T(2,128)(2,1)S(1)} %fusion.65), channel_id=1, replica_groups=mesh['req'=4,'seq'=4,'hid'=2] {'seq'}, dimensions={0}, use_global_device_ids=true | all-gather | bytes 2560 | tf_op jit(solution)/shard_map/all_gather | solution.py:26
  200.5 17.8 %all-gather.12.cloned.1.call-done = bf16[4,256,512]{2,1,0:T(8,128)(2,1)} async-done(((bf16[1,256,512]{2,1,0:T(8,128)(2,1)}), bf16[4,256,512]{2,1,0:T(8,128)(2,1)}) %all-gather.12.cloned.1.call-update) | async-done | bytes 1048592 | tf_op jit(solution)/shard_map/all_gather | solution.py:26
  218.6 5.6 %multiply_reduce_fusion = (f32[16,64]{1,0:T(8,128)S(1)}, f32[16,1,64,512]{3,2,0,1:T(8,128)}) fusion(f32[16,64,256]{2,0,1:T(8,128)} %get-tuple-element.223, f32[1,256,512]{2,1,0:T(8,128)S(1)} %get-tuple-element.98, f32[16,1,64,512]{3,2,1,0:T(8,128)} %get-tuple-element.96), kind=kOutput, calls=%fused_computation.77 | convolution fusion | flops 1612184576 | bytes 5771264 | tf_op jit(solution)/shard_map/dlof,lfg->dlog/dot_general | solution.py:178
  224.3 6.1 %fusion.44 = bf16[1024,512]{1,0:T(8,128)(2,1)S(1)} fusion(f32[16,1,64,512]{3,2,0,1:T(8,128)} %get-tuple-element.231, f32[512]{0:T(512)S(1)} %convert_element_type.163, f32[1024]{0:T(1024)S(1)} %rsqrt.29, bf16[2048,512]{1,0:T(8,128)(2,1)} %param.27, bf16[1024,2048]{1,0:T(8,128)(2,1)} %param.20, f32[2048]{0:T(1024)S(1)} %convert_element_type.146, ...), kind=kOutput, calls=%fused_computation.76 | convolution fusion | flops 2160066560 | bytes 9455616 | tf_op jit(solution)/shard_map/dot_general | solution.py:186
  230.5 4.4 convolution_convert_fusion.1
  236.9 29.5 %all-reduce.2.cloned.1.call-done = bf16[1024,2048]{1,0:T(8,128)(2,1)} async-done(((bf16[1024,2048]{1,0:T(8,128)(2,1)}), bf16[1024,2048]{1,0:T(8,128)(2,1)}) %all-reduce.2.cloned.1.call-update) | async-done | bytes 4194320 | tf_op jit(solution)/shard_map/psum | solution.py:195
  266.4 7.8 %fusion.26 = (f32[1024]{0:T(1024)S(1)}, bf16[1024,2048]{1,0:T(8,128)(2,1)}) fusion(bf16[1024,2048]{1,0:T(8,128)(2,1)} %all-reduce.2.cloned.1.call-done, bf16[1024,2048]{1,0:T(8,128)(2,1)} %param.20), kind=kLoop, calls=%fused_computation.44 | loop fusion | flops 14679040 | bytes 12587008 | tf_op jit(solution)/shard_map/reduce_sum | solution.py:47
  274.2 31.7 %all-gather.6.cloned.1.call-done = bf16[2048,1408]{1,0:T(8,128)(2,1)} async-done(((bf16[512,1408]{1,0:T(8,128)(2,1)}), bf16[2048,1408]{1,0:T(8,128)(2,1)}) %all-gather.6.cloned.1.call-update) | async-done | bytes 5767184 | tf_op jit(solution)/shard_map/all_gather | solution.py:203
  305.9 12.0 %fusion.47 = f32[1024,1408]{1,0:T(8,128)} fusion(bf16[2048,1408]{1,0:T(8,128)(2,1)} %all-gather.6.cloned.1.call-done, bf16[1024,2048]{1,0:T(8,128)(2,1)} %get-tuple-element.218, f32[2048]{0:T(1024)S(1)} %convert_element_type.170, f32[1024]{0:T(1024)S(1)} %add_rsqrt_fusion.1), kind=kOutput, calls=%fused_computation.81 | convolution fusion | flops 5913968640 | bytes 15740928 | tf_op jit(solution)/shard_map/dot_general | solution.py:201
  317.9 55.4 %all-gather.10.cloned.1.call-done = bf16[1408,2048]{1,0:T(8,128)(2,1)} async-done(((bf16[1408,512]{1,0:T(8,128)(2,1)}), bf16[1408,2048]{1,0:T(8,128)(2,1)}) %all-gather.10.cloned.1.call-update) | async-done | bytes 5767184 | tf_op jit(solution)/shard_map/all_gather | solution.py:208
  373.2 67.5 %all-gather.8.cloned.1.call-done = bf16[2048,1408]{1,0:T(8,128)(2,1)} async-done(((bf16[512,1408]{1,0:T(8,128)(2,1)}), bf16[2048,1408]{1,0:T(8,128)(2,1)}) %all-gather.8.cloned.1.call-update) | async-done | bytes 5767184 | tf_op jit(solution)/shard_map/all_gather | solution.py:204
  440.8 20.9 %convolution_convert_fusion = bf16[1024,2048]{1,0:T(8,128)(2,1)} fusion(bf16[1408,2048]{1,0:T(8,128)(2,1)} %all-gather.10.cloned.1.call-done, f32[1024,1408]{1,0:T(8,128)} %fusion.47, bf16[2048,1408]{1,0:T(8,128)(2,1)} %all-gather.8.cloned.1.call-done, bf16[1024,2048]{1,0:T(8,128)(2,1)} %get-tuple-element.218, f32[2048]{0:T(1024)S(1)} %convert_element_type.170, ...), kind=kOutput, calls=%fused_computation.68 | convolution fusion | flops 11830296576 | bytes 25702400 | tf_op jit(solution)/shard_map/dot_general | solution.py:206
  463.5 5.4 %add_convert_fusion = bf16[16,1,256,512]{3,2,1,0:T(8,128)(2,1)} fusion(f32[16,1,256,512]{3,2,1,0:T(8,128)} %get-tuple-element.99, f32[256,512]{1,0:T(8,128)S(1)} %bitcast.155, f32[16,256]{1,0:T(8,128)S(1)} %bitcast_multiply_fusion.1), kind=kLoop, calls=%fused_computation.51 | loop fusion | flops 6291456 | bytes 13123584 | tf_op jit(solution)/shard_map/convert_element_type | solution.py:215
  468.8 5.0 %reduce-scatter.2.cloned.1.call-done = bf16[512,2048]{1,0:T(8,128)(2,1)} async-done(((bf16[1024,2048]{1,0:T(8,128)(2,1)}), bf16[512,2048]{1,0:T(8,128)(2,1)}) %reduce-scatter.2.cloned.1.call-update) | async-done | bytes 2097168 | tf_op jit(solution)/shard_map/reduce_scatter | solution.py:211
  473.9 4.4 add_convert_fusion.1
  (256 shorter events, 152.0 us)
Async XLA Ops:
  8.0 222.4 %copy-start = (bf16[512,2048]{1,0:T(8,128)(2,1)S(1)}, bf16[512,2048]{1,0:T(8,128)(2,1)}, u32[]{:S(2)}) copy-start(bf16[512,2048]{1,0:T(8,128)(2,1)} %param.29) | copy-start | bytes 6291460
  8.0 3.3 copy-start.7
  8.0 210.3 %all-gather.12.cloned.1.call-start = ((), (), s32[]{:S(2)}) async-start(), calls=%async_computation.6 | async-start | bytes 1310720 | tf_op jit(solution)/shard_map/all_gather | solution.py:26
  8.1 3.6 copy-start.2
  18.8 5.2 %copy-start.5 = (bf16[1024,1024]{1,0:T(8,128)(2,1)}, bf16[1024,1024]{1,0:T(8,128)(2,1)S(1)}, u32[]{:S(2)}) copy-start(bf16[1024,1024]{1,0:T(8,128)(2,1)S(1)} %convolution_convert_fusion.2) | copy-start | bytes 6291460
  18.9 8.4 %copy-start.9 = (s32[1,16]{1,0:T(1,128)S(1)}, s32[1,16]{1,0:T(1,128)}, u32[]{:S(2)}) copy-start(s32[1,16]{1,0:T(1,128)} %param.35) | copy-start | bytes 196
  18.9 8.4 %copy-start.11 = (s32[1,16]{1,0:T(1,128)S(1)}, s32[1,16]{1,0:T(1,128)}, u32[]{:S(2)}) copy-start(s32[1,16]{1,0:T(1,128)} %param.34) | copy-start | bytes 196
  18.9 8.5 %copy-start.6 = (bf16[4,1024]{1,0:T(4,128)(2,1)S(1)}, bf16[4,1024]{1,0:T(4,128)(2,1)}, u32[]{:S(2)}) copy-start(bf16[4,1024]{1,0:T(4,128)(2,1)} %param.23) | copy-start | bytes 24580
  18.9 8.5 %copy-start.12 = (bf16[2048,16]{0,1:T(8,128)(2,1)S(1)}, bf16[2048,16]{0,1:T(8,128)(2,1)}, u32[]{:S(2)}) copy-start(bf16[2048,16]{0,1:T(8,128)(2,1)} %param.24) | copy-start | bytes 196612
  18.9 8.5 %copy-start.13 = (bf16[16,256]{1,0:T(8,128)(2,1)S(1)}, bf16[16,256]{1,0:T(8,128)(2,1)}, u32[]{:S(2)}) copy-start(bf16[16,256]{1,0:T(8,128)(2,1)} %param.25) | copy-start | bytes 24580
  18.9 8.5 %copy-start.14 = (f32[256]{0:T(256)S(1)}, f32[256]{0:T(256)}, u32[]{:S(2)}) copy-start(f32[256]{0:T(256)} %param.26) | copy-start | bytes 3076
  18.9 15.9 %collective-permute-start = (bf16[3,1024]{1,0:T(4,128)(2,1)S(1)}, bf16[3,1024]{1,0:T(4,128)(2,1)S(1)}, u32[]{:S(2)}, u32[]{:S(2)}) collective-permute-start(bf16[3,1024]{1,0:T(4,128)(2,1)S(1)} %slice_bitcast_fusion.2), channel_id=1, source_target_pairs={{0,2},{2,4},{4,6},{1,3},{3,5},{5,7},{8,10},{10,12},{12,14},{9,11},... | collective-permute-start | bytes 18440 | tf_op jit(solution)/shard_map/ppermute | solution.py:20
  32.3 1.0 copy-start.3
  42.3 1.6 copy-start.4
  46.0 144.7 %copy-start.10 = (bf16[512]{0:T(512)(128)(2,1)S(1)}, bf16[512]{0:T(512)(128)(2,1)}, u32[]{:S(2)}) copy-start(bf16[512]{0:T(512)(128)(2,1)} %param.28) | copy-start | bytes 3076
  190.0 76.3 %all-reduce.2.cloned.1.call-start = ((), (), s32[]{:S(2)}) async-start(), calls=%async_computation.1 | async-start | bytes 8388608 | tf_op jit(solution)/shard_map/psum | solution.py:195
  234.8 2.0 copy-start.8
  234.8 71.1 %all-gather.6.cloned.1.call-start = ((), (), s32[]{:S(2)}) async-start(), calls=%async_computation.2 | async-start | bytes 7208960 | tf_op jit(solution)/shard_map/all_gather | solution.py:203
  235.4 137.8 %all-gather.10.cloned.1.call-start = ((), (), s32[]{:S(2)}) async-start(), calls=%async_computation.4 | async-start | bytes 7208960 | tf_op jit(solution)/shard_map/all_gather | solution.py:208
  236.0 204.8 %all-gather.8.cloned.1.call-start = ((), (), s32[]{:S(2)}) async-start(), calls=%async_computation.3 | async-start | bytes 7208960 | tf_op jit(solution)/shard_map/all_gather | solution.py:204
  236.6 237.3 %reduce-scatter.2.cloned.1.call-start = ((), (), s32[]{:S(2)}) async-start(), calls=%async_computation.5 | async-start | bytes 6291456 | tf_op jit(solution)/shard_map/reduce_scatter | solution.py:211
  463.5 14.8 %copy-start.1 = (bf16[512,2048]{1,0:T(8,128)(2,1)S(1)}, bf16[512,2048]{1,0:T(8,128)(2,1)}, u32[]{:S(2)}) copy-start(bf16[512,2048]{1,0:T(8,128)(2,1)} %param.29) | copy-start | bytes 6291460
Sparse Core Ops, SparseCore 0:
  190.1 28.1 all-gather.11
  235.0 31.3 all-reduce.1
  461.8 12.0 reduce-scatter.1
Sparse Core Ops, SparseCore 1:
  237.3 68.5 all-gather.5
  307.7 65.4 all-gather.9
  375.1 65.6 all-gather.7
where the time goes:
time: 488 us; the launch traced here: 486 us
  waiting for transfers between devices  209 us (43%)
  matrix products  132 us (27%)
  local copies, waits for them, and re-layouts  77.3 us (16%)
  other arithmetic  36.1 us (7%)
  between operations  15.8 us (3%)
  blocking collectives  9.14 us (2%)
  starting transfers between devices  5.52 us (1%)
    dynamic_slice x80, local copies, waits for them, and re-layouts, on_device(): lax.scan(page_step, start_memory, (query_rows, key_rows, value_matrix, de...  70.5 us
    all_gather x1, waiting for transfers between devices, on_device(): up_part = widen(lax.all_gather(up_weight, 'req', axis=0, tiled=True))  67.5 us
    all_gather x1, waiting for transfers between devices, on_device(): lax.all_gather(down_weight, 'req', axis=1, tiled=True)  55.4 us
    dot_general x16, matrix products, page_step(): jnp.einsum('lte,ltb->leb', weighted_rows, value_matrix, precision=TOP_PRE...  35.4 us
    all_gather x1, waiting for transfers between devices, on_device(): gate_part = widen(lax.all_gather(gate_weight, 'req', axis=0, tiled=True))  31.7 us
    psum x1, waiting for transfers between devices, on_device(): lax.psum(partial_value.astype(jnp.bfloat16), 'hid').astype(jnp.float32)  29.5 us
    dot_general x16, matrix products, page_step(): jnp.einsum('eow,ews->eos', raised_rows, memory_state, precision=TOP_PRECI...  29 us
    dot_general x1, matrix products, on_device(): jnp.dot(hidden, lax.all_gather(down_weight, 'req', axis=1, tiled=True), p...  20.9 us
  transfers between devices with their start and end apart: 7, of which 6 were waited for; matrix products, arithmetic and copies ran while one was open for 8% of the time, Pallas kernels for 0%

commit v1 on v0

v1 whole, which is shorter than its diff:
```python
import functools

import jax
import jax.numpy as jnp
from jax import lax
from jax.experimental import pallas as pl
from jax.experimental.pallas import tpu as pltpu
from jax.sharding import PartitionSpec as P

HK = 256
HV = 512
KCONV = 4
PAGE = 64
CONVW = 1024
EPSILON = 1e-06
TILE = 256
PAGES_T = TILE // PAGE
RIM = 16
BF16 = jnp.bfloat16
F32 = jnp.float32
VMEM_LIMIT = 56 * 1024 * 1024


def params():
    return pltpu.CompilerParams(
        dimension_semantics=("arbitrary",), vmem_limit_bytes=VMEM_LIMIT
    )


def cost(flops, moved):
    return pl.CostEstimate(flops=flops, bytes_accessed=moved, transcendentals=0)


def fixed(shape):
    return pl.BlockSpec(
        shape, lambda *_: (0,) * len(shape), pipeline_mode=pl.Buffered(1)
    )


def whole_smem():
    return pl.BlockSpec(memory_space=pltpu.SMEM)


def dot(a, b):
    return jnp.dot(a, b, preferred_element_type=F32)


def dot_nt(a, b):
    return lax.dot_general(a, b, (((1,), (1,)), ((), ())), preferred_element_type=F32)


def dot_tn(a, b):
    return lax.dot_general(a, b, (((0,), (0,)), ((), ())), preferred_element_type=F32)


def silu(x):
    return x / (1.0 + jnp.exp(-x))


def column(row):
    return jnp.transpose(jnp.broadcast_to(row, (128, row.shape[1])))[:, :1]


def normalised(x, gain):
    return x * lax.rsqrt(jnp.mean(x * x, axis=-1, keepdims=True) + EPSILON) * gain


def front_kernel(
    carried_ref, tokens_ref, rim_ref, gain_ref, project_ref, gate_ref, down_ref, up_ref, bias_ref,
    conv_ref, raised_ref, lowered_ref, weighted_ref, value_ref, ends_ref, edges_ref, opening_ref,
    state_ref, decay_ref, carry, state, decay,
):
    step = pl.program_id(0)

    @pl.when(step == 0)
    def _():
        state[...] = jnp.zeros_like(state)
        decay[...] = jnp.ones_like(decay)

    gain = gain_ref[...].astype(F32)
    rows = jnp.concatenate([tokens_ref[...], rim_ref[...]], axis=0).astype(F32)
    normed_all = normalised(rows, gain).astype(BF16)
    normed = normed_all[:TILE]
    projected_low = dot(normed_all, project_ref[...]).astype(BF16)
    projected = projected_low[:TILE].astype(F32)
    rim = projected_low[TILE:].astype(F32)[RIM - 8 :]
    previous = jnp.where(step == 0, rim, carry[...])
    carry[...] = projected[TILE - 8 :]
    opening_ref[...] = silu(dot(normed, gate_ref[...])).astype(BF16)

    lowrank = dot(normed, down_ref[...]).astype(BF16)
    logits = dot(lowrank, up_ref[...]) + bias_ref[...]
    decay_log = (jnp.minimum(logits, 0.0) - jnp.log1p(jnp.exp(-jnp.abs(logits)))) / 16.0
    row = lax.broadcasted_iota(jnp.int32, (TILE, TILE), 0)
    col = lax.broadcasted_iota(jnp.int32, (TILE, TILE), 1)
    lower = jnp.where((row >= col) & ((row // PAGE) == (col // PAGE)), 1.0, 0.0).astype(F32)
    sums = jnp.dot(lower, decay_log, preferred_element_type=F32, precision=lax.Precision.HIGHEST)

    taps = conv_ref[...].astype(F32)
    suffix = jnp.ones((1, HK), F32)
    pieces = [None] * PAGES_T
    for j in reversed(range(PAGES_T)):
        carried = carried_ref[0, step * PAGES_T + j]
        now = projected[j * PAGE : (j + 1) * PAGE]
        before = previous if j == 0 else projected[j * PAGE - 8 : j * PAGE]
        widened = jnp.concatenate([before * carried, now], axis=0)
        mixed = taps[0:1] * now
        for i in range(1, KCONV):
            mixed = mixed + taps[i : i + 1] * widened[8 - i : 8 - i + PAGE]
        query = silu(mixed[:, :HK])
        key = silu(mixed[:, HK : 2 * HK]) * HK ** (-0.5)
        value = mixed[:, 2 * HK :].astype(BF16)
        sums_j = sums[j * PAGE : (j + 1) * PAGE]
        end = sums_j[PAGE - 1 :]
        weighted = key * jnp.exp(end - sums_j)
        span = pl.ds(j * PAGE, PAGE)
        raised_ref[span, :] = (query * jnp.exp(sums_j)).astype(BF16)
        lowered_ref[span, :] = (key * jnp.exp(-sums_j)).astype(BF16)
        weighted_ref[span, :] = weighted.astype(BF16)
        value_ref[span, :] = value
        kept = jnp.exp(end)
        ends_ref[j] = jnp.broadcast_to(kept, (8, HK))
        edges_ref[j] = projected_low[(j + 1) * PAGE - (KCONV - 1) : (j + 1) * PAGE]
        pieces[j] = ((weighted * suffix).astype(BF16), value)
        suffix = suffix * (kept * carried)
    keys = jnp.concatenate([p[0] for p in pieces], axis=0)
    values = jnp.concatenate([p[1] for p in pieces], axis=0)
    state[...] = column(suffix) * state[...] + dot_tn(keys, values)
    decay[...] = decay[...] * suffix

    @pl.when(step == pl.num_programs(0) - 1)
    def _():
        state_ref[...] = state[...].astype(BF16)
        decay_ref[...] = decay[...]


def front(carried, tokens, rim, gain, project, gate, down, up, bias, conv):
    count, width = tokens.shape
    rank = down.shape[1]
    pages = count // PAGE
    rows = lambda n: pl.BlockSpec((TILE, n), lambda i: (i, 0))
    shape = jax.ShapeDtypeStruct
    return pl.pallas_call(
        front_kernel,
        name="front",
        grid=(count // TILE,),
        in_specs=[
            whole_smem(), rows(width), fixed((RIM, width)), fixed((1, width)),
            fixed((width, CONVW)), fixed((width, HV)), fixed((width, rank)), fixed((rank, HK)),
            fixed((1, HK)), fixed((KCONV, CONVW)),
        ],
        out_specs=[
            rows(HK), rows(HK), rows(HK), rows(HV),
            pl.BlockSpec((PAGES_T, 8, HK), lambda i: (i, 0, 0)),
            pl.BlockSpec((PAGES_T, KCONV - 1, CONVW), lambda i: (i, 0, 0)),
            rows(HV), fixed((HK, HV)), fixed((8, HK)),
        ],
        out_shape=[
            shape((count, HK), BF16), shape((count, HK), BF16), shape((count, HK), BF16),
            shape((count, HV), BF16), shape((pages, 8, HK), F32),
            shape((pages, KCONV - 1, CONVW), BF16), shape((count, HV), BF16),
            shape((HK, HV), BF16), shape((8, HK), F32),
        ],
        scratch_shapes=[
            pltpu.VMEM((8, CONVW), F32), pltpu.VMEM((HK, HV), F32), pltpu.VMEM((8, HK), F32)
        ],
        compiler_params=params(),
        cost_estimate=cost(1000, 1000),
    )(carried, tokens, rim, gain, project, gate, down, up, bias, conv)


def pages_kernel(
    carried_ref, raised_ref, lowered_ref, weighted_ref, value_ref, ends_ref, opening_ref, gain_ref,
    one_ref, two_ref, three_ref, decay_one_ref, decay_two_ref, states_ref, gated_ref, memory,
):
    step = pl.program_id(0)

    @pl.when(step == 0)
    def _():
        far = two_ref[...].astype(F32) + column(decay_two_ref[:1]) * three_ref[...].astype(F32)
        memory[...] = one_ref[...].astype(F32) + column(decay_one_ref[:1]) * far

    row = lax.broadcasted_iota(jnp.int32, (PAGE, PAGE), 0)
    col = lax.broadcasted_iota(jnp.int32, (PAGE, PAGE), 1)
    gain = gain_ref[...].astype(F32)
    held = memory[...]
    for j in range(PAGES_T):
        span = pl.ds(j * PAGE, PAGE)
        raised, value = raised_ref[span, :], value_ref[span, :]
        held = held * carried_ref[0, step * PAGES_T + j]
        scores = dot_nt(raised, lowered_ref[span, :])
        scores = jnp.where(row >= col, scores, 0.0).astype(BF16)
        attended = dot(scores, value) + dot(raised, held.astype(BF16))
        held = column(ends_ref[j][:1]) * held + dot_tn(weighted_ref[span, :], value)
        states_ref[j, 0] = held.astype(BF16)
        gated = normalised(attended, gain) * opening_ref[span, :].astype(F32)
        gated_ref[span, :] = gated.astype(BF16)
    memory[...] = held


def pages(carried, raised, lowered, weighted, value, ends, opening, gain, one, two, three, decay_one, decay_two):
    count = raised.shape[0]
    total = count // PAGE
    rows = lambda n: pl.BlockSpec((TILE, n), lambda i: (i, 0))
    return pl.pallas_call(
        pages_kernel,
        name="pages",
        grid=(count // TILE,),
        in_specs=[
            whole_smem(), rows(HK), rows(HK), rows(HK), rows(HV),
            pl.BlockSpec((PAGES_T, 8, HK), lambda i: (i, 0, 0)), rows(HV), fixed((1, HV)),
            fixed((HK, HV)), fixed((HK, HV)), fixed((HK, HV)), fixed((8, HK)), fixed((8, HK)),
        ],
        out_specs=[
            pl.BlockSpec((PAGES_T, 1, HK, HV), lambda i: (i, 0, 0, 0)), rows(HV),
        ],
        out_shape=[
            jax.ShapeDtypeStruct((total, 1, HK, HV), BF16),
            jax.ShapeDtypeStruct((count, HV), BF16),
        ],
        scratch_shapes=[pltpu.VMEM((HK, HV), F32)],
        compiler_params=params(),
        cost_estimate=cost(1000, 1000),
    )(carried, raised, lowered, weighted, value, ends, opening, gain, one, two, three, decay_one, decay_two)


def mix_kernel(tokens_ref, own_ref, other_ref, own_weight_ref, other_weight_ref, gain_ref, residual_ref, feed_ref):
    mixed = dot(own_ref[...], own_weight_ref[...]) + dot(other_ref[...], other_weight_ref[...])
    residual = (tokens_ref[...].astype(F32) + mixed).astype(BF16)
    residual_ref[...] = residual
    feed_ref[...] = normalised(residual.astype(F32), gain_ref[...].astype(F32)).astype(BF16)


def mix(tokens, own, other, own_weight, other_weight, gain):
    count, width = tokens.shape
    rows = lambda n: pl.BlockSpec((TILE, n), lambda i: (i, 0))
    return pl.pallas_call(
        mix_kernel,
        name="mix",
        grid=(count // TILE,),
        in_specs=[
            rows(width), rows(HV), rows(HV), fixed((HV, width)), fixed((HV, width)), fixed((1, width)),
        ],
        out_specs=[rows(width), rows(width)],
        out_shape=[jax.ShapeDtypeStruct((count, width), BF16)] * 2,
        compiler_params=params(),
        cost_estimate=cost(1000, 1000),
    )(tokens, own, other, own_weight, other_weight, gain)


def widen_kernel(places, offset_ref, feed_ref, *refs):
    out_ref = refs[-1]
    sums = []
    slot = 0
    for matrix in places:
        total = None
        for size in matrix:
            start = pl.multiple_of(offset_ref[0, slot], 128)
            part = dot(feed_ref[:, pl.ds(start, size)], refs[slot][...])
            total = part if total is None else total + part
            slot += 1
        sums.append(total)
    out_ref[...] = (silu(sums[0]) * sums[1]).astype(BF16)


def widen(feed, matrices):
    count, width = feed.shape
    pieces = [piece for matrix in matrices for piece, _ in matrix]
    offsets = jnp.stack([jnp.asarray(at, jnp.int32) for matrix in matrices for _, at in matrix])
    places = [[piece.shape[0] for piece, _ in matrix] for matrix in matrices]
    hidden = pieces[0].shape[1]
    wide = 256
    return pl.pallas_call(
        functools.partial(widen_kernel, places),
        name="widen",
        grid=(pl.cdiv(hidden, wide),),
        in_specs=[whole_smem(), fixed((count, width))]
        + [pl.BlockSpec((piece.shape[0], wide), lambda i: (0, i)) for piece in pieces],
        out_specs=pl.BlockSpec((count, wide), lambda i: (0, i)),
        out_shape=jax.ShapeDtypeStruct((count, hidden), BF16),
        compiler_params=params(),
        cost_estimate=cost(1000, 1000),
    )(offsets[None], feed, *pieces)


def narrow_kernel(offset_ref, hidden_ref, *refs):
    out_ref = refs[-1]
    hidden = hidden_ref[...]
    for slot, ref in enumerate(refs[:-1]):
        start = pl.multiple_of(offset_ref[slot + 1], 128)
        out_ref[:, pl.ds(start, ref.shape[1])] = dot(hidden, ref[...]).astype(BF16)


def narrow(hidden, half, pieces, width):
    count, depth = hidden.shape
    rows = count // 2
    tiles = rows // TILE
    offsets = jnp.stack([jnp.asarray(at, jnp.int32) for at in [half] + [at for _, at in pieces]])
    whole = lambda shape: pl.BlockSpec(
        shape, lambda i, s: (0, 0), pipeline_mode=pl.Buffered(1)
    )
    return pl.pallas_call(
        narrow_kernel,
        name="narrow",
        grid_spec=pltpu.PrefetchScalarGridSpec(
            num_scalar_prefetch=1,
            grid=(tiles,),
            in_specs=[pl.BlockSpec((TILE, depth), lambda i, s: (s[0] * tiles + i, 0))]
            + [whole(piece.shape) for piece, _ in pieces],
            out_specs=pl.BlockSpec((TILE, width), lambda i, s: (i, 0)),
        ),
        out_shape=jax.ShapeDtypeStruct((rows, width), BF16),
        compiler_params=params(),
        cost_estimate=cost(1000, 1000),
    )(offsets, hidden, *[piece for piece, _ in pieces])


def page_segments(page_counts, starts, total_pages):
    position = jnp.arange(total_pages, dtype=jnp.int32)
    inside = (position[None, :] >= starts[:, None]) & (
        position[None, :] < starts[:, None] + page_counts[:, None]
    )
    labels = jnp.arange(1, page_counts.shape[0] + 1, dtype=jnp.int32)
    segment = jnp.sum(jnp.where(inside, labels[:, None], 0), axis=0) - 1
    earlier = jnp.concatenate([jnp.full((1,), -1, jnp.int32), segment[:-1]])
    return ((segment == earlier) & (segment >= 0)).astype(F32)


def shifted(value, steps):
    count = lax.axis_size("seq")
    return lax.ppermute(value, "seq", [(i, i + steps) for i in range(count - steps)])


def swapped(value, axis, flip):
    count = lax.axis_size(axis)
    return lax.ppermute(value, axis, [(i, i ^ flip) for i in range(count)])


def after(value, *others):
    return lax.optimization_barrier((value, *others))[0]


def on_device(
    tokens, attention_gain, project_weight, conv_weight, decay_down, decay_up, decay_bias,
    output_gate, head_gain, output_weight, mixer_gain, gate_weight, up_weight, down_weight,
    prompt_pages, prompt_start,
):
    count, width = tokens.shape
    page_count = count // PAGE
    seq_index, hid_index = lax.axis_index("seq"), lax.axis_index("hid")
    req_index = lax.axis_index("req")
    two_by_two = lax.axis_size("req") == 4 and lax.axis_size("seq") % 2 == 0
    group_pages = page_count * lax.axis_size("seq")
    flags = page_segments(prompt_pages[0], prompt_start[0], group_pages)
    carried = lax.dynamic_slice_in_dim(flags, seq_index * page_count, page_count)[None]

    rim = shifted(tokens[-RIM:], 1)
    other_output = swapped(output_weight, "hid", 1)

    depth = gate_weight.shape[0]
    half = depth // 2
    if two_by_two:
        parity = lax.rem(seq_index, 2)
        up_mine = lax.dynamic_slice_in_dim(up_weight, parity * half, half, 0)
        down_mine = lax.dynamic_slice_in_dim(down_weight, parity * half, half, 1)
        gate_0, gate_1 = gate_weight[:half], gate_weight[half:]
        up_a, up_b = swapped(up_mine, "req", 1), swapped(up_mine, "req", 2)
        down_mine = after(down_mine, rim)
        down_a, down_b = swapped(down_mine, "req", 1), swapped(down_mine, "req", 2)

    front_out = front(
        carried, tokens, rim, attention_gain[None], project_weight, output_gate, decay_down,
        decay_up, decay_bias[None], conv_weight,
    )
    raised, lowered, weighted, value, ends, edges, opening, state, decay = front_out
    one, two, three = (shifted(state, i) for i in (1, 2, 3))
    decay_one, decay_two = shifted(decay, 1), shifted(decay, 2)
    if two_by_two:
        up_a, up_b, raised = lax.optimization_barrier((up_a, up_b, raised))
        up_c = swapped(up_b, "req", 1)
        far_a, far_b = swapped(up_a, "seq", 1), swapped(up_b, "seq", 1)
        gate_0 = after(gate_0, up_a, up_b)
        gate_a0, gate_b0 = swapped(gate_0, "req", 1), swapped(gate_0, "req", 2)
    states, gated = pages(
        carried, raised, lowered, weighted, value, ends, opening, head_gain[None],
        one, two, three, decay_one, decay_two,
    )
    other_gated = swapped(gated, "hid", 1)
    if two_by_two:
        up_c, down_a, down_b, gated = lax.optimization_barrier((up_c, down_a, down_b, gated))
        down_c = swapped(down_a, "req", 2)
        far_c = swapped(up_c, "seq", 1)
        gate_1 = after(gate_1, down_a, down_b)
        gate_a1, gate_b1 = swapped(gate_1, "req", 1), swapped(gate_1, "req", 2)
        gate_c0 = swapped(gate_b0, "req", 1)
        gate_c1 = swapped(gate_a1, "req", 2)
        down_far = [swapped(piece, "seq", 1) for piece in (down_a, down_b, down_c)]
    residual, feed = mix(tokens, gated, other_gated, output_weight, other_output, mixer_gain[None])

    if two_by_two:
        base = [(req_index ^ flip) * depth for flip in (0, 1, 2, 3)]
        mine, theirs = parity * half, (1 - parity) * half
        gate_list = [(gate_weight, base[0])]
        for at, pair in zip(base[1:], ((gate_a0, gate_a1), (gate_b0, gate_b1), (gate_c0, gate_c1))):
            gate_list += [(pair[0], at), (pair[1], at + half)]
        up_list = [(up_weight, base[0])]
        down_list = [(down_weight, base[0])]
        for at, near, far in zip(base[1:], (up_a, up_b, up_c), (far_a, far_b, far_c)):
            up_list += [(near, at + mine), (far, at + theirs)]
        for at, near, far in zip(base[1:], (down_a, down_b, down_c), down_far):
            down_list += [(near, at + mine), (far, at + theirs)]
    else:
        gate_list = [(lax.all_gather(gate_weight, "req", axis=0, tiled=True), 0)]
        up_list = [(lax.all_gather(up_weight, "req", axis=0, tiled=True), 0)]
        down_list = [(lax.all_gather(down_weight, "req", axis=1, tiled=True), 0)]

    hidden = widen(feed, (gate_list, up_list))
    theirs_sum = narrow(hidden, 1 - hid_index, down_list, width)
    received = swapped(theirs_sum, "hid", 1)
    own_sum = narrow(hidden, hid_index, down_list, width)
    own_rows = lax.dynamic_slice_in_dim(residual, hid_index * (count // 2), count // 2, 0)
    result = (
        own_rows.astype(F32) + (own_sum.astype(F32) + received.astype(F32))
    ).astype(BF16)
    return result, states, edges


def solution(mesh):
    return jax.shard_map(
        on_device,
        mesh=mesh,
        in_specs=(
            P(("req", "seq"), None),
            P(),
            P(None, "hid"),
            P(None, "hid"),
            P(),
            P(None, "hid"),
            P("hid"),
            P(None, "hid"),
            P(),
            P("hid", None),
            P(),
            P("req", "hid"),
            P("req", "hid"),
            P("hid", "req"),
            P("req", None),
            P("req", None),
        ),
        out_specs=(
            P(("req", "seq", "hid"), None),
            P(("req", "seq"), "hid", None, None),
            P(("req", "seq"), None, "hid"),
        ),
        check_vma=False,
    )
```

time: 488 us -> 196 us (0.40)
  waiting for transfers between devices: 209 us -> 62.3 us
  matrix products: 132 us -> 0 us
  Pallas kernels: 0 us -> 74.1 us
  local copies, waits for them, and re-layouts: 77.3 us -> 12 us
  starting transfers between devices: 5.52 us -> 41.5 us
  other arithmetic: 36.1 us -> 4.35 us
  between operations: 15.8 us -> 1.02 us
  blocking collectives: 9.14 us -> 0 us
    all_gather x4 -> x0, waiting for transfers between devices: 172 us -> none  [the longest x1 67.5 us: on_device(): up_part = widen(lax.all_gather(up_weight, 'req', axis=0, tiled=True))]
    dot_general x71 -> x0, matrix products: 132 us -> none  [the longest x16 35.4 us: page_step(): jnp.einsum('lte,ltb->leb', weighted_rows, value_matrix, precision=TOP_PRE...]
    pallas_call x0 -> x6, Pallas kernels: none -> 74.1 us  [the longest x1 19.6 us: front(): pl.pallas_call(front_kernel, name='front', grid=(count // TILE,), in_spec...]
    dynamic_slice x81 -> x2, local copies, waits for them, and re-layouts: 70.5 us -> 2.15 us  [the longest x1 1.17 us: on_device(): up_mine = lax.dynamic_slice_in_dim(up_weight, parity * half, half, 0)]
    ppermute x1 -> x27, waiting for transfers between devices: 0.01 us -> 62.3 us  [the longest x21 53.5 us: swapped(): return lax.ppermute(value, axis, [(i, i ^ flip) for i in range(count)])]
    ppermute x1 -> x27, starting transfers between devices: 5.06 us -> 41.5 us  [the longest x21 25.7 us: swapped(): return lax.ppermute(value, axis, [(i, i ^ flip) for i in range(count)])]
    psum x1 -> x0, waiting for transfers between devices: 29.5 us -> none  [on_device(): lax.psum(partial_value.astype(jnp.bfloat16), 'hid').astype(jnp.float32)]
    reduce_sum x2 -> x0, other arithmetic: 11 us -> none  [rms_scaled(): jnp.mean(values * values, axis=-1, keepdims=True) + EPSILON]
  transfers between devices with their start and end apart: 7 -> 27, of which waited for: 6 -> 8; matrix products, arithmetic and copies ran while one was open for 8% -> 5% of each run, Pallas kernels for 0% -> 34%
where the time goes in v1:
time: 196 us; the launch traced here: 195 us
  Pallas kernels  74.1 us (38%)
  waiting for transfers between devices  62.3 us (32%)
  starting transfers between devices  41.5 us (21%)
  local copies, waits for them, and re-layouts  12 us (6%)
  other arithmetic  4.35 us (2%)
    ppermute x21, waiting for transfers between devices, swapped(): return lax.ppermute(value, axis, [(i, i ^ flip) for i in range(count)])  53.5 us
    ppermute x21, starting transfers between devices, swapped(): return lax.ppermute(value, axis, [(i, i ^ flip) for i in range(count)])  25.7 us
    pallas_call x1, Pallas kernels, front(): pl.pallas_call(front_kernel, name='front', grid=(count // TILE,), in_spec...  19.6 us
    pallas_call x1, Pallas kernels, widen(): pl.pallas_call(functools.partial(widen_kernel, places), name='widen', gri...  18.7 us
    pallas_call x2, Pallas kernels, narrow(): pl.pallas_call(narrow_kernel, name='narrow', grid_spec=pltpu.PrefetchScal...  17.1 us
    ppermute x6, starting transfers between devices, shifted(): lax.ppermute(value, 'seq', [(i, i + steps) for i in range(count - steps)])  15.8 us
    pallas_call x1, Pallas kernels, mix(): pl.pallas_call(mix_kernel, name='mix', grid=(count // TILE,), in_specs=[r...  10.5 us
    ppermute x6, waiting for transfers between devices, shifted(): lax.ppermute(value, 'seq', [(i, i + steps) for i in range(count - steps)])  8.84 us
  transfers between devices with their start and end apart: 27, of which 8 were waited for; matrix products, arithmetic and copies ran while one was open for 5% of the time, Pallas kernels for 34%

profile of v1, /device:TPU:0, one launch (start us, length us, event | category | flops | bytes accessed | tf_op | source)
XLA Modules:
  0.0 195.2 jit_solution(17144693983806363836)
XLA Ops:
  1.8 3.0 %collective-permute-start = (bf16[256,1408]{1,0:T(8,128)(2,1)S(1)}, bf16[256,1408]{1,0:T(8,128)(2,1)S(1)}, u32[]{:S(2)}, u32[]{:S(2)}) collective-permute-start(bf16[256,1408]{1,0:T(8,128)(2,1)S(1)} %constant_dynamic-slice_fusion.1), channel_id=1, source_target_pairs={{0,8},{8,0},{16,24},{24,16},{1,9},{9,1},{17,25},{25,17},{2,10},{10... | collective-permute-start | bytes 2162696 | tf_op jit(solution)/shard_map/ppermute | solution.py:336
  7.2 3.5 %collective-permute-start.2 = (bf16[16,2048]{1,0:T(8,128)(2,1)S(1)}, bf16[16,2048]{1,0:T(8,128)(2,1)S(1)}, u32[]{:S(2)}, u32[]{:S(2)}) collective-permute-start(bf16[16,2048]{1,0:T(8,128)(2,1)S(1)} %slice.13), channel_id=1, source_target_pairs={{0,2},{2,4},{4,6},{1,3},{3,5},{5,7},{8,10},{10,12},{12,14},{9,11},... | collective-permute-start | bytes 196616 | tf_op jit(solution)/shard_map/ppermute | solution.py:331
  10.7 1.8 copy.21.down_ref
  14.6 19.6 %front.1 = (bf16[1024,256]{1,0:T(8,128)(2,1)}, bf16[1024,256]{1,0:T(8,128)(2,1)}, bf16[1024,256]{1,0:T(8,128)(2,1)}, bf16[1024,512]{1,0:T(8,128)(2,1)}, f32[16,8...) custom-call(f32[1,16]{1,0:T(1,128)} %dynamic-slice_bitcast_fusion.ca, ...), custom_call_target="tpu_custom_call" | custom-call | flops 1000 | bytes 1000 | tf_op jit(solution)/shard_map/front/pallas_call | solution.py:143
  34.3 4.8 %collective-permute-start.10 = (f32[8,256]{1,0:T(8,128)}, f32[8,256]{1,0:T(8,128)S(1)}, u32[]{:S(2)}, u32[]{:S(2)}) collective-permute-start(f32[8,256]{1,0:T(8,128)} %get-tuple-element.36), channel_id=1, source_target_pairs={{0,4},{2,6},{1,5},{3,7},{8,12},{10,14},{9,13},{11,15},{16,20},{18,... | collective-permute-start | bytes 24584 | tf_op jit(solution)/shard_map/ppermute | solution.py:331
  40.0 2.9 %collective-permute-start.6 = (bf16[256,512]{1,0:T(8,128)(2,1)}, bf16[256,512]{1,0:T(8,128)(2,1)S(1)}, u32[]{:S(2)}, u32[]{:S(2)}) collective-permute-start(bf16[256,512]{1,0:T(8,128)(2,1)} %get-tuple-element.35), channel_id=1, source_target_pairs={{0,2},{2,4},{4,6},{1,3},{3,5},{5,7},{8,10},{10,12},{12,14},{9,11},... | collective-permute-start | bytes 786440 | tf_op jit(solution)/shard_map/ppermute | solution.py:331
  44.2 2.0 %collective-permute-start.8 = (bf16[256,512]{1,0:T(8,128)(2,1)}, bf16[256,512]{1,0:T(8,128)(2,1)S(1)}, u32[]{:S(2)}, u32[]{:S(2)}) collective-permute-start(bf16[256,512]{1,0:T(8,128)(2,1)} %get-tuple-element.35), channel_id=1, source_target_pairs={{0,6},{1,7},{8,14},{9,15},{16,22},{17,23},{24,30},{25,31}} | collective-permute-start | bytes 786440 | tf_op jit(solution)/shard_map/ppermute | solution.py:331
  49.6 8.8 %collective-permute-done.9.decay_one_ref = f32[8,256]{1,0:T(8,128)S(1)} collective-permute-done((f32[8,256]{1,0:T(8,128)}, f32[8,256]{1,0:T(8,128)S(1)}, u32[]{:S(2)}, u32[]{:S(2)}) %collective-permute-start.9) | collective-permute-done | bytes 8224 | tf_op jit(solution)/shard_map/ppermute | solution.py:331
  61.7 8.2 %pages.1 = (bf16[16,1,256,512]{3,2,1,0:T(8,128)(2,1)}, bf16[1024,512]{1,0:T(8,128)(2,1)}) custom-call(f32[1,16]{1,0:T(1,128)} %dynamic-slice_bitcast_fusion.carried_ref, bf16[1024,256]{1,0:T(8,128)(2,1)} %get-tuple-element.29.raised_ref, bf16[1024,256]{1,0:T(8,128)(2,1)} %get-tuple-element.30.lowered_ref, bf16[1024,256]{1,0:T(8,128)(2,1)} %get-tuple-element.31.weighted_ref, ...), custom_call_target="tpu_custom_call" | custom-call | flops 1000 | bytes 1000 | tf_op jit(solution)/shard_map/pages/pallas_call | solution.py:205
  70.4 7.2 %collective-permute-done.5.refs_3_ = bf16[1408,256]{1,0:T(8,128)(2,1)S(1)} collective-permute-done((bf16[1408,256]{1,0:T(8,128)(2,1)}, bf16[1408,256]{1,0:T(8,128)(2,1)S(1)}, u32[]{:S(2)}, u32[]{:S(2)}) %collective-permute-start.5) | collective-permute-done | bytes 720928 | tf_op jit(solution)/shard_map/ppermute | solution.py:336
  78.2 4.4 %collective-permute-done.3.refs_12_ = bf16[256,1408]{1,0:T(8,128)(2,1)} collective-permute-done((bf16[256,1408]{1,0:T(8,128)(2,1)S(1)}, bf16[256,1408]{1,0:T(8,128)(2,1)}, u32[]{:S(2)}, u32[]{:S(2)}) %collective-permute-start.3) | collective-permute-done | bytes 720928 | tf_op jit(solution)/shard_map/ppermute | solution.py:336
  84.2 5.2 %collective-permute-done.15.refs_3_ = bf16[256,1408]{1,0:T(8,128)(2,1)} collective-permute-done((bf16[256,1408]{1,0:T(8,128)(2,1)}, bf16[256,1408]{1,0:T(8,128)(2,1)}, u32[]{:S(2)}, u32[]{:S(2)}) %collective-permute-start.15) | collective-permute-done | bytes 720928 | tf_op jit(solution)/shard_map/ppermute | solution.py:336
  89.4 6.4 %collective-permute-start.20 = (bf16[256,1408]{1,0:T(8,128)(2,1)S(1)}, bf16[256,1408]{1,0:T(8,128)(2,1)S(1)}, u32[]{:S(2)}, u32[]{:S(2)}) collective-permute-start(bf16[256,1408]{1,0:T(8,128)(2,1)S(1)} %collective-permute-done.1.refs_10_), channel_id=1, source_target_pairs={{0,2},{2,0},{4,6},{6,4},{1,3},{3,1},{5,7},{7,5},{8,10},{10,8},{12,... | collective-permute-start | bytes 2162696 | tf_op jit(solution)/shard_map/ppermute | solution.py:336
  96.8 12.7 %collective-permute-done.20.refs_11_ = bf16[256,1408]{1,0:T(8,128)(2,1)S(1)} collective-permute-done((bf16[256,1408]{1,0:T(8,128)(2,1)S(1)}, bf16[256,1408]{1,0:T(8,128)(2,1)S(1)}, u32[]{:S(2)}, u32[]{:S(2)}) %collective-permute-start.20) | collective-permute-done | bytes 720928 | tf_op jit(solution)/shard_map/ppermute | solution.py:336
  111.0 2.0 %collective-permute-start.21 = (bf16[256,1408]{1,0:T(8,128)(2,1)}, bf16[256,1408]{1,0:T(8,128)(2,1)}, u32[]{:S(2)}, u32[]{:S(2)}) collective-permute-start(bf16[256,1408]{1,0:T(8,128)(2,1)} %collective-permute-done.3.refs_12_), channel_id=1, source_target_pairs={{0,2},{2,0},{4,6},{6,4},{1,3},{3,1},{5,7},{7,5},{8,10},{10,8},{12,... | collective-permute-start | bytes 2162696 | tf_op jit(solution)/shard_map/ppermute | solution.py:336
  114.6 11.3 %collective-permute-done.17.refs_5_ = bf16[256,1408]{1,0:T(8,128)(2,1)S(1)} collective-permute-done((bf16[256,1408]{1,0:T(8,128)(2,1)}, bf16[256,1408]{1,0:T(8,128)(2,1)S(1)}, u32[]{:S(2)}, u32[]{:S(2)}) %collective-permute-start.17) | collective-permute-done | bytes 720928 | tf_op jit(solution)/shard_map/ppermute | solution.py:336
  126.6 3.0 %collective-permute-done.24.refs_5_ = bf16[1408,256]{1,0:T(8,128)(2,1)S(1)} collective-permute-done((bf16[1408,256]{1,0:T(8,128)(2,1)S(1)}, bf16[1408,256]{1,0:T(8,128)(2,1)S(1)}, u32[]{:S(2)}, u32[]{:S(2)}) %collective-permute-start.24) | collective-permute-done | bytes 720928 | tf_op jit(solution)/shard_map/ppermute | solution.py:336
  129.6 2.0 %collective-permute-start.25 = (bf16[1408,256]{1,0:T(8,128)(2,1)S(1)}, bf16[1408,256]{1,0:T(8,128)(2,1)}, u32[]{:S(2)}, u32[]{:S(2)}) collective-permute-start(bf16[1408,256]{1,0:T(8,128)(2,1)S(1)} %collective-permute-done.24.refs_5_), channel_id=1, source_target_pairs={{0,2},{2,0},{4,6},{6,4},{1,3},{3,1},{5,7},{7,5},{8,10},{10,8},{12,... | collective-permute-start | bytes 2162696 | tf_op jit(solution)/shard_map/ppermute | solution.py:336
  133.6 10.5 %mix.1 = (bf16[1024,2048]{1,0:T(8,128)(2,1)}, bf16[1024,2048]{1,0:T(8,128)(2,1)}) custom-call(bf16[1024,2048]{1,0:T(8,128)(2,1)} %tokens_ref.3, bf16[1024,512]{1,0:T(8,128)(2,1)} %get-tuple-element.38.own_ref, bf16[1024,512]{1,0:T(8,128)(2,1)} %copy-done.8, bf16[512,2048]{1,0:T(8,128)(2,1)} %own_weight_ref.1, bf16[512,2048]{1,0:T(8,128)(2,1)} %copy-done.7, ...), custom_call_target="tpu_custom_call" | custom-call | flops 1000 | bytes 1000 | tf_op jit(solution)/shard_map/mix/pallas_call | solution.py:237
  144.2 18.7 %widen.1.hidden_ref = bf16[1024,1408]{1,0:T(8,128)(2,1)} custom-call(s32[1,14]{1,0:T(1,128)} %bitcast.24, bf16[1024,2048]{1,0:T(8,128)(2,1)} %get-tuple-element.40.feed_ref, bf16[512,1408]{1,0:T(8,128)(2,1)} %refs_0_.3, bf16[256,1408]{1,0:T(8,128)(2,1)} %copy-done.12, bf16[256,1408]{1,0:T(8,128)(2,1)} %collective-permute-done.14.refs_2_, ...), custom_call_target="tpu_custom_call" | custom-call | flops 1000 | bytes 1000 | tf_op jit(solution)/shard_map/widen/pallas_call | solution.py:273
  162.9 9.7 %collective-permute-done.25.refs_6_ = bf16[1408,256]{1,0:T(8,128)(2,1)} collective-permute-done((bf16[1408,256]{1,0:T(8,128)(2,1)S(1)}, bf16[1408,256]{1,0:T(8,128)(2,1)}, u32[]{:S(2)}, u32[]{:S(2)}) %collective-permute-start.25) | collective-permute-done | bytes 720928 | tf_op jit(solution)/shard_map/ppermute | solution.py:336
  172.7 8.3 %narrow.3 = bf16[512,2048]{1,0:T(8,128)(2,1)} custom-call(s32[8]{0:T(128)} %stack.86.offset_ref, bf16[1024,1408]{1,0:T(8,128)(2,1)} %widen.1.hidden_ref, bf16[1408,512]{1,0:T(8,128)(2,1)} %refs_0_.5, bf16[1408,256]{1,0:T(8,128)(2,1)} %copy-done.2, bf16[1408,256]{1,0:T(8,128)(2,1)} %copy-done.5, bf16[1408,256]{1,0:T(8,128)(2,1)} %copy-done.3, ...), custom_call_target="tpu_custom_call" | custom-call | flops 1000 | bytes 1000 | tf_op jit(solution)/shard_map/narrow/pallas_call | solution.py:302
  182.3 8.8 %narrow.2 = bf16[512,2048]{1,0:T(8,128)(2,1)} custom-call(s32[8]{0:T(128)} %stack.77.offset_ref, bf16[1024,1408]{1,0:T(8,128)(2,1)} %widen.1.hidden_ref, bf16[1408,512]{1,0:T(8,128)(2,1)} %refs_0_.5, bf16[1408,256]{1,0:T(8,128)(2,1)} %copy-done.2, bf16[1408,256]{1,0:T(8,128)(2,1)} %copy-done.5, bf16[1408,256]{1,0:T(8,128)(2,1)} %copy-done.3, ...), custom_call_target="tpu_custom_call" | custom-call | flops 1000 | bytes 1000 | tf_op jit(solution)/shard_map/narrow/pallas_call | solution.py:302
  191.1 4.2 %add_convert_fusion = bf16[512,2048]{1,0:T(8,128)(2,1)} fusion(bf16[512,2048]{1,0:T(8,128)(2,1)S(1)} %collective-permute-done.26, bf16[512,2048]{1,0:T(8,128)(2,1)} %narrow.2, bf16[1024,2048]{1,0:T(8,128)(2,1)S(1)} %copy-done.9, s32[]{:T(128)S(6)} %select_n.17), kind=kLoop, calls=%fused_computation | loop fusion | flops 6291456 | bytes 8388612 | tf_op jit(solution)/shard_map/convert_element_type | solution.py:424
  (112 shorter events, 25.4 us)
Async XLA Ops:
  1.8 44.4 %collective-permute-start = (bf16[256,1408]{1,0:T(8,128)(2,1)S(1)}, bf16[256,1408]{1,0:T(8,128)(2,1)S(1)}, u32[]{:S(2)}, u32[]{:S(2)}) collective-permute-start(bf16[256,1408]{1,0:T(8,128)(2,1)S(1)} %constant_dynamic-slice_fusion.1), channel_id=1, source_target_pairs={{0,8},{8,0},{16,24},{24,16},{1,9},{9,1},{17,25},{25,17},{2,10},{10... | collective-permute-start | bytes 2162696 | tf_op jit(solution)/shard_map/ppermute | solution.py:336
  4.8 42.9 %collective-permute-start.1 = (bf16[256,1408]{1,0:T(8,128)(2,1)S(1)}, bf16[256,1408]{1,0:T(8,128)(2,1)S(1)}, u32[]{:S(2)}, u32[]{:S(2)}) collective-permute-start(bf16[256,1408]{1,0:T(8,128)(2,1)S(1)} %constant_dynamic-slice_fusion.1), channel_id=1, source_target_pairs={{0,16},{8,24},{16,0},{24,8},{1,17},{9,25},{17,1},{25,9},{2,18},{10... | collective-permute-start | bytes 2162696 | tf_op jit(solution)/shard_map/ppermute | solution.py:336
  40.0 18.9 %collective-permute-start.6 = (bf16[256,512]{1,0:T(8,128)(2,1)}, bf16[256,512]{1,0:T(8,128)(2,1)S(1)}, u32[]{:S(2)}, u32[]{:S(2)}) collective-permute-start(bf16[256,512]{1,0:T(8,128)(2,1)} %get-tuple-element.35), channel_id=1, source_target_pairs={{0,2},{2,4},{4,6},{1,3},{3,5},{5,7},{8,10},{10,12},{12,14},{9,11},... | collective-permute-start | bytes 786440 | tf_op jit(solution)/shard_map/ppermute | solution.py:331
  42.9 16.5 %collective-permute-start.7 = (bf16[256,512]{1,0:T(8,128)(2,1)}, bf16[256,512]{1,0:T(8,128)(2,1)S(1)}, u32[]{:S(2)}, u32[]{:S(2)}) collective-permute-start(bf16[256,512]{1,0:T(8,128)(2,1)} %get-tuple-element.35), channel_id=1, source_target_pairs={{0,4},{2,6},{1,5},{3,7},{8,12},{10,14},{9,13},{11,15},{16,20},{18,... | collective-permute-start | bytes 786440 | tf_op jit(solution)/shard_map/ppermute | solution.py:331
  44.2 16.7 %collective-permute-start.8 = (bf16[256,512]{1,0:T(8,128)(2,1)}, bf16[256,512]{1,0:T(8,128)(2,1)S(1)}, u32[]{:S(2)}, u32[]{:S(2)}) collective-permute-start(bf16[256,512]{1,0:T(8,128)(2,1)} %get-tuple-element.35), channel_id=1, source_target_pairs={{0,6},{1,7},{8,14},{9,15},{16,22},{17,23},{24,30},{25,31}} | collective-permute-start | bytes 786440 | tf_op jit(solution)/shard_map/ppermute | solution.py:331
  46.2 12.2 %collective-permute-start.9 = (f32[8,256]{1,0:T(8,128)}, f32[8,256]{1,0:T(8,128)S(1)}, u32[]{:S(2)}, u32[]{:S(2)}) collective-permute-start(f32[8,256]{1,0:T(8,128)} %get-tuple-element.36), channel_id=1, source_target_pairs={{0,2},{2,4},{4,6},{1,3},{3,5},{5,7},{8,10},{10,12},{12,14},{9,11},... | collective-permute-start | bytes 24584 | tf_op jit(solution)/shard_map/ppermute | solution.py:331
  47.7 22.2 %collective-permute-start.4 = (bf16[1408,256]{1,0:T(8,128)(2,1)}, bf16[1408,256]{1,0:T(8,128)(2,1)S(1)}, u32[]{:S(2)}, u32[]{:S(2)}) collective-permute-start(bf16[1408,256]{1,0:T(8,128)(2,1)} %constant_dynamic-slice_fusion), channel_id=1, source_target_pairs={{0,8},{8,0},{16,24},{24,16},{1,9},{9,1},{17,25},{25,17},{2,10},{10... | collective-permute-start | bytes 2162696 | tf_op jit(solution)/shard_map/ppermute | solution.py:336
  58.4 19.3 %collective-permute-start.5 = (bf16[1408,256]{1,0:T(8,128)(2,1)}, bf16[1408,256]{1,0:T(8,128)(2,1)S(1)}, u32[]{:S(2)}, u32[]{:S(2)}) collective-permute-start(bf16[1408,256]{1,0:T(8,128)(2,1)} %constant_dynamic-slice_fusion), channel_id=1, source_target_pairs={{0,16},{8,24},{16,0},{24,8},{1,17},{9,25},{17,1},{25,9},{2,18},{10... | collective-permute-start | bytes 2162696 | tf_op jit(solution)/shard_map/ppermute | solution.py:336
  58.9 23.7 %collective-permute-start.3 = (bf16[256,1408]{1,0:T(8,128)(2,1)S(1)}, bf16[256,1408]{1,0:T(8,128)(2,1)}, u32[]{:S(2)}, u32[]{:S(2)}) collective-permute-start(bf16[256,1408]{1,0:T(8,128)(2,1)S(1)} %collective-permute-done.1.refs_10_), channel_id=1, source_target_pairs={{0,8},{8,0},{16,24},{24,16},{1,9},{9,1},{17,25},{25,17},{2,10},{10... | collective-permute-start | bytes 2162696 | tf_op jit(solution)/shard_map/ppermute | solution.py:336
  59.4 29.9 %collective-permute-start.15 = (bf16[256,1408]{1,0:T(8,128)(2,1)}, bf16[256,1408]{1,0:T(8,128)(2,1)}, u32[]{:S(2)}, u32[]{:S(2)}) collective-permute-start(bf16[256,1408]{1,0:T(8,128)(2,1)} %get-tuple-element.42), channel_id=1, source_target_pairs={{0,16},{8,24},{16,0},{24,8},{1,17},{9,25},{17,1},{25,9},{2,18},{10... | collective-permute-start | bytes 2162696 | tf_op jit(solution)/shard_map/ppermute | solution.py:336
  61.0 50.0 %collective-permute-start.12 = (bf16[512,2048]{1,0:T(8,128)(2,1)S(1)}, bf16[512,2048]{1,0:T(8,128)(2,1)S(1)}, u32[]{:S(2)}, u32[]{:S(2)}) collective-permute-start(bf16[512,2048]{1,0:T(8,128)(2,1)S(1)} %copy-done.6), channel_id=1, source_target_pairs={{0,1},{1,0},{2,3},{3,2},{4,5},{5,4},{6,7},{7,6},{8,9},{9,8},{10,11... | collective-permute-start | bytes 6291464 | tf_op jit(solution)/shard_map/ppermute | solution.py:336
  69.9 40.5 %collective-permute-start.11 = (bf16[1024,512]{1,0:T(8,128)(2,1)}, bf16[1024,512]{1,0:T(8,128)(2,1)S(1)}, u32[]{:S(2)}, u32[]{:S(2)}) collective-permute-start(bf16[1024,512]{1,0:T(8,128)(2,1)} %get-tuple-element.38.own_ref), channel_id=1, source_target_pairs={{0,1},{1,0},{2,3},{3,2},{4,5},{5,4},{6,7},{7,6},{8,9},{9,8},{10,11... | collective-permute-start | bytes 3145736 | tf_op jit(solution)/shard_map/ppermute | solution.py:336
  77.7 18.1 %collective-permute-start.13 = (bf16[256,1408]{1,0:T(8,128)(2,1)}, bf16[256,1408]{1,0:T(8,128)(2,1)S(1)}, u32[]{:S(2)}, u32[]{:S(2)}) collective-permute-start(bf16[256,1408]{1,0:T(8,128)(2,1)} %get-tuple-element.42), channel_id=1, source_target_pairs={{0,8},{8,0},{16,24},{24,16},{1,9},{9,1},{17,25},{25,17},{2,10},{10... | collective-permute-start | bytes 2162696 | tf_op jit(solution)/shard_map/ppermute | solution.py:336
  82.6 13.7 %collective-permute-start.19 = (bf16[256,1408]{1,0:T(8,128)(2,1)S(1)}, bf16[256,1408]{1,0:T(8,128)(2,1)S(1)}, u32[]{:S(2)}, u32[]{:S(2)}) collective-permute-start(bf16[256,1408]{1,0:T(8,128)(2,1)S(1)} %collective-permute-done.refs_8_), channel_id=1, source_target_pairs={{0,2},{2,0},{4,6},{6,4},{1,3},{3,1},{5,7},{7,5},{8,10},{10,8},{12,... | collective-permute-start | bytes 2162696 | tf_op jit(solution)/shard_map/ppermute | solution.py:336
  89.4 20.1 %collective-permute-start.20 = (bf16[256,1408]{1,0:T(8,128)(2,1)S(1)}, bf16[256,1408]{1,0:T(8,128)(2,1)S(1)}, u32[]{:S(2)}, u32[]{:S(2)}) collective-permute-start(bf16[256,1408]{1,0:T(8,128)(2,1)S(1)} %collective-permute-done.1.refs_10_), channel_id=1, source_target_pairs={{0,2},{2,0},{4,6},{6,4},{1,3},{3,1},{5,7},{7,5},{8,10},{10,8},{12,... | collective-permute-start | bytes 2162696 | tf_op jit(solution)/shard_map/ppermute | solution.py:336
  95.8 17.2 %collective-permute-start.14 = (bf16[256,1408]{1,0:T(8,128)(2,1)}, bf16[256,1408]{1,0:T(8,128)(2,1)}, u32[]{:S(2)}, u32[]{:S(2)}) collective-permute-start(bf16[256,1408]{1,0:T(8,128)(2,1)} %get-tuple-element.45), channel_id=1, source_target_pairs={{0,8},{8,0},{16,24},{24,16},{1,9},{9,1},{17,25},{25,17},{2,10},{10... | collective-permute-start | bytes 2162696 | tf_op jit(solution)/shard_map/ppermute | solution.py:336
  96.3 18.2 %collective-permute-start.16 = (bf16[256,1408]{1,0:T(8,128)(2,1)}, bf16[256,1408]{1,0:T(8,128)(2,1)S(1)}, u32[]{:S(2)}, u32[]{:S(2)}) collective-permute-start(bf16[256,1408]{1,0:T(8,128)(2,1)} %get-tuple-element.45), channel_id=1, source_target_pairs={{0,16},{8,24},{16,0},{24,8},{1,17},{9,25},{17,1},{25,9},{2,18},{10... | collective-permute-start | bytes 2162696 | tf_op jit(solution)/shard_map/ppermute | solution.py:336
  109.5 16.3 %collective-permute-start.17 = (bf16[256,1408]{1,0:T(8,128)(2,1)}, bf16[256,1408]{1,0:T(8,128)(2,1)S(1)}, u32[]{:S(2)}, u32[]{:S(2)}) collective-permute-start(bf16[256,1408]{1,0:T(8,128)(2,1)} %collective-permute-done.15.refs_3_), channel_id=1, source_target_pairs={{0,8},{8,0},{16,24},{24,16},{1,9},{9,1},{17,25},{25,17},{2,10},{10... | collective-permute-start | bytes 2162696 | tf_op jit(solution)/shard_map/ppermute | solution.py:336
  110.5 19.1 %collective-permute-start.24 = (bf16[1408,256]{1,0:T(8,128)(2,1)S(1)}, bf16[1408,256]{1,0:T(8,128)(2,1)S(1)}, u32[]{:S(2)}, u32[]{:S(2)}) collective-permute-start(bf16[1408,256]{1,0:T(8,128)(2,1)S(1)} %collective-permute-done.4.refs_1_), channel_id=1, source_target_pairs={{0,16},{8,24},{16,0},{24,8},{1,17},{9,25},{17,1},{25,9},{2,18},{10... | collective-permute-start | bytes 2162696 | tf_op jit(solution)/shard_map/ppermute | solution.py:336
  111.0 33.1 %collective-permute-start.21 = (bf16[256,1408]{1,0:T(8,128)(2,1)}, bf16[256,1408]{1,0:T(8,128)(2,1)}, u32[]{:S(2)}, u32[]{:S(2)}) collective-permute-start(bf16[256,1408]{1,0:T(8,128)(2,1)} %collective-permute-done.3.refs_12_), channel_id=1, source_target_pairs={{0,2},{2,0},{4,6},{6,4},{1,3},{3,1},{5,7},{7,5},{8,10},{10,8},{12,... | collective-permute-start | bytes 2162696 | tf_op jit(solution)/shard_map/ppermute | solution.py:336
  113.0 31.2 %collective-permute-start.18 = (bf16[256,1408]{1,0:T(8,128)(2,1)}, bf16[256,1408]{1,0:T(8,128)(2,1)}, u32[]{:S(2)}, u32[]{:S(2)}) collective-permute-start(bf16[256,1408]{1,0:T(8,128)(2,1)} %collective-permute-done.14.refs_2_), channel_id=1, source_target_pairs={{0,16},{8,24},{16,0},{24,8},{1,17},{9,25},{17,1},{25,9},{2,18},{10... | collective-permute-start | bytes 2162696 | tf_op jit(solution)/shard_map/ppermute | solution.py:336
  114.5 48.4 %collective-permute-start.22 = (bf16[1408,256]{1,0:T(8,128)(2,1)S(1)}, bf16[1408,256]{1,0:T(8,128)(2,1)S(1)}, u32[]{:S(2)}, u32[]{:S(2)}) collective-permute-start(bf16[1408,256]{1,0:T(8,128)(2,1)S(1)} %collective-permute-done.4.refs_1_), channel_id=1, source_target_pairs={{0,2},{2,0},{4,6},{6,4},{1,3},{3,1},{5,7},{7,5},{8,10},{10,8},{12,... | collective-permute-start | bytes 2162696 | tf_op jit(solution)/shard_map/ppermute | solution.py:336
  125.8 37.1 %collective-permute-start.23 = (bf16[1408,256]{1,0:T(8,128)(2,1)S(1)}, bf16[1408,256]{1,0:T(8,128)(2,1)}, u32[]{:S(2)}, u32[]{:S(2)}) collective-permute-start(bf16[1408,256]{1,0:T(8,128)(2,1)S(1)} %collective-permute-done.5.refs_3_), channel_id=1, source_target_pairs={{0,2},{2,0},{4,6},{6,4},{1,3},{3,1},{5,7},{7,5},{8,10},{10,8},{12,... | collective-permute-start | bytes 2162696 | tf_op jit(solution)/shard_map/ppermute | solution.py:336
  129.6 43.0 %collective-permute-start.25 = (bf16[1408,256]{1,0:T(8,128)(2,1)S(1)}, bf16[1408,256]{1,0:T(8,128)(2,1)}, u32[]{:S(2)}, u32[]{:S(2)}) collective-permute-start(bf16[1408,256]{1,0:T(8,128)(2,1)S(1)} %collective-permute-done.24.refs_5_), channel_id=1, source_target_pairs={{0,2},{2,0},{4,6},{6,4},{1,3},{3,1},{5,7},{7,5},{8,10},{10,8},{12,... | collective-permute-start | bytes 2162696 | tf_op jit(solution)/shard_map/ppermute | solution.py:336
  (32 other events, 667.1 us)

commit v2 on v1

v2 whole, which is shorter than its diff:
```python
import functools

import jax
import jax.numpy as jnp
from jax import lax
from jax.experimental import pallas as pl
from jax.experimental.pallas import tpu as pltpu
from jax.sharding import PartitionSpec as P

HK = 256
HV = 512
KCONV = 4
PAGE = 64
CONVW = 1024
EPSILON = 1e-06
TILE = 256
PAGES_T = TILE // PAGE
RIM = 16
BF16 = jnp.bfloat16
F32 = jnp.float32
VMEM_LIMIT = 56 * 1024 * 1024
WIDE = 256


def params():
    return pltpu.CompilerParams(
        dimension_semantics=("arbitrary",), vmem_limit_bytes=VMEM_LIMIT
    )


def cost(flops, moved):
    return pl.CostEstimate(flops=flops, bytes_accessed=moved, transcendentals=0)


def fixed(shape):
    return pl.BlockSpec(
        shape, lambda *_: (0,) * len(shape), pipeline_mode=pl.Buffered(1)
    )


def whole_smem():
    return pl.BlockSpec(memory_space=pltpu.SMEM)


def dot(a, b):
    return jnp.dot(a, b, preferred_element_type=F32)


def dot_nt(a, b):
    return lax.dot_general(a, b, (((1,), (1,)), ((), ())), preferred_element_type=F32)


def dot_tn(a, b):
    return lax.dot_general(a, b, (((0,), (0,)), ((), ())), preferred_element_type=F32)


def silu(x):
    return x / (1.0 + jnp.exp(-x))


def column(row):
    return jnp.transpose(jnp.broadcast_to(row, (128, row.shape[1])))[:, :1]


def normalised(x, gain):
    return x * lax.rsqrt(jnp.mean(x * x, axis=-1, keepdims=True) + EPSILON) * gain


def carried_flag(pages_ref, start_ref, page):
    page = lax.axis_index("seq") * (pl.num_programs(0) * PAGES_T) + page
    same = jnp.int32(0)
    for i in range(pages_ref.shape[1]):
        first = start_ref[0, i]
        same = jnp.where((page > first) & (page < first + pages_ref[0, i]), 1, same)
    return same.astype(F32)


def front_kernel(
    pages_ref, start_ref, tokens_ref, rim_ref, gain_ref, project_ref, gate_ref, down_ref, up_ref, bias_ref,
    conv_ref, raised_ref, lowered_ref, weighted_ref, value_ref, ends_ref, edges_ref, opening_ref,
    state_ref, carry, state, decay,
):
    step = pl.program_id(0)

    @pl.when(step == 0)
    def _():
        state[...] = jnp.zeros_like(state)
        decay[...] = jnp.ones_like(decay)

    gain = gain_ref[...].astype(F32)
    rows = jnp.concatenate([tokens_ref[...], rim_ref[...]], axis=0).astype(F32)
    normed_all = normalised(rows, gain).astype(BF16)
    normed = normed_all[:TILE]
    projected_low = dot(normed_all, project_ref[...]).astype(BF16)
    projected = projected_low[:TILE].astype(F32)
    rim = projected_low[TILE:].astype(F32)[RIM - 8 :]
    previous = jnp.where(step == 0, rim, carry[...])
    carry[...] = projected[TILE - 8 :]
    opening_ref[...] = silu(dot(normed, gate_ref[...])).astype(BF16)

    lowrank = dot_nt(normed, down_ref[...]).astype(BF16)
    logits = dot(lowrank, up_ref[...]) + bias_ref[...]
    decay_log = (jnp.minimum(logits, 0.0) - jnp.log1p(jnp.exp(-jnp.abs(logits)))) / 16.0
    row = lax.broadcasted_iota(jnp.int32, (TILE, TILE), 0)
    col = lax.broadcasted_iota(jnp.int32, (TILE, TILE), 1)
    lower = jnp.where((row >= col) & ((row // PAGE) == (col // PAGE)), 1.0, 0.0).astype(F32)
    sums = jnp.dot(lower, decay_log, preferred_element_type=F32, precision=lax.Precision.HIGHEST)

    taps = conv_ref[...].astype(F32)
    suffix = jnp.ones((1, HK), F32)
    pieces = [None] * PAGES_T
    for j in reversed(range(PAGES_T)):
        carried = carried_flag(pages_ref, start_ref, step * PAGES_T + j)
        now = projected[j * PAGE : (j + 1) * PAGE]
        before = previous if j == 0 else projected[j * PAGE - 8 : j * PAGE]
        widened = jnp.concatenate([before * carried, now], axis=0)
        mixed = taps[0:1] * now
        for i in range(1, KCONV):
            mixed = mixed + taps[i : i + 1] * widened[8 - i : 8 - i + PAGE]
        query = silu(mixed[:, :HK])
        key = silu(mixed[:, HK : 2 * HK]) * HK ** (-0.5)
        value = mixed[:, 2 * HK :].astype(BF16)
        sums_j = sums[j * PAGE : (j + 1) * PAGE]
        end = sums_j[PAGE - 1 :]
        weighted = key * jnp.exp(end - sums_j)
        span = pl.ds(j * PAGE, PAGE)
        raised_ref[span, :] = (query * jnp.exp(sums_j)).astype(BF16)
        lowered_ref[span, :] = (key * jnp.exp(-sums_j)).astype(BF16)
        weighted_ref[span, :] = weighted.astype(BF16)
        value_ref[span, :] = value
        kept = jnp.exp(end)
        ends_ref[j] = jnp.broadcast_to(kept, (8, HK))
        edges_ref[j] = projected_low[(j + 1) * PAGE - (KCONV - 1) : (j + 1) * PAGE]
        pieces[j] = ((weighted * suffix).astype(BF16), value)
        suffix = suffix * (kept * carried)
    keys = jnp.concatenate([p[0] for p in pieces], axis=0)
    values = jnp.concatenate([p[1] for p in pieces], axis=0)
    state[...] = column(suffix) * state[...] + dot_tn(keys, values)
    decay[...] = decay[...] * suffix

    @pl.when(step == pl.num_programs(0) - 1)
    def _():
        state_ref[:HK] = state[...].astype(BF16)
        block = jnp.concatenate([decay[...]] * (HV // HK), axis=1)
        state_ref[HK:] = jnp.concatenate([block] * (RIM // 8), axis=0).astype(BF16)


def front(prompts, tokens, rim, gain, project, gate, down, up, bias, conv):
    count, width = tokens.shape
    rank = down.shape[0]
    pages = count // PAGE
    rows = lambda n: pl.BlockSpec((TILE, n), lambda i: (i, 0))
    shape = jax.ShapeDtypeStruct
    return pl.pallas_call(
        front_kernel,
        name="front",
        grid=(count // TILE,),
        in_specs=[
            whole_smem(), whole_smem(), rows(width), fixed((RIM, width)), fixed((1, width)),
            fixed((width, CONVW)), fixed((width, HV)), fixed((rank, width)), fixed((rank, HK)),
            fixed((1, HK)), fixed((KCONV, CONVW)),
        ],
        out_specs=[
            rows(HK), rows(HK), rows(HK), rows(HV),
            pl.BlockSpec((PAGES_T, 8, HK), lambda i: (i, 0, 0)),
            pl.BlockSpec((PAGES_T, KCONV - 1, CONVW), lambda i: (i, 0, 0)),
            rows(HV), fixed((HK + RIM, HV)),
        ],
        out_shape=[
            shape((count, HK), BF16), shape((count, HK), BF16), shape((count, HK), BF16),
            shape((count, HV), BF16), shape((pages, 8, HK), F32),
            shape((pages, KCONV - 1, CONVW), BF16), shape((count, HV), BF16),
            shape((HK + RIM, HV), BF16),
        ],
        scratch_shapes=[
            pltpu.VMEM((8, CONVW), F32), pltpu.VMEM((HK, HV), F32), pltpu.VMEM((8, HK), F32)
        ],
        compiler_params=params(),
        cost_estimate=cost(1000, 1000),
    )(*prompts, tokens, rim, gain, project, gate, down, up, bias, conv)


def halves(count):
    half = count // TILE // 2
    return [
        pl.BlockSpec((TILE, HV), lambda i: (jnp.minimum(i, half - 1), 0)),
        pl.BlockSpec((TILE, HV), lambda i: (jnp.maximum(i - half, 0), 0)),
    ]


def pages_kernel(
    pages_ref, start_ref, raised_ref, lowered_ref, weighted_ref, value_ref, ends_ref, opening_ref, gain_ref,
    one_ref, two_ref, three_ref, states_ref, low_ref, high_ref, memory,
):
    step = pl.program_id(0)

    @pl.when(step == 0)
    def _():
        part = lambda ref: ref[:HK].astype(F32)
        kept = lambda ref: column(ref[HK:].astype(F32)[:1, :HK])
        memory[...] = part(one_ref) + kept(one_ref) * (part(two_ref) + kept(two_ref) * part(three_ref))

    row = lax.broadcasted_iota(jnp.int32, (PAGE, PAGE), 0)
    col = lax.broadcasted_iota(jnp.int32, (PAGE, PAGE), 1)
    gain = gain_ref[...].astype(F32)
    held = memory[...]
    gated_tile = []
    for j in range(PAGES_T):
        span = pl.ds(j * PAGE, PAGE)
        raised, value = raised_ref[span, :], value_ref[span, :]
        held = held * carried_flag(pages_ref, start_ref, step * PAGES_T + j)
        scores = dot_nt(raised, lowered_ref[span, :])
        scores = jnp.where(row >= col, scores, 0.0).astype(BF16)
        attended = dot(scores, value) + dot(raised, held.astype(BF16))
        held = column(ends_ref[j][:1]) * held + dot_tn(weighted_ref[span, :], value)
        states_ref[j, 0] = held.astype(BF16)
        gated = normalised(attended, gain) * opening_ref[span, :].astype(F32)
        gated_tile.append(gated.astype(BF16))
    memory[...] = held
    half = pl.num_programs(0) // 2

    @pl.when(step < half)
    def _():
        low_ref[...] = jnp.concatenate(gated_tile, axis=0)

    @pl.when(step >= half)
    def _():
        high_ref[...] = jnp.concatenate(gated_tile, axis=0)


def pages(prompts, raised, lowered, weighted, value, ends, opening, gain, one, two, three):
    count = raised.shape[0]
    total = count // PAGE
    rows = lambda n: pl.BlockSpec((TILE, n), lambda i: (i, 0))
    return pl.pallas_call(
        pages_kernel,
        name="pages",
        grid=(count // TILE,),
        in_specs=[
            whole_smem(), whole_smem(), rows(HK), rows(HK), rows(HK), rows(HV),
            pl.BlockSpec((PAGES_T, 8, HK), lambda i: (i, 0, 0)), rows(HV), fixed((1, HV)),
            fixed((HK + RIM, HV)), fixed((HK + RIM, HV)), fixed((HK + RIM, HV)),
        ],
        out_specs=[
            pl.BlockSpec((PAGES_T, 1, HK, HV), lambda i: (i, 0, 0, 0)), *halves(count),
        ],
        out_shape=[
            jax.ShapeDtypeStruct((total, 1, HK, HV), BF16),
            jax.ShapeDtypeStruct((count // 2, HV), BF16),
            jax.ShapeDtypeStruct((count // 2, HV), BF16),
        ],
        scratch_shapes=[pltpu.VMEM((HK, HV), F32)],
        compiler_params=params(),
        cost_estimate=cost(1000, 1000),
    )(*prompts, raised, lowered, weighted, value, ends, opening, gain, one, two, three)


def mix_kernel(tokens_ref, low_ref, high_ref, other_low_ref, other_high_ref, weight_ref, gain_ref, residual_ref, feed_ref):
    step, half = pl.program_id(0), pl.num_programs(0) // 2
    own = jnp.where(step < half, low_ref[...], high_ref[...])
    other = jnp.where(step < half, other_low_ref[...], other_high_ref[...])
    mine = lax.axis_index("hid")
    rows = lambda head: pl.ds(pl.multiple_of(head * HV, HV), HV)
    mixed = dot(own, weight_ref[rows(mine), :]) + dot(other, weight_ref[rows(1 - mine), :])
    residual = (tokens_ref[...].astype(F32) + mixed).astype(BF16)
    residual_ref[...] = residual
    feed_ref[...] = normalised(residual.astype(F32), gain_ref[...].astype(F32)).astype(BF16)


def mix(tokens, own, others, weight, gain):
    count, width = tokens.shape
    rows = lambda n: pl.BlockSpec((TILE, n), lambda i: (i, 0))
    return pl.pallas_call(
        mix_kernel,
        name="mix",
        grid=(count // TILE,),
        in_specs=[
            rows(width), *halves(count), *halves(count), fixed(weight.shape), fixed((1, width)),
        ],
        out_specs=[rows(width), rows(width)],
        out_shape=[jax.ShapeDtypeStruct((count, width), BF16)] * 2,
        compiler_params=params(),
        cost_estimate=cost(1000, 1000),
    )(tokens, *own, *others, weight, gain)


def widen_kernel(places, feed_hbm, *refs):
    pieces, (out_ref, feed, weight, feed_sem, sems) = refs[:-5], refs[-5:]
    hidden = out_ref.shape[1]
    full = hidden // WIDE
    starts = [place() for _, place in places]

    def copies(chunk, wide):
        low = chunk * WIDE
        for i, ((matrix, _), start, ref) in enumerate(zip(places, starts, pieces)):
            rows = pl.ds(pl.multiple_of(start, 128), ref.shape[0])
            columns = pl.ds(pl.multiple_of(2 * low + matrix * wide, 128), wide)
            yield pltpu.make_async_copy(
                ref.at[:, pl.ds(pl.multiple_of(low, 128), wide)], weight.at[rows, columns], sems.at[chunk, i]
            )

    def compute(chunk, wide):
        for copy in copies(chunk, wide):
            copy.wait()
        low = pl.multiple_of(chunk * WIDE, 128)
        both = dot(feed[...], weight[:, pl.ds(pl.multiple_of(2 * low, 128), 2 * wide)])
        out_ref[:, pl.ds(low, wide)] = (silu(both[:, :wide]) * both[:, wide:]).astype(BF16)

    whole = pltpu.make_async_copy(feed_hbm, feed, feed_sem)
    whole.start()
    rest = hidden - full * WIDE
    for chunk in range(full):
        for copy in copies(chunk, WIDE):
            copy.start()
    if rest:
        for copy in copies(full, rest):
            copy.start()
    whole.wait()

    @pl.loop(0, full)
    def _(chunk):
        compute(chunk, WIDE)

    if rest:
        compute(full, rest)


def widen(feed, matrices):
    count, width = feed.shape
    pieces = [piece for matrix in matrices for piece, _ in matrix]
    places = [(i, place) for i, matrix in enumerate(matrices) for _, place in matrix]
    hidden = pieces[0].shape[1]
    chunks = pl.cdiv(hidden, WIDE)
    return pl.pallas_call(
        functools.partial(widen_kernel, places),
        name="widen",
        in_specs=[pl.BlockSpec(memory_space=pl.ANY)] * (1 + len(pieces)),
        out_specs=pl.BlockSpec(memory_space=pltpu.VMEM),
        out_shape=jax.ShapeDtypeStruct((count, hidden), BF16),
        scratch_shapes=[
            pltpu.VMEM((count, width), BF16), pltpu.VMEM((width, 2 * hidden), BF16),
            pltpu.SemaphoreType.DMA, pltpu.SemaphoreType.DMA((chunks, len(pieces))),
        ],
        compiler_params=pltpu.CompilerParams(vmem_limit_bytes=VMEM_LIMIT),
        cost_estimate=cost(1000, 1000),
    )(feed, *pieces)


def narrow_kernel(places, half, hidden_hbm, *refs):
    count = len(places)
    pieces, out_ref = refs[:count], refs[count]
    hidden, weights, sem, sems = refs[count + 1], refs[count + 2 : -2], refs[-2], refs[-1]
    rows = hidden.shape[0]
    start = pl.multiple_of(half() * rows, rows)
    whole = pltpu.make_async_copy(hidden_hbm.at[pl.ds(start, rows), :], hidden, sem)
    whole.start()
    copies = [
        pltpu.make_async_copy(ref, weight, sems.at[i])
        for i, (ref, weight) in enumerate(zip(pieces, weights))
    ]
    for copy in copies:
        copy.start()
    whole.wait()
    for place, copy, weight in zip(places, copies, weights):
        copy.wait()
        columns = pl.ds(pl.multiple_of(place(), 128), weight.shape[1])
        out_ref[:, columns] = dot(hidden[...], weight[...]).astype(BF16)


def narrow(hidden, half, pieces, width):
    count, depth = hidden.shape
    rows = count // 2
    return pl.pallas_call(
        functools.partial(narrow_kernel, [place for _, place in pieces], half),
        name="narrow",
        in_specs=[pl.BlockSpec(memory_space=pl.ANY)] * (1 + len(pieces)),
        out_specs=pl.BlockSpec(memory_space=pltpu.VMEM),
        out_shape=jax.ShapeDtypeStruct((rows, width), BF16),
        scratch_shapes=[pltpu.VMEM((rows, depth), BF16)]
        + [pltpu.VMEM(piece.shape, BF16) for piece, _ in pieces]
        + [pltpu.SemaphoreType.DMA, pltpu.SemaphoreType.DMA((len(pieces),))],
        compiler_params=pltpu.CompilerParams(vmem_limit_bytes=VMEM_LIMIT),
        cost_estimate=cost(1000, 1000),
    )(hidden, *[piece for piece, _ in pieces])


def shifted(value, steps):
    count = lax.axis_size("seq")
    return lax.ppermute(value, "seq", [(i, i + steps) for i in range(count - steps)])


def swapped(value, axis, flip):
    count = lax.axis_size(axis)
    return lax.ppermute(value, axis, [(i, i ^ flip) for i in range(count)])


def after(value, *others):
    return lax.optimization_barrier((value, *others))[0]


def on_device(
    tokens, attention_gain, project_weight, conv_weight, decay_down, decay_up, decay_bias,
    output_gate, head_gain, output_weight, mixer_gain, gate_weight, up_weight, down_weight,
    prompt_pages, prompt_start,
):
    count, width = tokens.shape
    prompts = (prompt_pages, prompt_start)
    two_by_two = lax.axis_size("req") == 4 and lax.axis_size("seq") % 2 == 0
    hid_index = lax.axis_index("hid")
    x, y = functools.partial(swapped, axis="req", flip=1), functools.partial(swapped, axis="req", flip=2)
    z = functools.partial(swapped, axis="seq", flip=1)
    depth = gate_weight.shape[0]
    half = depth // 2

    if two_by_two:
        parity = lax.rem(lax.axis_index("seq"), 2)
        up_mine = lax.dynamic_slice_in_dim(up_weight, parity * half, half, 0)
        up_a, up_b = x(up_mine), y(up_mine)
        gate_a, gate_b = x(gate_weight), y(gate_weight)
        down_mine = lax.dynamic_slice_in_dim(down_weight, parity * half, half, 1)
        down_rest = lax.dynamic_slice_in_dim(down_weight, (1 - parity) * half, half, 1)
    rim = shifted(tokens[-RIM:], 1)
    both_output = lax.all_gather(output_weight, "hid", axis=0, tiled=True)

    raised, lowered, weighted, value, ends, edges, opening, state = front(
        prompts, tokens, rim, attention_gain[None], project_weight, output_gate, decay_down.T,
        decay_up, decay_bias[None], conv_weight,
    )
    one, two, three = (shifted(state, i) for i in (1, 2, 3))
    if two_by_two:
        one, two, three, up_a, up_b, gate_a, gate_b = lax.optimization_barrier(
            (one, two, three, up_a, up_b, gate_a, gate_b)
        )
        up_c, down_a = y(up_a), x(down_mine)
        far_a, far_b = z(up_a), z(up_b)
        gate_c = x(gate_b)
    states, *gated = pages(
        prompts, raised, lowered, weighted, value, ends, opening, head_gain[None], one, two, three,
    )
    others = [swapped(part, "hid", 1) for part in gated]
    if two_by_two:
        others, up_c, down_a, far_a = lax.optimization_barrier((others, up_c, down_a, far_a))
        down_b_rest = y(down_rest)
        far_c = z(up_c)
        down_c = y(down_a)
        down_a_far = z(down_a)
    residual, feed = mix(tokens, gated, others, both_output, mixer_gain[None])

    if two_by_two:
        feed, far_b, far_c, gate_c, down_b_rest = lax.optimization_barrier(
            (feed, far_b, far_c, gate_c, down_b_rest)
        )
        down_c_rest = x(down_b_rest)
        down_b = y(down_mine)
        at = lambda flip, more=0: lambda: (lax.axis_index("req") ^ flip) * depth + more
        own = lambda flip: lambda: at(flip)() + lax.rem(lax.axis_index("seq"), 2) * half
        far = lambda flip: lambda: at(flip)() + (1 - lax.rem(lax.axis_index("seq"), 2)) * half
        gate_list = [(gate_weight, at(0)), (gate_a, at(1)), (gate_b, at(2)), (gate_c, at(3))]
        up_list = [
            (up_weight, at(0)), (up_a, own(1)), (far_a, far(1)), (up_b, own(2)), (far_b, far(2)),
            (up_c, own(3)), (far_c, far(3)),
        ]
        down_list = [
            (down_weight, at(0)), (down_a, own(1)), (down_b_rest, far(2)), (down_c, own(3)),
            (down_a_far, far(1)), (down_b, own(2)), (down_c_rest, far(3)),
        ]
    else:
        first = lambda: 0
        gate_list = [(lax.all_gather(gate_weight, "req", axis=0, tiled=True), first)]
        up_list = [(lax.all_gather(up_weight, "req", axis=0, tiled=True), first)]
        down_list = [(lax.all_gather(down_weight, "req", axis=1, tiled=True), first)]

    hidden = widen(feed, (gate_list, up_list))
    theirs_sum = narrow(hidden, lambda: 1 - lax.axis_index("hid"), down_list, width)
    received = swapped(theirs_sum, "hid", 1)
    own_sum = narrow(hidden, lambda: lax.axis_index("hid"), down_list, width)
    own_rows = lax.dynamic_slice_in_dim(residual, hid_index * (count // 2), count // 2, 0)
    result = (
        own_rows.astype(F32) + (own_sum.astype(F32) + received.astype(F32))
    ).astype(BF16)
    return result, states, edges


def solution(mesh):
    return jax.shard_map(
        on_device,
        mesh=mesh,
        in_specs=(
            P(("req", "seq"), None),
            P(),
            P(None, "hid"),
            P(None, "hid"),
            P(),
            P(None, "hid"),
            P("hid"),
            P(None, "hid"),
            P(),
            P("hid", None),
            P(),
            P("req", "hid"),
            P("req", "hid"),
            P("hid", "req"),
            P("req", None),
            P("req", None),
        ),
        out_specs=(
            P(("req", "seq", "hid"), None),
            P(("req", "seq"), "hid", None, None),
            P(("req", "seq"), None, "hid"),
        ),
        check_vma=False,
    )
```

time: 196 us -> 194 us (0.990)
  waiting for transfers between devices: 62.3 us -> 38.8 us
  between operations: 1.02 us -> 14.3 us
  Pallas kernels: 74.1 us -> 83.6 us
  local copies, waits for them, and re-layouts: 12 us -> 9.23 us
    ppermute x21 -> x18, waiting for transfers between devices: 53.5 us -> 29.5 us  [swapped(): return lax.ppermute(value, axis, [(i, i ^ flip) for i in range(count)])]
    pallas_call x3, Pallas kernels: 35.8 us -> 43.8 us  [the longest x2 22.6 us: narrow(): pl.pallas_call(functools.partial(narrow_kernel, [place for _, place in pi...]
    ppermute x21 -> x18, starting transfers between devices: 25.7 us -> 28.5 us  [swapped(): return lax.ppermute(value, axis, [(i, i ^ flip) for i in range(count)])]
    another operation x3 -> x0, local copies, waits for them, and re-layouts: 2.02 us -> none  [the longest x2 1.35 us: narrow(): jnp.stack([jnp.asarray(at, jnp.int32) for at in [half] + [at for _, at in...]
    ppermute x6 -> x4, starting transfers between devices: 15.8 us -> 14.6 us  [shifted(): lax.ppermute(value, 'seq', [(i, i + steps) for i in range(count - steps)])]
    unnamed x60 -> x43, local copies, waits for them, and re-layouts: 3.28 us -> 4.46 us
    ppermute x6 -> x4, waiting for transfers between devices: 8.84 us -> 8.66 us  [shifted(): lax.ppermute(value, 'seq', [(i, i + steps) for i in range(count - steps)])]
  transfers between devices with their start and end apart: 27 -> 23, of which waited for: 8 -> 9; matrix products, arithmetic and copies ran while one was open for 5% -> 3% of each run, Pallas kernels for 34% -> 37%
where the time goes in v2:
time: 194 us; the launch traced here: 193 us
  Pallas kernels  83.6 us (43%)
  starting transfers between devices  43.2 us (22%)
  waiting for transfers between devices  38.8 us (20%)
  between operations  14.3 us (7%)
  local copies, waits for them, and re-layouts  9.23 us (5%)
  other arithmetic  4.16 us (2%)
    ppermute x18, waiting for transfers between devices, swapped(): return lax.ppermute(value, axis, [(i, i ^ flip) for i in range(count)])  29.5 us
    ppermute x18, starting transfers between devices, swapped(): return lax.ppermute(value, axis, [(i, i ^ flip) for i in range(count)])  28.5 us
    pallas_call x2, Pallas kernels, narrow(): pl.pallas_call(functools.partial(narrow_kernel, [place for _, place in pi...  22.6 us
    pallas_call x1, Pallas kernels, widen(): pl.pallas_call(functools.partial(widen_kernel, places), name='widen', in_...  21.2 us
    pallas_call x1, Pallas kernels, front(): pl.pallas_call(front_kernel, name='front', grid=(count // TILE,), in_spec...  20.7 us
    ppermute x4, starting transfers between devices, shifted(): lax.ppermute(value, 'seq', [(i, i + steps) for i in range(count - steps)])  14.6 us
    pallas_call x1, Pallas kernels, mix(): pl.pallas_call(mix_kernel, name='mix', grid=(count // TILE,), in_specs=[r...  10.7 us
    ppermute x4, waiting for transfers between devices, shifted(): lax.ppermute(value, 'seq', [(i, i + steps) for i in range(count - steps)])  8.66 us
  transfers between devices with their start and end apart: 23, of which 9 were waited for; matrix products, arithmetic and copies ran while one was open for 3% of the time, Pallas kernels for 37%

profile of v2, /device:TPU:0, one launch (start us, length us, event | category | flops | bytes accessed | tf_op | source)
XLA Modules:
  0.0 193.3 jit_solution(13897816669441258216)
XLA Ops:
  7.9 3.0 %collective-permute-start.6 = (bf16[512,1408]{1,0:T(8,128)(2,1)}, bf16[512,1408]{1,0:T(8,128)(2,1)}, u32[]{:S(2)}, u32[]{:S(2)}) collective-permute-start(bf16[512,1408]{1,0:T(8,128)(2,1)} %refs_0_.3), channel_id=1, source_target_pairs={{0,8},{8,0},{16,24},{24,16},{1,9},{9,1},{17,25},{25,17},{2,10},{10... | collective-permute-start | bytes 4325384 | tf_op jit(solution)/shard_map/ppermute | solution.py:394
  13.3 3.5 %collective-permute-start = (bf16[16,2048]{1,0:T(8,128)(2,1)S(1)}, bf16[16,2048]{1,0:T(8,128)(2,1)S(1)}, u32[]{:S(2)}, u32[]{:S(2)}) collective-permute-start(bf16[16,2048]{1,0:T(8,128)(2,1)S(1)} %slice.3), channel_id=1, source_target_pairs={{0,2},{2,4},{4,6},{1,3},{3,5},{5,7},{8,10},{10,12},{12,14},{9,11},... | collective-permute-start | bytes 196616 | tf_op jit(solution)/shard_map/ppermute | solution.py:389
  19.3 20.7 %front.1 = (bf16[1024,256]{1,0:T(8,128)(2,1)}, bf16[1024,256]{1,0:T(8,128)(2,1)}, bf16[1024,256]{1,0:T(8,128)(2,1)}, bf16[1024,512]{1,0:T(8,128)(2,1)}, f32[16,8...) custom-call(s32[1,16]{1,0:T(1,128)} %pages_ref.3, ...), custom_call_target="tpu_custom_call" | custom-call | flops 1000 | bytes 1000 | tf_op jit(solution)/shard_map/front/pallas_call | solution.py:154
  40.0 4.6 %collective-permute-start.1 = (bf16[272,512]{1,0:T(8,128)(2,1)}, bf16[272,512]{1,0:T(8,128)(2,1)S(1)}, u32[]{:S(2)}, u32[]{:S(2)}) collective-permute-start(bf16[272,512]{1,0:T(8,128)(2,1)} %get-tuple-element.39), channel_id=1, source_target_pairs={{0,2},{2,4},{4,6},{1,3},{3,5},{5,7},{8,10},{10,12},{12,14},{9,11},... | collective-permute-start | bytes 835592 | tf_op jit(solution)/shard_map/ppermute | solution.py:389
  44.6 4.5 %collective-permute-start.2 = (bf16[272,512]{1,0:T(8,128)(2,1)}, bf16[272,512]{1,0:T(8,128)(2,1)S(1)}, u32[]{:S(2)}, u32[]{:S(2)}) collective-permute-start(bf16[272,512]{1,0:T(8,128)(2,1)} %get-tuple-element.39), channel_id=1, source_target_pairs={{0,4},{2,6},{1,5},{3,7},{8,12},{10,14},{9,13},{11,15},{16,20},{18,... | collective-permute-start | bytes 835592 | tf_op jit(solution)/shard_map/ppermute | solution.py:389
  49.1 2.0 %collective-permute-start.3 = (bf16[272,512]{1,0:T(8,128)(2,1)}, bf16[272,512]{1,0:T(8,128)(2,1)}, u32[]{:S(2)}, u32[]{:S(2)}) collective-permute-start(bf16[272,512]{1,0:T(8,128)(2,1)} %get-tuple-element.39), channel_id=1, source_target_pairs={{0,6},{1,7},{8,14},{9,15},{16,22},{17,23},{24,30},{25,31}} | collective-permute-start | bytes 835592 | tf_op jit(solution)/shard_map/ppermute | solution.py:389
  52.3 4.7 %collective-permute-done.2.two_ref = bf16[272,512]{1,0:T(8,128)(2,1)S(1)} collective-permute-done((bf16[272,512]{1,0:T(8,128)(2,1)}, bf16[272,512]{1,0:T(8,128)(2,1)S(1)}, u32[]{:S(2)}, u32[]{:S(2)}) %collective-permute-start.2) | collective-permute-done | bytes 278560 | tf_op jit(solution)/shard_map/ppermute | solution.py:389
  58.6 2.7 %collective-permute-done.3.three_ref = bf16[272,512]{1,0:T(8,128)(2,1)} collective-permute-done((bf16[272,512]{1,0:T(8,128)(2,1)}, bf16[272,512]{1,0:T(8,128)(2,1)}, u32[]{:S(2)}, u32[]{:S(2)}) %collective-permute-start.3) | collective-permute-done | bytes 278560 | tf_op jit(solution)/shard_map/ppermute | solution.py:389
  61.8 9.5 %collective-permute-done.4.refs_5_ = bf16[256,1408]{1,0:T(8,128)(2,1)S(1)} collective-permute-done((bf16[256,1408]{1,0:T(8,128)(2,1)}, bf16[256,1408]{1,0:T(8,128)(2,1)S(1)}, u32[]{:S(2)}, u32[]{:S(2)}) %collective-permute-start.4) | collective-permute-done | bytes 720928 | tf_op jit(solution)/shard_map/ppermute | solution.py:394
  71.3 2.2 %collective-permute-done.5.refs_7_ = bf16[256,1408]{1,0:T(8,128)(2,1)} collective-permute-done((bf16[256,1408]{1,0:T(8,128)(2,1)}, bf16[256,1408]{1,0:T(8,128)(2,1)}, u32[]{:S(2)}, u32[]{:S(2)}) %collective-permute-start.5) | collective-permute-done | bytes 720928 | tf_op jit(solution)/shard_map/ppermute | solution.py:394
  73.9 11.9 %collective-permute-start.12 = (bf16[256,1408]{1,0:T(8,128)(2,1)S(1)}, bf16[256,1408]{1,0:T(8,128)(2,1)S(1)}, u32[]{:S(2)}, u32[]{:S(2)}) collective-permute-start(bf16[256,1408]{1,0:T(8,128)(2,1)S(1)} %collective-permute-done.4.refs_5_), channel_id=1, source_target_pairs={{0,2},{2,0},{4,6},{6,4},{1,3},{3,1},{5,7},{7,5},{8,10},{10,8},{12,... | collective-permute-start | bytes 2162696 | tf_op jit(solution)/shard_map/ppermute | solution.py:394
  86.6 8.4 %pages.1 = (bf16[16,1,256,512]{3,2,1,0:T(8,128)(2,1)}, bf16[512,512]{1,0:T(8,128)(2,1)}, bf16[512,512]{1,0:T(8,128)(2,1)}) custom-call(s32[1,16]{1,0:T(1,128)} %pages_ref.3, s32[1,16]{1,0:T(1,128)} %start_ref.3, bf16[1024,256]{1,0:T(8,128)(2,1)} %get-tuple-element.33.raised_ref, bf16[1024,256]{1,0:T(8,128)(2,1)} %get-tuple-element.34.lowered_ref, ...), custom_call_target="tpu_custom_call" | custom-call | flops 1000 | bytes 1000 | tf_op jit(solution)/shard_map/pages/pallas_call | solution.py:235
  95.6 1.6 collective-permute-done.8.other_low_ref
  97.2 1.9 collective-permute-start.16
  99.1 1.7 collective-permute-start.13
  103.3 10.7 %mix.1 = (bf16[1024,2048]{1,0:T(8,128)(2,1)}, bf16[1024,2048]{1,0:T(8,128)(2,1)}) custom-call(bf16[1024,2048]{1,0:T(8,128)(2,1)} %tokens_ref.3, bf16[512,512]{1,0:T(8,128)(2,1)} %get-tuple-element.43.low_ref, bf16[512,512]{1,0:T(8,128)(2,1)} %get-tuple-element.44.high_ref, bf16[512,512]{1,0:T(8,128)(2,1)} %copy-done.12, bf16[512,512]{1,0:T(8,128)(2,1)} %copy-done.13, ...), custom_call_target="tpu_custom_call" | custom-call | flops 1000 | bytes 1000 | tf_op jit(solution)/shard_map/mix/pallas_call | solution.py:273
  114.0 2.4 %collective-permute-done.16.refs_2_ = bf16[1408,256]{1,0:T(8,128)(2,1)S(1)} collective-permute-done((bf16[1408,256]{1,0:T(8,128)(2,1)}, bf16[1408,256]{1,0:T(8,128)(2,1)S(1)}, u32[]{:S(2)}, u32[]{:S(2)}) %collective-permute-start.16) | collective-permute-done | bytes 720928 | tf_op jit(solution)/shard_map/ppermute | solution.py:394
  116.4 1.9 collective-permute-start.17
  118.4 1.7 collective-permute-start.18
  120.1 13.6 %collective-permute-done.14.refs_10_ = bf16[256,1408]{1,0:T(8,128)(2,1)S(1)} collective-permute-done((bf16[256,1408]{1,0:T(8,128)(2,1)}, bf16[256,1408]{1,0:T(8,128)(2,1)S(1)}, u32[]{:S(2)}, u32[]{:S(2)}) %collective-permute-start.14) | collective-permute-done | bytes 720928 | tf_op jit(solution)/shard_map/ppermute | solution.py:394
  135.3 21.2 %widen.1.hidden_hbm = bf16[1024,1408]{1,0:T(8,128)(2,1)} custom-call(bf16[1024,2048]{1,0:T(8,128)(2,1)} %get-tuple-element.53.feed_hbm, bf16[512,1408]{1,0:T(8,128)(2,1)} %refs_0_.3, bf16[512,1408]{1,0:T(8,128)(2,1)} %collective-permute-done.6.refs_1_, bf16[512,1408]{1,0:T(8,128)(2,1)} %collective-permute-done.7.refs_2_, ...), custom_call_target="tpu_custom_call" | custom-call | flops 1000 | bytes 1000 | tf_op jit(solution)/shard_map/widen/pallas_call | solution.py:334
  158.9 11.2 %narrow.3 = bf16[512,2048]{1,0:T(8,128)(2,1)} custom-call(bf16[1024,1408]{1,0:T(8,128)(2,1)} %widen.1.hidden_hbm, bf16[1408,512]{1,0:T(8,128)(2,1)} %refs_0_.5, bf16[1408,256]{1,0:T(8,128)(2,1)} %copy-done.2, bf16[1408,256]{1,0:T(8,128)(2,1)} %copy-done.3, bf16[1408,256]{1,0:T(8,128)(2,1)} %copy-done.5, bf16[1408,256]{1,0:T(8,128)(2,1)} %copy-done.6, ...), custom_call_target="tpu_custom_call" | custom-call | flops 1000 | bytes 1000 | tf_op jit(solution)/shard_map/narrow/pallas_call | solution.py:373
  170.9 11.4 %narrow.2 = bf16[512,2048]{1,0:T(8,128)(2,1)} custom-call(bf16[1024,1408]{1,0:T(8,128)(2,1)} %widen.1.hidden_hbm, bf16[1408,512]{1,0:T(8,128)(2,1)} %refs_0_.5, bf16[1408,256]{1,0:T(8,128)(2,1)} %copy-done.2, bf16[1408,256]{1,0:T(8,128)(2,1)} %copy-done.3, bf16[1408,256]{1,0:T(8,128)(2,1)} %copy-done.5, bf16[1408,256]{1,0:T(8,128)(2,1)} %copy-done.6, ...), custom_call_target="tpu_custom_call" | custom-call | flops 1000 | bytes 1000 | tf_op jit(solution)/shard_map/narrow/pallas_call | solution.py:373
  182.3 4.2 %add_convert_fusion = bf16[512,2048]{1,0:T(8,128)(2,1)} fusion(bf16[512,2048]{1,0:T(8,128)(2,1)S(1)} %collective-permute-done.21, bf16[512,2048]{1,0:T(8,128)(2,1)} %narrow.2, bf16[1024,2048]{1,0:T(8,128)(2,1)S(1)} %copy-done.8, s32[]{:T(128)S(6)} %select_n.11), kind=kLoop, calls=%fused_computation | loop fusion | flops 6291456 | bytes 8388612 | tf_op jit(solution)/shard_map/convert_element_type | solution.py:480
  (79 shorter events, 17.8 us)
Async XLA Ops:
  7.2 96.2 %all-gather.2.cloned.1.call-start = ((), (), s32[]{:S(2)}) async-start(), calls=%async_computation | async-start | bytes 6291456 | tf_op jit(solution)/shard_map/all_gather | solution.py:423
  7.9 65.6 %collective-permute-start.6 = (bf16[512,1408]{1,0:T(8,128)(2,1)}, bf16[512,1408]{1,0:T(8,128)(2,1)}, u32[]{:S(2)}, u32[]{:S(2)}) collective-permute-start(bf16[512,1408]{1,0:T(8,128)(2,1)} %refs_0_.3), channel_id=1, source_target_pairs={{0,8},{8,0},{16,24},{24,16},{1,9},{9,1},{17,25},{25,17},{2,10},{10... | collective-permute-start | bytes 4325384 | tf_op jit(solution)/shard_map/ppermute | solution.py:394
  10.9 62.6 %collective-permute-start.7 = (bf16[512,1408]{1,0:T(8,128)(2,1)}, bf16[512,1408]{1,0:T(8,128)(2,1)}, u32[]{:S(2)}, u32[]{:S(2)}) collective-permute-start(bf16[512,1408]{1,0:T(8,128)(2,1)} %refs_0_.3), channel_id=1, source_target_pairs={{0,16},{8,24},{16,0},{24,8},{1,17},{9,25},{17,1},{25,9},{2,18},{10... | collective-permute-start | bytes 4325384 | tf_op jit(solution)/shard_map/ppermute | solution.py:394
  13.3 5.4 %collective-permute-start = (bf16[16,2048]{1,0:T(8,128)(2,1)S(1)}, bf16[16,2048]{1,0:T(8,128)(2,1)S(1)}, u32[]{:S(2)}, u32[]{:S(2)}) collective-permute-start(bf16[16,2048]{1,0:T(8,128)(2,1)S(1)} %slice.3), channel_id=1, source_target_pairs={{0,2},{2,4},{4,6},{1,3},{3,5},{5,7},{8,10},{10,12},{12,14},{9,11},... | collective-permute-start | bytes 196616 | tf_op jit(solution)/shard_map/ppermute | solution.py:389
  40.0 12.1 %collective-permute-start.1 = (bf16[272,512]{1,0:T(8,128)(2,1)}, bf16[272,512]{1,0:T(8,128)(2,1)S(1)}, u32[]{:S(2)}, u32[]{:S(2)}) collective-permute-start(bf16[272,512]{1,0:T(8,128)(2,1)} %get-tuple-element.39), channel_id=1, source_target_pairs={{0,2},{2,4},{4,6},{1,3},{3,5},{5,7},{8,10},{10,12},{12,14},{9,11},... | collective-permute-start | bytes 835592 | tf_op jit(solution)/shard_map/ppermute | solution.py:389
  44.6 12.5 %collective-permute-start.2 = (bf16[272,512]{1,0:T(8,128)(2,1)}, bf16[272,512]{1,0:T(8,128)(2,1)S(1)}, u32[]{:S(2)}, u32[]{:S(2)}) collective-permute-start(bf16[272,512]{1,0:T(8,128)(2,1)} %get-tuple-element.39), channel_id=1, source_target_pairs={{0,4},{2,6},{1,5},{3,7},{8,12},{10,14},{9,13},{11,15},{16,20},{18,... | collective-permute-start | bytes 835592 | tf_op jit(solution)/shard_map/ppermute | solution.py:389
  49.1 12.2 %collective-permute-start.3 = (bf16[272,512]{1,0:T(8,128)(2,1)}, bf16[272,512]{1,0:T(8,128)(2,1)}, u32[]{:S(2)}, u32[]{:S(2)}) collective-permute-start(bf16[272,512]{1,0:T(8,128)(2,1)} %get-tuple-element.39), channel_id=1, source_target_pairs={{0,6},{1,7},{8,14},{9,15},{16,22},{17,23},{24,30},{25,31}} | collective-permute-start | bytes 835592 | tf_op jit(solution)/shard_map/ppermute | solution.py:389
  52.0 19.3 %collective-permute-start.4 = (bf16[256,1408]{1,0:T(8,128)(2,1)}, bf16[256,1408]{1,0:T(8,128)(2,1)S(1)}, u32[]{:S(2)}, u32[]{:S(2)}) collective-permute-start(bf16[256,1408]{1,0:T(8,128)(2,1)} %constant_dynamic-slice_fusion.2), channel_id=1, source_target_pairs={{0,8},{8,0},{16,24},{24,16},{1,9},{9,1},{17,25},{25,17},{2,10},{10... | collective-permute-start | bytes 2162696 | tf_op jit(solution)/shard_map/ppermute | solution.py:394
  57.0 16.5 %collective-permute-start.5 = (bf16[256,1408]{1,0:T(8,128)(2,1)}, bf16[256,1408]{1,0:T(8,128)(2,1)}, u32[]{:S(2)}, u32[]{:S(2)}) collective-permute-start(bf16[256,1408]{1,0:T(8,128)(2,1)} %constant_dynamic-slice_fusion.2), channel_id=1, source_target_pairs={{0,16},{8,24},{16,0},{24,8},{1,17},{9,25},{17,1},{25,9},{2,18},{10... | collective-permute-start | bytes 2162696 | tf_op jit(solution)/shard_map/ppermute | solution.py:394
  61.3 33.8 %collective-permute-start.11 = (bf16[1408,256]{1,0:T(8,128)(2,1)}, bf16[1408,256]{1,0:T(8,128)(2,1)S(1)}, u32[]{:S(2)}, u32[]{:S(2)}) collective-permute-start(bf16[1408,256]{1,0:T(8,128)(2,1)} %get-tuple-element.67), channel_id=1, source_target_pairs={{0,8},{8,0},{16,24},{24,16},{1,9},{9,1},{17,25},{25,17},{2,10},{10... | collective-permute-start | bytes 2162696 | tf_op jit(solution)/shard_map/ppermute | solution.py:394
  73.5 27.3 %collective-permute-start.10 = (bf16[256,1408]{1,0:T(8,128)(2,1)S(1)}, bf16[256,1408]{1,0:T(8,128)(2,1)}, u32[]{:S(2)}, u32[]{:S(2)}) collective-permute-start(bf16[256,1408]{1,0:T(8,128)(2,1)S(1)} %collective-permute-done.4.refs_5_), channel_id=1, source_target_pairs={{0,16},{8,24},{16,0},{24,8},{1,17},{9,25},{17,1},{25,9},{2,18},{10... | collective-permute-start | bytes 2162696 | tf_op jit(solution)/shard_map/ppermute | solution.py:394
  73.9 26.9 %collective-permute-start.12 = (bf16[256,1408]{1,0:T(8,128)(2,1)S(1)}, bf16[256,1408]{1,0:T(8,128)(2,1)S(1)}, u32[]{:S(2)}, u32[]{:S(2)}) collective-permute-start(bf16[256,1408]{1,0:T(8,128)(2,1)S(1)} %collective-permute-done.4.refs_5_), channel_id=1, source_target_pairs={{0,2},{2,0},{4,6},{6,4},{1,3},{3,1},{5,7},{7,5},{8,10},{10,8},{12,... | collective-permute-start | bytes 2162696 | tf_op jit(solution)/shard_map/ppermute | solution.py:394
  85.8 47.9 %collective-permute-start.15 = (bf16[512,1408]{1,0:T(8,128)(2,1)}, bf16[512,1408]{1,0:T(8,128)(2,1)}, u32[]{:S(2)}, u32[]{:S(2)}) collective-permute-start(bf16[512,1408]{1,0:T(8,128)(2,1)} %collective-permute-done.7.refs_2_), channel_id=1, source_target_pairs={{0,8},{8,0},{16,24},{24,16},{1,9},{9,1},{17,25},{25,17},{2,10},{10... | collective-permute-start | bytes 4325384 | tf_op jit(solution)/shard_map/ppermute | solution.py:394
  95.0 2.2 %collective-permute-start.8 = (bf16[512,512]{1,0:T(8,128)(2,1)}, bf16[512,512]{1,0:T(8,128)(2,1)S(1)}, u32[]{:S(2)}, u32[]{:S(2)}) collective-permute-start(bf16[512,512]{1,0:T(8,128)(2,1)} %get-tuple-element.43.low_ref), channel_id=1, source_target_pairs={{0,1},{1,0},{2,3},{3,2},{4,5},{5,4},{6,7},{7,6},{8,9},{9,8},{10,11... | collective-permute-start | bytes 1572872 | tf_op jit(solution)/shard_map/ppermute | solution.py:394
  95.1 4.0 %collective-permute-start.9 = (bf16[512,512]{1,0:T(8,128)(2,1)}, bf16[512,512]{1,0:T(8,128)(2,1)S(1)}, u32[]{:S(2)}, u32[]{:S(2)}) collective-permute-start(bf16[512,512]{1,0:T(8,128)(2,1)} %get-tuple-element.44.high_ref), channel_id=1, source_target_pairs={{0,1},{1,0},{2,3},{3,2},{4,5},{5,4},{6,7},{7,6},{8,9},{9,8},{10,11... | collective-permute-start | bytes 1572872 | tf_op jit(solution)/shard_map/ppermute | solution.py:394
  97.2 19.2 %collective-permute-start.16 = (bf16[1408,256]{1,0:T(8,128)(2,1)}, bf16[1408,256]{1,0:T(8,128)(2,1)S(1)}, u32[]{:S(2)}, u32[]{:S(2)}) collective-permute-start(bf16[1408,256]{1,0:T(8,128)(2,1)} %get-tuple-element.66), channel_id=1, source_target_pairs={{0,16},{8,24},{16,0},{24,8},{1,17},{9,25},{17,1},{25,9},{2,18},{10... | collective-permute-start | bytes 2162696 | tf_op jit(solution)/shard_map/ppermute | solution.py:394
  99.1 19.3 %collective-permute-start.13 = (bf16[256,1408]{1,0:T(8,128)(2,1)}, bf16[256,1408]{1,0:T(8,128)(2,1)}, u32[]{:S(2)}, u32[]{:S(2)}) collective-permute-start(bf16[256,1408]{1,0:T(8,128)(2,1)} %collective-permute-done.5.refs_7_), channel_id=1, source_target_pairs={{0,2},{2,0},{4,6},{6,4},{1,3},{3,1},{5,7},{7,5},{8,10},{10,8},{12,... | collective-permute-start | bytes 2162696 | tf_op jit(solution)/shard_map/ppermute | solution.py:394
  101.7 32.0 %collective-permute-start.14 = (bf16[256,1408]{1,0:T(8,128)(2,1)}, bf16[256,1408]{1,0:T(8,128)(2,1)S(1)}, u32[]{:S(2)}, u32[]{:S(2)}) collective-permute-start(bf16[256,1408]{1,0:T(8,128)(2,1)} %collective-permute-done.10.refs_9_), channel_id=1, source_target_pairs={{0,2},{2,0},{4,6},{6,4},{1,3},{3,1},{5,7},{7,5},{8,10},{10,8},{12,... | collective-permute-start | bytes 2162696 | tf_op jit(solution)/shard_map/ppermute | solution.py:394
  102.5 54.1 %collective-permute-start.19 = (bf16[1408,256]{1,0:T(8,128)(2,1)}, bf16[1408,256]{1,0:T(8,128)(2,1)S(1)}, u32[]{:S(2)}, u32[]{:S(2)}) collective-permute-start(bf16[1408,256]{1,0:T(8,128)(2,1)} %get-tuple-element.67), channel_id=1, source_target_pairs={{0,16},{8,24},{16,0},{24,8},{1,17},{9,25},{17,1},{25,9},{2,18},{10... | collective-permute-start | bytes 2162696 | tf_op jit(solution)/shard_map/ppermute | solution.py:394
  116.4 40.2 %copy-start.3 = (bf16[1408,256]{1,0:T(8,128)(2,1)}, bf16[1408,256]{1,0:T(8,128)(2,1)S(1)}, u32[]{:S(2)}) copy-start(bf16[1408,256]{1,0:T(8,128)(2,1)S(1)} %collective-permute-done.16.refs_2_) | copy-start | bytes 2162692
  116.4 40.2 %collective-permute-start.17 = (bf16[1408,256]{1,0:T(8,128)(2,1)S(1)}, bf16[1408,256]{1,0:T(8,128)(2,1)S(1)}, u32[]{:S(2)}, u32[]{:S(2)}) collective-permute-start(bf16[1408,256]{1,0:T(8,128)(2,1)S(1)} %collective-permute-done.11.refs_1_), channel_id=1, source_target_pairs={{0,16},{8,24},{16,0},{24,8},{1,17},{9,25},{17,1},{25,9},{2,18},{10... | collective-permute-start | bytes 2162696 | tf_op jit(solution)/shard_map/ppermute | solution.py:394
  118.4 38.2 %collective-permute-start.18 = (bf16[1408,256]{1,0:T(8,128)(2,1)S(1)}, bf16[1408,256]{1,0:T(8,128)(2,1)S(1)}, u32[]{:S(2)}, u32[]{:S(2)}) collective-permute-start(bf16[1408,256]{1,0:T(8,128)(2,1)S(1)} %collective-permute-done.11.refs_1_), channel_id=1, source_target_pairs={{0,2},{2,0},{4,6},{6,4},{1,3},{3,1},{5,7},{7,5},{8,10},{10,8},{12,... | collective-permute-start | bytes 2162696 | tf_op jit(solution)/shard_map/ppermute | solution.py:394
  133.7 22.9 %collective-permute-start.20 = (bf16[1408,256]{1,0:T(8,128)(2,1)S(1)}, bf16[1408,256]{1,0:T(8,128)(2,1)S(1)}, u32[]{:S(2)}, u32[]{:S(2)}) collective-permute-start(bf16[1408,256]{1,0:T(8,128)(2,1)S(1)} %collective-permute-done.16.refs_2_), channel_id=1, source_target_pairs={{0,8},{8,0},{16,24},{24,16},{1,9},{9,1},{17,25},{25,17},{2,10},{10... | collective-permute-start | bytes 2162696 | tf_op jit(solution)/shard_map/ppermute | solution.py:394
  170.1 12.2 %collective-permute-start.21 = (bf16[512,2048]{1,0:T(8,128)(2,1)}, bf16[512,2048]{1,0:T(8,128)(2,1)S(1)}, u32[]{:S(2)}, u32[]{:S(2)}) collective-permute-start(bf16[512,2048]{1,0:T(8,128)(2,1)} %narrow.3), channel_id=1, source_target_pairs={{0,1},{1,0},{2,3},{3,2},{4,5},{5,4},{6,7},{7,6},{8,9},{9,8},{10,11... | collective-permute-start | bytes 6291464 | tf_op jit(solution)/shard_map/ppermute | solution.py:394
  (20 other events, 263.2 us)
Sparse Core Ops, SparseCore 0:
  9.6 16.3 all-gather.1

commit v3 on v2

--- a/solution.py
+++ b/solution.py
@@ -180,6 +180,26 @@
     )(*prompts, tokens, rim, gain, project, gate, down, up, bias, conv)
 
 
+def composed(later, earlier):
+    kept = column(later[HK:].astype(F32)[:1, :HK])
+    return later[:HK].astype(F32) + kept * earlier[:HK].astype(F32)
+
+
+def joined_kernel(later_ref, earlier_ref, out_ref):
+    out_ref[:HK] = composed(later_ref, earlier_ref).astype(BF16)
+    out_ref[HK:] = later_ref[HK:]
+
+
+def joined(later, earlier):
+    return pl.pallas_call(
+        joined_kernel, name="joined",
+        in_specs=[pl.BlockSpec(memory_space=pltpu.VMEM)] * 2,
+        out_specs=pl.BlockSpec(memory_space=pltpu.VMEM),
+        out_shape=jax.ShapeDtypeStruct(later.shape, BF16),
+        cost_estimate=cost(1000, 1000),
+    )(later, earlier)
+
+
 def halves(count):
     half = count // TILE // 2
     return [
@@ -190,15 +210,13 @@
 
 def pages_kernel(
     pages_ref, start_ref, raised_ref, lowered_ref, weighted_ref, value_ref, ends_ref, opening_ref, gain_ref,
-    one_ref, two_ref, three_ref, states_ref, low_ref, high_ref, memory,
+    one_ref, two_ref, states_ref, low_ref, high_ref, memory,
 ):
     step = pl.program_id(0)
 
     @pl.when(step == 0)
     def _():
-        part = lambda ref: ref[:HK].astype(F32)
-        kept = lambda ref: column(ref[HK:].astype(F32)[:1, :HK])
-        memory[...] = part(one_ref) + kept(one_ref) * (part(two_ref) + kept(two_ref) * part(three_ref))
+        memory[...] = composed(one_ref, two_ref)
 
     row = lax.broadcasted_iota(jnp.int32, (PAGE, PAGE), 0)
     col = lax.broadcasted_iota(jnp.int32, (PAGE, PAGE), 1)
@@ -228,7 +246,7 @@
         high_ref[...] = jnp.concatenate(gated_tile, axis=0)
 
 
-def pages(prompts, raised, lowered, weighted, value, ends, opening, gain, one, two, three):
+def pages(prompts, raised, lowered, weighted, value, ends, opening, gain, one, two):
     count = raised.shape[0]
     total = count // PAGE
     rows = lambda n: pl.BlockSpec((TILE, n), lambda i: (i, 0))
@@ -239,7 +257,7 @@
         in_specs=[
             whole_smem(), whole_smem(), rows(HK), rows(HK), rows(HK), rows(HV),
             pl.BlockSpec((PAGES_T, 8, HK), lambda i: (i, 0, 0)), rows(HV), fixed((1, HV)),
-            fixed((HK + RIM, HV)), fixed((HK + RIM, HV)), fixed((HK + RIM, HV)),
+            fixed((HK + RIM, HV)), fixed((HK + RIM, HV)),
         ],
         out_specs=[
             pl.BlockSpec((PAGES_T, 1, HK, HV), lambda i: (i, 0, 0, 0)), *halves(count),
@@ -252,7 +270,7 @@
         scratch_shapes=[pltpu.VMEM((HK, HV), F32)],
         compiler_params=params(),
         cost_estimate=cost(1000, 1000),
-    )(*prompts, raised, lowered, weighted, value, ends, opening, gain, one, two, three)
+    )(*prompts, raised, lowered, weighted, value, ends, opening, gain, one, two)
 
 
 def mix_kernel(tokens_ref, low_ref, high_ref, other_low_ref, other_high_ref, weight_ref, gain_ref, residual_ref, feed_ref):
@@ -284,45 +302,14 @@
     )(tokens, *own, *others, weight, gain)
 
 
-def widen_kernel(places, feed_hbm, *refs):
-    pieces, (out_ref, feed, weight, feed_sem, sems) = refs[:-5], refs[-5:]
-    hidden = out_ref.shape[1]
-    full = hidden // WIDE
-    starts = [place() for _, place in places]
-
-    def copies(chunk, wide):
-        low = chunk * WIDE
-        for i, ((matrix, _), start, ref) in enumerate(zip(places, starts, pieces)):
-            rows = pl.ds(pl.multiple_of(start, 128), ref.shape[0])
-            columns = pl.ds(pl.multiple_of(2 * low + matrix * wide, 128), wide)
-            yield pltpu.make_async_copy(
-                ref.at[:, pl.ds(pl.multiple_of(low, 128), wide)], weight.at[rows, columns], sems.at[chunk, i]
-            )
-
-    def compute(chunk, wide):
-        for copy in copies(chunk, wide):
-            copy.wait()
-        low = pl.multiple_of(chunk * WIDE, 128)
-        both = dot(feed[...], weight[:, pl.ds(pl.multiple_of(2 * low, 128), 2 * wide)])
-        out_ref[:, pl.ds(low, wide)] = (silu(both[:, :wide]) * both[:, wide:]).astype(BF16)
-
-    whole = pltpu.make_async_copy(feed_hbm, feed, feed_sem)
-    whole.start()
-    rest = hidden - full * WIDE
-    for chunk in range(full):
-        for copy in copies(chunk, WIDE):
-            copy.start()
-    if rest:
-        for copy in copies(full, rest):
-            copy.start()
-    whole.wait()
-
-    @pl.loop(0, full)
-    def _(chunk):
-        compute(chunk, WIDE)
-
-    if rest:
-        compute(full, rest)
+def widen_kernel(places, feed_ref, *refs):
+    pieces, out_ref = refs[:-1], refs[-1]
+    sums = [None, None]
+    for (matrix, place), ref in zip(places, pieces):
+        columns = pl.ds(pl.multiple_of(place(), 128), ref.shape[0])
+        part = dot(feed_ref[:, columns], ref[...])
+        sums[matrix] = part if sums[matrix] is None else sums[matrix] + part
+    out_ref[...] = (silu(sums[0]) * sums[1]).astype(BF16)
 
 
 def widen(feed, matrices):
@@ -330,58 +317,108 @@
     pieces = [piece for matrix in matrices for piece, _ in matrix]
     places = [(i, place) for i, matrix in enumerate(matrices) for _, place in matrix]
     hidden = pieces[0].shape[1]
-    chunks = pl.cdiv(hidden, WIDE)
     return pl.pallas_call(
         functools.partial(widen_kernel, places),
         name="widen",
-        in_specs=[pl.BlockSpec(memory_space=pl.ANY)] * (1 + len(pieces)),
-        out_specs=pl.BlockSpec(memory_space=pltpu.VMEM),
+        grid=(pl.cdiv(hidden, WIDE),),
+        in_specs=[fixed((count, width))]
+        + [pl.BlockSpec((piece.shape[0], WIDE), lambda i: (0, i)) for piece in pieces],
+        out_specs=pl.BlockSpec((count, WIDE), lambda i: (0, i)),
         out_shape=jax.ShapeDtypeStruct((count, hidden), BF16),
-        scratch_shapes=[
-            pltpu.VMEM((count, width), BF16), pltpu.VMEM((width, 2 * hidden), BF16),
-            pltpu.SemaphoreType.DMA, pltpu.SemaphoreType.DMA((chunks, len(pieces))),
-        ],
-        compiler_params=pltpu.CompilerParams(vmem_limit_bytes=VMEM_LIMIT),
+        compiler_params=params(),
         cost_estimate=cost(1000, 1000),
     )(feed, *pieces)
 
 
-def narrow_kernel(places, half, hidden_hbm, *refs):
-    count = len(places)
-    pieces, out_ref = refs[:count], refs[count]
-    hidden, weights, sem, sems = refs[count + 1], refs[count + 2 : -2], refs[-2], refs[-1]
-    rows = hidden.shape[0]
-    start = pl.multiple_of(half() * rows, rows)
-    whole = pltpu.make_async_copy(hidden_hbm.at[pl.ds(start, rows), :], hidden, sem)
-    whole.start()
+def narrow_kernel(hidden_hbm, *refs):
+    count = (len(refs) - 5) // 2
+    pieces, theirs_ref, own_ref, hidden = refs[:count], *refs[count : count + 3]
+    weights, sem, sems = refs[count + 3 : -2], refs[-2], refs[-1]
+    rows = hidden.shape[0] // 2
+    mine = lax.axis_index("hid")
+    wholes = [
+        pltpu.make_async_copy(
+            hidden_hbm.at[pl.ds(pl.multiple_of(half * rows, rows), rows), :],
+            hidden.at[pl.ds(i * rows, rows), :],
+            sem.at[i],
+        )
+        for i, half in enumerate((1 - mine, mine))
+    ]
     copies = [
         pltpu.make_async_copy(ref, weight, sems.at[i])
         for i, (ref, weight) in enumerate(zip(pieces, weights))
     ]
-    for copy in copies:
+    for copy in wholes + copies:
         copy.start()
-    whole.wait()
-    for place, copy, weight in zip(places, copies, weights):
+    for copy in wholes:
         copy.wait()
-        columns = pl.ds(pl.multiple_of(place(), 128), weight.shape[1])
-        out_ref[:, columns] = dot(hidden[...], weight[...]).astype(BF16)
-
-
-def narrow(hidden, half, pieces, width):
+    depth = hidden.shape[1]
+    at = 0
+    for copy, weight in zip(copies, weights):
+        copy.wait()
+        for low in range(0, weight.shape[1], WIDE):
+            total = None
+            for k in range(0, depth, WIDE):
+                span = pl.ds(k, min(WIDE, depth - k))
+                part = dot(hidden[:, span], weight[span, pl.ds(low, WIDE)])
+                total = part if total is None else total + part
+            columns = pl.ds(at, WIDE)
+            theirs_ref[:, columns] = total[:rows].astype(BF16)
+            own_ref[:, columns] = total[rows:].astype(BF16)
+            at += WIDE
+
+
+def narrow(hidden, pieces):
     count, depth = hidden.shape
-    rows = count // 2
-    return pl.pallas_call(
-        functools.partial(narrow_kernel, [place for _, place in pieces], half),
+    width = sum(piece.shape[1] for piece in pieces)
+    return pl.pallas_call(
+        narrow_kernel,
         name="narrow",
         in_specs=[pl.BlockSpec(memory_space=pl.ANY)] * (1 + len(pieces)),
-        out_specs=pl.BlockSpec(memory_space=pltpu.VMEM),
-        out_shape=jax.ShapeDtypeStruct((rows, width), BF16),
-        scratch_shapes=[pltpu.VMEM((rows, depth), BF16)]
-        + [pltpu.VMEM(piece.shape, BF16) for piece, _ in pieces]
-        + [pltpu.SemaphoreType.DMA, pltpu.SemaphoreType.DMA((len(pieces),))],
+        out_specs=[pl.BlockSpec(memory_space=pltpu.VMEM)] * 2,
+        out_shape=[jax.ShapeDtypeStruct((count // 2, width), BF16)] * 2,
+        scratch_shapes=[pltpu.VMEM((count, depth), BF16)]
+        + [pltpu.VMEM(piece.shape, BF16) for piece in pieces]
+        + [pltpu.SemaphoreType.DMA((2,)), pltpu.SemaphoreType.DMA((len(pieces),))],
         compiler_params=pltpu.CompilerParams(vmem_limit_bytes=VMEM_LIMIT),
         cost_estimate=cost(1000, 1000),
-    )(hidden, *[piece for piece, _ in pieces])
+    )(hidden, *pieces)
+
+
+def close_kernel(places, residual_ref, *refs):
+    out_ref = refs[-1]
+    for group, (own_ref, received_ref) in zip(places, zip(refs[:-1:2], refs[1:-1:2])):
+        at = 0
+        for size, place in group:
+            columns, span = pl.ds(pl.multiple_of(place(), 128), size), pl.ds(at, size)
+            total = own_ref[:, span].astype(F32) + received_ref[:, span].astype(F32)
+            out_ref[:, columns] = (residual_ref[:, columns].astype(F32) + total).astype(BF16)
+            at += size
+
+
+def close(hid_index, residual, groups):
+    count, width = residual.shape
+    tiles = count // TILE // 2
+    rows = lambda n: pl.BlockSpec((TILE, n), lambda i, s: (i, 0))
+    arrays = [array for own, received, _ in groups for array in (own, received)]
+    return pl.pallas_call(
+        functools.partial(close_kernel_, [group[2] for group in groups]),
+        name="close",
+        grid_spec=pltpu.PrefetchScalarGridSpec(
+            num_scalar_prefetch=1,
+            grid=(tiles,),
+            in_specs=[pl.BlockSpec((TILE, width), lambda i, s: (s[0] * tiles + i, 0))]
+            + [rows(array.shape[1]) for array in arrays],
+            out_specs=rows(width),
+        ),
+        out_shape=jax.ShapeDtypeStruct((count // 2, width), BF16),
+        compiler_params=params(),
+        cost_estimate=cost(1000, 1000),
+    )(hid_index.astype(jnp.int32)[None], residual, *arrays)
+
+
+def close_kernel_(places, half_ref, *refs):
+    close_kernel(places, *refs)
 
 
 def shifted(value, steps):
@@ -412,13 +449,12 @@
     depth = gate_weight.shape[0]
     half = depth // 2
 
+    tied = lax.optimization_barrier
     if two_by_two:
         parity = lax.rem(lax.axis_index("seq"), 2)
         up_mine = lax.dynamic_slice_in_dim(up_weight, parity * half, half, 0)
         up_a, up_b = x(up_mine), y(up_mine)
         gate_a, gate_b = x(gate_weight), y(gate_weight)
-        down_mine = lax.dynamic_slice_in_dim(down_weight, parity * half, half, 1)
-        down_rest = lax.dynamic_slice_in_dim(down_weight, (1 - parity) * half, half, 1)
     rim = shifted(tokens[-RIM:], 1)
     both_output = lax.all_gather(output_weight, "hid", axis=0, tiled=True)
 
@@ -426,32 +462,30 @@
         prompts, tokens, rim, attention_gain[None], project_weight, output_gate, decay_down.T,
         decay_up, decay_bias[None], conv_weight,
     )
-    one, two, three = (shifted(state, i) for i in (1, 2, 3))
     if two_by_two:
-        one, two, three, up_a, up_b, gate_a, gate_b = lax.optimization_barrier(
-            (one, two, three, up_a, up_b, gate_a, gate_b)
-        )
-        up_c, down_a = y(up_a), x(down_mine)
-        far_a, far_b = z(up_a), z(up_b)
-        gate_c = x(gate_b)
+        state, gate_a, gate_b = tied((state, gate_a, gate_b))
+        down_0, down_1 = down_weight[:, :half], down_weight[:, half:]
+        gate_c, down_b1 = x(gate_b), y(down_1)
+    one = shifted(state, 1)
+    two = shifted(joined(state, one), 2)
+    if two_by_two:
+        one, two, up_a, up_b, down_0 = tied((one, two, up_a, up_b, down_0))
+        up_c, far_a, far_b, down_a0 = y(up_a), z(up_a), z(up_b), x(down_0)
+        down_c0 = y(down_a0)
     states, *gated = pages(
-        prompts, raised, lowered, weighted, value, ends, opening, head_gain[None], one, two, three,
+        prompts, raised, lowered, weighted, value, ends, opening, head_gain[None], one, two,
     )
     others = [swapped(part, "hid", 1) for part in gated]
     if two_by_two:
-        others, up_c, down_a, far_a = lax.optimization_barrier((others, up_c, down_a, far_a))
-        down_b_rest = y(down_rest)
-        far_c = z(up_c)
-        down_c = y(down_a)
-        down_a_far = z(down_a)
+        others, up_c, gate_c, far_a, down_b1 = tied((others, up_c, gate_c, far_a, down_b1))
+        far_c = y(far_a)
     residual, feed = mix(tokens, gated, others, both_output, mixer_gain[None])
 
     if two_by_two:
-        feed, far_b, far_c, gate_c, down_b_rest = lax.optimization_barrier(
-            (feed, far_b, far_c, gate_c, down_b_rest)
-        )
-        down_c_rest = x(down_b_rest)
-        down_b = y(down_mine)
+        feed, down_0, down_1 = tied((feed, down_0, down_1))
+        down_b0, down_a1 = y(down_0), x(down_1)
+        feed, far_b, far_c, down_b1 = tied((feed, far_b, far_c, down_b1))
+        down_c1 = x(down_b1)
         at = lambda flip, more=0: lambda: (lax.axis_index("req") ^ flip) * depth + more
         own = lambda flip: lambda: at(flip)() + lax.rem(lax.axis_index("seq"), 2) * half
         far = lambda flip: lambda: at(flip)() + (1 - lax.rem(lax.axis_index("seq"), 2)) * half
@@ -460,24 +494,23 @@
             (up_weight, at(0)), (up_a, own(1)), (far_a, far(1)), (up_b, own(2)), (far_b, far(2)),
             (up_c, own(3)), (far_c, far(3)),
         ]
-        down_list = [
-            (down_weight, at(0)), (down_a, own(1)), (down_b_rest, far(2)), (down_c, own(3)),
-            (down_a_far, far(1)), (down_b, own(2)), (down_c_rest, far(3)),
+        down_lists = [
+            [(down_weight, at(0)), (down_a0, at(1)), (down_b1, at(2, half)), (down_b0, at(2))],
+            [(down_a1, at(1, half)), (down_c0, at(3)), (down_c1, at(3, half))],
         ]
     else:
         first = lambda: 0
         gate_list = [(lax.all_gather(gate_weight, "req", axis=0, tiled=True), first)]
         up_list = [(lax.all_gather(up_weight, "req", axis=0, tiled=True), first)]
-        down_list = [(lax.all_gather(down_weight, "req", axis=1, tiled=True), first)]
+        down_lists = [[(lax.all_gather(down_weight, "req", axis=1, tiled=True), first)]]
 
     hidden = widen(feed, (gate_list, up_list))
-    theirs_sum = narrow(hidden, lambda: 1 - lax.axis_index("hid"), down_list, width)
-    received = swapped(theirs_sum, "hid", 1)
-    own_sum = narrow(hidden, lambda: lax.axis_index("hid"), down_list, width)
-    own_rows = lax.dynamic_slice_in_dim(residual, hid_index * (count // 2), count // 2, 0)
-    result = (
-        own_rows.astype(F32) + (own_sum.astype(F32) + received.astype(F32))
-    ).astype(BF16)
+    groups = []
+    for pieces in down_lists:
+        theirs, mine = narrow(hidden, [piece for piece, _ in pieces])
+        received = swapped(theirs, "hid", 1)
+        groups.append((mine, received, [(piece.shape[1], place) for piece, place in pieces]))
+    result = close(hid_index, residual, groups)
     return result, states, edges
 
 

time: 194 us -> 169 us (0.87)
  waiting for transfers between devices: 38.8 us -> 23.2 us
  starting transfers between devices: 43.2 us -> 35.5 us
  other arithmetic: 4.16 us -> 0 us
    ppermute x18 -> x19, waiting for transfers between devices: 29.5 us -> 17.3 us  [swapped(): return lax.ppermute(value, axis, [(i, i ^ flip) for i in range(count)])]
    ppermute x18 -> x19, starting transfers between devices: 28.5 us -> 22.9 us  [swapped(): return lax.ppermute(value, axis, [(i, i ^ flip) for i in range(count)])]
    convert_element_type x1 -> x0, other arithmetic: 4.16 us -> none  [on_device(): result = (own_rows.astype(F32) + (own_sum.astype(F32) + received.astype(F...]
    ppermute x4 -> x3, waiting for transfers between devices: 8.66 us -> 5.23 us  [shifted(): lax.ppermute(value, 'seq', [(i, i + steps) for i in range(count - steps)])]
    ppermute x4 -> x3, starting transfers between devices: 14.6 us -> 12.6 us  [shifted(): lax.ppermute(value, 'seq', [(i, i + steps) for i in range(count - steps)])]
    unnamed x43 -> x41, local copies, waits for them, and re-layouts: 4.46 us -> 6.21 us
    pallas_call x3 -> x5, Pallas kernels: 43.8 us -> 44.6 us  [the longest x2 20.1 us: narrow(): pl.pallas_call(narrow_kernel, name='narrow', in_specs=[pl.BlockSpec(memor...]
  transfers between devices with their start and end apart: 23 -> 23, of which waited for: 9 -> 11; matrix products, arithmetic and copies ran while one was open for 3% -> 3% of each run, Pallas kernels for 37% -> 48%
where the time goes in v3:
time: 169 us; the launch traced here: 168 us
  Pallas kernels  84.4 us (50%)
  starting transfers between devices  35.5 us (21%)
  waiting for transfers between devices  23.2 us (14%)
  between operations  14.3 us (8%)
  local copies, waits for them, and re-layouts  10.9 us (6%)
    ppermute x19, starting transfers between devices, swapped(): return lax.ppermute(value, axis, [(i, i ^ flip) for i in range(count)])  22.9 us
    pallas_call x1, Pallas kernels, front(): pl.pallas_call(front_kernel, name='front', grid=(count // TILE,), in_spec...  20.8 us
    pallas_call x2, Pallas kernels, narrow(): pl.pallas_call(narrow_kernel, name='narrow', in_specs=[pl.BlockSpec(memor...  20.1 us
    pallas_call x1, Pallas kernels, widen(): pl.pallas_call(functools.partial(widen_kernel, places), name='widen', gri...  18.5 us
    ppermute x19, waiting for transfers between devices, swapped(): return lax.ppermute(value, axis, [(i, i ^ flip) for i in range(count)])  17.3 us
    ppermute x3, starting transfers between devices, shifted(): lax.ppermute(value, 'seq', [(i, i + steps) for i in range(count - steps)])  12.6 us
    pallas_call x1, Pallas kernels, mix(): pl.pallas_call(mix_kernel, name='mix', grid=(count // TILE,), in_specs=[r...  10.7 us
    pallas_call x1, Pallas kernels, pages(): pl.pallas_call(pages_kernel, name='pages', grid=(count // TILE,), in_spec...  8.2 us
  transfers between devices with their start and end apart: 23, of which 11 were waited for; matrix products, arithmetic and copies ran while one was open for 3% of the time, Pallas kernels for 48%

profile of v3, /device:TPU:0, one launch (start us, length us, event | category | flops | bytes accessed | tf_op | source)
XLA Modules:
  0.0 168.3 jit_solution(13840249883897446610)
XLA Ops:
  7.9 3.0 %collective-permute-start.1 = (bf16[512,1408]{1,0:T(8,128)(2,1)}, bf16[512,1408]{1,0:T(8,128)(2,1)}, u32[]{:S(2)}, u32[]{:S(2)}) collective-permute-start(bf16[512,1408]{1,0:T(8,128)(2,1)} %refs_0_.2), channel_id=1, source_target_pairs={{0,8},{8,0},{16,24},{24,16},{1,9},{9,1},{17,25},{25,17},{2,10},{10... | collective-permute-start | bytes 4325384 | tf_op jit(solution)/shard_map/ppermute | solution.py:431
  10.9 1.5 collective-permute-start.2
  13.3 3.5 %collective-permute-start = (bf16[16,2048]{1,0:T(8,128)(2,1)S(1)}, bf16[16,2048]{1,0:T(8,128)(2,1)S(1)}, u32[]{:S(2)}, u32[]{:S(2)}) collective-permute-start(bf16[16,2048]{1,0:T(8,128)(2,1)S(1)} %slice.9), channel_id=1, source_target_pairs={{0,2},{2,4},{4,6},{1,3},{3,5},{5,7},{8,10},{10,12},{12,14},{9,11},... | collective-permute-start | bytes 196616 | tf_op jit(solution)/shard_map/ppermute | solution.py:426
  20.0 20.8 %front.1 = (bf16[1024,256]{1,0:T(8,128)(2,1)}, bf16[1024,256]{1,0:T(8,128)(2,1)}, bf16[1024,256]{1,0:T(8,128)(2,1)}, bf16[1024,512]{1,0:T(8,128)(2,1)}, f32[16,8...) custom-call(s32[1,16]{1,0:T(1,128)} %pages_ref.3, ...), custom_call_target="tpu_custom_call" | custom-call | flops 1000 | bytes 1000 | tf_op jit(solution)/shard_map/front/pallas_call | solution.py:154
  40.8 2.8 %collective-permute-done.1.refs_1_ = bf16[512,1408]{1,0:T(8,128)(2,1)} collective-permute-done((bf16[512,1408]{1,0:T(8,128)(2,1)}, bf16[512,1408]{1,0:T(8,128)(2,1)}, u32[]{:S(2)}, u32[]{:S(2)}) %collective-permute-start.1) | collective-permute-done | bytes 1441824 | tf_op jit(solution)/shard_map/ppermute | solution.py:431
  43.7 2.1 %collective-permute-done.2.refs_2_ = bf16[512,1408]{1,0:T(8,128)(2,1)} collective-permute-done((bf16[512,1408]{1,0:T(8,128)(2,1)}, bf16[512,1408]{1,0:T(8,128)(2,1)}, u32[]{:S(2)}, u32[]{:S(2)}) %collective-permute-start.2) | collective-permute-done | bytes 1441824 | tf_op jit(solution)/shard_map/ppermute | solution.py:431
  45.8 3.6 %collective-permute-start.3 = (bf16[272,512]{1,0:T(8,128)(2,1)}, bf16[272,512]{1,0:T(8,128)(2,1)S(1)}, u32[]{:S(2)}, u32[]{:S(2)}) collective-permute-start(bf16[272,512]{1,0:T(8,128)(2,1)} %get-tuple-element.48.later_ref), channel_id=1, source_target_pairs={{0,2},{2,4},{4,6},{1,3},{3,5},{5,7},{8,10},{10,12},{12,14},{9,11},... | collective-permute-start | bytes 835592 | tf_op jit(solution)/shard_map/ppermute | solution.py:426
  51.2 1.5 collective-permute-start.12
  54.4 2.0 %joined.1 = bf16[272,512]{1,0:T(8,128)(2,1)} custom-call(bf16[272,512]{1,0:T(8,128)(2,1)} %get-tuple-element.48.later_ref, bf16[272,512]{1,0:T(8,128)(2,1)} %copy-done.4), custom_call_target="tpu_custom_call" | custom-call | flops 1000 | bytes 1000 | tf_op jit(solution)/shard_map/joined/pallas_call | solution.py:194
  56.4 5.5 %collective-permute-start.4 = (bf16[272,512]{1,0:T(8,128)(2,1)}, bf16[272,512]{1,0:T(8,128)(2,1)S(1)}, u32[]{:S(2)}, u32[]{:S(2)}) collective-permute-start(bf16[272,512]{1,0:T(8,128)(2,1)} %joined.1), channel_id=1, source_target_pairs={{0,4},{2,6},{1,5},{3,7},{8,12},{10,14},{9,13},{11,15},{16,20},{18,... | collective-permute-start | bytes 835592 | tf_op jit(solution)/shard_map/ppermute | solution.py:426
  61.9 4.2 %collective-permute-done.4.two_ref = bf16[272,512]{1,0:T(8,128)(2,1)S(1)} collective-permute-done((bf16[272,512]{1,0:T(8,128)(2,1)}, bf16[272,512]{1,0:T(8,128)(2,1)S(1)}, u32[]{:S(2)}, u32[]{:S(2)}) %collective-permute-start.4) | collective-permute-done | bytes 278560 | tf_op jit(solution)/shard_map/ppermute | solution.py:426
  66.1 5.8 %collective-permute-start.11 = (bf16[256,1408]{1,0:T(8,128)(2,1)}, bf16[256,1408]{1,0:T(8,128)(2,1)S(1)}, u32[]{:S(2)}, u32[]{:S(2)}) collective-permute-start(bf16[256,1408]{1,0:T(8,128)(2,1)} %collective-permute-done.5.refs_5_), channel_id=1, source_target_pairs={{0,2},{2,0},{4,6},{6,4},{1,3},{3,1},{5,7},{7,5},{8,10},{10,8},{12,... | collective-permute-start | bytes 2162696 | tf_op jit(solution)/shard_map/ppermute | solution.py:431
  71.9 1.5 collective-permute-start.9
  74.0 8.2 %pages.1 = (bf16[16,1,256,512]{3,2,1,0:T(8,128)(2,1)}, bf16[512,512]{1,0:T(8,128)(2,1)}, bf16[512,512]{1,0:T(8,128)(2,1)}) custom-call(s32[1,16]{1,0:T(1,128)} %pages_ref.3, s32[1,16]{1,0:T(1,128)} %start_ref.3, bf16[1024,256]{1,0:T(8,128)(2,1)} %get-tuple-element.41.raised_ref, bf16[1024,256]{1,0:T(8,128)(2,1)} %get-tuple-element.42.lowered_ref, ...), custom_call_target="tpu_custom_call" | custom-call | flops 1000 | bytes 1000 | tf_op jit(solution)/shard_map/pages/pallas_call | solution.py:253
  82.8 1.6 collective-permute-done.7.other_low_ref
  87.1 3.5 %collective-permute-done.9.refs_9_ = bf16[256,1408]{1,0:T(8,128)(2,1)S(1)} collective-permute-done((bf16[256,1408]{1,0:T(8,128)(2,1)}, bf16[256,1408]{1,0:T(8,128)(2,1)S(1)}, u32[]{:S(2)}, u32[]{:S(2)}) %collective-permute-start.9) | collective-permute-done | bytes 720928 | tf_op jit(solution)/shard_map/ppermute | solution.py:431
  90.5 1.6 collective-permute-start.14
  92.7 10.7 %mix.1 = (bf16[1024,2048]{1,0:T(8,128)(2,1)}, bf16[1024,2048]{1,0:T(8,128)(2,1)}) custom-call(bf16[1024,2048]{1,0:T(8,128)(2,1)} %tokens_ref.3, bf16[512,512]{1,0:T(8,128)(2,1)} %get-tuple-element.51.low_ref, bf16[512,512]{1,0:T(8,128)(2,1)} %get-tuple-element.52.high_ref, bf16[512,512]{1,0:T(8,128)(2,1)} %copy-done.12, bf16[512,512]{1,0:T(8,128)(2,1)} %copy-done.13, ...), custom_call_target="tpu_custom_call" | custom-call | flops 1000 | bytes 1000 | tf_op jit(solution)/shard_map/mix/pallas_call | solution.py:291
  104.6 1.8 %collective-permute-start.19 = (bf16[1408,256]{1,0:T(8,128)(2,1)}, bf16[1408,256]{1,0:T(8,128)(2,1)S(1)}, u32[]{:S(2)}, u32[]{:S(2)}) collective-permute-start(bf16[1408,256]{1,0:T(8,128)(2,1)} %collective-permute-done.15.refs_1_), channel_id=1, source_target_pairs={{0,16},{8,24},{16,0},{24,8},{1,17},{9,25},{17,1},{25,9},{2,18},{10... | collective-permute-start | bytes 2162696 | tf_op jit(solution)/shard_map/ppermute | solution.py:431
  106.4 3.4 %collective-permute-done.14.refs_10_ = bf16[256,1408]{1,0:T(8,128)(2,1)} collective-permute-done((bf16[256,1408]{1,0:T(8,128)(2,1)S(1)}, bf16[256,1408]{1,0:T(8,128)(2,1)}, u32[]{:S(2)}, u32[]{:S(2)}) %collective-permute-start.14) | collective-permute-done | bytes 720928 | tf_op jit(solution)/shard_map/ppermute | solution.py:431
  111.8 18.5 %widen.1.hidden_hbm = bf16[1024,1408]{1,0:T(8,128)(2,1)} custom-call(bf16[1024,2048]{1,0:T(8,128)(2,1)} %get-tuple-element.64.feed_ref, bf16[512,1408]{1,0:T(8,128)(2,1)} %refs_0_.2, bf16[512,1408]{1,0:T(8,128)(2,1)} %collective-permute-done.1.refs_1_, bf16[512,1408]{1,0:T(8,128)(2,1)} %collective-permute-done.2.refs_2_, bf16[512,1408]{1,0:T(8,128)(2,1)} %copy-done.2, ...), custom_call_target="tpu_custom_call" | custom-call | flops 1000 | bytes 1000 | tf_op jit(solution)/shard_map/widen/pallas_call | solution.py:320
  131.2 12.2 %narrow.2 = (bf16[512,1280]{1,0:T(8,128)(2,1)}, bf16[512,1280]{1,0:T(8,128)(2,1)}) custom-call(bf16[1024,1408]{1,0:T(8,128)(2,1)} %widen.1.hidden_hbm, bf16[1408,512]{1,0:T(8,128)(2,1)} %refs_0_.3, bf16[1408,256]{1,0:T(8,128)(2,1)} %collective-permute-done.15.refs_1_, bf16[1408,256]{1,0:T(8,128)(2,1)} %collective-permute-done.12.refs_2_, ...), custom_call_target="tpu_custom_call" | custom-call | flops 1000 | bytes 1000 | tf_op jit(solution)/shard_map/narrow/pallas_call | solution.py:374
  145.5 7.8 %narrow.3 = (bf16[512,768]{1,0:T(8,128)(2,1)}, bf16[512,768]{1,0:T(8,128)(2,1)}) custom-call(bf16[1024,1408]{1,0:T(8,128)(2,1)} %widen.1.hidden_hbm, bf16[1408,256]{1,0:T(8,128)(2,1)} %copy-done.10, bf16[1408,256]{1,0:T(8,128)(2,1)} %copy-done.8, bf16[1408,256]{1,0:T(8,128)(2,1)} %copy-done.9), custom_call_target="tpu_custom_call" | custom-call | flops 1000 | bytes 1000 | tf_op jit(solution)/shard_map/narrow/pallas_call | solution.py:374
  157.4 4.1 %close.1 = bf16[512,2048]{1,0:T(8,128)(2,1)} custom-call(s32[1]{0:T(128)} %bitcast.half_ref, bf16[1024,2048]{1,0:T(8,128)(2,1)} %get-tuple-element.57.refs_0_, bf16[512,1280]{1,0:T(8,128)(2,1)} %get-tuple-element.72.refs_1_, bf16[512,1280]{1,0:T(8,128)(2,1)} %copy-done.3, bf16[512,768]{1,0:T(8,128)(2,1)} %get-tuple-element.75.refs_3_, bf16[512,768]{1,0:T(8,128)(2,1)} %copy-done.5), custom_call_target="tpu_custom_call" | custom-call | flops 1000 | bytes 1000 | tf_op jit(solution)/shard_map/close/pallas_call | solution.py:404
  (78 shorter events, 22.8 us)
Async XLA Ops:
  7.2 85.6 %all-gather.2.cloned.1.call-start = ((), (), s32[]{:S(2)}) async-start(), calls=%async_computation | async-start | bytes 6291456 | tf_op jit(solution)/shard_map/all_gather | solution.py:459
  7.9 35.7 %collective-permute-start.1 = (bf16[512,1408]{1,0:T(8,128)(2,1)}, bf16[512,1408]{1,0:T(8,128)(2,1)}, u32[]{:S(2)}, u32[]{:S(2)}) collective-permute-start(bf16[512,1408]{1,0:T(8,128)(2,1)} %refs_0_.2), channel_id=1, source_target_pairs={{0,8},{8,0},{16,24},{24,16},{1,9},{9,1},{17,25},{25,17},{2,10},{10... | collective-permute-start | bytes 4325384 | tf_op jit(solution)/shard_map/ppermute | solution.py:431
  10.9 34.8 %collective-permute-start.2 = (bf16[512,1408]{1,0:T(8,128)(2,1)}, bf16[512,1408]{1,0:T(8,128)(2,1)}, u32[]{:S(2)}, u32[]{:S(2)}) collective-permute-start(bf16[512,1408]{1,0:T(8,128)(2,1)} %refs_0_.2), channel_id=1, source_target_pairs={{0,16},{8,24},{16,0},{24,8},{1,17},{9,25},{17,1},{25,9},{2,18},{10... | collective-permute-start | bytes 4325384 | tf_op jit(solution)/shard_map/ppermute | solution.py:431
  13.3 6.1 %collective-permute-start = (bf16[16,2048]{1,0:T(8,128)(2,1)S(1)}, bf16[16,2048]{1,0:T(8,128)(2,1)S(1)}, u32[]{:S(2)}, u32[]{:S(2)}) collective-permute-start(bf16[16,2048]{1,0:T(8,128)(2,1)S(1)} %slice.9), channel_id=1, source_target_pairs={{0,2},{2,4},{4,6},{1,3},{3,5},{5,7},{8,10},{10,12},{12,14},{9,11},... | collective-permute-start | bytes 196616 | tf_op jit(solution)/shard_map/ppermute | solution.py:426
  17.7 44.2 %collective-permute-start.5 = (bf16[256,1408]{1,0:T(8,128)(2,1)}, bf16[256,1408]{1,0:T(8,128)(2,1)}, u32[]{:S(2)}, u32[]{:S(2)}) collective-permute-start(bf16[256,1408]{1,0:T(8,128)(2,1)} %constant_dynamic-slice_fusion), channel_id=1, source_target_pairs={{0,8},{8,0},{16,24},{24,16},{1,9},{9,1},{17,25},{25,17},{2,10},{10... | collective-permute-start | bytes 2162696 | tf_op jit(solution)/shard_map/ppermute | solution.py:431
  18.2 43.7 %collective-permute-start.6 = (bf16[256,1408]{1,0:T(8,128)(2,1)}, bf16[256,1408]{1,0:T(8,128)(2,1)}, u32[]{:S(2)}, u32[]{:S(2)}) collective-permute-start(bf16[256,1408]{1,0:T(8,128)(2,1)} %constant_dynamic-slice_fusion), channel_id=1, source_target_pairs={{0,16},{8,24},{16,0},{24,8},{1,17},{9,25},{17,1},{25,9},{2,18},{10... | collective-permute-start | bytes 2162696 | tf_op jit(solution)/shard_map/ppermute | solution.py:431
  20.0 30.0 %copy-start = (bf16[1408,512]{1,0:T(8,128)(2,1)S(1)}, bf16[1408,512]{1,0:T(8,128)(2,1)}, u32[]{:S(2)}) copy-start(bf16[1408,512]{1,0:T(8,128)(2,1)} %refs_0_.3) | copy-start | bytes 4325380
  45.8 8.0 %collective-permute-start.3 = (bf16[272,512]{1,0:T(8,128)(2,1)}, bf16[272,512]{1,0:T(8,128)(2,1)S(1)}, u32[]{:S(2)}, u32[]{:S(2)}) collective-permute-start(bf16[272,512]{1,0:T(8,128)(2,1)} %get-tuple-element.48.later_ref), channel_id=1, source_target_pairs={{0,2},{2,4},{4,6},{1,3},{3,5},{5,7},{8,10},{10,12},{12,14},{9,11},... | collective-permute-start | bytes 835592 | tf_op jit(solution)/shard_map/ppermute | solution.py:426
  49.4 41.2 %collective-permute-start.10 = (bf16[512,1408]{1,0:T(8,128)(2,1)}, bf16[512,1408]{1,0:T(8,128)(2,1)S(1)}, u32[]{:S(2)}, u32[]{:S(2)}) collective-permute-start(bf16[512,1408]{1,0:T(8,128)(2,1)} %collective-permute-done.2.refs_2_), channel_id=1, source_target_pairs={{0,8},{8,0},{16,24},{24,16},{1,9},{9,1},{17,25},{25,17},{2,10},{10... | collective-permute-start | bytes 4325384 | tf_op jit(solution)/shard_map/ppermute | solution.py:431
  51.2 31.2 %collective-permute-start.12 = (bf16[1408,256]{1,0:T(8,128)(2,1)}, bf16[1408,256]{1,0:T(8,128)(2,1)}, u32[]{:S(2)}, u32[]{:S(2)}) collective-permute-start(bf16[1408,256]{1,0:T(8,128)(2,1)} %get-tuple-element.74), channel_id=1, source_target_pairs={{0,16},{8,24},{16,0},{24,8},{1,17},{9,25},{17,1},{25,9},{2,18},{10... | collective-permute-start | bytes 2162696 | tf_op jit(solution)/shard_map/ppermute | solution.py:431
  56.4 9.7 %collective-permute-start.4 = (bf16[272,512]{1,0:T(8,128)(2,1)}, bf16[272,512]{1,0:T(8,128)(2,1)S(1)}, u32[]{:S(2)}, u32[]{:S(2)}) collective-permute-start(bf16[272,512]{1,0:T(8,128)(2,1)} %joined.1), channel_id=1, source_target_pairs={{0,4},{2,6},{1,5},{3,7},{8,12},{10,14},{9,13},{11,15},{16,20},{18,... | collective-permute-start | bytes 835592 | tf_op jit(solution)/shard_map/ppermute | solution.py:426
  66.1 21.0 %collective-permute-start.11 = (bf16[256,1408]{1,0:T(8,128)(2,1)}, bf16[256,1408]{1,0:T(8,128)(2,1)S(1)}, u32[]{:S(2)}, u32[]{:S(2)}) collective-permute-start(bf16[256,1408]{1,0:T(8,128)(2,1)} %collective-permute-done.5.refs_5_), channel_id=1, source_target_pairs={{0,2},{2,0},{4,6},{6,4},{1,3},{3,1},{5,7},{7,5},{8,10},{10,8},{12,... | collective-permute-start | bytes 2162696 | tf_op jit(solution)/shard_map/ppermute | solution.py:431
  71.9 18.6 %collective-permute-start.9 = (bf16[256,1408]{1,0:T(8,128)(2,1)}, bf16[256,1408]{1,0:T(8,128)(2,1)S(1)}, u32[]{:S(2)}, u32[]{:S(2)}) collective-permute-start(bf16[256,1408]{1,0:T(8,128)(2,1)} %collective-permute-done.5.refs_5_), channel_id=1, source_target_pairs={{0,16},{8,24},{16,0},{24,8},{1,17},{9,25},{17,1},{25,9},{2,18},{10... | collective-permute-start | bytes 2162696 | tf_op jit(solution)/shard_map/ppermute | solution.py:431
  82.2 2.2 %collective-permute-start.7 = (bf16[512,512]{1,0:T(8,128)(2,1)}, bf16[512,512]{1,0:T(8,128)(2,1)S(1)}, u32[]{:S(2)}, u32[]{:S(2)}) collective-permute-start(bf16[512,512]{1,0:T(8,128)(2,1)} %get-tuple-element.51.low_ref), channel_id=1, source_target_pairs={{0,1},{1,0},{2,3},{3,2},{4,5},{5,4},{6,7},{7,6},{8,9},{9,8},{10,11... | collective-permute-start | bytes 1572872 | tf_op jit(solution)/shard_map/ppermute | solution.py:431
  82.3 2.8 %collective-permute-start.8 = (bf16[512,512]{1,0:T(8,128)(2,1)}, bf16[512,512]{1,0:T(8,128)(2,1)S(1)}, u32[]{:S(2)}, u32[]{:S(2)}) collective-permute-start(bf16[512,512]{1,0:T(8,128)(2,1)} %get-tuple-element.52.high_ref), channel_id=1, source_target_pairs={{0,1},{1,0},{2,3},{3,2},{4,5},{5,4},{6,7},{7,6},{8,9},{9,8},{10,11... | collective-permute-start | bytes 1572872 | tf_op jit(solution)/shard_map/ppermute | solution.py:431
  84.4 22.0 %collective-permute-start.13 = (bf16[256,1408]{1,0:T(8,128)(2,1)}, bf16[256,1408]{1,0:T(8,128)(2,1)}, u32[]{:S(2)}, u32[]{:S(2)}) collective-permute-start(bf16[256,1408]{1,0:T(8,128)(2,1)} %collective-permute-done.6.refs_7_), channel_id=1, source_target_pairs={{0,2},{2,0},{4,6},{6,4},{1,3},{3,1},{5,7},{7,5},{8,10},{10,8},{12,... | collective-permute-start | bytes 2162696 | tf_op jit(solution)/shard_map/ppermute | solution.py:431
  85.2 19.4 %collective-permute-start.15 = (bf16[1408,256]{1,0:T(8,128)(2,1)}, bf16[1408,256]{1,0:T(8,128)(2,1)}, u32[]{:S(2)}, u32[]{:S(2)}) collective-permute-start(bf16[1408,256]{1,0:T(8,128)(2,1)} %get-tuple-element.71), channel_id=1, source_target_pairs={{0,8},{8,0},{16,24},{24,16},{1,9},{9,1},{17,25},{25,17},{2,10},{10... | collective-permute-start | bytes 2162696 | tf_op jit(solution)/shard_map/ppermute | solution.py:431
  90.5 19.2 %collective-permute-start.14 = (bf16[256,1408]{1,0:T(8,128)(2,1)S(1)}, bf16[256,1408]{1,0:T(8,128)(2,1)}, u32[]{:S(2)}, u32[]{:S(2)}) collective-permute-start(bf16[256,1408]{1,0:T(8,128)(2,1)S(1)} %collective-permute-done.11.refs_6_), channel_id=1, source_target_pairs={{0,16},{8,24},{16,0},{24,8},{1,17},{9,25},{17,1},{25,9},{2,18},{10... | collective-permute-start | bytes 2162696 | tf_op jit(solution)/shard_map/ppermute | solution.py:431
  103.5 26.9 %collective-permute-start.16 = (bf16[1408,256]{1,0:T(8,128)(2,1)}, bf16[1408,256]{1,0:T(8,128)(2,1)S(1)}, u32[]{:S(2)}, u32[]{:S(2)}) collective-permute-start(bf16[1408,256]{1,0:T(8,128)(2,1)} %get-tuple-element.71), channel_id=1, source_target_pairs={{0,16},{8,24},{16,0},{24,8},{1,17},{9,25},{17,1},{25,9},{2,18},{10... | collective-permute-start | bytes 2162696 | tf_op jit(solution)/shard_map/ppermute | solution.py:431
  104.6 38.9 %collective-permute-start.19 = (bf16[1408,256]{1,0:T(8,128)(2,1)}, bf16[1408,256]{1,0:T(8,128)(2,1)S(1)}, u32[]{:S(2)}, u32[]{:S(2)}) collective-permute-start(bf16[1408,256]{1,0:T(8,128)(2,1)} %collective-permute-done.15.refs_1_), channel_id=1, source_target_pairs={{0,16},{8,24},{16,0},{24,8},{1,17},{9,25},{17,1},{25,9},{2,18},{10... | collective-permute-start | bytes 2162696 | tf_op jit(solution)/shard_map/ppermute | solution.py:431
  109.8 33.7 %collective-permute-start.20 = (bf16[1408,256]{1,0:T(8,128)(2,1)}, bf16[1408,256]{1,0:T(8,128)(2,1)S(1)}, u32[]{:S(2)}, u32[]{:S(2)}) collective-permute-start(bf16[1408,256]{1,0:T(8,128)(2,1)} %collective-permute-done.12.refs_2_), channel_id=1, source_target_pairs={{0,8},{8,0},{16,24},{24,16},{1,9},{9,1},{17,25},{25,17},{2,10},{10... | collective-permute-start | bytes 2162696 | tf_op jit(solution)/shard_map/ppermute | solution.py:431
  110.9 32.6 %collective-permute-start.18 = (bf16[1408,256]{1,0:T(8,128)(2,1)}, bf16[1408,256]{1,0:T(8,128)(2,1)S(1)}, u32[]{:S(2)}, u32[]{:S(2)}) collective-permute-start(bf16[1408,256]{1,0:T(8,128)(2,1)} %get-tuple-element.74), channel_id=1, source_target_pairs={{0,8},{8,0},{16,24},{24,16},{1,9},{9,1},{17,25},{25,17},{2,10},{10... | collective-permute-start | bytes 2162696 | tf_op jit(solution)/shard_map/ppermute | solution.py:431
  143.4 12.6 %collective-permute-start.17 = (bf16[512,1280]{1,0:T(8,128)(2,1)}, bf16[512,1280]{1,0:T(8,128)(2,1)S(1)}, u32[]{:S(2)}, u32[]{:S(2)}) collective-permute-start(bf16[512,1280]{1,0:T(8,128)(2,1)} %get-tuple-element.73), channel_id=1, source_target_pairs={{0,1},{1,0},{2,3},{3,2},{4,5},{5,4},{6,7},{7,6},{8,9},{9,8},{10,11... | collective-permute-start | bytes 3932168 | tf_op jit(solution)/shard_map/ppermute | solution.py:431
  153.3 2.7 %collective-permute-start.21 = (bf16[512,768]{1,0:T(8,128)(2,1)}, bf16[512,768]{1,0:T(8,128)(2,1)S(1)}, u32[]{:S(2)}, u32[]{:S(2)}) collective-permute-start(bf16[512,768]{1,0:T(8,128)(2,1)} %get-tuple-element.76), channel_id=1, source_target_pairs={{0,1},{1,0},{2,3},{3,2},{4,5},{5,4},{6,7},{7,6},{8,9},{9,8},{10,11... | collective-permute-start | bytes 2359304 | tf_op jit(solution)/shard_map/ppermute | solution.py:431
  (19 other events, 148.5 us)
Sparse Core Ops, SparseCore 0:
  9.6 16.3 all-gather.1

commit v4 on v3

--- a/solution.py
+++ b/solution.py
@@ -20,6 +20,8 @@
 F32 = jnp.float32
 VMEM_LIMIT = 56 * 1024 * 1024
 WIDE = 256
+FRONT = 512
+MIX = 256
 
 
 def params():
@@ -66,8 +68,8 @@
     return x * lax.rsqrt(jnp.mean(x * x, axis=-1, keepdims=True) + EPSILON) * gain
 
 
-def carried_flag(pages_ref, start_ref, page):
-    page = lax.axis_index("seq") * (pl.num_programs(0) * PAGES_T) + page
+def carried_flag(pages_ref, start_ref, page, count):
+    page = lax.axis_index("seq") * count + page
     same = jnp.int32(0)
     for i in range(pages_ref.shape[1]):
         first = start_ref[0, i]
@@ -75,68 +77,104 @@
     return same.astype(F32)
 
 
+def product(left, rows, weight_ref, columns, step=512):
+    depth = weight_ref.shape[0]
+    total = None
+    for k in range(0, depth, step):
+        span = pl.ds(k, min(step, depth - k))
+        part = dot(left[rows, span], weight_ref[span, columns])
+        total = part if total is None else total + part
+    return total
+
+
+def rms_columns(read, write, gain_ref, width):
+    total = None
+    for low in range(0, width, WIDE):
+        x = read(pl.ds(low, WIDE))
+        square = x * x
+        part = square[:, : WIDE // 2] + square[:, WIDE // 2 :]
+        total = part if total is None else total + part
+    scale = lax.rsqrt(jnp.sum(total, axis=-1, keepdims=True) * (1.0 / width) + EPSILON)
+    for low in range(0, width, WIDE):
+        columns = pl.ds(low, WIDE)
+        write(columns, read(columns) * scale * gain_ref[:, columns].astype(F32))
+
+
 def front_kernel(
     pages_ref, start_ref, tokens_ref, rim_ref, gain_ref, project_ref, gate_ref, down_ref, up_ref, bias_ref,
     conv_ref, raised_ref, lowered_ref, weighted_ref, value_ref, ends_ref, edges_ref, opening_ref,
-    state_ref, carry, state, decay,
+    state_ref, normed, carry, state, decay, keys,
 ):
     step = pl.program_id(0)
+    tile, width = tokens_ref.shape
+    pages = tile // PAGE
 
     @pl.when(step == 0)
     def _():
         state[...] = jnp.zeros_like(state)
         decay[...] = jnp.ones_like(decay)
 
-    gain = gain_ref[...].astype(F32)
-    rows = jnp.concatenate([tokens_ref[...], rim_ref[...]], axis=0).astype(F32)
-    normed_all = normalised(rows, gain).astype(BF16)
-    normed = normed_all[:TILE]
-    projected_low = dot(normed_all, project_ref[...]).astype(BF16)
-    projected = projected_low[:TILE].astype(F32)
-    rim = projected_low[TILE:].astype(F32)[RIM - 8 :]
-    previous = jnp.where(step == 0, rim, carry[...])
-    carry[...] = projected[TILE - 8 :]
-    opening_ref[...] = silu(dot(normed, gate_ref[...])).astype(BF16)
-
-    lowrank = dot_nt(normed, down_ref[...]).astype(BF16)
+    blocks = [(rim_ref, 0, tile, RIM)] + [(tokens_ref, r, r, 128) for r in range(0, tile, 128)]
+    for ref, source, target, count in blocks:
+        def write(columns, x, target=target, count=count):
+            normed[pl.ds(target, count), columns] = x.astype(BF16)
+        rms_columns(
+            lambda columns, ref=ref, source=source, count=count: ref[pl.ds(source, count), columns].astype(F32),
+            write, gain_ref, width,
+        )
+
+    lowrank = dot_nt(normed[:tile], down_ref[...]).astype(BF16)
     logits = dot(lowrank, up_ref[...]) + bias_ref[...]
     decay_log = (jnp.minimum(logits, 0.0) - jnp.log1p(jnp.exp(-jnp.abs(logits)))) / 16.0
-    row = lax.broadcasted_iota(jnp.int32, (TILE, TILE), 0)
-    col = lax.broadcasted_iota(jnp.int32, (TILE, TILE), 1)
+    row = lax.broadcasted_iota(jnp.int32, (HK, HK), 0)
+    col = lax.broadcasted_iota(jnp.int32, (HK, HK), 1)
     lower = jnp.where((row >= col) & ((row // PAGE) == (col // PAGE)), 1.0, 0.0).astype(F32)
-    sums = jnp.dot(lower, decay_log, preferred_element_type=F32, precision=lax.Precision.HIGHEST)
-
-    taps = conv_ref[...].astype(F32)
-    suffix = jnp.ones((1, HK), F32)
-    pieces = [None] * PAGES_T
-    for j in reversed(range(PAGES_T)):
-        carried = carried_flag(pages_ref, start_ref, step * PAGES_T + j)
-        now = projected[j * PAGE : (j + 1) * PAGE]
-        before = previous if j == 0 else projected[j * PAGE - 8 : j * PAGE]
-        widened = jnp.concatenate([before * carried, now], axis=0)
-        mixed = taps[0:1] * now
-        for i in range(1, KCONV):
-            mixed = mixed + taps[i : i + 1] * widened[8 - i : 8 - i + PAGE]
-        query = silu(mixed[:, :HK])
-        key = silu(mixed[:, HK : 2 * HK]) * HK ** (-0.5)
-        value = mixed[:, 2 * HK :].astype(BF16)
-        sums_j = sums[j * PAGE : (j + 1) * PAGE]
-        end = sums_j[PAGE - 1 :]
-        weighted = key * jnp.exp(end - sums_j)
-        span = pl.ds(j * PAGE, PAGE)
-        raised_ref[span, :] = (query * jnp.exp(sums_j)).astype(BF16)
-        lowered_ref[span, :] = (key * jnp.exp(-sums_j)).astype(BF16)
-        weighted_ref[span, :] = weighted.astype(BF16)
-        value_ref[span, :] = value
-        kept = jnp.exp(end)
+    sums = [
+        jnp.dot(lower, decay_log[r : r + HK], preferred_element_type=F32, precision=lax.Precision.HIGHEST)
+        for r in range(0, tile, HK)
+    ]
+    sums = [part[r : r + PAGE] for part in sums for r in range(0, HK, PAGE)]
+    ends = [part[PAGE - 1 :] for part in sums]
+    carried = [carried_flag(pages_ref, start_ref, step * pages + j, pl.num_programs(0) * pages) for j in range(pages)]
+    suffix = [None] * pages + [jnp.ones((1, HK), F32)]
+    for j in reversed(range(pages)):
+        kept = jnp.exp(ends[j])
         ends_ref[j] = jnp.broadcast_to(kept, (8, HK))
-        edges_ref[j] = projected_low[(j + 1) * PAGE - (KCONV - 1) : (j + 1) * PAGE]
-        pieces[j] = ((weighted * suffix).astype(BF16), value)
-        suffix = suffix * (kept * carried)
-    keys = jnp.concatenate([p[0] for p in pieces], axis=0)
-    values = jnp.concatenate([p[1] for p in pieces], axis=0)
-    state[...] = column(suffix) * state[...] + dot_tn(keys, values)
-    decay[...] = decay[...] * suffix
+        suffix[j] = suffix[j + 1] * (kept * carried[j])
+
+    everything = slice(None)
+    for chunk in (1, 2, 3, 0):
+        columns = pl.ds(chunk * WIDE, WIDE)
+        low = product(normed, everything, project_ref, columns).astype(BF16)
+        projected = low[:tile].astype(F32)
+        previous = jnp.where(step == 0, low[tile:].astype(F32)[RIM - 8 :], carry[:, columns])
+        carry[:, columns] = projected[tile - 8 :]
+        taps = conv_ref[:, columns].astype(F32)
+        for j in range(pages):
+            now = projected[j * PAGE : (j + 1) * PAGE]
+            before = previous if j == 0 else projected[j * PAGE - 8 : j * PAGE]
+            widened = jnp.concatenate([before * carried[j], now], axis=0)
+            mixed = taps[0:1] * now
+            for i in range(1, KCONV):
+                mixed = mixed + taps[i : i + 1] * widened[8 - i : 8 - i + PAGE]
+            span = pl.ds(j * PAGE, PAGE)
+            edges_ref[j, :, columns] = low[(j + 1) * PAGE - (KCONV - 1) : (j + 1) * PAGE]
+            if chunk == 0:
+                raised_ref[span, :] = (silu(mixed) * jnp.exp(sums[j])).astype(BF16)
+            elif chunk == 1:
+                key = silu(mixed) * HK ** (-0.5)
+                weighted = key * jnp.exp(ends[j] - sums[j])
+                lowered_ref[span, :] = (key * jnp.exp(-sums[j])).astype(BF16)
+                weighted_ref[span, :] = weighted.astype(BF16)
+                keys[span, :] = (weighted * suffix[j + 1]).astype(BF16)
+            else:
+                at = pl.ds((chunk - 2) * WIDE, WIDE)
+                value_ref[span, at] = mixed.astype(BF16)
+    state[...] = column(suffix[0]) * state[...] + dot_tn(keys[...], value_ref[...])
+    decay[...] = decay[...] * suffix[0]
+    for low in range(0, HV, WIDE):
+        columns = pl.ds(low, WIDE)
+        opening_ref[:, columns] = silu(product(normed, pl.ds(0, tile), gate_ref, columns)).astype(BF16)
 
     @pl.when(step == pl.num_programs(0) - 1)
     def _():
@@ -149,12 +187,13 @@
     count, width = tokens.shape
     rank = down.shape[0]
     pages = count // PAGE
-    rows = lambda n: pl.BlockSpec((TILE, n), lambda i: (i, 0))
+    tile = FRONT
+    rows = lambda n: pl.BlockSpec((tile, n), lambda i: (i, 0))
     shape = jax.ShapeDtypeStruct
     return pl.pallas_call(
         front_kernel,
         name="front",
-        grid=(count // TILE,),
+        grid=(count // tile,),
         in_specs=[
             whole_smem(), whole_smem(), rows(width), fixed((RIM, width)), fixed((1, width)),
             fixed((width, CONVW)), fixed((width, HV)), fixed((rank, width)), fixed((rank, HK)),
@@ -162,8 +201,8 @@
         ],
         out_specs=[
             rows(HK), rows(HK), rows(HK), rows(HV),
-            pl.BlockSpec((PAGES_T, 8, HK), lambda i: (i, 0, 0)),
-            pl.BlockSpec((PAGES_T, KCONV - 1, CONVW), lambda i: (i, 0, 0)),
+            pl.BlockSpec((tile // PAGE, 8, HK), lambda i: (i, 0, 0)),
+            pl.BlockSpec((tile // PAGE, KCONV - 1, CONVW), lambda i: (i, 0, 0)),
             rows(HV), fixed((HK + RIM, HV)),
         ],
         out_shape=[
@@ -173,7 +212,8 @@
             shape((HK + RIM, HV), BF16),
         ],
         scratch_shapes=[
-            pltpu.VMEM((8, CONVW), F32), pltpu.VMEM((HK, HV), F32), pltpu.VMEM((8, HK), F32)
+            pltpu.VMEM((tile + RIM, width), BF16), pltpu.VMEM((8, CONVW), F32),
+            pltpu.VMEM((HK, HV), F32), pltpu.VMEM((8, HK), F32), pltpu.VMEM((tile, HK), BF16),
         ],
         compiler_params=params(),
         cost_estimate=cost(1000, 1000),
@@ -200,11 +240,11 @@
     )(later, earlier)
 
 
-def halves(count):
-    half = count // TILE // 2
+def halves(count, tile):
+    half = count // tile // 2
     return [
-        pl.BlockSpec((TILE, HV), lambda i: (jnp.minimum(i, half - 1), 0)),
-        pl.BlockSpec((TILE, HV), lambda i: (jnp.maximum(i - half, 0), 0)),
+        pl.BlockSpec((tile, HV), lambda i: (jnp.minimum(i, half - 1), 0)),
+        pl.BlockSpec((tile, HV), lambda i: (jnp.maximum(i - half, 0), 0)),
     ]
 
 
@@ -226,7 +266,7 @@
     for j in range(PAGES_T):
         span = pl.ds(j * PAGE, PAGE)
         raised, value = raised_ref[span, :], value_ref[span, :]
-        held = held * carried_flag(pages_ref, start_ref, step * PAGES_T + j)
+        held = held * carried_flag(pages_ref, start_ref, step * PAGES_T + j, pl.num_programs(0) * PAGES_T)
         scores = dot_nt(raised, lowered_ref[span, :])
         scores = jnp.where(row >= col, scores, 0.0).astype(BF16)
         attended = dot(scores, value) + dot(raised, held.astype(BF16))
@@ -260,7 +300,7 @@
             fixed((HK + RIM, HV)), fixed((HK + RIM, HV)),
         ],
         out_specs=[
-            pl.BlockSpec((PAGES_T, 1, HK, HV), lambda i: (i, 0, 0, 0)), *halves(count),
+            pl.BlockSpec((PAGES_T, 1, HK, HV), lambda i: (i, 0, 0, 0)), *halves(count, TILE),
         ],
         out_shape=[
             jax.ShapeDtypeStruct((total, 1, HK, HV), BF16),
@@ -273,33 +313,42 @@
     )(*prompts, raised, lowered, weighted, value, ends, opening, gain, one, two)
 
 
-def mix_kernel(tokens_ref, low_ref, high_ref, other_low_ref, other_high_ref, weight_ref, gain_ref, residual_ref, feed_ref):
-    step, half = pl.program_id(0), pl.num_programs(0) // 2
-    own = jnp.where(step < half, low_ref[...], high_ref[...])
-    other = jnp.where(step < half, other_low_ref[...], other_high_ref[...])
-    mine = lax.axis_index("hid")
-    rows = lambda head: pl.ds(pl.multiple_of(head * HV, HV), HV)
-    mixed = dot(own, weight_ref[rows(mine), :]) + dot(other, weight_ref[rows(1 - mine), :])
-    residual = (tokens_ref[...].astype(F32) + mixed).astype(BF16)
-    residual_ref[...] = residual
-    feed_ref[...] = normalised(residual.astype(F32), gain_ref[...].astype(F32)).astype(BF16)
-
-
-def mix(tokens, own, others, weight, gain):
+def mix_kernel(
+    tokens_ref, low_ref, high_ref, other_low_ref, other_high_ref, own_weight_ref, other_weight_ref,
+    gain_ref, residual_ref, feed_ref,
+):
+    first = pl.program_id(0) < pl.num_programs(0) // 2
+    own = jnp.where(first, low_ref[...], high_ref[...])
+    other = jnp.where(first, other_low_ref[...], other_high_ref[...])
+    width = tokens_ref.shape[1]
+    for at in range(0, width, WIDE):
+        columns = pl.ds(at, WIDE)
+        mixed = dot(own, own_weight_ref[:, columns]) + dot(other, other_weight_ref[:, columns])
+        residual_ref[:, columns] = (tokens_ref[:, columns].astype(F32) + mixed).astype(BF16)
+
+    def write(columns, x):
+        feed_ref[:, columns] = x.astype(BF16)
+
+    rms_columns(lambda columns: residual_ref[:, columns].astype(F32), write, gain_ref, width)
+
+
+def mix(tokens, own, others, own_weight, other_weight, gain):
     count, width = tokens.shape
-    rows = lambda n: pl.BlockSpec((TILE, n), lambda i: (i, 0))
+    tile = MIX
+    rows = pl.BlockSpec((tile, width), lambda i: (i, 0))
     return pl.pallas_call(
         mix_kernel,
         name="mix",
-        grid=(count // TILE,),
+        grid=(count // tile,),
         in_specs=[
-            rows(width), *halves(count), *halves(count), fixed(weight.shape), fixed((1, width)),
-        ],
-        out_specs=[rows(width), rows(width)],
+            rows, *halves(count, tile), *halves(count, tile), fixed((HV, width)), fixed((HV, width)),
+            fixed((1, width)),
+        ],
+        out_specs=[rows, rows],
         out_shape=[jax.ShapeDtypeStruct((count, width), BF16)] * 2,
         compiler_params=params(),
         cost_estimate=cost(1000, 1000),
-    )(tokens, *own, *others, weight, gain)
+    )(tokens, *own, *others, own_weight, other_weight, gain)
 
 
 def widen_kernel(places, feed_ref, *refs):
@@ -330,7 +379,7 @@
     )(feed, *pieces)
 
 
-def narrow_kernel(hidden_hbm, *refs):
+def narrow_kernel(block, hidden_hbm, *refs):
     count = (len(refs) - 5) // 2
     pieces, theirs_ref, own_ref, hidden = refs[:count], *refs[count : count + 3]
     weights, sem, sems = refs[count + 3 : -2], refs[-2], refs[-1]
@@ -352,27 +401,24 @@
         copy.start()
     for copy in wholes:
         copy.wait()
-    depth = hidden.shape[1]
     at = 0
     for copy, weight in zip(copies, weights):
         copy.wait()
         for low in range(0, weight.shape[1], WIDE):
-            total = None
-            for k in range(0, depth, WIDE):
-                span = pl.ds(k, min(WIDE, depth - k))
-                part = dot(hidden[:, span], weight[span, pl.ds(low, WIDE)])
-                total = part if total is None else total + part
-            columns = pl.ds(at, WIDE)
-            theirs_ref[:, columns] = total[:rows].astype(BF16)
-            own_ref[:, columns] = total[rows:].astype(BF16)
+            for first in range(0, 2 * rows, block):
+                total = product(hidden, pl.ds(first, block), weight, pl.ds(low, WIDE)).astype(BF16)
+                for out_ref, start in ((theirs_ref, 0), (own_ref, rows)):
+                    if first < start + rows and start < first + block:
+                        taken = total[max(start - first, 0) : start + rows - first]
+                        out_ref[pl.ds(max(first - start, 0), taken.shape[0]), pl.ds(at, WIDE)] = taken
             at += WIDE
 
 
-def narrow(hidden, pieces):
+def narrow(hidden, pieces, block):
     count, depth = hidden.shape
     width = sum(piece.shape[1] for piece in pieces)
     return pl.pallas_call(
-        narrow_kernel,
+        functools.partial(narrow_kernel, block),
         name="narrow",
         in_specs=[pl.BlockSpec(memory_space=pl.ANY)] * (1 + len(pieces)),
         out_specs=[pl.BlockSpec(memory_space=pltpu.VMEM)] * 2,
@@ -456,7 +502,7 @@
         up_a, up_b = x(up_mine), y(up_mine)
         gate_a, gate_b = x(gate_weight), y(gate_weight)
     rim = shifted(tokens[-RIM:], 1)
-    both_output = lax.all_gather(output_weight, "hid", axis=0, tiled=True)
+    rim, other_output = lax.optimization_barrier((rim, swapped(output_weight, "hid", 1)))
 
     raised, lowered, weighted, value, ends, edges, opening, state = front(
         prompts, tokens, rim, attention_gain[None], project_weight, output_gate, decay_down.T,
@@ -479,7 +525,7 @@
     if two_by_two:
         others, up_c, gate_c, far_a, down_b1 = tied((others, up_c, gate_c, far_a, down_b1))
         far_c = y(far_a)
-    residual, feed = mix(tokens, gated, others, both_output, mixer_gain[None])
+    residual, feed = mix(tokens, gated, others, output_weight, other_output, mixer_gain[None])
 
     if two_by_two:
         feed, down_0, down_1 = tied((feed, down_0, down_1))
@@ -506,8 +552,8 @@
 
     hidden = widen(feed, (gate_list, up_list))
     groups = []
-    for pieces in down_lists:
-        theirs, mine = narrow(hidden, [piece for piece, _ in pieces])
+    for pieces, parts in zip(down_lists, (1, 2)):
+        theirs, mine = narrow(hidden, [piece for piece, _ in pieces], count // parts)
         received = swapped(theirs, "hid", 1)
         groups.append((mine, received, [(piece.shape[1], place) for piece, place in pieces]))
     result = close(hid_index, residual, groups)

time: 169 us -> 154 us (0.911)
  between operations: 14.3 us -> 0.87 us
  Pallas kernels: 84.4 us -> 82.5 us
    pallas_call x4, Pallas kernels: 51.6 us -> 49.6 us  [the longest x1 20.2 us: front(): pl.pallas_call(front_kernel, name='front', grid=(count // tile,), in_spec...]
    ppermute x19 -> x20, waiting for transfers between devices: 17.3 us -> 16.4 us  [swapped(): return lax.ppermute(value, axis, [(i, i ^ flip) for i in range(count)])]
    unnamed x41 -> x49, local copies, waits for them, and re-layouts: 6.21 us -> 5.36 us
    ppermute x19 -> x20, starting transfers between devices: 22.9 us -> 23.7 us  [swapped(): return lax.ppermute(value, axis, [(i, i ^ flip) for i in range(count)])]
  transfers between devices with their start and end apart: 23 -> 23, of which waited for: 11 -> 10; matrix products, arithmetic and copies ran while one was open for 3% -> 4% of each run, Pallas kernels for 48% -> 51%
where the time goes in v4:
time: 154 us; the launch traced here: 153 us
  Pallas kernels  82.5 us (54%)
  starting transfers between devices  36.3 us (24%)
  waiting for transfers between devices  22.1 us (14%)
  local copies, waits for them, and re-layouts  11.4 us (7%)
    ppermute x20, starting transfers between devices, swapped(): return lax.ppermute(value, axis, [(i, i ^ flip) for i in range(count)])  23.7 us
    pallas_call x1, Pallas kernels, front(): pl.pallas_call(front_kernel, name='front', grid=(count // tile,), in_spec...  20.2 us
    pallas_call x2, Pallas kernels, narrow(): pl.pallas_call(functools.partial(narrow_kernel, block), name='narrow', in...  18.7 us
    pallas_call x1, Pallas kernels, widen(): pl.pallas_call(functools.partial(widen_kernel, places), name='widen', gri...  18.5 us
    ppermute x20, waiting for transfers between devices, swapped(): return lax.ppermute(value, axis, [(i, i ^ flip) for i in range(count)])  16.4 us
    ppermute x3, starting transfers between devices, shifted(): lax.ppermute(value, 'seq', [(i, i + steps) for i in range(count - steps)])  12.6 us
    pallas_call x1, Pallas kernels, mix(): pl.pallas_call(mix_kernel, name='mix', grid=(count // tile,), in_specs=[r...  10.7 us
    pallas_call x1, Pallas kernels, pages(): pl.pallas_call(pages_kernel, name='pages', grid=(count // TILE,), in_spec...  8.29 us
  transfers between devices with their start and end apart: 23, of which 10 were waited for; matrix products, arithmetic and copies ran while one was open for 4% of the time, Pallas kernels for 51%

profile of v4, /device:TPU:0, one launch (start us, length us, event | category | flops | bytes accessed | tf_op | source)
XLA Modules:
  0.0 153.1 jit_solution(4307953525829115565)
XLA Ops:
  1.2 2.6 %collective-permute-start.2 = (bf16[512,1408]{1,0:T(8,128)(2,1)}, bf16[512,1408]{1,0:T(8,128)(2,1)}, u32[]{:S(2)}, u32[]{:S(2)}) collective-permute-start(bf16[512,1408]{1,0:T(8,128)(2,1)} %refs_0_.2), channel_id=1, source_target_pairs={{0,8},{8,0},{16,24},{24,16},{1,9},{9,1},{17,25},{25,17},{2,10},{10... | collective-permute-start | bytes 4325384 | tf_op jit(solution)/shard_map/ppermute | solution.py:477
  3.7 1.5 collective-permute-start.3
  6.1 3.5 %collective-permute-start = (bf16[16,2048]{1,0:T(8,128)(2,1)S(1)}, bf16[16,2048]{1,0:T(8,128)(2,1)S(1)}, u32[]{:S(2)}, u32[]{:S(2)}) collective-permute-start(bf16[16,2048]{1,0:T(8,128)(2,1)S(1)} %slice.9), channel_id=1, source_target_pairs={{0,2},{2,4},{4,6},{1,3},{3,5},{5,7},{8,10},{10,12},{12,14},{9,11},... | collective-permute-start | bytes 196616 | tf_op jit(solution)/shard_map/ppermute | solution.py:472
  9.6 2.0 %constant_dynamic-slice_fusion = bf16[256,1408]{1,0:T(8,128)(2,1)} fusion(bf16[512,1408]{1,0:T(8,128)(2,1)} %refs_4_.1, s32[]{:T(128)S(6)} %select_n.3), kind=kLoop, calls=%fused_computation | loop fusion | bytes 1441796 | tf_op jit(solution)/shard_map/dynamic_slice | solution.py:501
  13.4 20.2 %front.1 = (bf16[1024,256]{1,0:T(8,128)(2,1)}, bf16[1024,256]{1,0:T(8,128)(2,1)}, bf16[1024,256]{1,0:T(8,128)(2,1)}, bf16[1024,512]{1,0:T(8,128)(2,1)}, f32[16,8...) custom-call(s32[1,16]{1,0:T(1,128)} %pages_ref.3, ...), custom_call_target="tpu_custom_call" | custom-call | flops 1000 | bytes 1000 | tf_op jit(solution)/shard_map/front/pallas_call | solution.py:193
  33.6 2.9 %collective-permute-done.2.refs_1_ = bf16[512,1408]{1,0:T(8,128)(2,1)} collective-permute-done((bf16[512,1408]{1,0:T(8,128)(2,1)}, bf16[512,1408]{1,0:T(8,128)(2,1)}, u32[]{:S(2)}, u32[]{:S(2)}) %collective-permute-start.2) | collective-permute-done | bytes 1441824 | tf_op jit(solution)/shard_map/ppermute | solution.py:477
  36.5 2.0 %collective-permute-done.3.refs_2_ = bf16[512,1408]{1,0:T(8,128)(2,1)} collective-permute-done((bf16[512,1408]{1,0:T(8,128)(2,1)}, bf16[512,1408]{1,0:T(8,128)(2,1)}, u32[]{:S(2)}, u32[]{:S(2)}) %collective-permute-start.3) | collective-permute-done | bytes 1441824 | tf_op jit(solution)/shard_map/ppermute | solution.py:477
  38.5 3.6 %collective-permute-start.4 = (bf16[272,512]{1,0:T(8,128)(2,1)}, bf16[272,512]{1,0:T(8,128)(2,1)S(1)}, u32[]{:S(2)}, u32[]{:S(2)}) collective-permute-start(bf16[272,512]{1,0:T(8,128)(2,1)} %get-tuple-element.51.later_ref), channel_id=1, source_target_pairs={{0,2},{2,4},{4,6},{1,3},{3,5},{5,7},{8,10},{10,12},{12,14},{9,11},... | collective-permute-start | bytes 835592 | tf_op jit(solution)/shard_map/ppermute | solution.py:472
  43.9 1.5 collective-permute-start.13
  45.4 1.6 %collective-permute-done.4.earlier_ref.one_ref = bf16[272,512]{1,0:T(8,128)(2,1)S(1)} collective-permute-done((bf16[272,512]{1,0:T(8,128)(2,1)}, bf16[272,512]{1,0:T(8,128)(2,1)S(1)}, u32[]{:S(2)}, u32[]{:S(2)}) %collective-permute-start.4) | collective-permute-done | bytes 278560 | tf_op jit(solution)/shard_map/ppermute | solution.py:472
  47.7 2.0 %joined.1 = bf16[272,512]{1,0:T(8,128)(2,1)} custom-call(bf16[272,512]{1,0:T(8,128)(2,1)} %get-tuple-element.51.later_ref, bf16[272,512]{1,0:T(8,128)(2,1)} %copy-done.4), custom_call_target="tpu_custom_call" | custom-call | flops 1000 | bytes 1000 | tf_op jit(solution)/shard_map/joined/pallas_call | solution.py:234
  49.7 5.5 %collective-permute-start.5 = (bf16[272,512]{1,0:T(8,128)(2,1)}, bf16[272,512]{1,0:T(8,128)(2,1)S(1)}, u32[]{:S(2)}, u32[]{:S(2)}) collective-permute-start(bf16[272,512]{1,0:T(8,128)(2,1)} %joined.1), channel_id=1, source_target_pairs={{0,4},{2,6},{1,5},{3,7},{8,12},{10,14},{9,13},{11,15},{16,20},{18,... | collective-permute-start | bytes 835592 | tf_op jit(solution)/shard_map/ppermute | solution.py:472
  55.2 4.1 %collective-permute-done.5.two_ref = bf16[272,512]{1,0:T(8,128)(2,1)S(1)} collective-permute-done((bf16[272,512]{1,0:T(8,128)(2,1)}, bf16[272,512]{1,0:T(8,128)(2,1)S(1)}, u32[]{:S(2)}, u32[]{:S(2)}) %collective-permute-start.5) | collective-permute-done | bytes 278560 | tf_op jit(solution)/shard_map/ppermute | solution.py:472
  59.3 1.5 collective-permute-start.10
  60.9 7.2 %collective-permute-start.12 = (bf16[256,1408]{1,0:T(8,128)(2,1)}, bf16[256,1408]{1,0:T(8,128)(2,1)S(1)}, u32[]{:S(2)}, u32[]{:S(2)}) collective-permute-start(bf16[256,1408]{1,0:T(8,128)(2,1)} %collective-permute-done.6.refs_5_), channel_id=1, source_target_pairs={{0,2},{2,0},{4,6},{6,4},{1,3},{3,1},{5,7},{7,5},{8,10},{10,8},{12,... | collective-permute-start | bytes 2162696 | tf_op jit(solution)/shard_map/ppermute | solution.py:477
  68.6 8.3 %pages.1 = (bf16[16,1,256,512]{3,2,1,0:T(8,128)(2,1)}, bf16[512,512]{1,0:T(8,128)(2,1)}, bf16[512,512]{1,0:T(8,128)(2,1)}) custom-call(s32[1,16]{1,0:T(1,128)} %pages_ref.3, s32[1,16]{1,0:T(1,128)} %start_ref.3, bf16[1024,256]{1,0:T(8,128)(2,1)} %get-tuple-element.44.raised_ref, bf16[1024,256]{1,0:T(8,128)(2,1)} %get-tuple-element.45.lowered_ref, ...), custom_call_target="tpu_custom_call" | custom-call | flops 1000 | bytes 1000 | tf_op jit(solution)/shard_map/pages/pallas_call | solution.py:293
  77.5 1.6 %collective-permute-done.8.other_low_ref = bf16[512,512]{1,0:T(8,128)(2,1)S(1)} collective-permute-done((bf16[512,512]{1,0:T(8,128)(2,1)}, bf16[512,512]{1,0:T(8,128)(2,1)S(1)}, u32[]{:S(2)}, u32[]{:S(2)}) %collective-permute-start.8) | collective-permute-done | bytes 524320 | tf_op jit(solution)/shard_map/ppermute | solution.py:477
  80.6 3.4 %collective-permute-done.10.refs_9_ = bf16[256,1408]{1,0:T(8,128)(2,1)S(1)} collective-permute-done((bf16[256,1408]{1,0:T(8,128)(2,1)}, bf16[256,1408]{1,0:T(8,128)(2,1)S(1)}, u32[]{:S(2)}, u32[]{:S(2)}) %collective-permute-start.10) | collective-permute-done | bytes 720928 | tf_op jit(solution)/shard_map/ppermute | solution.py:477
  86.6 10.7 %mix.1 = (bf16[1024,2048]{1,0:T(8,128)(2,1)}, bf16[1024,2048]{1,0:T(8,128)(2,1)}) custom-call(bf16[1024,2048]{1,0:T(8,128)(2,1)} %tokens_ref.3, bf16[512,512]{1,0:T(8,128)(2,1)} %get-tuple-element.54.low_ref, bf16[512,512]{1,0:T(8,128)(2,1)} %get-tuple-element.55.high_ref, bf16[512,512]{1,0:T(8,128)(2,1)} %copy-done.16, bf16[512,512]{1,0:T(8,128)(2,1)} %copy-done.17, ...), custom_call_target="tpu_custom_call" | custom-call | flops 1000 | bytes 1000 | tf_op jit(solution)/shard_map/mix/pallas_call | solution.py:339
  101.2 2.9 %collective-permute-done.15.refs_10_ = bf16[256,1408]{1,0:T(8,128)(2,1)S(1)} collective-permute-done((bf16[256,1408]{1,0:T(8,128)(2,1)S(1)}, bf16[256,1408]{1,0:T(8,128)(2,1)S(1)}, u32[]{:S(2)}, u32[]{:S(2)}) %collective-permute-start.15) | collective-permute-done | bytes 720928 | tf_op jit(solution)/shard_map/ppermute | solution.py:477
  105.1 18.5 %widen.1.hidden_hbm = bf16[1024,1408]{1,0:T(8,128)(2,1)} custom-call(bf16[1024,2048]{1,0:T(8,128)(2,1)} %get-tuple-element.68.feed_ref, bf16[512,1408]{1,0:T(8,128)(2,1)} %refs_0_.2, bf16[512,1408]{1,0:T(8,128)(2,1)} %collective-permute-done.2.refs_1_, bf16[512,1408]{1,0:T(8,128)(2,1)} %collective-permute-done.3.refs_2_, bf16[512,1408]{1,0:T(8,128)(2,1)} %copy-done.2, ...), custom_call_target="tpu_custom_call" | custom-call | flops 1000 | bytes 1000 | tf_op jit(solution)/shard_map/widen/pallas_call | solution.py:369
  124.5 12.2 %narrow.2 = (bf16[512,1280]{1,0:T(8,128)(2,1)}, bf16[512,1280]{1,0:T(8,128)(2,1)}) custom-call(bf16[1024,1408]{1,0:T(8,128)(2,1)} %widen.1.hidden_hbm, bf16[1408,512]{1,0:T(8,128)(2,1)} %refs_0_.3, bf16[1408,256]{1,0:T(8,128)(2,1)} %copy-done.10, bf16[1408,256]{1,0:T(8,128)(2,1)} %collective-permute-done.13.refs_2_, bf16[1408,256]{1,0:T(8,128)(2,1)} %copy-done.14), custom_call_target="tpu_custom_call" | custom-call | flops 1000 | bytes 1000 | tf_op jit(solution)/shard_map/narrow/pallas_call | solution.py:420
  138.9 6.4 %narrow.3 = (bf16[512,768]{1,0:T(8,128)(2,1)}, bf16[512,768]{1,0:T(8,128)(2,1)}) custom-call(bf16[1024,1408]{1,0:T(8,128)(2,1)} %widen.1.hidden_hbm, bf16[1408,256]{1,0:T(8,128)(2,1)} %copy-done.12, bf16[1408,256]{1,0:T(8,128)(2,1)} %copy-done.11, bf16[1408,256]{1,0:T(8,128)(2,1)} %copy-done.13), custom_call_target="tpu_custom_call" | custom-call | flops 1000 | bytes 1000 | tf_op jit(solution)/shard_map/narrow/pallas_call | solution.py:420
  149.0 4.1 %close.1 = bf16[512,2048]{1,0:T(8,128)(2,1)} custom-call(s32[1]{0:T(128)} %bitcast.half_ref, bf16[1024,2048]{1,0:T(8,128)(2,1)} %get-tuple-element.61.refs_0_, bf16[512,1280]{1,0:T(8,128)(2,1)} %get-tuple-element.76.refs_1_, bf16[512,1280]{1,0:T(8,128)(2,1)} %copy-done.3, bf16[512,768]{1,0:T(8,128)(2,1)} %get-tuple-element.79.refs_3_, bf16[512,768]{1,0:T(8,128)(2,1)} %copy-done.5), custom_call_target="tpu_custom_call" | custom-call | flops 1000 | bytes 1000 | tf_op jit(solution)/shard_map/close/pallas_call | solution.py:450
  (85 shorter events, 22.3 us)
Async XLA Ops:
  0.6 12.6 %collective-permute-start.1 = (bf16[512,2048]{1,0:T(8,128)(2,1)}, bf16[512,2048]{1,0:T(8,128)(2,1)S(1)}, u32[]{:S(2)}, u32[]{:S(2)}) collective-permute-start(bf16[512,2048]{1,0:T(8,128)(2,1)} %own_weight_ref.1), channel_id=1, source_target_pairs={{0,1},{1,0},{2,3},{3,2},{4,5},{5,4},{6,7},{7,6},{8,9},{9,8},{10,11... | collective-permute-start | bytes 6291464 | tf_op jit(solution)/shard_map/ppermute | solution.py:477
  1.2 35.3 %collective-permute-start.2 = (bf16[512,1408]{1,0:T(8,128)(2,1)}, bf16[512,1408]{1,0:T(8,128)(2,1)}, u32[]{:S(2)}, u32[]{:S(2)}) collective-permute-start(bf16[512,1408]{1,0:T(8,128)(2,1)} %refs_0_.2), channel_id=1, source_target_pairs={{0,8},{8,0},{16,24},{24,16},{1,9},{9,1},{17,25},{25,17},{2,10},{10... | collective-permute-start | bytes 4325384 | tf_op jit(solution)/shard_map/ppermute | solution.py:477
  3.7 34.7 %collective-permute-start.3 = (bf16[512,1408]{1,0:T(8,128)(2,1)}, bf16[512,1408]{1,0:T(8,128)(2,1)}, u32[]{:S(2)}, u32[]{:S(2)}) collective-permute-start(bf16[512,1408]{1,0:T(8,128)(2,1)} %refs_0_.2), channel_id=1, source_target_pairs={{0,16},{8,24},{16,0},{24,8},{1,17},{9,25},{17,1},{25,9},{2,18},{10... | collective-permute-start | bytes 4325384 | tf_op jit(solution)/shard_map/ppermute | solution.py:477
  6.1 6.7 %collective-permute-start = (bf16[16,2048]{1,0:T(8,128)(2,1)S(1)}, bf16[16,2048]{1,0:T(8,128)(2,1)S(1)}, u32[]{:S(2)}, u32[]{:S(2)}) collective-permute-start(bf16[16,2048]{1,0:T(8,128)(2,1)S(1)} %slice.9), channel_id=1, source_target_pairs={{0,2},{2,4},{4,6},{1,3},{3,5},{5,7},{8,10},{10,12},{12,14},{9,11},... | collective-permute-start | bytes 196616 | tf_op jit(solution)/shard_map/ppermute | solution.py:472
  11.6 43.6 %collective-permute-start.6 = (bf16[256,1408]{1,0:T(8,128)(2,1)}, bf16[256,1408]{1,0:T(8,128)(2,1)}, u32[]{:S(2)}, u32[]{:S(2)}) collective-permute-start(bf16[256,1408]{1,0:T(8,128)(2,1)} %constant_dynamic-slice_fusion), channel_id=1, source_target_pairs={{0,8},{8,0},{16,24},{24,16},{1,9},{9,1},{17,25},{25,17},{2,10},{10... | collective-permute-start | bytes 2162696 | tf_op jit(solution)/shard_map/ppermute | solution.py:477
  12.7 42.4 %collective-permute-start.7 = (bf16[256,1408]{1,0:T(8,128)(2,1)}, bf16[256,1408]{1,0:T(8,128)(2,1)}, u32[]{:S(2)}, u32[]{:S(2)}) collective-permute-start(bf16[256,1408]{1,0:T(8,128)(2,1)} %constant_dynamic-slice_fusion), channel_id=1, source_target_pairs={{0,16},{8,24},{16,0},{24,8},{1,17},{9,25},{17,1},{25,9},{2,18},{10... | collective-permute-start | bytes 2162696 | tf_op jit(solution)/shard_map/ppermute | solution.py:477
  38.5 29.6 %copy-start.23 = (bf16[512]{0:T(512)(128)(2,1)S(1)}, bf16[512]{0:T(512)(128)(2,1)}, u32[]{:S(2)}) copy-start(bf16[512]{0:T(512)(128)(2,1)} %param.24) | copy-start | bytes 3076
  38.5 8.5 %collective-permute-start.4 = (bf16[272,512]{1,0:T(8,128)(2,1)}, bf16[272,512]{1,0:T(8,128)(2,1)S(1)}, u32[]{:S(2)}, u32[]{:S(2)}) collective-permute-start(bf16[272,512]{1,0:T(8,128)(2,1)} %get-tuple-element.51.later_ref), channel_id=1, source_target_pairs={{0,2},{2,4},{4,6},{1,3},{3,5},{5,7},{8,10},{10,12},{12,14},{9,11},... | collective-permute-start | bytes 835592 | tf_op jit(solution)/shard_map/ppermute | solution.py:472
  42.1 43.2 %collective-permute-start.11 = (bf16[512,1408]{1,0:T(8,128)(2,1)}, bf16[512,1408]{1,0:T(8,128)(2,1)S(1)}, u32[]{:S(2)}, u32[]{:S(2)}) collective-permute-start(bf16[512,1408]{1,0:T(8,128)(2,1)} %collective-permute-done.3.refs_2_), channel_id=1, source_target_pairs={{0,8},{8,0},{16,24},{24,16},{1,9},{9,1},{17,25},{25,17},{2,10},{10... | collective-permute-start | bytes 4325384 | tf_op jit(solution)/shard_map/ppermute | solution.py:477
  43.9 33.1 %collective-permute-start.13 = (bf16[1408,256]{1,0:T(8,128)(2,1)}, bf16[1408,256]{1,0:T(8,128)(2,1)}, u32[]{:S(2)}, u32[]{:S(2)}) collective-permute-start(bf16[1408,256]{1,0:T(8,128)(2,1)} %get-tuple-element.78), channel_id=1, source_target_pairs={{0,16},{8,24},{16,0},{24,8},{1,17},{9,25},{17,1},{25,9},{2,18},{10... | collective-permute-start | bytes 2162696 | tf_op jit(solution)/shard_map/ppermute | solution.py:477
  49.7 9.7 %collective-permute-start.5 = (bf16[272,512]{1,0:T(8,128)(2,1)}, bf16[272,512]{1,0:T(8,128)(2,1)S(1)}, u32[]{:S(2)}, u32[]{:S(2)}) collective-permute-start(bf16[272,512]{1,0:T(8,128)(2,1)} %joined.1), channel_id=1, source_target_pairs={{0,4},{2,6},{1,5},{3,7},{8,12},{10,14},{9,13},{11,15},{16,20},{18,... | collective-permute-start | bytes 835592 | tf_op jit(solution)/shard_map/ppermute | solution.py:472
  59.3 24.6 %collective-permute-start.10 = (bf16[256,1408]{1,0:T(8,128)(2,1)}, bf16[256,1408]{1,0:T(8,128)(2,1)S(1)}, u32[]{:S(2)}, u32[]{:S(2)}) collective-permute-start(bf16[256,1408]{1,0:T(8,128)(2,1)} %collective-permute-done.6.refs_5_), channel_id=1, source_target_pairs={{0,16},{8,24},{16,0},{24,8},{1,17},{9,25},{17,1},{25,9},{2,18},{10... | collective-permute-start | bytes 2162696 | tf_op jit(solution)/shard_map/ppermute | solution.py:477
  60.9 24.4 %collective-permute-start.12 = (bf16[256,1408]{1,0:T(8,128)(2,1)}, bf16[256,1408]{1,0:T(8,128)(2,1)S(1)}, u32[]{:S(2)}, u32[]{:S(2)}) collective-permute-start(bf16[256,1408]{1,0:T(8,128)(2,1)} %collective-permute-done.6.refs_5_), channel_id=1, source_target_pairs={{0,2},{2,0},{4,6},{6,4},{1,3},{3,1},{5,7},{7,5},{8,10},{10,8},{12,... | collective-permute-start | bytes 2162696 | tf_op jit(solution)/shard_map/ppermute | solution.py:477
  76.9 2.2 %collective-permute-start.8 = (bf16[512,512]{1,0:T(8,128)(2,1)}, bf16[512,512]{1,0:T(8,128)(2,1)S(1)}, u32[]{:S(2)}, u32[]{:S(2)}) collective-permute-start(bf16[512,512]{1,0:T(8,128)(2,1)} %get-tuple-element.54.low_ref), channel_id=1, source_target_pairs={{0,1},{1,0},{2,3},{3,2},{4,5},{5,4},{6,7},{7,6},{8,9},{9,8},{10,11... | collective-permute-start | bytes 1572872 | tf_op jit(solution)/shard_map/ppermute | solution.py:477
  77.0 2.8 %collective-permute-start.9 = (bf16[512,512]{1,0:T(8,128)(2,1)}, bf16[512,512]{1,0:T(8,128)(2,1)S(1)}, u32[]{:S(2)}, u32[]{:S(2)}) collective-permute-start(bf16[512,512]{1,0:T(8,128)(2,1)} %get-tuple-element.55.high_ref), channel_id=1, source_target_pairs={{0,1},{1,0},{2,3},{3,2},{4,5},{5,4},{6,7},{7,6},{8,9},{9,8},{10,11... | collective-permute-start | bytes 1572872 | tf_op jit(solution)/shard_map/ppermute | solution.py:477
  79.1 22.1 %collective-permute-start.14 = (bf16[256,1408]{1,0:T(8,128)(2,1)}, bf16[256,1408]{1,0:T(8,128)(2,1)S(1)}, u32[]{:S(2)}, u32[]{:S(2)}) collective-permute-start(bf16[256,1408]{1,0:T(8,128)(2,1)} %collective-permute-done.7.refs_7_), channel_id=1, source_target_pairs={{0,2},{2,0},{4,6},{6,4},{1,3},{3,1},{5,7},{7,5},{8,10},{10,8},{12,... | collective-permute-start | bytes 2162696 | tf_op jit(solution)/shard_map/ppermute | solution.py:477
  79.9 18.9 %collective-permute-start.16 = (bf16[1408,256]{1,0:T(8,128)(2,1)S(1)}, bf16[1408,256]{1,0:T(8,128)(2,1)S(1)}, u32[]{:S(2)}, u32[]{:S(2)}) collective-permute-start(bf16[1408,256]{1,0:T(8,128)(2,1)S(1)} %copy-done.15), channel_id=1, source_target_pairs={{0,8},{8,0},{16,24},{24,16},{1,9},{9,1},{17,25},{25,17},{2,10},{10... | collective-permute-start | bytes 2162696 | tf_op jit(solution)/shard_map/ppermute | solution.py:477
  85.3 18.8 %collective-permute-start.15 = (bf16[256,1408]{1,0:T(8,128)(2,1)S(1)}, bf16[256,1408]{1,0:T(8,128)(2,1)S(1)}, u32[]{:S(2)}, u32[]{:S(2)}) collective-permute-start(bf16[256,1408]{1,0:T(8,128)(2,1)S(1)} %collective-permute-done.12.refs_6_), channel_id=1, source_target_pairs={{0,16},{8,24},{16,0},{24,8},{1,17},{9,25},{17,1},{25,9},{2,18},{10... | collective-permute-start | bytes 2162696 | tf_op jit(solution)/shard_map/ppermute | solution.py:477
  97.4 26.3 %collective-permute-start.17 = (bf16[1408,256]{1,0:T(8,128)(2,1)S(1)}, bf16[1408,256]{1,0:T(8,128)(2,1)S(1)}, u32[]{:S(2)}, u32[]{:S(2)}) collective-permute-start(bf16[1408,256]{1,0:T(8,128)(2,1)S(1)} %copy-done.15), channel_id=1, source_target_pairs={{0,16},{8,24},{16,0},{24,8},{1,17},{9,25},{17,1},{25,9},{2,18},{10... | collective-permute-start | bytes 2162696 | tf_op jit(solution)/shard_map/ppermute | solution.py:477
  98.8 38.1 %collective-permute-start.20 = (bf16[1408,256]{1,0:T(8,128)(2,1)S(1)}, bf16[1408,256]{1,0:T(8,128)(2,1)S(1)}, u32[]{:S(2)}, u32[]{:S(2)}) collective-permute-start(bf16[1408,256]{1,0:T(8,128)(2,1)S(1)} %collective-permute-done.16.refs_1_), channel_id=1, source_target_pairs={{0,16},{8,24},{16,0},{24,8},{1,17},{9,25},{17,1},{25,9},{2,18},{10... | collective-permute-start | bytes 2162696 | tf_op jit(solution)/shard_map/ppermute | solution.py:477
  99.7 37.2 %collective-permute-start.19 = (bf16[1408,256]{1,0:T(8,128)(2,1)}, bf16[1408,256]{1,0:T(8,128)(2,1)S(1)}, u32[]{:S(2)}, u32[]{:S(2)}) collective-permute-start(bf16[1408,256]{1,0:T(8,128)(2,1)} %get-tuple-element.78), channel_id=1, source_target_pairs={{0,8},{8,0},{16,24},{24,16},{1,9},{9,1},{17,25},{25,17},{2,10},{10... | collective-permute-start | bytes 2162696 | tf_op jit(solution)/shard_map/ppermute | solution.py:477
  104.1 32.8 %collective-permute-start.21 = (bf16[1408,256]{1,0:T(8,128)(2,1)}, bf16[1408,256]{1,0:T(8,128)(2,1)S(1)}, u32[]{:S(2)}, u32[]{:S(2)}) collective-permute-start(bf16[1408,256]{1,0:T(8,128)(2,1)} %collective-permute-done.13.refs_2_), channel_id=1, source_target_pairs={{0,8},{8,0},{16,24},{24,16},{1,9},{9,1},{17,25},{25,17},{2,10},{10... | collective-permute-start | bytes 2162696 | tf_op jit(solution)/shard_map/ppermute | solution.py:477
  136.8 9.8 %collective-permute-start.18 = (bf16[512,1280]{1,0:T(8,128)(2,1)}, bf16[512,1280]{1,0:T(8,128)(2,1)S(1)}, u32[]{:S(2)}, u32[]{:S(2)}) collective-permute-start(bf16[512,1280]{1,0:T(8,128)(2,1)} %get-tuple-element.77), channel_id=1, source_target_pairs={{0,1},{1,0},{2,3},{3,2},{4,5},{5,4},{6,7},{7,6},{8,9},{9,8},{10,11... | collective-permute-start | bytes 3932168 | tf_op jit(solution)/shard_map/ppermute | solution.py:477
  145.4 2.7 %collective-permute-start.22 = (bf16[512,768]{1,0:T(8,128)(2,1)}, bf16[512,768]{1,0:T(8,128)(2,1)S(1)}, u32[]{:S(2)}, u32[]{:S(2)}) collective-permute-start(bf16[512,768]{1,0:T(8,128)(2,1)} %get-tuple-element.80), channel_id=1, source_target_pairs={{0,1},{1,0},{2,3},{3,2},{4,5},{5,4},{6,7},{7,6},{8,9},{9,8},{10,11... | collective-permute-start | bytes 2359304 | tf_op jit(solution)/shard_map/ppermute | solution.py:477
  (23 other events, 197.0 us)

commit v5 on v4

--- a/solution.py
+++ b/solution.py
@@ -18,10 +18,11 @@
 RIM = 16
 BF16 = jnp.bfloat16
 F32 = jnp.float32
-VMEM_LIMIT = 56 * 1024 * 1024
+VMEM_LIMIT = 60 * 1024 * 1024
 WIDE = 256
 FRONT = 512
 MIX = 256
+ROWS = 512
 
 
 def params():
@@ -100,13 +101,38 @@
         write(columns, read(columns) * scale * gain_ref[:, columns].astype(F32))
 
 
+def norm_into(normed, gain_ref, blocks):
+    for ref, source, target, count in blocks:
+        def read(columns, ref=ref, source=source, count=count):
+            return ref[pl.ds(source, count), columns].astype(F32)
+
+        def write(columns, x, target=target, count=count):
+            normed[pl.ds(target, count), columns] = x.astype(BF16)
+
+        rms_columns(read, write, gain_ref, normed.shape[1])
+
+
+def short_conv(projected, previous, carried, taps, j):
+    now = projected[j * PAGE : (j + 1) * PAGE]
+    before = previous if j == 0 else projected[j * PAGE - 8 : j * PAGE]
+    widened = jnp.concatenate([before * carried, now], axis=0)
+    mixed = taps[0:1] * now
+    for i in range(1, KCONV):
+        mixed = mixed + taps[i : i + 1] * widened[8 - i : 8 - i + PAGE]
+    return mixed
+
+
+def page_edge(low, j):
+    return low[(j + 1) * PAGE - (KCONV - 1) : (j + 1) * PAGE]
+
+
 def front_kernel(
-    pages_ref, start_ref, tokens_ref, rim_ref, gain_ref, project_ref, gate_ref, down_ref, up_ref, bias_ref,
-    conv_ref, raised_ref, lowered_ref, weighted_ref, value_ref, ends_ref, edges_ref, opening_ref,
+    pages_ref, start_ref, tokens_ref, rim_ref, gain_ref, key_ref, first_ref, second_ref, down_ref, up_ref,
+    bias_ref, conv_ref, normed_ref, sums_ref, lowered_ref, weighted_ref, value_ref, ends_ref, edges_ref,
     state_ref, normed, carry, state, decay, keys,
 ):
     step = pl.program_id(0)
-    tile, width = tokens_ref.shape
+    tile = tokens_ref.shape[0]
     pages = tile // PAGE
 
     @pl.when(step == 0)
@@ -114,67 +140,54 @@
         state[...] = jnp.zeros_like(state)
         decay[...] = jnp.ones_like(decay)
 
-    blocks = [(rim_ref, 0, tile, RIM)] + [(tokens_ref, r, r, 128) for r in range(0, tile, 128)]
-    for ref, source, target, count in blocks:
-        def write(columns, x, target=target, count=count):
-            normed[pl.ds(target, count), columns] = x.astype(BF16)
-        rms_columns(
-            lambda columns, ref=ref, source=source, count=count: ref[pl.ds(source, count), columns].astype(F32),
-            write, gain_ref, width,
-        )
-
+    norm_into(
+        normed, gain_ref,
+        [(rim_ref, 0, tile, RIM)] + [(tokens_ref, r, r, 128) for r in range(0, tile, 128)],
+    )
+    normed_ref[...] = normed[:tile]
     lowrank = dot_nt(normed[:tile], down_ref[...]).astype(BF16)
     logits = dot(lowrank, up_ref[...]) + bias_ref[...]
     decay_log = (jnp.minimum(logits, 0.0) - jnp.log1p(jnp.exp(-jnp.abs(logits)))) / 16.0
     row = lax.broadcasted_iota(jnp.int32, (HK, HK), 0)
     col = lax.broadcasted_iota(jnp.int32, (HK, HK), 1)
     lower = jnp.where((row >= col) & ((row // PAGE) == (col // PAGE)), 1.0, 0.0).astype(F32)
-    sums = [
-        jnp.dot(lower, decay_log[r : r + HK], preferred_element_type=F32, precision=lax.Precision.HIGHEST)
-        for r in range(0, tile, HK)
+    for r in range(0, tile, HK):
+        sums_ref[pl.ds(r, HK), :] = jnp.dot(
+            lower, decay_log[r : r + HK], preferred_element_type=F32, precision=lax.Precision.HIGHEST
+        )
+    carried = [
+        carried_flag(pages_ref, start_ref, step * pages + j, pl.num_programs(0) * pages)
+        for j in range(pages)
     ]
-    sums = [part[r : r + PAGE] for part in sums for r in range(0, HK, PAGE)]
-    ends = [part[PAGE - 1 :] for part in sums]
-    carried = [carried_flag(pages_ref, start_ref, step * pages + j, pl.num_programs(0) * pages) for j in range(pages)]
+    ends = [sums_ref[pl.ds((j + 1) * PAGE - 8, 8), :][7:] for j in range(pages)]
     suffix = [None] * pages + [jnp.ones((1, HK), F32)]
     for j in reversed(range(pages)):
         kept = jnp.exp(ends[j])
         ends_ref[j] = jnp.broadcast_to(kept, (8, HK))
         suffix[j] = suffix[j + 1] * (kept * carried[j])
 
-    everything = slice(None)
-    for chunk in (1, 2, 3, 0):
+    for chunk, weight_ref in enumerate((key_ref, first_ref, second_ref)):
         columns = pl.ds(chunk * WIDE, WIDE)
-        low = product(normed, everything, project_ref, columns).astype(BF16)
+        low = product(normed, slice(None), weight_ref, slice(None)).astype(BF16)
         projected = low[:tile].astype(F32)
         previous = jnp.where(step == 0, low[tile:].astype(F32)[RIM - 8 :], carry[:, columns])
         carry[:, columns] = projected[tile - 8 :]
-        taps = conv_ref[:, columns].astype(F32)
+        taps = conv_ref[:, pl.ds(HK + chunk * WIDE, WIDE)].astype(F32)
         for j in range(pages):
-            now = projected[j * PAGE : (j + 1) * PAGE]
-            before = previous if j == 0 else projected[j * PAGE - 8 : j * PAGE]
-            widened = jnp.concatenate([before * carried[j], now], axis=0)
-            mixed = taps[0:1] * now
-            for i in range(1, KCONV):
-                mixed = mixed + taps[i : i + 1] * widened[8 - i : 8 - i + PAGE]
+            mixed = short_conv(projected, previous, carried[j], taps, j)
             span = pl.ds(j * PAGE, PAGE)
-            edges_ref[j, :, columns] = low[(j + 1) * PAGE - (KCONV - 1) : (j + 1) * PAGE]
+            edges_ref[j, :, columns] = page_edge(low, j)
             if chunk == 0:
-                raised_ref[span, :] = (silu(mixed) * jnp.exp(sums[j])).astype(BF16)
-            elif chunk == 1:
                 key = silu(mixed) * HK ** (-0.5)
-                weighted = key * jnp.exp(ends[j] - sums[j])
-                lowered_ref[span, :] = (key * jnp.exp(-sums[j])).astype(BF16)
+                sums = sums_ref[span, :]
+                weighted = key * jnp.exp(ends[j] - sums)
+                lowered_ref[span, :] = (key * jnp.exp(-sums)).astype(BF16)
                 weighted_ref[span, :] = weighted.astype(BF16)
                 keys[span, :] = (weighted * suffix[j + 1]).astype(BF16)
             else:
-                at = pl.ds((chunk - 2) * WIDE, WIDE)
-                value_ref[span, at] = mixed.astype(BF16)
+                value_ref[span, pl.ds((chunk - 1) * WIDE, WIDE)] = mixed.astype(BF16)
     state[...] = column(suffix[0]) * state[...] + dot_tn(keys[...], value_ref[...])
     decay[...] = decay[...] * suffix[0]
-    for low in range(0, HV, WIDE):
-        columns = pl.ds(low, WIDE)
-        opening_ref[:, columns] = silu(product(normed, pl.ds(0, tile), gate_ref, columns)).astype(BF16)
 
     @pl.when(step == pl.num_programs(0) - 1)
     def _():
@@ -183,7 +196,11 @@
         state_ref[HK:] = jnp.concatenate([block] * (RIM // 8), axis=0).astype(BF16)
 
 
-def front(prompts, tokens, rim, gain, project, gate, down, up, bias, conv):
+def column_block(height, i):
+    return pl.BlockSpec((height, WIDE), lambda *_: (0, i), pipeline_mode=pl.Buffered(1))
+
+
+def front(prompts, tokens, rim, gain, project, down, up, bias, conv):
     count, width = tokens.shape
     rank = down.shape[0]
     pages = count // PAGE
@@ -196,28 +213,83 @@
         grid=(count // tile,),
         in_specs=[
             whole_smem(), whole_smem(), rows(width), fixed((RIM, width)), fixed((1, width)),
-            fixed((width, CONVW)), fixed((width, HV)), fixed((rank, width)), fixed((rank, HK)),
-            fixed((1, HK)), fixed((KCONV, CONVW)),
+            column_block(width, 1), column_block(width, 2), column_block(width, 3),
+            fixed((rank, width)), fixed((rank, HK)), fixed((1, HK)), fixed((KCONV, CONVW)),
         ],
         out_specs=[
-            rows(HK), rows(HK), rows(HK), rows(HV),
+            rows(width), rows(HK), rows(HK), rows(HK), rows(HV),
             pl.BlockSpec((tile // PAGE, 8, HK), lambda i: (i, 0, 0)),
-            pl.BlockSpec((tile // PAGE, KCONV - 1, CONVW), lambda i: (i, 0, 0)),
-            rows(HV), fixed((HK + RIM, HV)),
+            pl.BlockSpec((tile // PAGE, KCONV - 1, HK + HV), lambda i: (i, 0, 0)),
+            fixed((HK + RIM, HV)),
         ],
         out_shape=[
-            shape((count, HK), BF16), shape((count, HK), BF16), shape((count, HK), BF16),
-            shape((count, HV), BF16), shape((pages, 8, HK), F32),
-            shape((pages, KCONV - 1, CONVW), BF16), shape((count, HV), BF16),
-            shape((HK + RIM, HV), BF16),
+            shape((count, width), BF16), shape((count, HK), F32), shape((count, HK), BF16),
+            shape((count, HK), BF16), shape((count, HV), BF16), shape((pages, 8, HK), F32),
+            shape((pages, KCONV - 1, HK + HV), BF16), shape((HK + RIM, HV), BF16),
         ],
         scratch_shapes=[
-            pltpu.VMEM((tile + RIM, width), BF16), pltpu.VMEM((8, CONVW), F32),
+            pltpu.VMEM((tile + RIM, width), BF16), pltpu.VMEM((8, HK + HV), F32),
             pltpu.VMEM((HK, HV), F32), pltpu.VMEM((8, HK), F32), pltpu.VMEM((tile, HK), BF16),
         ],
         compiler_params=params(),
         cost_estimate=cost(1000, 1000),
-    )(*prompts, tokens, rim, gain, project, gate, down, up, bias, conv)
+    )(*prompts, tokens, rim, gain, project, project, project, down, up, bias, conv)
+
+
+def query_kernel(
+    pages_ref, start_ref, normed_ref, rim_ref, gain_ref, query_ref, gate_ref, conv_ref, sums_ref,
+    raised_ref, edges_ref, opening_ref, normed_rim, carry,
+):
+    step = pl.program_id(0)
+    tile = normed_ref.shape[0]
+    pages = tile // PAGE
+
+    @pl.when(step == 0)
+    def _():
+        norm_into(normed_rim, gain_ref, [(rim_ref, 0, 0, RIM)])
+        low = product(normed_rim, slice(None), query_ref, slice(None)).astype(BF16)
+        carry[...] = low.astype(F32)[RIM - 8 :]
+
+    low = product(normed_ref, slice(None), query_ref, slice(None)).astype(BF16)
+    projected = low.astype(F32)
+    previous = carry[...]
+    taps = conv_ref[:, :HK].astype(F32)
+    for j in range(pages):
+        carried = carried_flag(pages_ref, start_ref, step * pages + j, pl.num_programs(0) * pages)
+        mixed = short_conv(projected, previous, carried, taps, j)
+        span = pl.ds(j * PAGE, PAGE)
+        edges_ref[j] = page_edge(low, j)
+        raised_ref[span, :] = (silu(mixed) * jnp.exp(sums_ref[span, :])).astype(BF16)
+    carry[...] = projected[tile - 8 :]
+    for at in range(0, HV, WIDE):
+        columns = pl.ds(at, WIDE)
+        opening_ref[:, columns] = silu(product(normed_ref, slice(None), gate_ref, columns)).astype(BF16)
+
+
+def query(prompts, normed, rim, gain, project, gate, conv, sums):
+    count, width = normed.shape
+    pages = count // PAGE
+    tile = FRONT
+    rows = lambda n: pl.BlockSpec((tile, n), lambda i: (i, 0))
+    shape = jax.ShapeDtypeStruct
+    return pl.pallas_call(
+        query_kernel,
+        name="query",
+        grid=(count // tile,),
+        in_specs=[
+            whole_smem(), whole_smem(), rows(width), fixed((RIM, width)), fixed((1, width)),
+            column_block(width, 0), fixed((width, HV)), fixed((KCONV, CONVW)), rows(HK),
+        ],
+        out_specs=[
+            rows(HK), pl.BlockSpec((tile // PAGE, KCONV - 1, HK), lambda i: (i, 0, 0)), rows(HV),
+        ],
+        out_shape=[
+            shape((count, HK), BF16), shape((pages, KCONV - 1, HK), BF16), shape((count, HV), BF16),
+        ],
+        scratch_shapes=[pltpu.VMEM((RIM, width), BF16), pltpu.VMEM((8, HK), F32)],
+        compiler_params=params(),
+        cost_estimate=cost(2 * count * width * (HK + HV), 2 * count * width),
+    )(*prompts, normed, rim, gain, project, gate, conv, sums)
 
 
 def composed(later, earlier):
@@ -315,7 +387,7 @@
 
 def mix_kernel(
     tokens_ref, low_ref, high_ref, other_low_ref, other_high_ref, own_weight_ref, other_weight_ref,
-    gain_ref, residual_ref, feed_ref,
+    gain_ref, residual_ref, feed_ref, residual,
 ):
     first = pl.program_id(0) < pl.num_programs(0) // 2
     own = jnp.where(first, low_ref[...], high_ref[...])
@@ -324,41 +396,57 @@
     for at in range(0, width, WIDE):
         columns = pl.ds(at, WIDE)
         mixed = dot(own, own_weight_ref[:, columns]) + dot(other, other_weight_ref[:, columns])
-        residual_ref[:, columns] = (tokens_ref[:, columns].astype(F32) + mixed).astype(BF16)
+        residual[:, columns] = (tokens_ref[:, columns].astype(F32) + mixed).astype(BF16)
+
+    @pl.when(first == (lax.axis_index("hid") == 0))
+    def _():
+        residual_ref[...] = residual[...]
 
     def write(columns, x):
         feed_ref[:, columns] = x.astype(BF16)
 
-    rms_columns(lambda columns: residual_ref[:, columns].astype(F32), write, gain_ref, width)
-
-
-def mix(tokens, own, others, own_weight, other_weight, gain):
+    rms_columns(lambda columns: residual[:, columns].astype(F32), write, gain_ref, width)
+
+
+def mix(hid_index, tokens, own, others, own_weight, other_weight, gain):
     count, width = tokens.shape
     tile = MIX
-    rows = pl.BlockSpec((tile, width), lambda i: (i, 0))
-    return pl.pallas_call(
-        mix_kernel,
+    half = count // tile // 2
+    rows = pl.BlockSpec((tile, width), lambda i, s: (i, 0))
+    halves = [
+        pl.BlockSpec((tile, HV), lambda i, s: (jnp.minimum(i, half - 1), 0)),
+        pl.BlockSpec((tile, HV), lambda i, s: (jnp.maximum(i - half, 0), 0)),
+    ]
+    mine = pl.BlockSpec((tile, width), lambda i, s: (jnp.clip(i - s[0] * half, 0, half - 1), 0))
+    return pl.pallas_call(
+        lambda s, *refs: mix_kernel(*refs),
         name="mix",
-        grid=(count // tile,),
-        in_specs=[
-            rows, *halves(count, tile), *halves(count, tile), fixed((HV, width)), fixed((HV, width)),
-            fixed((1, width)),
-        ],
-        out_specs=[rows, rows],
-        out_shape=[jax.ShapeDtypeStruct((count, width), BF16)] * 2,
+        grid_spec=pltpu.PrefetchScalarGridSpec(
+            num_scalar_prefetch=1,
+            grid=(count // tile,),
+            in_specs=[rows, *halves, *halves, fixed((HV, width)), fixed((HV, width)), fixed((1, width))],
+            out_specs=[mine, rows],
+            scratch_shapes=[pltpu.VMEM((tile, width), BF16)],
+        ),
+        out_shape=[
+            jax.ShapeDtypeStruct((count // 2, width), BF16), jax.ShapeDtypeStruct((count, width), BF16),
+        ],
         compiler_params=params(),
         cost_estimate=cost(1000, 1000),
-    )(tokens, *own, *others, own_weight, other_weight, gain)
+    )(hid_index, tokens, *own, *others, own_weight, other_weight, gain)
 
 
 def widen_kernel(places, feed_ref, *refs):
     pieces, out_ref = refs[:-1], refs[-1]
-    sums = [None, None]
-    for (matrix, place), ref in zip(places, pieces):
-        columns = pl.ds(pl.multiple_of(place(), 128), ref.shape[0])
-        part = dot(feed_ref[:, columns], ref[...])
-        sums[matrix] = part if sums[matrix] is None else sums[matrix] + part
-    out_ref[...] = (silu(sums[0]) * sums[1]).astype(BF16)
+    count = feed_ref.shape[0]
+    for first in range(0, count, ROWS):
+        rows = pl.ds(first, ROWS)
+        sums = [None, None]
+        for (matrix, place), ref in zip(places, pieces):
+            columns = pl.ds(pl.multiple_of(place(), 128), ref.shape[0])
+            part = dot(feed_ref[rows, columns], ref[...])
+            sums[matrix] = part if sums[matrix] is None else sums[matrix] + part
+        out_ref[rows, :] = (silu(sums[0]) * sums[1]).astype(BF16)
 
 
 def widen(feed, matrices):
@@ -442,29 +530,20 @@
             at += size
 
 
-def close(hid_index, residual, groups):
+def close(residual, groups):
     count, width = residual.shape
-    tiles = count // TILE // 2
-    rows = lambda n: pl.BlockSpec((TILE, n), lambda i, s: (i, 0))
+    rows = lambda n: pl.BlockSpec((TILE, n), lambda i: (i, 0))
     arrays = [array for own, received, _ in groups for array in (own, received)]
     return pl.pallas_call(
-        functools.partial(close_kernel_, [group[2] for group in groups]),
+        functools.partial(close_kernel, [group[2] for group in groups]),
         name="close",
-        grid_spec=pltpu.PrefetchScalarGridSpec(
-            num_scalar_prefetch=1,
-            grid=(tiles,),
-            in_specs=[pl.BlockSpec((TILE, width), lambda i, s: (s[0] * tiles + i, 0))]
-            + [rows(array.shape[1]) for array in arrays],
-            out_specs=rows(width),
-        ),
-        out_shape=jax.ShapeDtypeStruct((count // 2, width), BF16),
+        grid=(count // TILE,),
+        in_specs=[rows(width)] + [rows(array.shape[1]) for array in arrays],
+        out_specs=rows(width),
+        out_shape=jax.ShapeDtypeStruct((count, width), BF16),
         compiler_params=params(),
         cost_estimate=cost(1000, 1000),
-    )(hid_index.astype(jnp.int32)[None], residual, *arrays)
-
-
-def close_kernel_(places, half_ref, *refs):
-    close_kernel(places, *refs)
+    )(residual, *arrays)
 
 
 def shifted(value, steps):
@@ -489,7 +568,7 @@
     count, width = tokens.shape
     prompts = (prompt_pages, prompt_start)
     two_by_two = lax.axis_size("req") == 4 and lax.axis_size("seq") % 2 == 0
-    hid_index = lax.axis_index("hid")
+    hid_index = lax.axis_index("hid").astype(jnp.int32)[None]
     x, y = functools.partial(swapped, axis="req", flip=1), functools.partial(swapped, axis="req", flip=2)
     z = functools.partial(swapped, axis="seq", flip=1)
     depth = gate_weight.shape[0]
@@ -504,18 +583,21 @@
     rim = shifted(tokens[-RIM:], 1)
     rim, other_output = lax.optimization_barrier((rim, swapped(output_weight, "hid", 1)))
 
-    raised, lowered, weighted, value, ends, edges, opening, state = front(
-        prompts, tokens, rim, attention_gain[None], project_weight, output_gate, decay_down.T,
-        decay_up, decay_bias[None], conv_weight,
+    normed, sums, lowered, weighted, value, ends, edges, state = front(
+        prompts, tokens, rim, attention_gain[None], project_weight, decay_down.T, decay_up,
+        decay_bias[None], conv_weight,
     )
-    if two_by_two:
-        state, gate_a, gate_b = tied((state, gate_a, gate_b))
-        down_0, down_1 = down_weight[:, :half], down_weight[:, half:]
-        gate_c, down_b1 = x(gate_b), y(down_1)
     one = shifted(state, 1)
     two = shifted(joined(state, one), 2)
     if two_by_two:
-        one, two, up_a, up_b, down_0 = tied((one, two, up_a, up_b, down_0))
+        down_0, down_1 = down_weight[:, :half], down_weight[:, half:]
+        normed, gate_a, gate_b = tied((normed, gate_a, gate_b))
+        gate_c, down_b1 = x(gate_b), y(down_1)
+    raised, query_edges, opening = query(
+        prompts, normed, rim, attention_gain[None], project_weight, output_gate, conv_weight, sums,
+    )
+    if two_by_two:
+        one, two, raised, up_a, up_b, down_0 = tied((one, two, raised, up_a, up_b, down_0))
         up_c, far_a, far_b, down_a0 = y(up_a), z(up_a), z(up_b), x(down_0)
         down_c0 = y(down_a0)
     states, *gated = pages(
@@ -525,7 +607,7 @@
     if two_by_two:
         others, up_c, gate_c, far_a, down_b1 = tied((others, up_c, gate_c, far_a, down_b1))
         far_c = y(far_a)
-    residual, feed = mix(tokens, gated, others, output_weight, other_output, mixer_gain[None])
+    residual, feed = mix(hid_index, tokens, gated, others, output_weight, other_output, mixer_gain[None])
 
     if two_by_two:
         feed, down_0, down_1 = tied((feed, down_0, down_1))
@@ -552,12 +634,12 @@
 
     hidden = widen(feed, (gate_list, up_list))
     groups = []
-    for pieces, parts in zip(down_lists, (1, 2)):
-        theirs, mine = narrow(hidden, [piece for piece, _ in pieces], count // parts)
+    for pieces in down_lists:
+        theirs, mine = narrow(hidden, [piece for piece, _ in pieces], ROWS)
         received = swapped(theirs, "hid", 1)
         groups.append((mine, received, [(piece.shape[1], place) for piece, place in pieces]))
-    result = close(hid_index, residual, groups)
-    return result, states, edges
+    result = close(residual, groups)
+    return result, states, jnp.concatenate([query_edges, edges], axis=-1)
 
 
 def solution(mesh):

time: 154 us -> 148 us (0.961)
  starting transfers between devices: 36.3 us -> 31.7 us
  waiting for transfers between devices: 22.1 us -> 19.6 us
  Pallas kernels: 82.5 us -> 84.9 us
    pallas_call x2 -> x3, Pallas kernels: 14.8 us -> 23.9 us  [the longest x1 11.2 us: mix(): pl.pallas_call(lambda s, *refs: mix_kernel(*refs), name='mix', grid_spec=...]
    ppermute x3, waiting for transfers between devices: 5.74 us -> 0.01 us  [shifted(): lax.ppermute(value, 'seq', [(i, i + steps) for i in range(count - steps)])]
    pallas_call x1, Pallas kernels: 20.2 us -> 16.4 us  [front(): pl.pallas_call(front_kernel, name='front', grid=(count // tile,), in_spec...]
    ppermute x20, starting transfers between devices: 23.7 us -> 20 us  [swapped(): return lax.ppermute(value, axis, [(i, i ^ flip) for i in range(count)])]
    ppermute x20, waiting for transfers between devices: 16.4 us -> 19.6 us  [swapped(): return lax.ppermute(value, axis, [(i, i ^ flip) for i in range(count)])]
    pallas_call x2, Pallas kernels: 18.7 us -> 15.6 us  [narrow(): pl.pallas_call(functools.partial(narrow_kernel, block), name='narrow', in...]
    unnamed x49 -> x39, local copies, waits for them, and re-layouts: 5.36 us -> 4.31 us
  transfers between devices with their start and end apart: 23 -> 23, of which waited for: 10 -> 8; matrix products, arithmetic and copies ran while one was open for 4% -> 5% of each run, Pallas kernels for 51% -> 55%
where the time goes in v5:
time: 148 us
  Pallas kernels  84.9 us (57%)
  starting transfers between devices  31.7 us (21%)
  waiting for transfers between devices  19.6 us (13%)
  local copies, waits for them, and re-layouts  10.9 us (7%)
    ppermute x20, starting transfers between devices, swapped(): return lax.ppermute(value, axis, [(i, i ^ flip) for i in range(count)])  20 us
    ppermute x20, waiting for transfers between devices, swapped(): return lax.ppermute(value, axis, [(i, i ^ flip) for i in range(count)])  19.6 us
    pallas_call x1, Pallas kernels, widen(): pl.pallas_call(functools.partial(widen_kernel, places), name='widen', gri...  18.8 us
    pallas_call x1, Pallas kernels, front(): pl.pallas_call(front_kernel, name='front', grid=(count // tile,), in_spec...  16.4 us
    pallas_call x2, Pallas kernels, narrow(): pl.pallas_call(functools.partial(narrow_kernel, block), name='narrow', in...  15.6 us
    ppermute x3, starting transfers between devices, shifted(): lax.ppermute(value, 'seq', [(i, i + steps) for i in range(count - steps)])  11.6 us
    pallas_call x1, Pallas kernels, mix(): pl.pallas_call(lambda s, *refs: mix_kernel(*refs), name='mix', grid_spec=...  11.2 us
    pallas_call x1, Pallas kernels, query(): pl.pallas_call(query_kernel, name='query', grid=(count // tile,), in_spec...  8.55 us
  transfers between devices with their start and end apart: 23, of which 8 were waited for; matrix products, arithmetic and copies ran while one was open for 5% of the time, Pallas kernels for 55%

profile of v5, /device:TPU:0, one launch (start us, length us, event | category | flops | bytes accessed | tf_op | source)
XLA Modules:
  0.0 148.1 jit_solution(7430703931670895149)
XLA Ops:
  1.1 2.6 %collective-permute-start.4 = (bf16[512,1408]{1,0:T(8,128)(2,1)}, bf16[512,1408]{1,0:T(8,128)(2,1)}, u32[]{:S(2)}, u32[]{:S(2)}) collective-permute-start(bf16[512,1408]{1,0:T(8,128)(2,1)} %refs_0_.4), channel_id=1, source_target_pairs={{0,8},{8,0},{16,24},{24,16},{1,9},{9,1},{17,25},{25,17},{2,10},{10... | collective-permute-start | bytes 4325384 | tf_op jit(solution)/shard_map/ppermute | solution.py:556
  3.7 1.5 %collective-permute-start.5 = (bf16[512,1408]{1,0:T(8,128)(2,1)}, bf16[512,1408]{1,0:T(8,128)(2,1)}, u32[]{:S(2)}, u32[]{:S(2)}) collective-permute-start(bf16[512,1408]{1,0:T(8,128)(2,1)} %refs_0_.4), channel_id=1, source_target_pairs={{0,16},{8,24},{16,0},{24,8},{1,17},{9,25},{17,1},{25,9},{2,18},{10... | collective-permute-start | bytes 4325384 | tf_op jit(solution)/shard_map/ppermute | solution.py:556
  6.1 3.5 %collective-permute-start = (bf16[16,2048]{1,0:T(8,128)(2,1)S(1)}, bf16[16,2048]{1,0:T(8,128)(2,1)S(1)}, u32[]{:S(2)}, u32[]{:S(2)}) collective-permute-start(bf16[16,2048]{1,0:T(8,128)(2,1)S(1)} %slice.9), channel_id=1, source_target_pairs={{0,2},{2,4},{4,6},{1,3},{3,5},{5,7},{8,10},{10,12},{12,14},{9,11},... | collective-permute-start | bytes 196616 | tf_op jit(solution)/shard_map/ppermute | solution.py:551
  9.6 2.1 %constant_dynamic-slice_fusion = bf16[256,1408]{1,0:T(8,128)(2,1)} fusion(bf16[512,1408]{1,0:T(8,128)(2,1)} %refs_4_.1, s32[]{:T(128)S(6)} %select_n.3), kind=kLoop, calls=%fused_computation.1 | loop fusion | bytes 1441796 | tf_op jit(solution)/shard_map/dynamic_slice | solution.py:580
  14.1 16.4 %front.1 = (bf16[1024,2048]{1,0:T(8,128)(2,1)}, f32[1024,256]{1,0:T(8,128)}, bf16[1024,256]{1,0:T(8,128)(2,1)}, bf16[1024,256]{1,0:T(8,128)(2,1)}, bf16[1024,512...) custom-call(s32[1,16]{1,0:T(1,128)} %pages_ref.5, ...), custom_call_target="tpu_custom_call" | custom-call | flops 1000 | bytes 1000 | tf_op jit(solution)/shard_map/front/pallas_call | solution.py:210
  30.6 3.5 %collective-permute-start.2 = (bf16[272,512]{1,0:T(8,128)(2,1)}, bf16[272,512]{1,0:T(8,128)(2,1)S(1)}, u32[]{:S(2)}, u32[]{:S(2)}) collective-permute-start(bf16[272,512]{1,0:T(8,128)(2,1)} %get-tuple-element.48.later_ref), channel_id=1, source_target_pairs={{0,2},{2,4},{4,6},{1,3},{3,5},{5,7},{8,10},{10,12},{12,14},{9,11},... | collective-permute-start | bytes 835592 | tf_op jit(solution)/shard_map/ppermute | solution.py:551
  34.1 2.4 %collective-permute-done.4.refs_1_ = bf16[512,1408]{1,0:T(8,128)(2,1)} collective-permute-done((bf16[512,1408]{1,0:T(8,128)(2,1)}, bf16[512,1408]{1,0:T(8,128)(2,1)}, u32[]{:S(2)}, u32[]{:S(2)}) %collective-permute-start.4) | collective-permute-done | bytes 1441824 | tf_op jit(solution)/shard_map/ppermute | solution.py:556
  36.5 2.0 %collective-permute-done.5.refs_2_ = bf16[512,1408]{1,0:T(8,128)(2,1)} collective-permute-done((bf16[512,1408]{1,0:T(8,128)(2,1)}, bf16[512,1408]{1,0:T(8,128)(2,1)}, u32[]{:S(2)}, u32[]{:S(2)}) %collective-permute-start.5) | collective-permute-done | bytes 1441824 | tf_op jit(solution)/shard_map/ppermute | solution.py:556
  39.7 2.0 %collective-permute-start.13 = (bf16[1408,256]{1,0:T(8,128)(2,1)}, bf16[1408,256]{1,0:T(8,128)(2,1)}, u32[]{:S(2)}, u32[]{:S(2)}) collective-permute-start(bf16[1408,256]{1,0:T(8,128)(2,1)} %get-tuple-element.85), channel_id=1, source_target_pairs={{0,16},{8,24},{16,0},{24,8},{1,17},{9,25},{17,1},{25,9},{2,18},{10... | collective-permute-start | bytes 2162696 | tf_op jit(solution)/shard_map/ppermute | solution.py:556
  42.4 2.0 %joined.1 = bf16[272,512]{1,0:T(8,128)(2,1)} custom-call(bf16[272,512]{1,0:T(8,128)(2,1)} %get-tuple-element.48.later_ref, bf16[272,512]{1,0:T(8,128)(2,1)} %copy-done.4), custom_call_target="tpu_custom_call" | custom-call | flops 1000 | bytes 1000 | tf_op jit(solution)/shard_map/joined/pallas_call | solution.py:306
  44.4 4.7 %collective-permute-start.3 = (bf16[272,512]{1,0:T(8,128)(2,1)}, bf16[272,512]{1,0:T(8,128)(2,1)S(1)}, u32[]{:S(2)}, u32[]{:S(2)}) collective-permute-start(bf16[272,512]{1,0:T(8,128)(2,1)} %joined.1), channel_id=1, source_target_pairs={{0,4},{2,6},{1,5},{3,7},{8,12},{10,14},{9,13},{11,15},{16,20},{18,... | collective-permute-start | bytes 835592 | tf_op jit(solution)/shard_map/ppermute | solution.py:551
  49.1 8.5 %query.1 = (bf16[1024,256]{1,0:T(8,128)(2,1)}, bf16[16,3,256]{2,1,0:T(4,128)(2,1)}, bf16[1024,512]{1,0:T(8,128)(2,1)}) custom-call(s32[1,16]{1,0:T(1,128)} %pages_ref.5, s32[1,16]{1,0:T(1,128)} %start_ref.5, bf16[1024,2048]{1,0:T(8,128)(2,1)} %get-tuple-element.50.normed_ref, bf16[16,2048]{1,0:T(8,128)(2,1)} %copy-done.15, ...), custom_call_target="tpu_custom_call" | custom-call | flops 3221225472 | bytes 4194304 | tf_op jit(solution)/shard_map/query/pallas_call | solution.py:275
  58.3 3.0 %collective-permute-start.12 = (bf16[256,1408]{1,0:T(8,128)(2,1)}, bf16[256,1408]{1,0:T(8,128)(2,1)S(1)}, u32[]{:S(2)}, u32[]{:S(2)}) collective-permute-start(bf16[256,1408]{1,0:T(8,128)(2,1)} %collective-permute-done.6.refs_5_), channel_id=1, source_target_pairs={{0,2},{2,0},{4,6},{6,4},{1,3},{3,1},{5,7},{7,5},{8,10},{10,8},{12,... | collective-permute-start | bytes 2162696 | tf_op jit(solution)/shard_map/ppermute | solution.py:556
  61.9 8.2 %pages.1 = (bf16[16,1,256,512]{3,2,1,0:T(8,128)(2,1)}, bf16[512,512]{1,0:T(8,128)(2,1)}, bf16[512,512]{1,0:T(8,128)(2,1)}) custom-call(s32[1,16]{1,0:T(1,128)} %pages_ref.5, s32[1,16]{1,0:T(1,128)} %start_ref.5, bf16[1024,256]{1,0:T(8,128)(2,1)} %get-tuple-element.53.raised_ref, bf16[1024,256]{1,0:T(8,128)(2,1)} %get-tuple-element.54.lowered_ref, ...), custom_call_target="tpu_custom_call" | custom-call | flops 1000 | bytes 1000 | tf_op jit(solution)/shard_map/pages/pallas_call | solution.py:365
  70.7 1.6 %collective-permute-done.8.refs_3_ = bf16[512,512]{1,0:T(8,128)(2,1)S(1)} collective-permute-done((bf16[512,512]{1,0:T(8,128)(2,1)}, bf16[512,512]{1,0:T(8,128)(2,1)S(1)}, u32[]{:S(2)}, u32[]{:S(2)}) %collective-permute-start.8) | collective-permute-done | bytes 524320 | tf_op jit(solution)/shard_map/ppermute | solution.py:556
  74.5 9.4 %collective-permute-done.10.refs_9_ = bf16[256,1408]{1,0:T(8,128)(2,1)S(1)} collective-permute-done((bf16[256,1408]{1,0:T(8,128)(2,1)}, bf16[256,1408]{1,0:T(8,128)(2,1)S(1)}, u32[]{:S(2)}, u32[]{:S(2)}) %collective-permute-start.10) | collective-permute-done | bytes 720928 | tf_op jit(solution)/shard_map/ppermute | solution.py:556
  84.0 1.6 %collective-permute-start.15 = (bf16[256,1408]{1,0:T(8,128)(2,1)S(1)}, bf16[256,1408]{1,0:T(8,128)(2,1)}, u32[]{:S(2)}, u32[]{:S(2)}) collective-permute-start(bf16[256,1408]{1,0:T(8,128)(2,1)S(1)} %collective-permute-done.12.refs_6_), channel_id=1, source_target_pairs={{0,16},{8,24},{16,0},{24,8},{1,17},{9,25},{17,1},{25,9},{2,18},{10... | collective-permute-start | bytes 2162696 | tf_op jit(solution)/shard_map/ppermute | solution.py:556
  86.2 11.2 %mix.1 = (bf16[512,2048]{1,0:T(8,128)(2,1)}, bf16[1024,2048]{1,0:T(8,128)(2,1)}) custom-call(s32[1]{0:T(128)} %bitcast.s, bf16[1024,2048]{1,0:T(8,128)(2,1)} %refs_0_.3, bf16[512,512]{1,0:T(8,128)(2,1)} %get-tuple-element.61.refs_1_, bf16[512,512]{1,0:T(8,128)(2,1)} %get-tuple-element.62.refs_2_, bf16[512,512]{1,0:T(8,128)(2,1)} %copy-done.11, ...), custom_call_target="tpu_custom_call" | custom-call | flops 1000 | bytes 1000 | tf_op jit(solution)/shard_map/mix/pallas_call | solution.py:421
  98.3 1.5 %collective-permute-start.20 = (bf16[1408,256]{1,0:T(8,128)(2,1)}, bf16[1408,256]{1,0:T(8,128)(2,1)S(1)}, u32[]{:S(2)}, u32[]{:S(2)}) collective-permute-start(bf16[1408,256]{1,0:T(8,128)(2,1)} %collective-permute-done.16.refs_1_), channel_id=1, source_target_pairs={{0,16},{8,24},{16,0},{24,8},{1,17},{9,25},{17,1},{25,9},{2,18},{10... | collective-permute-start | bytes 2162696 | tf_op jit(solution)/shard_map/ppermute | solution.py:556
  101.3 1.9 %collective-permute-done.15.refs_10_ = bf16[256,1408]{1,0:T(8,128)(2,1)} collective-permute-done((bf16[256,1408]{1,0:T(8,128)(2,1)S(1)}, bf16[256,1408]{1,0:T(8,128)(2,1)}, u32[]{:S(2)}, u32[]{:S(2)}) %collective-permute-start.15) | collective-permute-done | bytes 720928 | tf_op jit(solution)/shard_map/ppermute | solution.py:556
  103.8 18.8 %widen.1.hidden_hbm = bf16[1024,1408]{1,0:T(8,128)(2,1)} custom-call(bf16[1024,2048]{1,0:T(8,128)(2,1)} %get-tuple-element.75.feed_ref, bf16[512,1408]{1,0:T(8,128)(2,1)} %refs_0_.4, bf16[512,1408]{1,0:T(8,128)(2,1)} %collective-permute-done.4.refs_1_, bf16[512,1408]{1,0:T(8,128)(2,1)} %collective-permute-done.5.refs_2_, bf16[512,1408]{1,0:T(8,128)(2,1)} %copy-done.2, ...), custom_call_target="tpu_custom_call" | custom-call | flops 1000 | bytes 1000 | tf_op jit(solution)/shard_map/widen/pallas_call | solution.py:457
  123.5 9.2 %narrow.2 = (bf16[512,1280]{1,0:T(8,128)(2,1)}, bf16[512,1280]{1,0:T(8,128)(2,1)}) custom-call(bf16[1024,1408]{1,0:T(8,128)(2,1)} %widen.1.hidden_hbm, bf16[1408,512]{1,0:T(8,128)(2,1)} %refs_0_.5, bf16[1408,256]{1,0:T(8,128)(2,1)} %collective-permute-done.16.refs_1_, bf16[1408,256]{1,0:T(8,128)(2,1)} %collective-permute-done.13.refs_2_, ...), custom_call_target="tpu_custom_call" | custom-call | flops 1000 | bytes 1000 | tf_op jit(solution)/shard_map/narrow/pallas_call | solution.py:508
  134.0 6.4 %narrow.3 = (bf16[512,768]{1,0:T(8,128)(2,1)}, bf16[512,768]{1,0:T(8,128)(2,1)}) custom-call(bf16[1024,1408]{1,0:T(8,128)(2,1)} %widen.1.hidden_hbm, bf16[1408,256]{1,0:T(8,128)(2,1)} %copy-done.9, bf16[1408,256]{1,0:T(8,128)(2,1)} %copy-done.8, bf16[1408,256]{1,0:T(8,128)(2,1)} %collective-permute-done.21.refs_2_), custom_call_target="tpu_custom_call" | custom-call | flops 1000 | bytes 1000 | tf_op jit(solution)/shard_map/narrow/pallas_call | solution.py:508
  143.9 4.1 %close.1 = bf16[512,2048]{1,0:T(8,128)(2,1)} custom-call(bf16[512,2048]{1,0:T(8,128)(2,1)} %get-tuple-element.68.residual_ref, bf16[512,1280]{1,0:T(8,128)(2,1)} %get-tuple-element.83.refs_0_, bf16[512,1280]{1,0:T(8,128)(2,1)} %copy-done.3, bf16[512,768]{1,0:T(8,128)(2,1)} %get-tuple-element.86.refs_2_, bf16[512,768]{1,0:T(8,128)(2,1)} %copy-done.5), custom_call_target="tpu_custom_call" | custom-call | flops 1000 | bytes 1000 | tf_op jit(solution)/shard_map/close/pallas_call | solution.py:537
  (77 shorter events, 19.0 us)
Async XLA Ops:
  0.6 13.4 %collective-permute-start.1 = (bf16[512,2048]{1,0:T(8,128)(2,1)}, bf16[512,2048]{1,0:T(8,128)(2,1)S(1)}, u32[]{:S(2)}, u32[]{:S(2)}) collective-permute-start(bf16[512,2048]{1,0:T(8,128)(2,1)} %refs_5_.1), channel_id=1, source_target_pairs={{0,1},{1,0},{2,3},{3,2},{4,5},{5,4},{6,7},{7,6},{8,9},{9,8},{10,11... | collective-permute-start | bytes 6291464 | tf_op jit(solution)/shard_map/ppermute | solution.py:556
  1.1 35.3 %collective-permute-start.4 = (bf16[512,1408]{1,0:T(8,128)(2,1)}, bf16[512,1408]{1,0:T(8,128)(2,1)}, u32[]{:S(2)}, u32[]{:S(2)}) collective-permute-start(bf16[512,1408]{1,0:T(8,128)(2,1)} %refs_0_.4), channel_id=1, source_target_pairs={{0,8},{8,0},{16,24},{24,16},{1,9},{9,1},{17,25},{25,17},{2,10},{10... | collective-permute-start | bytes 4325384 | tf_op jit(solution)/shard_map/ppermute | solution.py:556
  3.7 34.7 %collective-permute-start.5 = (bf16[512,1408]{1,0:T(8,128)(2,1)}, bf16[512,1408]{1,0:T(8,128)(2,1)}, u32[]{:S(2)}, u32[]{:S(2)}) collective-permute-start(bf16[512,1408]{1,0:T(8,128)(2,1)} %refs_0_.4), channel_id=1, source_target_pairs={{0,16},{8,24},{16,0},{24,8},{1,17},{9,25},{17,1},{25,9},{2,18},{10... | collective-permute-start | bytes 4325384 | tf_op jit(solution)/shard_map/ppermute | solution.py:556
  6.1 7.4 %collective-permute-start = (bf16[16,2048]{1,0:T(8,128)(2,1)S(1)}, bf16[16,2048]{1,0:T(8,128)(2,1)S(1)}, u32[]{:S(2)}, u32[]{:S(2)}) collective-permute-start(bf16[16,2048]{1,0:T(8,128)(2,1)S(1)} %slice.9), channel_id=1, source_target_pairs={{0,2},{2,4},{4,6},{1,3},{3,5},{5,7},{8,10},{10,12},{12,14},{9,11},... | collective-permute-start | bytes 196616 | tf_op jit(solution)/shard_map/ppermute | solution.py:551
  11.7 46.0 %collective-permute-start.6 = (bf16[256,1408]{1,0:T(8,128)(2,1)}, bf16[256,1408]{1,0:T(8,128)(2,1)}, u32[]{:S(2)}, u32[]{:S(2)}) collective-permute-start(bf16[256,1408]{1,0:T(8,128)(2,1)} %constant_dynamic-slice_fusion), channel_id=1, source_target_pairs={{0,8},{8,0},{16,24},{24,16},{1,9},{9,1},{17,25},{25,17},{2,10},{10... | collective-permute-start | bytes 2162696 | tf_op jit(solution)/shard_map/ppermute | solution.py:556
  13.5 44.2 %collective-permute-start.7 = (bf16[256,1408]{1,0:T(8,128)(2,1)}, bf16[256,1408]{1,0:T(8,128)(2,1)}, u32[]{:S(2)}, u32[]{:S(2)}) collective-permute-start(bf16[256,1408]{1,0:T(8,128)(2,1)} %constant_dynamic-slice_fusion), channel_id=1, source_target_pairs={{0,16},{8,24},{16,0},{24,8},{1,17},{9,25},{17,1},{25,9},{2,18},{10... | collective-permute-start | bytes 2162696 | tf_op jit(solution)/shard_map/ppermute | solution.py:556
  14.1 24.4 %copy-start = (bf16[1408,512]{1,0:T(8,128)(2,1)S(1)}, bf16[1408,512]{1,0:T(8,128)(2,1)}, u32[]{:S(2)}) copy-start(bf16[1408,512]{1,0:T(8,128)(2,1)} %refs_0_.5) | copy-start | bytes 4325380
  30.6 11.1 %collective-permute-start.2 = (bf16[272,512]{1,0:T(8,128)(2,1)}, bf16[272,512]{1,0:T(8,128)(2,1)S(1)}, u32[]{:S(2)}, u32[]{:S(2)}) collective-permute-start(bf16[272,512]{1,0:T(8,128)(2,1)} %get-tuple-element.48.later_ref), channel_id=1, source_target_pairs={{0,2},{2,4},{4,6},{1,3},{3,5},{5,7},{8,10},{10,12},{12,14},{9,11},... | collective-permute-start | bytes 835592 | tf_op jit(solution)/shard_map/ppermute | solution.py:551
  38.5 45.5 %collective-permute-start.11 = (bf16[512,1408]{1,0:T(8,128)(2,1)}, bf16[512,1408]{1,0:T(8,128)(2,1)S(1)}, u32[]{:S(2)}, u32[]{:S(2)}) collective-permute-start(bf16[512,1408]{1,0:T(8,128)(2,1)} %collective-permute-done.5.refs_2_), channel_id=1, source_target_pairs={{0,8},{8,0},{16,24},{24,16},{1,9},{9,1},{17,25},{25,17},{2,10},{10... | collective-permute-start | bytes 4325384 | tf_op jit(solution)/shard_map/ppermute | solution.py:556
  39.7 30.4 %collective-permute-start.13 = (bf16[1408,256]{1,0:T(8,128)(2,1)}, bf16[1408,256]{1,0:T(8,128)(2,1)}, u32[]{:S(2)}, u32[]{:S(2)}) collective-permute-start(bf16[1408,256]{1,0:T(8,128)(2,1)} %get-tuple-element.85), channel_id=1, source_target_pairs={{0,16},{8,24},{16,0},{24,8},{1,17},{9,25},{17,1},{25,9},{2,18},{10... | collective-permute-start | bytes 2162696 | tf_op jit(solution)/shard_map/ppermute | solution.py:556
  44.4 13.3 %collective-permute-start.3 = (bf16[272,512]{1,0:T(8,128)(2,1)}, bf16[272,512]{1,0:T(8,128)(2,1)S(1)}, u32[]{:S(2)}, u32[]{:S(2)}) collective-permute-start(bf16[272,512]{1,0:T(8,128)(2,1)} %joined.1), channel_id=1, source_target_pairs={{0,4},{2,6},{1,5},{3,7},{8,12},{10,14},{9,13},{11,15},{16,20},{18,... | collective-permute-start | bytes 835592 | tf_op jit(solution)/shard_map/ppermute | solution.py:551
  57.7 26.2 %collective-permute-start.10 = (bf16[256,1408]{1,0:T(8,128)(2,1)}, bf16[256,1408]{1,0:T(8,128)(2,1)S(1)}, u32[]{:S(2)}, u32[]{:S(2)}) collective-permute-start(bf16[256,1408]{1,0:T(8,128)(2,1)} %collective-permute-done.6.refs_5_), channel_id=1, source_target_pairs={{0,16},{8,24},{16,0},{24,8},{1,17},{9,25},{17,1},{25,9},{2,18},{10... | collective-permute-start | bytes 2162696 | tf_op jit(solution)/shard_map/ppermute | solution.py:556
  58.3 25.7 %collective-permute-start.12 = (bf16[256,1408]{1,0:T(8,128)(2,1)}, bf16[256,1408]{1,0:T(8,128)(2,1)S(1)}, u32[]{:S(2)}, u32[]{:S(2)}) collective-permute-start(bf16[256,1408]{1,0:T(8,128)(2,1)} %collective-permute-done.6.refs_5_), channel_id=1, source_target_pairs={{0,2},{2,0},{4,6},{6,4},{1,3},{3,1},{5,7},{7,5},{8,10},{10,8},{12,... | collective-permute-start | bytes 2162696 | tf_op jit(solution)/shard_map/ppermute | solution.py:556
  70.1 2.2 %collective-permute-start.8 = (bf16[512,512]{1,0:T(8,128)(2,1)}, bf16[512,512]{1,0:T(8,128)(2,1)S(1)}, u32[]{:S(2)}, u32[]{:S(2)}) collective-permute-start(bf16[512,512]{1,0:T(8,128)(2,1)} %get-tuple-element.61.refs_1_), channel_id=1, source_target_pairs={{0,1},{1,0},{2,3},{3,2},{4,5},{5,4},{6,7},{7,6},{8,9},{9,8},{10,11... | collective-permute-start | bytes 1572872 | tf_op jit(solution)/shard_map/ppermute | solution.py:556
  70.2 2.8 %collective-permute-start.9 = (bf16[512,512]{1,0:T(8,128)(2,1)}, bf16[512,512]{1,0:T(8,128)(2,1)S(1)}, u32[]{:S(2)}, u32[]{:S(2)}) collective-permute-start(bf16[512,512]{1,0:T(8,128)(2,1)} %get-tuple-element.62.refs_2_), channel_id=1, source_target_pairs={{0,1},{1,0},{2,3},{3,2},{4,5},{5,4},{6,7},{7,6},{8,9},{9,8},{10,11... | collective-permute-start | bytes 1572872 | tf_op jit(solution)/shard_map/ppermute | solution.py:556
  72.3 29.0 %collective-permute-start.14 = (bf16[256,1408]{1,0:T(8,128)(2,1)}, bf16[256,1408]{1,0:T(8,128)(2,1)}, u32[]{:S(2)}, u32[]{:S(2)}) collective-permute-start(bf16[256,1408]{1,0:T(8,128)(2,1)} %collective-permute-done.7.refs_7_), channel_id=1, source_target_pairs={{0,2},{2,0},{4,6},{6,4},{1,3},{3,1},{5,7},{7,5},{8,10},{10,8},{12,... | collective-permute-start | bytes 2162696 | tf_op jit(solution)/shard_map/ppermute | solution.py:556
  73.1 25.2 %collective-permute-start.16 = (bf16[1408,256]{1,0:T(8,128)(2,1)}, bf16[1408,256]{1,0:T(8,128)(2,1)}, u32[]{:S(2)}, u32[]{:S(2)}) collective-permute-start(bf16[1408,256]{1,0:T(8,128)(2,1)} %get-tuple-element.82), channel_id=1, source_target_pairs={{0,8},{8,0},{16,24},{24,16},{1,9},{9,1},{17,25},{25,17},{2,10},{10... | collective-permute-start | bytes 2162696 | tf_op jit(solution)/shard_map/ppermute | solution.py:556
  84.0 19.2 %collective-permute-start.15 = (bf16[256,1408]{1,0:T(8,128)(2,1)S(1)}, bf16[256,1408]{1,0:T(8,128)(2,1)}, u32[]{:S(2)}, u32[]{:S(2)}) collective-permute-start(bf16[256,1408]{1,0:T(8,128)(2,1)S(1)} %collective-permute-done.12.refs_6_), channel_id=1, source_target_pairs={{0,16},{8,24},{16,0},{24,8},{1,17},{9,25},{17,1},{25,9},{2,18},{10... | collective-permute-start | bytes 2162696 | tf_op jit(solution)/shard_map/ppermute | solution.py:556
  97.4 25.3 %collective-permute-start.17 = (bf16[1408,256]{1,0:T(8,128)(2,1)}, bf16[1408,256]{1,0:T(8,128)(2,1)S(1)}, u32[]{:S(2)}, u32[]{:S(2)}) collective-permute-start(bf16[1408,256]{1,0:T(8,128)(2,1)} %get-tuple-element.82), channel_id=1, source_target_pairs={{0,16},{8,24},{16,0},{24,8},{1,17},{9,25},{17,1},{25,9},{2,18},{10... | collective-permute-start | bytes 2162696 | tf_op jit(solution)/shard_map/ppermute | solution.py:556
  98.3 34.6 %collective-permute-start.20 = (bf16[1408,256]{1,0:T(8,128)(2,1)}, bf16[1408,256]{1,0:T(8,128)(2,1)S(1)}, u32[]{:S(2)}, u32[]{:S(2)}) collective-permute-start(bf16[1408,256]{1,0:T(8,128)(2,1)} %collective-permute-done.16.refs_1_), channel_id=1, source_target_pairs={{0,16},{8,24},{16,0},{24,8},{1,17},{9,25},{17,1},{25,9},{2,18},{10... | collective-permute-start | bytes 2162696 | tf_op jit(solution)/shard_map/ppermute | solution.py:556
  99.8 33.1 %collective-permute-start.19 = (bf16[1408,256]{1,0:T(8,128)(2,1)}, bf16[1408,256]{1,0:T(8,128)(2,1)S(1)}, u32[]{:S(2)}, u32[]{:S(2)}) collective-permute-start(bf16[1408,256]{1,0:T(8,128)(2,1)} %get-tuple-element.85), channel_id=1, source_target_pairs={{0,8},{8,0},{16,24},{24,16},{1,9},{9,1},{17,25},{25,17},{2,10},{10... | collective-permute-start | bytes 2162696 | tf_op jit(solution)/shard_map/ppermute | solution.py:556
  103.2 29.8 %collective-permute-start.21 = (bf16[1408,256]{1,0:T(8,128)(2,1)}, bf16[1408,256]{1,0:T(8,128)(2,1)}, u32[]{:S(2)}, u32[]{:S(2)}) collective-permute-start(bf16[1408,256]{1,0:T(8,128)(2,1)} %collective-permute-done.13.refs_2_), channel_id=1, source_target_pairs={{0,8},{8,0},{16,24},{24,16},{1,9},{9,1},{17,25},{25,17},{2,10},{10... | collective-permute-start | bytes 2162696 | tf_op jit(solution)/shard_map/ppermute | solution.py:556
  132.8 8.9 %collective-permute-start.18 = (bf16[512,1280]{1,0:T(8,128)(2,1)}, bf16[512,1280]{1,0:T(8,128)(2,1)S(1)}, u32[]{:S(2)}, u32[]{:S(2)}) collective-permute-start(bf16[512,1280]{1,0:T(8,128)(2,1)} %get-tuple-element.84), channel_id=1, source_target_pairs={{0,1},{1,0},{2,3},{3,2},{4,5},{5,4},{6,7},{7,6},{8,9},{9,8},{10,11... | collective-permute-start | bytes 3932168 | tf_op jit(solution)/shard_map/ppermute | solution.py:556
  140.4 2.7 %collective-permute-start.22 = (bf16[512,768]{1,0:T(8,128)(2,1)}, bf16[512,768]{1,0:T(8,128)(2,1)S(1)}, u32[]{:S(2)}, u32[]{:S(2)}) collective-permute-start(bf16[512,768]{1,0:T(8,128)(2,1)} %get-tuple-element.87), channel_id=1, source_target_pairs={{0,1},{1,0},{2,3},{3,2},{4,5},{5,4},{6,7},{7,6},{8,9},{9,8},{10,11... | collective-permute-start | bytes 2359304 | tf_op jit(solution)/shard_map/ppermute | solution.py:556
  (18 other events, 144.5 us)

commit v6 on v5

--- a/solution.py
+++ b/solution.py
@@ -18,17 +18,15 @@
 RIM = 16
 BF16 = jnp.bfloat16
 F32 = jnp.float32
-VMEM_LIMIT = 60 * 1024 * 1024
 WIDE = 256
-FRONT = 512
+FRONT = 256
+QUERY = 512
 MIX = 256
 ROWS = 512
 
 
-def params():
-    return pltpu.CompilerParams(
-        dimension_semantics=("arbitrary",), vmem_limit_bytes=VMEM_LIMIT
-    )
+def params(mebibytes):
+    return pltpu.CompilerParams(vmem_limit_bytes=mebibytes * 1024 * 1024)
 
 
 def cost(flops, moved):
@@ -231,7 +229,7 @@
             pltpu.VMEM((tile + RIM, width), BF16), pltpu.VMEM((8, HK + HV), F32),
             pltpu.VMEM((HK, HV), F32), pltpu.VMEM((8, HK), F32), pltpu.VMEM((tile, HK), BF16),
         ],
-        compiler_params=params(),
+        compiler_params=params(20),
         cost_estimate=cost(1000, 1000),
     )(*prompts, tokens, rim, gain, project, project, project, down, up, bias, conv)
 
@@ -269,7 +267,7 @@
 def query(prompts, normed, rim, gain, project, gate, conv, sums):
     count, width = normed.shape
     pages = count // PAGE
-    tile = FRONT
+    tile = QUERY
     rows = lambda n: pl.BlockSpec((tile, n), lambda i: (i, 0))
     shape = jax.ShapeDtypeStruct
     return pl.pallas_call(
@@ -287,7 +285,7 @@
             shape((count, HK), BF16), shape((pages, KCONV - 1, HK), BF16), shape((count, HV), BF16),
         ],
         scratch_shapes=[pltpu.VMEM((RIM, width), BF16), pltpu.VMEM((8, HK), F32)],
-        compiler_params=params(),
+        compiler_params=params(20),
         cost_estimate=cost(2 * count * width * (HK + HV), 2 * count * width),
     )(*prompts, normed, rim, gain, project, gate, conv, sums)
 
@@ -308,6 +306,7 @@
         in_specs=[pl.BlockSpec(memory_space=pltpu.VMEM)] * 2,
         out_specs=pl.BlockSpec(memory_space=pltpu.VMEM),
         out_shape=jax.ShapeDtypeStruct(later.shape, BF16),
+        compiler_params=params(6),
         cost_estimate=cost(1000, 1000),
     )(later, earlier)
 
@@ -380,7 +379,7 @@
             jax.ShapeDtypeStruct((count // 2, HV), BF16),
         ],
         scratch_shapes=[pltpu.VMEM((HK, HV), F32)],
-        compiler_params=params(),
+        compiler_params=params(12),
         cost_estimate=cost(1000, 1000),
     )(*prompts, raised, lowered, weighted, value, ends, opening, gain, one, two)
 
@@ -431,7 +430,7 @@
         out_shape=[
             jax.ShapeDtypeStruct((count // 2, width), BF16), jax.ShapeDtypeStruct((count, width), BF16),
         ],
-        compiler_params=params(),
+        compiler_params=params(20),
         cost_estimate=cost(1000, 1000),
     )(hid_index, tokens, *own, *others, own_weight, other_weight, gain)
 
@@ -462,7 +461,7 @@
         + [pl.BlockSpec((piece.shape[0], WIDE), lambda i: (0, i)) for piece in pieces],
         out_specs=pl.BlockSpec((count, WIDE), lambda i: (0, i)),
         out_shape=jax.ShapeDtypeStruct((count, hidden), BF16),
-        compiler_params=params(),
+        compiler_params=params(24),
         cost_estimate=cost(1000, 1000),
     )(feed, *pieces)
 
@@ -514,7 +513,7 @@
         scratch_shapes=[pltpu.VMEM((count, depth), BF16)]
         + [pltpu.VMEM(piece.shape, BF16) for piece in pieces]
         + [pltpu.SemaphoreType.DMA((2,)), pltpu.SemaphoreType.DMA((len(pieces),))],
-        compiler_params=pltpu.CompilerParams(vmem_limit_bytes=VMEM_LIMIT),
+        compiler_params=params(20),
         cost_estimate=cost(1000, 1000),
     )(hidden, *pieces)
 
@@ -541,7 +540,7 @@
         in_specs=[rows(width)] + [rows(array.shape[1]) for array in arrays],
         out_specs=rows(width),
         out_shape=jax.ShapeDtypeStruct((count, width), BF16),
-        compiler_params=params(),
+        compiler_params=params(12),
         cost_estimate=cost(1000, 1000),
     )(residual, *arrays)
 

time: 148 us -> 147 us (level)
  Pallas kernels: 84.9 us -> 63.5 us
  local copies, waits for them, and re-layouts: 10.9 us -> 28.2 us
  starting transfers between devices: 31.7 us -> 35.3 us
  waiting for transfers between devices: 19.6 us -> 17.6 us
    unnamed x39 -> x89, local copies, waits for them, and re-layouts: 4.31 us -> 23.8 us
    pallas_call x2, Pallas kernels: 15.6 us -> 10.5 us  [narrow(): pl.pallas_call(functools.partial(narrow_kernel, block), name='narrow', in...]
    pallas_call x1, Pallas kernels: 11.2 us -> 7.51 us  [mix(): pl.pallas_call(lambda s, *refs: mix_kernel(*refs), name='mix', grid_spec=...]
    ppermute x20, waiting for transfers between devices: 19.6 us -> 16.5 us  [swapped(): return lax.ppermute(value, axis, [(i, i ^ flip) for i in range(count)])]
    pallas_call x1, Pallas kernels: 16.4 us -> 13.5 us  [front(): pl.pallas_call(front_kernel, name='front', grid=(count // tile,), in_spec...]
    pallas_call x1, Pallas kernels: 8.55 us -> 5.9 us  [query(): pl.pallas_call(query_kernel, name='query', grid=(count // tile,), in_spec...]
    pallas_call x1, Pallas kernels: 4.12 us -> 1.76 us  [close(): pl.pallas_call(functools.partial(close_kernel, [group[2] for group in gro...]
    ppermute x20, starting transfers between devices: 20 us -> 22.2 us  [swapped(): return lax.ppermute(value, axis, [(i, i ^ flip) for i in range(count)])]
  transfers between devices with their start and end apart: 23 -> 23, of which waited for: 8 -> 5; matrix products, arithmetic and copies ran while one was open for 5% -> 3% of each run, Pallas kernels for 55% -> 42%
where the time goes in v6:
time: 147 us; the launch traced here: 146 us
  Pallas kernels  63.5 us (43%)
  starting transfers between devices  35.3 us (24%)
  local copies, waits for them, and re-layouts  28.2 us (19%)
  waiting for transfers between devices  17.6 us (12%)
    unnamed x89, local copies, waits for them, and re-layouts  23.8 us
    ppermute x20, starting transfers between devices, swapped(): return lax.ppermute(value, axis, [(i, i ^ flip) for i in range(count)])  22.2 us
    pallas_call x1, Pallas kernels, widen(): pl.pallas_call(functools.partial(widen_kernel, places), name='widen', gri...  17.4 us
    ppermute x20, waiting for transfers between devices, swapped(): return lax.ppermute(value, axis, [(i, i ^ flip) for i in range(count)])  16.5 us
    pallas_call x1, Pallas kernels, front(): pl.pallas_call(front_kernel, name='front', grid=(count // tile,), in_spec...  13.5 us
    ppermute x3, starting transfers between devices, shifted(): lax.ppermute(value, 'seq', [(i, i + steps) for i in range(count - steps)])  13.2 us
    pallas_call x2, Pallas kernels, narrow(): pl.pallas_call(functools.partial(narrow_kernel, block), name='narrow', in...  10.5 us
    pallas_call x1, Pallas kernels, mix(): pl.pallas_call(lambda s, *refs: mix_kernel(*refs), name='mix', grid_spec=...  7.51 us
  transfers between devices with their start and end apart: 23, of which 5 were waited for; matrix products, arithmetic and copies ran while one was open for 3% of the time, Pallas kernels for 42%

profile of v6, /device:TPU:0, one launch (start us, length us, event | category | flops | bytes accessed | tf_op | source)
XLA Modules:
  0.0 145.7 jit_solution(4286511822430482450)
XLA Ops:
  1.1 2.6 %collective-permute-start.4 = (bf16[512,1408]{1,0:T(8,128)(2,1)}, bf16[512,1408]{1,0:T(8,128)(2,1)S(1)}, u32[]{:S(2)}, u32[]{:S(2)}) collective-permute-start(bf16[512,1408]{1,0:T(8,128)(2,1)} %refs_0_.4), channel_id=1, source_target_pairs={{0,8},{8,0},{16,24},{24,16},{1,9},{9,1},{17,25},{25,17},{2,10},{10... | collective-permute-start | bytes 4325384 | tf_op jit(solution)/shard_map/ppermute | solution.py:555
  3.7 1.5 %collective-permute-start.5 = (bf16[512,1408]{1,0:T(8,128)(2,1)}, bf16[512,1408]{1,0:T(8,128)(2,1)}, u32[]{:S(2)}, u32[]{:S(2)}) collective-permute-start(bf16[512,1408]{1,0:T(8,128)(2,1)} %refs_0_.4), channel_id=1, source_target_pairs={{0,16},{8,24},{16,0},{24,8},{1,17},{9,25},{17,1},{25,9},{2,18},{10... | collective-permute-start | bytes 4325384 | tf_op jit(solution)/shard_map/ppermute | solution.py:555
  6.7 4.1 %collective-permute-start = (bf16[16,2048]{1,0:T(8,128)(2,1)}, bf16[16,2048]{1,0:T(8,128)(2,1)}, u32[]{:S(2)}, u32[]{:S(2)}) collective-permute-start(bf16[16,2048]{1,0:T(8,128)(2,1)} %slice.9), channel_id=1, source_target_pairs={{0,2},{2,4},{4,6},{1,3},{3,5},{5,7},{8,10},{10,12},{12,14},{9,11},... | collective-permute-start | bytes 196616 | tf_op jit(solution)/shard_map/ppermute | solution.py:550
  15.2 2.2 %copy-done = bf16[2048,1024]{1,0:T(8,128)(2,1)S(1)} copy-done((bf16[2048,1024]{1,0:T(8,128)(2,1)S(1)}, bf16[2048,1024]{1,0:T(8,128)(2,1)}, u32[]{:S(2)}) %copy-start) | copy-done | bytes 4194328
  17.4 2.2 %copy-done.2 = bf16[1024,2048]{1,0:T(8,128)(2,1)S(1)} copy-done((bf16[1024,2048]{1,0:T(8,128)(2,1)S(1)}, bf16[1024,2048]{1,0:T(8,128)(2,1)}, u32[]{:S(2)}) %copy-start.2) | copy-done | bytes 4194328
  23.8 13.5 %front.1 = (bf16[1024,2048]{1,0:T(8,128)(2,1)S(1)}, f32[1024,256]{1,0:T(8,128)S(1)}, bf16[1024,256]{1,0:T(8,128)(2,1)S(1)}, bf16[1024,256]{1,0:T(8,128)(2,1)S(1)...) custom-call(s32[1,16]{1,0:T(1,128)S(1)} %copy-done.36, ...), custom_call_target="tpu_custom_call" | custom-call | flops 1000 | bytes 1000 | tf_op jit(solution)/shard_map/front/pallas_call | solution.py:208
  37.3 3.5 %collective-permute-start.2 = (bf16[272,512]{1,0:T(8,128)(2,1)S(1)}, bf16[272,512]{1,0:T(8,128)(2,1)S(1)}, u32[]{:S(2)}, u32[]{:S(2)}) collective-permute-start(bf16[272,512]{1,0:T(8,128)(2,1)S(1)} %get-tuple-element.48.later_ref), channel_id=1, source_target_pairs={{0,2},{2,4},{4,6},{1,3},{3,5},{5,7},{8,10},{10,12},{12,14},{9,11},... | collective-permute-start | bytes 835592 | tf_op jit(solution)/shard_map/ppermute | solution.py:550
  42.9 1.5 %collective-permute-start.13 = (bf16[1408,256]{1,0:T(8,128)(2,1)S(1)}, bf16[1408,256]{1,0:T(8,128)(2,1)S(1)}, u32[]{:S(2)}, u32[]{:S(2)}) collective-permute-start(bf16[1408,256]{1,0:T(8,128)(2,1)S(1)} %get-tuple-element.85), channel_id=1, source_target_pairs={{0,16},{8,24},{16,0},{24,8},{1,17},{9,25},{17,1},{25,9},{2,18},{10... | collective-permute-start | bytes 2162696 | tf_op jit(solution)/shard_map/ppermute | solution.py:555
  45.8 5.6 %collective-permute-start.3 = (bf16[272,512]{1,0:T(8,128)(2,1)S(1)}, bf16[272,512]{1,0:T(8,128)(2,1)S(1)}, u32[]{:S(2)}, u32[]{:S(2)}) collective-permute-start(bf16[272,512]{1,0:T(8,128)(2,1)S(1)} %joined.1), channel_id=1, source_target_pairs={{0,4},{2,6},{1,5},{3,7},{8,12},{10,14},{9,13},{11,15},{16,20},{18,... | collective-permute-start | bytes 835592 | tf_op jit(solution)/shard_map/ppermute | solution.py:550
  51.4 5.9 %query.1 = (bf16[1024,256]{1,0:T(8,128)(2,1)S(1)}, bf16[16,3,256]{2,1,0:T(4,128)(2,1)S(1)}, bf16[1024,512]{1,0:T(8,128)(2,1)S(1)}) custom-call(s32[1,16]{1,0:T(1,128)S(1)} %copy-done.36, s32[1,16]{1,0:T(1,128)S(1)} %copy-done.37, bf16[1024,2048]{1,0:T(8,128)(2,1)S(1)} %get-tuple-element.50.normed_ref, bf16[16,2048]{1,0:T(8,128)(2,1)} %collective-permute-done.rim_ref, ...), custom_call_target="tpu_custom_call" | custom-call | flops 3221225472 | bytes 4194304 | tf_op jit(solution)/shard_map/query/pallas_call | solution.py:273
  57.4 1.6 %collective-permute-start.10 = (bf16[256,1408]{1,0:T(8,128)(2,1)S(1)}, bf16[256,1408]{1,0:T(8,128)(2,1)S(1)}, u32[]{:S(2)}, u32[]{:S(2)}) collective-permute-start(bf16[256,1408]{1,0:T(8,128)(2,1)S(1)} %collective-permute-done.6.refs_5_), channel_id=1, source_target_pairs={{0,16},{8,24},{16,0},{24,8},{1,17},{9,25},{17,1},{25,9},{2,18},{10... | collective-permute-start | bytes 2162696 | tf_op jit(solution)/shard_map/ppermute | solution.py:555
  59.0 5.1 %collective-permute-start.12 = (bf16[256,1408]{1,0:T(8,128)(2,1)S(1)}, bf16[256,1408]{1,0:T(8,128)(2,1)}, u32[]{:S(2)}, u32[]{:S(2)}) collective-permute-start(bf16[256,1408]{1,0:T(8,128)(2,1)S(1)} %collective-permute-done.6.refs_5_), channel_id=1, source_target_pairs={{0,2},{2,0},{4,6},{6,4},{1,3},{3,1},{5,7},{7,5},{8,10},{10,8},{12,... | collective-permute-start | bytes 2162696 | tf_op jit(solution)/shard_map/ppermute | solution.py:555
  64.1 6.6 %pages.1 = (bf16[16,1,256,512]{3,2,1,0:T(8,128)(2,1)}, bf16[512,512]{1,0:T(8,128)(2,1)S(1)}, bf16[512,512]{1,0:T(8,128)(2,1)S(1)}) custom-call(s32[1,16]{1,0:T(1,128)S(1)} %copy-done.36, s32[1,16]{1,0:T(1,128)S(1)} %copy-done.37, bf16[1024,256]{1,0:T(8,128)(2,1)S(1)} %get-tuple-element.53.raised_ref, bf16[1024,256]{1,0:T(8,128)(2,1)S(1)} %get-tuple-element.54.lowered_ref, ...), custom_call_target="tpu_custom_call" | custom-call | flops 1000 | bytes 1000 | tf_op jit(solution)/shard_map/pages/pallas_call | solution.py:364
  75.2 8.7 %collective-permute-done.10.refs_9_ = bf16[256,1408]{1,0:T(8,128)(2,1)S(1)} collective-permute-done((bf16[256,1408]{1,0:T(8,128)(2,1)S(1)}, bf16[256,1408]{1,0:T(8,128)(2,1)S(1)}, u32[]{:S(2)}, u32[]{:S(2)}) %collective-permute-start.10) | collective-permute-done | bytes 720928 | tf_op jit(solution)/shard_map/ppermute | solution.py:555
  85.9 1.5 %collective-permute-start.15 = (bf16[256,1408]{1,0:T(8,128)(2,1)}, bf16[256,1408]{1,0:T(8,128)(2,1)}, u32[]{:S(2)}, u32[]{:S(2)}) collective-permute-start(bf16[256,1408]{1,0:T(8,128)(2,1)} %collective-permute-done.12.refs_6_), channel_id=1, source_target_pairs={{0,16},{8,24},{16,0},{24,8},{1,17},{9,25},{17,1},{25,9},{2,18},{10... | collective-permute-start | bytes 2162696 | tf_op jit(solution)/shard_map/ppermute | solution.py:555
  87.5 2.2 %copy-done.3 = bf16[1024,2048]{1,0:T(8,128)(2,1)S(1)} copy-done((bf16[1024,2048]{1,0:T(8,128)(2,1)S(1)}, bf16[1024,2048]{1,0:T(8,128)(2,1)}, u32[]{:S(2)}) %copy-start.3) | copy-done | bytes 4194328
  89.7 1.6 %copy-done.8 = bf16[512,2048]{1,0:T(8,128)(2,1)S(1)} copy-done((bf16[512,2048]{1,0:T(8,128)(2,1)S(1)}, bf16[512,2048]{1,0:T(8,128)(2,1)}, u32[]{:S(2)}) %copy-start.8) | copy-done | bytes 2097176
  95.5 7.5 %mix.1 = (bf16[512,2048]{1,0:T(8,128)(2,1)S(1)}, bf16[1024,2048]{1,0:T(8,128)(2,1)S(1)}) custom-call(s32[1]{0:T(128)} %bitcast.s, bf16[1024,2048]{1,0:T(8,128)(2,1)S(1)} %copy-done.3, bf16[512,512]{1,0:T(8,128)(2,1)S(1)} %copy-done.21, bf16[512,512]{1,0:T(8,128)(2,1)S(1)} %copy-done.23, bf16[512,512]{1,0:T(8,128)(2,1)S(1)} %copy-done.25, ...), custom_call_target="tpu_custom_call" | custom-call | flops 1000 | bytes 1000 | tf_op jit(solution)/shard_map/mix/pallas_call | solution.py:420
  105.6 1.6 %collective-permute-start.21 = (bf16[1408,256]{1,0:T(8,128)(2,1)S(1)}, bf16[1408,256]{1,0:T(8,128)(2,1)S(1)}, u32[]{:S(2)}, u32[]{:S(2)}) collective-permute-start(bf16[1408,256]{1,0:T(8,128)(2,1)S(1)} %copy-done.19), channel_id=1, source_target_pairs={{0,8},{8,0},{16,24},{24,16},{1,9},{9,1},{17,25},{25,17},{2,10},{10... | collective-permute-start | bytes 2162696 | tf_op jit(solution)/shard_map/ppermute | solution.py:555
  107.2 17.4 %widen.1.hidden_hbm = bf16[1024,1408]{1,0:T(8,128)(2,1)S(1)} custom-call(bf16[1024,2048]{1,0:T(8,128)(2,1)S(1)} %get-tuple-element.75.feed_ref, bf16[512,1408]{1,0:T(8,128)(2,1)S(1)} %copy-done.9, bf16[512,1408]{1,0:T(8,128)(2,1)S(1)} %copy-done.11, bf16[512,1408]{1,0:T(8,128)(2,1)} %collective-permute-done.5.refs_2_, bf16[512,1408]{1,0:T(8,128)(2,1)S(1)} %copy-done.13, ...), custom_call_target="tpu_custom_call" | custom-call | flops 1000 | bytes 1000 | tf_op jit(solution)/shard_map/widen/pallas_call | solution.py:456
  124.7 6.1 %narrow.2 = (bf16[512,1280]{1,0:T(8,128)(2,1)S(1)}, bf16[512,1280]{1,0:T(8,128)(2,1)S(1)}) custom-call(bf16[1024,1408]{1,0:T(8,128)(2,1)S(1)} %widen.1.hidden_hbm, bf16[1408,512]{1,0:T(8,128)(2,1)S(1)} %copy-done.4, bf16[1408,256]{1,0:T(8,128)(2,1)} %collective-permute-done.16.refs_1_, bf16[1408,256]{1,0:T(8,128)(2,1)S(1)} %copy-done.19, ...), custom_call_target="tpu_custom_call" | custom-call | flops 1000 | bytes 1000 | tf_op jit(solution)/shard_map/narrow/pallas_call | solution.py:507
  131.0 5.0 %collective-permute-done.20.refs_1_ = bf16[1408,256]{1,0:T(8,128)(2,1)S(1)} collective-permute-done((bf16[1408,256]{1,0:T(8,128)(2,1)}, bf16[1408,256]{1,0:T(8,128)(2,1)S(1)}, u32[]{:S(2)}, u32[]{:S(2)}) %collective-permute-start.20) | collective-permute-done | bytes 720928 | tf_op jit(solution)/shard_map/ppermute | solution.py:555
  137.2 4.4 %narrow.3 = (bf16[512,768]{1,0:T(8,128)(2,1)S(1)}, bf16[512,768]{1,0:T(8,128)(2,1)S(1)}) custom-call(bf16[1024,1408]{1,0:T(8,128)(2,1)S(1)} %widen.1.hidden_hbm, bf16[1408,256]{1,0:T(8,128)(2,1)S(1)} %collective-permute-done.19.refs_0_, bf16[1408,256]{1,0:T(8,128)(2,1)S(1)} %collective-permute-done.20.refs_1_, ...), custom_call_target="tpu_custom_call" | custom-call | flops 1000 | bytes 1000 | tf_op jit(solution)/shard_map/narrow/pallas_call | solution.py:507
  143.9 1.8 %close.1 = bf16[512,2048]{1,0:T(8,128)(2,1)} custom-call(bf16[512,2048]{1,0:T(8,128)(2,1)S(1)} %get-tuple-element.68.residual_ref, bf16[512,1280]{1,0:T(8,128)(2,1)S(1)} %get-tuple-element.83.refs_0_, bf16[512,1280]{1,0:T(8,128)(2,1)S(1)} %collective-permute-done.18.refs_1_, bf16[512,768]{1,0:T(8,128)(2,1)S(1)} %get-tuple-element.86.refs_2_, ...), custom_call_target="tpu_custom_call" | custom-call | flops 1000 | bytes 1000 | tf_op jit(solution)/shard_map/close/pallas_call | solution.py:536
  (127 shorter events, 31.0 us)
Async XLA Ops:
  0.6 13.2 %collective-permute-start.1 = (bf16[512,2048]{1,0:T(8,128)(2,1)}, bf16[512,2048]{1,0:T(8,128)(2,1)S(1)}, u32[]{:S(2)}, u32[]{:S(2)}) collective-permute-start(bf16[512,2048]{1,0:T(8,128)(2,1)} %refs_5_.1), channel_id=1, source_target_pairs={{0,1},{1,0},{2,3},{3,2},{4,5},{5,4},{6,7},{7,6},{8,9},{9,8},{10,11... | collective-permute-start | bytes 6291464 | tf_op jit(solution)/shard_map/ppermute | solution.py:555
  1.1 39.6 %collective-permute-start.4 = (bf16[512,1408]{1,0:T(8,128)(2,1)}, bf16[512,1408]{1,0:T(8,128)(2,1)S(1)}, u32[]{:S(2)}, u32[]{:S(2)}) collective-permute-start(bf16[512,1408]{1,0:T(8,128)(2,1)} %refs_0_.4), channel_id=1, source_target_pairs={{0,8},{8,0},{16,24},{24,16},{1,9},{9,1},{17,25},{25,17},{2,10},{10... | collective-permute-start | bytes 4325384 | tf_op jit(solution)/shard_map/ppermute | solution.py:555
  3.7 37.1 %collective-permute-start.5 = (bf16[512,1408]{1,0:T(8,128)(2,1)}, bf16[512,1408]{1,0:T(8,128)(2,1)}, u32[]{:S(2)}, u32[]{:S(2)}) collective-permute-start(bf16[512,1408]{1,0:T(8,128)(2,1)} %refs_0_.4), channel_id=1, source_target_pairs={{0,16},{8,24},{16,0},{24,8},{1,17},{9,25},{17,1},{25,9},{2,18},{10... | collective-permute-start | bytes 4325384 | tf_op jit(solution)/shard_map/ppermute | solution.py:555
  6.7 6.6 %collective-permute-start = (bf16[16,2048]{1,0:T(8,128)(2,1)}, bf16[16,2048]{1,0:T(8,128)(2,1)}, u32[]{:S(2)}, u32[]{:S(2)}) collective-permute-start(bf16[16,2048]{1,0:T(8,128)(2,1)} %slice.9), channel_id=1, source_target_pairs={{0,2},{2,4},{4,6},{1,3},{3,5},{5,7},{8,10},{10,12},{12,14},{9,11},... | collective-permute-start | bytes 196616 | tf_op jit(solution)/shard_map/ppermute | solution.py:550
  12.0 45.4 %collective-permute-start.6 = (bf16[256,1408]{1,0:T(8,128)(2,1)S(1)}, bf16[256,1408]{1,0:T(8,128)(2,1)S(1)}, u32[]{:S(2)}, u32[]{:S(2)}) collective-permute-start(bf16[256,1408]{1,0:T(8,128)(2,1)S(1)} %constant_dynamic-slice_fusion), channel_id=1, source_target_pairs={{0,8},{8,0},{16,24},{24,16},{1,9},{9,1},{17,25},{25,17},{2,10},{10... | collective-permute-start | bytes 2162696 | tf_op jit(solution)/shard_map/ppermute | solution.py:555
  13.3 44.1 %collective-permute-start.7 = (bf16[256,1408]{1,0:T(8,128)(2,1)S(1)}, bf16[256,1408]{1,0:T(8,128)(2,1)}, u32[]{:S(2)}, u32[]{:S(2)}) collective-permute-start(bf16[256,1408]{1,0:T(8,128)(2,1)S(1)} %constant_dynamic-slice_fusion), channel_id=1, source_target_pairs={{0,16},{8,24},{16,0},{24,8},{1,17},{9,25},{17,1},{25,9},{2,18},{10... | collective-permute-start | bytes 2162696 | tf_op jit(solution)/shard_map/ppermute | solution.py:555
  23.8 27.6 %copy-start.1 = (bf16[2048,1024]{1,0:T(8,128)(2,1)S(1)}, bf16[2048,1024]{1,0:T(8,128)(2,1)}, u32[]{:S(2)}) copy-start(bf16[2048,1024]{1,0:T(8,128)(2,1)} %query_ref.1) | copy-start | bytes 12582916
  37.3 8.3 %collective-permute-start.2 = (bf16[272,512]{1,0:T(8,128)(2,1)S(1)}, bf16[272,512]{1,0:T(8,128)(2,1)S(1)}, u32[]{:S(2)}, u32[]{:S(2)}) collective-permute-start(bf16[272,512]{1,0:T(8,128)(2,1)S(1)} %get-tuple-element.48.later_ref), channel_id=1, source_target_pairs={{0,2},{2,4},{4,6},{1,3},{3,5},{5,7},{8,10},{10,12},{12,14},{9,11},... | collective-permute-start | bytes 835592 | tf_op jit(solution)/shard_map/ppermute | solution.py:550
  40.8 44.0 %collective-permute-start.11 = (bf16[512,1408]{1,0:T(8,128)(2,1)}, bf16[512,1408]{1,0:T(8,128)(2,1)S(1)}, u32[]{:S(2)}, u32[]{:S(2)}) collective-permute-start(bf16[512,1408]{1,0:T(8,128)(2,1)} %collective-permute-done.5.refs_2_), channel_id=1, source_target_pairs={{0,8},{8,0},{16,24},{24,16},{1,9},{9,1},{17,25},{25,17},{2,10},{10... | collective-permute-start | bytes 4325384 | tf_op jit(solution)/shard_map/ppermute | solution.py:555
  42.9 28.7 %collective-permute-start.13 = (bf16[1408,256]{1,0:T(8,128)(2,1)S(1)}, bf16[1408,256]{1,0:T(8,128)(2,1)S(1)}, u32[]{:S(2)}, u32[]{:S(2)}) collective-permute-start(bf16[1408,256]{1,0:T(8,128)(2,1)S(1)} %get-tuple-element.85), channel_id=1, source_target_pairs={{0,16},{8,24},{16,0},{24,8},{1,17},{9,25},{17,1},{25,9},{2,18},{10... | collective-permute-start | bytes 2162696 | tf_op jit(solution)/shard_map/ppermute | solution.py:555
  45.8 11.6 %collective-permute-start.3 = (bf16[272,512]{1,0:T(8,128)(2,1)S(1)}, bf16[272,512]{1,0:T(8,128)(2,1)S(1)}, u32[]{:S(2)}, u32[]{:S(2)}) collective-permute-start(bf16[272,512]{1,0:T(8,128)(2,1)S(1)} %joined.1), channel_id=1, source_target_pairs={{0,4},{2,6},{1,5},{3,7},{8,12},{10,14},{9,13},{11,15},{16,20},{18,... | collective-permute-start | bytes 835592 | tf_op jit(solution)/shard_map/ppermute | solution.py:550
  57.4 26.5 %collective-permute-start.10 = (bf16[256,1408]{1,0:T(8,128)(2,1)S(1)}, bf16[256,1408]{1,0:T(8,128)(2,1)S(1)}, u32[]{:S(2)}, u32[]{:S(2)}) collective-permute-start(bf16[256,1408]{1,0:T(8,128)(2,1)S(1)} %collective-permute-done.6.refs_5_), channel_id=1, source_target_pairs={{0,16},{8,24},{16,0},{24,8},{1,17},{9,25},{17,1},{25,9},{2,18},{10... | collective-permute-start | bytes 2162696 | tf_op jit(solution)/shard_map/ppermute | solution.py:555
  59.0 25.8 %collective-permute-start.12 = (bf16[256,1408]{1,0:T(8,128)(2,1)S(1)}, bf16[256,1408]{1,0:T(8,128)(2,1)}, u32[]{:S(2)}, u32[]{:S(2)}) collective-permute-start(bf16[256,1408]{1,0:T(8,128)(2,1)S(1)} %collective-permute-done.6.refs_5_), channel_id=1, source_target_pairs={{0,2},{2,0},{4,6},{6,4},{1,3},{3,1},{5,7},{7,5},{8,10},{10,8},{12,... | collective-permute-start | bytes 2162696 | tf_op jit(solution)/shard_map/ppermute | solution.py:555
  70.8 2.2 %collective-permute-start.8 = (bf16[512,512]{1,0:T(8,128)(2,1)S(1)}, bf16[512,512]{1,0:T(8,128)(2,1)S(1)}, u32[]{:S(2)}, u32[]{:S(2)}) collective-permute-start(bf16[512,512]{1,0:T(8,128)(2,1)S(1)} %get-tuple-element.61.refs_1_), channel_id=1, source_target_pairs={{0,1},{1,0},{2,3},{3,2},{4,5},{5,4},{6,7},{7,6},{8,9},{9,8},{10,11... | collective-permute-start | bytes 1572872 | tf_op jit(solution)/shard_map/ppermute | solution.py:555
  71.6 2.1 %collective-permute-start.9 = (bf16[512,512]{1,0:T(8,128)(2,1)S(1)}, bf16[512,512]{1,0:T(8,128)(2,1)S(1)}, u32[]{:S(2)}, u32[]{:S(2)}) collective-permute-start(bf16[512,512]{1,0:T(8,128)(2,1)S(1)} %get-tuple-element.62.refs_2_), channel_id=1, source_target_pairs={{0,1},{1,0},{2,3},{3,2},{4,5},{5,4},{6,7},{7,6},{8,9},{9,8},{10,11... | collective-permute-start | bytes 1572872 | tf_op jit(solution)/shard_map/ppermute | solution.py:555
  73.7 31.9 %collective-permute-start.14 = (bf16[256,1408]{1,0:T(8,128)(2,1)}, bf16[256,1408]{1,0:T(8,128)(2,1)}, u32[]{:S(2)}, u32[]{:S(2)}) collective-permute-start(bf16[256,1408]{1,0:T(8,128)(2,1)} %collective-permute-done.7.refs_7_), channel_id=1, source_target_pairs={{0,2},{2,0},{4,6},{6,4},{1,3},{3,1},{5,7},{7,5},{8,10},{10,8},{12,... | collective-permute-start | bytes 2162696 | tf_op jit(solution)/shard_map/ppermute | solution.py:555
  74.5 29.0 %collective-permute-start.16 = (bf16[1408,256]{1,0:T(8,128)(2,1)}, bf16[1408,256]{1,0:T(8,128)(2,1)}, u32[]{:S(2)}, u32[]{:S(2)}) collective-permute-start(bf16[1408,256]{1,0:T(8,128)(2,1)} %get-tuple-element.82), channel_id=1, source_target_pairs={{0,8},{8,0},{16,24},{24,16},{1,9},{9,1},{17,25},{25,17},{2,10},{10... | collective-permute-start | bytes 2162696 | tf_op jit(solution)/shard_map/ppermute | solution.py:555
  85.9 19.7 %collective-permute-start.15 = (bf16[256,1408]{1,0:T(8,128)(2,1)}, bf16[256,1408]{1,0:T(8,128)(2,1)}, u32[]{:S(2)}, u32[]{:S(2)}) collective-permute-start(bf16[256,1408]{1,0:T(8,128)(2,1)} %collective-permute-done.12.refs_6_), channel_id=1, source_target_pairs={{0,16},{8,24},{16,0},{24,8},{1,17},{9,25},{17,1},{25,9},{2,18},{10... | collective-permute-start | bytes 2162696 | tf_op jit(solution)/shard_map/ppermute | solution.py:555
  103.0 21.7 %collective-permute-start.17 = (bf16[1408,256]{1,0:T(8,128)(2,1)}, bf16[1408,256]{1,0:T(8,128)(2,1)S(1)}, u32[]{:S(2)}, u32[]{:S(2)}) collective-permute-start(bf16[1408,256]{1,0:T(8,128)(2,1)} %get-tuple-element.82), channel_id=1, source_target_pairs={{0,16},{8,24},{16,0},{24,8},{1,17},{9,25},{17,1},{25,9},{2,18},{10... | collective-permute-start | bytes 2162696 | tf_op jit(solution)/shard_map/ppermute | solution.py:555
  103.6 32.3 %collective-permute-start.20 = (bf16[1408,256]{1,0:T(8,128)(2,1)}, bf16[1408,256]{1,0:T(8,128)(2,1)S(1)}, u32[]{:S(2)}, u32[]{:S(2)}) collective-permute-start(bf16[1408,256]{1,0:T(8,128)(2,1)} %collective-permute-done.16.refs_1_), channel_id=1, source_target_pairs={{0,16},{8,24},{16,0},{24,8},{1,17},{9,25},{17,1},{25,9},{2,18},{10... | collective-permute-start | bytes 2162696 | tf_op jit(solution)/shard_map/ppermute | solution.py:555
  105.1 30.8 %collective-permute-start.19 = (bf16[1408,256]{1,0:T(8,128)(2,1)S(1)}, bf16[1408,256]{1,0:T(8,128)(2,1)S(1)}, u32[]{:S(2)}, u32[]{:S(2)}) collective-permute-start(bf16[1408,256]{1,0:T(8,128)(2,1)S(1)} %copy-done.41), channel_id=1, source_target_pairs={{0,8},{8,0},{16,24},{24,16},{1,9},{9,1},{17,25},{25,17},{2,10},{10... | collective-permute-start | bytes 2162696 | tf_op jit(solution)/shard_map/ppermute | solution.py:555
  105.6 31.6 %collective-permute-start.21 = (bf16[1408,256]{1,0:T(8,128)(2,1)S(1)}, bf16[1408,256]{1,0:T(8,128)(2,1)S(1)}, u32[]{:S(2)}, u32[]{:S(2)}) collective-permute-start(bf16[1408,256]{1,0:T(8,128)(2,1)S(1)} %copy-done.19), channel_id=1, source_target_pairs={{0,8},{8,0},{16,24},{24,16},{1,9},{9,1},{17,25},{25,17},{2,10},{10... | collective-permute-start | bytes 2162696 | tf_op jit(solution)/shard_map/ppermute | solution.py:555
  130.9 11.6 %collective-permute-start.18 = (bf16[512,1280]{1,0:T(8,128)(2,1)S(1)}, bf16[512,1280]{1,0:T(8,128)(2,1)S(1)}, u32[]{:S(2)}, u32[]{:S(2)}) collective-permute-start(bf16[512,1280]{1,0:T(8,128)(2,1)S(1)} %get-tuple-element.84), channel_id=1, source_target_pairs={{0,1},{1,0},{2,3},{3,2},{4,5},{5,4},{6,7},{7,6},{8,9},{9,8},{10,11... | collective-permute-start | bytes 3932168 | tf_op jit(solution)/shard_map/ppermute | solution.py:555
  141.6 2.4 %collective-permute-start.22 = (bf16[512,768]{1,0:T(8,128)(2,1)S(1)}, bf16[512,768]{1,0:T(8,128)(2,1)S(1)}, u32[]{:S(2)}, u32[]{:S(2)}) collective-permute-start(bf16[512,768]{1,0:T(8,128)(2,1)S(1)} %get-tuple-element.87), channel_id=1, source_target_pairs={{0,1},{1,0},{2,3},{3,2},{4,5},{5,4},{6,7},{7,6},{8,9},{9,8},{10,11... | collective-permute-start | bytes 2359304 | tf_op jit(solution)/shard_map/ppermute | solution.py:555
  (43 other events, 319.2 us)

commit v7 on v6

--- a/solution.py
+++ b/solution.py
@@ -19,6 +19,8 @@
 BF16 = jnp.bfloat16
 F32 = jnp.float32
 WIDE = 256
+WIDEN_VMEM = 30
+FINISH_VMEM = 24
 FRONT = 256
 QUERY = 512
 MIX = 256
@@ -229,7 +231,7 @@
             pltpu.VMEM((tile + RIM, width), BF16), pltpu.VMEM((8, HK + HV), F32),
             pltpu.VMEM((HK, HV), F32), pltpu.VMEM((8, HK), F32), pltpu.VMEM((tile, HK), BF16),
         ],
-        compiler_params=params(20),
+        compiler_params=params(44),
         cost_estimate=cost(1000, 1000),
     )(*prompts, tokens, rim, gain, project, project, project, down, up, bias, conv)
 
@@ -435,35 +437,59 @@
     )(hid_index, tokens, *own, *others, own_weight, other_weight, gain)
 
 
+def widen_sums(places, pieces, feed_ref, rows):
+    sums = {}
+    for (matrix, place), ref in zip(places, pieces):
+        columns = pl.ds(pl.multiple_of(place(), 128), ref.shape[0])
+        part = dot(feed_ref[rows, columns], ref[...])
+        sums[matrix] = part if matrix not in sums else sums[matrix] + part
+    return sums
+
+
 def widen_kernel(places, feed_ref, *refs):
+    pieces, (gate_ref, up_ref) = refs[:-2], refs[-2:]
+    for first in range(0, feed_ref.shape[0], ROWS):
+        rows = pl.ds(first, ROWS)
+        sums = widen_sums(places, pieces, feed_ref, rows)
+        gate_ref[rows, :] = silu(sums[0]).astype(BF16)
+        up_ref[rows, :] = sums[1]
+
+
+def finish_kernel(places, feed_ref, gate_ref, up_ref, *refs):
     pieces, out_ref = refs[:-1], refs[-1]
-    count = feed_ref.shape[0]
-    for first in range(0, count, ROWS):
+    for first in range(0, feed_ref.shape[0], ROWS):
         rows = pl.ds(first, ROWS)
-        sums = [None, None]
-        for (matrix, place), ref in zip(places, pieces):
-            columns = pl.ds(pl.multiple_of(place(), 128), ref.shape[0])
-            part = dot(feed_ref[rows, columns], ref[...])
-            sums[matrix] = part if sums[matrix] is None else sums[matrix] + part
-        out_ref[rows, :] = (silu(sums[0]) * sums[1]).astype(BF16)
-
-
-def widen(feed, matrices):
+        total = up_ref[rows, :]
+        if pieces:
+            total = total + widen_sums(places, pieces, feed_ref, rows)[1]
+        out_ref[rows, :] = (gate_ref[rows, :].astype(F32) * total).astype(BF16)
+
+
+def widen_call(kernel, name, limit, kinds, feed, wholes, matrices):
     count, width = feed.shape
     pieces = [piece for matrix in matrices for piece, _ in matrix]
     places = [(i, place) for i, matrix in enumerate(matrices) for _, place in matrix]
-    hidden = pieces[0].shape[1]
+    hidden = (wholes or pieces)[0].shape[1]
+    block = pl.BlockSpec((count, WIDE), lambda i: (0, i))
     return pl.pallas_call(
-        functools.partial(widen_kernel, places),
-        name="widen",
+        functools.partial(kernel, places),
+        name=name,
         grid=(pl.cdiv(hidden, WIDE),),
-        in_specs=[fixed((count, width))]
+        in_specs=[fixed((count, width))] + [block] * len(wholes)
         + [pl.BlockSpec((piece.shape[0], WIDE), lambda i: (0, i)) for piece in pieces],
-        out_specs=pl.BlockSpec((count, WIDE), lambda i: (0, i)),
-        out_shape=jax.ShapeDtypeStruct((count, hidden), BF16),
-        compiler_params=params(24),
+        out_specs=[block] * len(kinds),
+        out_shape=[jax.ShapeDtypeStruct((count, hidden), kind) for kind in kinds],
+        compiler_params=params(limit),
         cost_estimate=cost(1000, 1000),
-    )(feed, *pieces)
+    )(feed, *wholes, *pieces)
+
+
+def widen(feed, matrices):
+    return widen_call(widen_kernel, "widen", WIDEN_VMEM, (BF16, F32), feed, (), matrices)
+
+
+def finish(feed, wholes, pieces):
+    return widen_call(finish_kernel, "finish", FINISH_VMEM, (BF16,), feed, wholes, ([], pieces))[0]
 
 
 def narrow_kernel(block, hidden_hbm, *refs):
@@ -587,51 +613,55 @@
         decay_bias[None], conv_weight,
     )
     one = shifted(state, 1)
-    two = shifted(joined(state, one), 2)
+    both = joined(state, one)
+    two = shifted(both, 2)
     if two_by_two:
-        down_0, down_1 = down_weight[:, :half], down_weight[:, half:]
-        normed, gate_a, gate_b = tied((normed, gate_a, gate_b))
-        gate_c, down_b1 = x(gate_b), y(down_1)
+        mine, rest = (
+            lax.dynamic_slice_in_dim(down_weight, p * half, half, 1) for p in (parity, 1 - parity)
+        )
+        normed, gate_a, gate_b, both = tied((normed, gate_a, gate_b, both))
+        gate_c = x(gate_b)
     raised, query_edges, opening = query(
         prompts, normed, rim, attention_gain[None], project_weight, output_gate, conv_weight, sums,
     )
     if two_by_two:
-        one, two, raised, up_a, up_b, down_0 = tied((one, two, raised, up_a, up_b, down_0))
-        up_c, far_a, far_b, down_a0 = y(up_a), z(up_a), z(up_b), x(down_0)
-        down_c0 = y(down_a0)
+        raised, up_a, up_b = tied((raised, up_a, up_b))
+        up_c, far_a = y(up_a), z(up_a)
     states, *gated = pages(
         prompts, raised, lowered, weighted, value, ends, opening, head_gain[None], one, two,
     )
     others = [swapped(part, "hid", 1) for part in gated]
     if two_by_two:
-        others, up_c, gate_c, far_a, down_b1 = tied((others, up_c, gate_c, far_a, down_b1))
-        far_c = y(far_a)
+        far_b, down_b_rest, down_a = z(up_b), y(rest), x(mine)
+        others, far_a, up_c = tied((others, far_a, up_c))
+        far_c = z(up_c)
     residual, feed = mix(hid_index, tokens, gated, others, output_weight, other_output, mixer_gain[None])
 
     if two_by_two:
-        feed, down_0, down_1 = tied((feed, down_0, down_1))
-        down_b0, down_a1 = y(down_0), x(down_1)
-        feed, far_b, far_c, down_b1 = tied((feed, far_b, far_c, down_b1))
-        down_c1 = x(down_b1)
-        at = lambda flip, more=0: lambda: (lax.axis_index("req") ^ flip) * depth + more
+        feed, mine = tied((feed, mine))
+        down_b = y(mine)
+        at = lambda flip: lambda: (lax.axis_index("req") ^ flip) * depth
         own = lambda flip: lambda: at(flip)() + lax.rem(lax.axis_index("seq"), 2) * half
         far = lambda flip: lambda: at(flip)() + (1 - lax.rem(lax.axis_index("seq"), 2)) * half
         gate_list = [(gate_weight, at(0)), (gate_a, at(1)), (gate_b, at(2)), (gate_c, at(3))]
         up_list = [
-            (up_weight, at(0)), (up_a, own(1)), (far_a, far(1)), (up_b, own(2)), (far_b, far(2)),
-            (up_c, own(3)), (far_c, far(3)),
+            (up_weight, at(0)), (up_a, own(1)), (far_a, far(1)), (up_b, own(2)), (up_c, own(3)),
         ]
+        sums = widen(feed, (gate_list, up_list))
+        sums, down_b_rest, down_a = tied((sums, down_b_rest, down_a))
+        down_c_rest, down_c, down_a_far = x(down_b_rest), y(down_a), z(down_a)
+        hidden = finish(feed, sums, [(far_b, far(2)), (far_c, far(3))])
         down_lists = [
-            [(down_weight, at(0)), (down_a0, at(1)), (down_b1, at(2, half)), (down_b0, at(2))],
-            [(down_a1, at(1, half)), (down_c0, at(3)), (down_c1, at(3, half))],
+            [(down_weight, at(0)), (down_a, own(1)), (down_b_rest, far(2)), (down_b, own(2))],
+            [(down_c_rest, far(3)), (down_c, own(3)), (down_a_far, far(1))],
         ]
     else:
         first = lambda: 0
         gate_list = [(lax.all_gather(gate_weight, "req", axis=0, tiled=True), first)]
         up_list = [(lax.all_gather(up_weight, "req", axis=0, tiled=True), first)]
         down_lists = [[(lax.all_gather(down_weight, "req", axis=1, tiled=True), first)]]
-
-    hidden = widen(feed, (gate_list, up_list))
+        hidden = finish(feed, widen(feed, (gate_list, up_list)), [])
+
     groups = []
     for pieces in down_lists:
         theirs, mine = narrow(hidden, [piece for piece, _ in pieces], ROWS)

time: 147 us -> 135 us (0.918)
  the two profiles are of different devices: /device:TPU:0 before, /device:TPU:27 now
where the time goes in v7:
time: 135 us; the launch traced here: 134 us
  Pallas kernels  69.1 us (51%)
  waiting for transfers between devices  27.9 us (21%)
  starting transfers between devices  21.8 us (16%)
  local copies, waits for them, and re-layouts  14.5 us (11%)
    pallas_call x2, Pallas kernels, widen_call(): pl.pallas_call(functools.partial(kernel, places), name=name, grid=(pl.cdi...  20.9 us
    ppermute x20, starting transfers between devices, swapped(): return lax.ppermute(value, axis, [(i, i ^ flip) for i in range(count)])  17.7 us
    ppermute x3, waiting for transfers between devices, shifted(): lax.ppermute(value, 'seq', [(i, i + steps) for i in range(count - steps)])  14.9 us
    pallas_call x1, Pallas kernels, front(): pl.pallas_call(front_kernel, name='front', grid=(count // tile,), in_spec...  14.8 us
    ppermute x20, waiting for transfers between devices, swapped(): return lax.ppermute(value, axis, [(i, i ^ flip) for i in range(count)])  12.9 us
    unnamed x35, local copies, waits for them, and re-layouts  11.6 us
    pallas_call x2, Pallas kernels, narrow(): pl.pallas_call(functools.partial(narrow_kernel, block), name='narrow', in...  10.2 us
    pallas_call x1, Pallas kernels, mix(): pl.pallas_call(lambda s, *refs: mix_kernel(*refs), name='mix', grid_spec=...  8.86 us
  transfers between devices with their start and end apart: 23, of which 8 were waited for; matrix products, arithmetic and copies ran while one was open for 3% of the time, Pallas kernels for 50%

profile of v7, /device:TPU:27, one launch (start us, length us, event | category | flops | bytes accessed | tf_op | source)
XLA Modules:
  0.0 134.2 jit_solution(13680103240858589254)
XLA Ops:
  5.7 3.4 %collective-permute-done.rim_ref = bf16[16,2048]{1,0:T(8,128)(2,1)S(1)} collective-permute-done((bf16[16,2048]{1,0:T(8,128)(2,1)S(1)}, bf16[16,2048]{1,0:T(8,128)(2,1)S(1)}, u32[]{:S(2)}, u32[]{:S(2)}) %collective-permute-start) | collective-permute-done | bytes 65568 | tf_op jit(solution)/shard_map/ppermute | solution.py:576
  9.1 1.3 copy-done.5
  14.7 14.8 %front.1 = (bf16[1024,2048]{1,0:T(8,128)(2,1)S(1)}, f32[1024,256]{1,0:T(8,128)S(1)}, bf16[1024,256]{1,0:T(8,128)(2,1)S(1)}, bf16[1024,256]{1,0:T(8,128)(2,1)S(1)...) custom-call(s32[1,16]{1,0:T(1,128)S(1)} %copy-done.11, ...), custom_call_target="tpu_custom_call" | custom-call | flops 1000 | bytes 1000 | tf_op jit(solution)/shard_map/front/pallas_call | solution.py:210
  29.5 1.4 %collective-permute-start.4 = (bf16[272,512]{1,0:T(8,128)(2,1)S(1)}, bf16[272,512]{1,0:T(8,128)(2,1)S(1)}, u32[]{:S(2)}, u32[]{:S(2)}) collective-permute-start(bf16[272,512]{1,0:T(8,128)(2,1)S(1)} %get-tuple-element.45.later_ref), channel_id=1, source_target_pairs={{0,2},{2,4},{4,6},{1,3},{3,5},{5,7},{8,10},{10,12},{12,14},{9,11},... | collective-permute-start | bytes 835592 | tf_op jit(solution)/shard_map/ppermute | solution.py:576
  32.5 5.9 %collective-permute-done.4.earlier_ref.one_ref = bf16[272,512]{1,0:T(8,128)(2,1)S(1)} collective-permute-done((bf16[272,512]{1,0:T(8,128)(2,1)S(1)}, bf16[272,512]{1,0:T(8,128)(2,1)S(1)}, u32[]{:S(2)}, u32[]{:S(2)}) %collective-permute-start.4) | collective-permute-done | bytes 278560 | tf_op jit(solution)/shard_map/ppermute | solution.py:576
  39.9 1.5 %collective-permute-start.7 = (bf16[272,512]{1,0:T(8,128)(2,1)S(1)}, bf16[272,512]{1,0:T(8,128)(2,1)S(1)}, u32[]{:S(2)}, u32[]{:S(2)}) collective-permute-start(bf16[272,512]{1,0:T(8,128)(2,1)S(1)} %joined.1), channel_id=1, source_target_pairs={{0,4},{2,6},{1,5},{3,7},{8,12},{10,14},{9,13},{11,15},{16,20},{18,... | collective-permute-start | bytes 835592 | tf_op jit(solution)/shard_map/ppermute | solution.py:576
  41.4 5.6 %query.1 = (bf16[1024,256]{1,0:T(8,128)(2,1)S(1)}, bf16[16,3,256]{2,1,0:T(4,128)(2,1)S(1)}, bf16[1024,512]{1,0:T(8,128)(2,1)S(1)}) custom-call(s32[1,16]{1,0:T(1,128)S(1)} %copy-done.11, s32[1,16]{1,0:T(1,128)S(1)} %copy-done.12, bf16[1024,2048]{1,0:T(8,128)(2,1)S(1)} %get-tuple-element.46.normed_ref, bf16[16,2048]{1,0:T(8,128)(2,1)S(1)} %collective-permute-done.rim_ref, ...), custom_call_target="tpu_custom_call" | custom-call | flops 3221225472 | bytes 4194304 | tf_op jit(solution)/shard_map/query/pallas_call | solution.py:275
  47.0 3.3 %collective-permute-done.5.refs_5_ = bf16[256,1408]{1,0:T(8,128)(2,1)} collective-permute-done((bf16[256,1408]{1,0:T(8,128)(2,1)S(1)}, bf16[256,1408]{1,0:T(8,128)(2,1)}, u32[]{:S(2)}, u32[]{:S(2)}) %collective-permute-start.5) | collective-permute-done | bytes 720928 | tf_op jit(solution)/shard_map/ppermute | solution.py:581
  51.6 5.6 %collective-permute-done.7.two_ref = bf16[272,512]{1,0:T(8,128)(2,1)S(1)} collective-permute-done((bf16[272,512]{1,0:T(8,128)(2,1)S(1)}, bf16[272,512]{1,0:T(8,128)(2,1)S(1)}, u32[]{:S(2)}, u32[]{:S(2)}) %collective-permute-start.7) | collective-permute-done | bytes 278560 | tf_op jit(solution)/shard_map/ppermute | solution.py:576
  57.2 6.7 %pages.1 = (bf16[16,1,256,512]{3,2,1,0:T(8,128)(2,1)}, bf16[512,512]{1,0:T(8,128)(2,1)S(1)}, bf16[512,512]{1,0:T(8,128)(2,1)}) custom-call(s32[1,16]{1,0:T(1,128)S(1)} %copy-done.11, s32[1,16]{1,0:T(1,128)S(1)} %copy-done.12, bf16[1024,256]{1,0:T(8,128)(2,1)S(1)} %get-tuple-element.49.raised_ref, bf16[1024,256]{1,0:T(8,128)(2,1)S(1)} %get-tuple-element.50.lowered_ref, ...), custom_call_target="tpu_custom_call" | custom-call | flops 1000 | bytes 1000 | tf_op jit(solution)/shard_map/pages/pallas_call | solution.py:366
  65.8 6.9 %collective-permute-done.10.refs_6_ = bf16[256,1408]{1,0:T(8,128)(2,1)} collective-permute-done((bf16[256,1408]{1,0:T(8,128)(2,1)}, bf16[256,1408]{1,0:T(8,128)(2,1)}, u32[]{:S(2)}, u32[]{:S(2)}) %collective-permute-start.10) | collective-permute-done | bytes 720928 | tf_op jit(solution)/shard_map/ppermute | solution.py:581
  73.3 2.2 %copy-done.1 = bf16[1024,2048]{1,0:T(8,128)(2,1)S(1)} copy-done((bf16[1024,2048]{1,0:T(8,128)(2,1)S(1)}, bf16[1024,2048]{1,0:T(8,128)(2,1)}, u32[]{:S(2)}) %copy-start.1) | copy-done | bytes 4194328
  75.4 1.6 %copy-done.4 = bf16[512,2048]{1,0:T(8,128)(2,1)S(1)} copy-done((bf16[512,2048]{1,0:T(8,128)(2,1)S(1)}, bf16[512,2048]{1,0:T(8,128)(2,1)}, u32[]{:S(2)}) %copy-start.4) | copy-done | bytes 2097176
  77.0 1.6 %copy-done.6 = bf16[512,2048]{1,0:T(8,128)(2,1)S(1)} copy-done((bf16[512,2048]{1,0:T(8,128)(2,1)S(1)}, bf16[512,2048]{1,0:T(8,128)(2,1)}, u32[]{:S(2)}) %copy-start.6) | copy-done | bytes 2097176
  78.6 8.9 %mix.1 = (bf16[512,2048]{1,0:T(8,128)(2,1)S(1)}, bf16[1024,2048]{1,0:T(8,128)(2,1)S(1)}) custom-call(s32[1]{0:T(128)} %bitcast.s, bf16[1024,2048]{1,0:T(8,128)(2,1)S(1)} %copy-done.1, bf16[512,512]{1,0:T(8,128)(2,1)S(1)} %get-tuple-element.55.refs_1_, bf16[512,512]{1,0:T(8,128)(2,1)} %get-tuple-element.56.refs_2_, ...), custom_call_target="tpu_custom_call" | custom-call | flops 1000 | bytes 1000 | tf_op jit(solution)/shard_map/mix/pallas_call | solution.py:422
  87.5 1.5 %collective-permute-start.16 = (bf16[256,1408]{1,0:T(8,128)(2,1)}, bf16[256,1408]{1,0:T(8,128)(2,1)S(1)}, u32[]{:S(2)}, u32[]{:S(2)}) collective-permute-start(bf16[256,1408]{1,0:T(8,128)(2,1)} %collective-permute-done.11.refs_8_), channel_id=1, source_target_pairs={{0,2},{2,0},{4,6},{6,4},{1,3},{3,1},{5,7},{7,5},{8,10},{10,8},{12,... | collective-permute-start | bytes 2162696 | tf_op jit(solution)/shard_map/ppermute | solution.py:581
  90.2 15.5 %widen.1 = (bf16[1024,1408]{1,0:T(8,128)(2,1)S(1)}, f32[1024,1408]{1,0:T(8,128)S(1)}) custom-call(bf16[1024,2048]{1,0:T(8,128)(2,1)S(1)} %get-tuple-element.63.feed_ref, bf16[512,1408]{1,0:T(8,128)(2,1)S(1)} %copy-done.7, bf16[512,1408]{1,0:T(8,128)(2,1)} %collective-permute-done.2.refs_1_, bf16[512,1408]{1,0:T(8,128)(2,1)} %collective-permute-done.3.refs_2_, ...), custom_call_target="tpu_custom_call" | custom-call | flops 1000 | bytes 1000 | tf_op jit(solution)/shard_map/widen/pallas_call | solution.py:474
  105.8 1.3 collective-permute-start.19
  107.4 5.4 %finish.1.hidden_hbm = bf16[1024,1408]{1,0:T(8,128)(2,1)S(1)} custom-call(bf16[1024,2048]{1,0:T(8,128)(2,1)S(1)} %get-tuple-element.63.feed_ref, bf16[1024,1408]{1,0:T(8,128)(2,1)S(1)} %get-tuple-element.71.gate_ref, f32[1024,1408]{1,0:T(8,128)S(1)} %get-tuple-element.72.up_ref, bf16[256,1408]{1,0:T(8,128)(2,1)} %collective-permute-done.15.refs_0_, ...), custom_call_target="tpu_custom_call" | custom-call | flops 1000 | bytes 1000 | tf_op jit(solution)/shard_map/finish/pallas_call | solution.py:474
  112.8 5.9 %narrow.2 = (bf16[512,1280]{1,0:T(8,128)(2,1)S(1)}, bf16[512,1280]{1,0:T(8,128)(2,1)S(1)}) custom-call(bf16[1024,1408]{1,0:T(8,128)(2,1)S(1)} %finish.1.hidden_hbm, bf16[1408,512]{1,0:T(8,128)(2,1)S(1)} %copy-done.2, bf16[1408,256]{1,0:T(8,128)(2,1)} %collective-permute-done.14.refs_1_, bf16[1408,256]{1,0:T(8,128)(2,1)} %collective-permute-done.13.refs_2_, ...), custom_call_target="tpu_custom_call" | custom-call | flops 1000 | bytes 1000 | tf_op jit(solution)/shard_map/narrow/pallas_call | solution.py:533
  118.7 2.5 %collective-permute-start.18 = (bf16[512,1280]{1,0:T(8,128)(2,1)S(1)}, bf16[512,1280]{1,0:T(8,128)(2,1)S(1)}, u32[]{:S(2)}, u32[]{:S(2)}) collective-permute-start(bf16[512,1280]{1,0:T(8,128)(2,1)S(1)} %get-tuple-element.77), channel_id=1, source_target_pairs={{0,1},{1,0},{2,3},{3,2},{4,5},{5,4},{6,7},{7,6},{8,9},{9,8},{10,11... | collective-permute-start | bytes 3932168 | tf_op jit(solution)/shard_map/ppermute | solution.py:581
  122.7 4.4 %narrow.3 = (bf16[512,768]{1,0:T(8,128)(2,1)S(1)}, bf16[512,768]{1,0:T(8,128)(2,1)S(1)}) custom-call(bf16[1024,1408]{1,0:T(8,128)(2,1)S(1)} %finish.1.hidden_hbm, bf16[1408,256]{1,0:T(8,128)(2,1)S(1)} %collective-permute-done.19.refs_0_, bf16[1408,256]{1,0:T(8,128)(2,1)S(1)} %collective-permute-done.20.refs_1_, ...), custom_call_target="tpu_custom_call" | custom-call | flops 1000 | bytes 1000 | tf_op jit(solution)/shard_map/narrow/pallas_call | solution.py:533
  127.1 3.4 %collective-permute-start.22 = (bf16[512,768]{1,0:T(8,128)(2,1)S(1)}, bf16[512,768]{1,0:T(8,128)(2,1)S(1)}, u32[]{:S(2)}, u32[]{:S(2)}) collective-permute-start(bf16[512,768]{1,0:T(8,128)(2,1)S(1)} %get-tuple-element.79), channel_id=1, source_target_pairs={{0,1},{1,0},{2,3},{3,2},{4,5},{5,4},{6,7},{7,6},{8,9},{9,8},{10,11... | collective-permute-start | bytes 2359304 | tf_op jit(solution)/shard_map/ppermute | solution.py:581
  132.4 1.8 %close.1 = bf16[512,2048]{1,0:T(8,128)(2,1)} custom-call(bf16[512,2048]{1,0:T(8,128)(2,1)S(1)} %get-tuple-element.61.residual_ref, bf16[512,1280]{1,0:T(8,128)(2,1)S(1)} %get-tuple-element.76.refs_0_, bf16[512,1280]{1,0:T(8,128)(2,1)S(1)} %collective-permute-done.18.refs_1_, bf16[512,768]{1,0:T(8,128)(2,1)S(1)} %get-tuple-element.78.refs_2_, ...), custom_call_target="tpu_custom_call" | custom-call | flops 1000 | bytes 1000 | tf_op jit(solution)/shard_map/close/pallas_call | solution.py:562
  (74 shorter events, 21.1 us)
Async XLA Ops:
  0.6 8.5 %collective-permute-start.1 = (bf16[512,2048]{1,0:T(8,128)(2,1)}, bf16[512,2048]{1,0:T(8,128)(2,1)S(1)}, u32[]{:S(2)}, u32[]{:S(2)}) collective-permute-start(bf16[512,2048]{1,0:T(8,128)(2,1)} %refs_5_.1), channel_id=1, source_target_pairs={{0,1},{1,0},{2,3},{3,2},{4,5},{5,4},{6,7},{7,6},{8,9},{9,8},{10,11... | collective-permute-start | bytes 6291464 | tf_op jit(solution)/shard_map/ppermute | solution.py:581
  1.4 37.3 %collective-permute-start.2 = (bf16[512,1408]{1,0:T(8,128)(2,1)}, bf16[512,1408]{1,0:T(8,128)(2,1)}, u32[]{:S(2)}, u32[]{:S(2)}) collective-permute-start(bf16[512,1408]{1,0:T(8,128)(2,1)} %refs_0_.4), channel_id=1, source_target_pairs={{0,8},{8,0},{16,24},{24,16},{1,9},{9,1},{17,25},{25,17},{2,10},{10... | collective-permute-start | bytes 4325384 | tf_op jit(solution)/shard_map/ppermute | solution.py:581
  1.6 37.0 %collective-permute-start.3 = (bf16[512,1408]{1,0:T(8,128)(2,1)}, bf16[512,1408]{1,0:T(8,128)(2,1)}, u32[]{:S(2)}, u32[]{:S(2)}) collective-permute-start(bf16[512,1408]{1,0:T(8,128)(2,1)} %refs_0_.4), channel_id=1, source_target_pairs={{0,16},{8,24},{16,0},{24,8},{1,17},{9,25},{17,1},{25,9},{2,18},{10... | collective-permute-start | bytes 4325384 | tf_op jit(solution)/shard_map/ppermute | solution.py:581
  3.7 5.4 %collective-permute-start = (bf16[16,2048]{1,0:T(8,128)(2,1)S(1)}, bf16[16,2048]{1,0:T(8,128)(2,1)S(1)}, u32[]{:S(2)}, u32[]{:S(2)}) collective-permute-start(bf16[16,2048]{1,0:T(8,128)(2,1)S(1)} %slice.3), channel_id=1, source_target_pairs={{0,2},{2,4},{4,6},{1,3},{3,5},{5,7},{8,10},{10,12},{12,14},{9,11},... | collective-permute-start | bytes 196616 | tf_op jit(solution)/shard_map/ppermute | solution.py:576
  14.7 26.7 %copy-start = (bf16[2048,1024]{1,0:T(8,128)(2,1)S(1)}, bf16[2048,1024]{1,0:T(8,128)(2,1)}, u32[]{:S(2)}) copy-start(bf16[2048,1024]{1,0:T(8,128)(2,1)} %query_ref.1) | copy-start | bytes 12582916
  29.5 8.9 %collective-permute-start.4 = (bf16[272,512]{1,0:T(8,128)(2,1)S(1)}, bf16[272,512]{1,0:T(8,128)(2,1)S(1)}, u32[]{:S(2)}, u32[]{:S(2)}) collective-permute-start(bf16[272,512]{1,0:T(8,128)(2,1)S(1)} %get-tuple-element.45.later_ref), channel_id=1, source_target_pairs={{0,2},{2,4},{4,6},{1,3},{3,5},{5,7},{8,10},{10,12},{12,14},{9,11},... | collective-permute-start | bytes 835592 | tf_op jit(solution)/shard_map/ppermute | solution.py:576
  31.0 19.3 %collective-permute-start.5 = (bf16[256,1408]{1,0:T(8,128)(2,1)S(1)}, bf16[256,1408]{1,0:T(8,128)(2,1)}, u32[]{:S(2)}, u32[]{:S(2)}) collective-permute-start(bf16[256,1408]{1,0:T(8,128)(2,1)S(1)} %constant_dynamic-slice_fusion.2), channel_id=1, source_target_pairs={{0,8},{8,0},{16,24},{24,16},{1,9},{9,1},{17,25},{25,17},{2,10},{10... | collective-permute-start | bytes 2162696 | tf_op jit(solution)/shard_map/ppermute | solution.py:581
  32.3 18.0 %collective-permute-start.6 = (bf16[256,1408]{1,0:T(8,128)(2,1)S(1)}, bf16[256,1408]{1,0:T(8,128)(2,1)}, u32[]{:S(2)}, u32[]{:S(2)}) collective-permute-start(bf16[256,1408]{1,0:T(8,128)(2,1)S(1)} %constant_dynamic-slice_fusion.2), channel_id=1, source_target_pairs={{0,16},{8,24},{16,0},{24,8},{1,17},{9,25},{17,1},{25,9},{2,18},{10... | collective-permute-start | bytes 2162696 | tf_op jit(solution)/shard_map/ppermute | solution.py:581
  38.7 50.3 %collective-permute-start.12 = (bf16[512,1408]{1,0:T(8,128)(2,1)}, bf16[512,1408]{1,0:T(8,128)(2,1)}, u32[]{:S(2)}, u32[]{:S(2)}) collective-permute-start(bf16[512,1408]{1,0:T(8,128)(2,1)} %collective-permute-done.3.refs_2_), channel_id=1, source_target_pairs={{0,8},{8,0},{16,24},{24,16},{1,9},{9,1},{17,25},{25,17},{2,10},{10... | collective-permute-start | bytes 4325384 | tf_op jit(solution)/shard_map/ppermute | solution.py:581
  39.9 17.3 %collective-permute-start.7 = (bf16[272,512]{1,0:T(8,128)(2,1)S(1)}, bf16[272,512]{1,0:T(8,128)(2,1)S(1)}, u32[]{:S(2)}, u32[]{:S(2)}) collective-permute-start(bf16[272,512]{1,0:T(8,128)(2,1)S(1)} %joined.1), channel_id=1, source_target_pairs={{0,4},{2,6},{1,5},{3,7},{8,12},{10,14},{9,13},{11,15},{16,20},{18,... | collective-permute-start | bytes 835592 | tf_op jit(solution)/shard_map/ppermute | solution.py:576
  50.3 22.4 %collective-permute-start.10 = (bf16[256,1408]{1,0:T(8,128)(2,1)}, bf16[256,1408]{1,0:T(8,128)(2,1)}, u32[]{:S(2)}, u32[]{:S(2)}) collective-permute-start(bf16[256,1408]{1,0:T(8,128)(2,1)} %collective-permute-done.5.refs_5_), channel_id=1, source_target_pairs={{0,2},{2,0},{4,6},{6,4},{1,3},{3,1},{5,7},{7,5},{8,10},{10,8},{12,... | collective-permute-start | bytes 2162696 | tf_op jit(solution)/shard_map/ppermute | solution.py:581
  50.3 22.6 %collective-permute-start.11 = (bf16[256,1408]{1,0:T(8,128)(2,1)}, bf16[256,1408]{1,0:T(8,128)(2,1)}, u32[]{:S(2)}, u32[]{:S(2)}) collective-permute-start(bf16[256,1408]{1,0:T(8,128)(2,1)} %collective-permute-done.5.refs_5_), channel_id=1, source_target_pairs={{0,16},{8,24},{16,0},{24,8},{1,17},{9,25},{17,1},{25,9},{2,18},{10... | collective-permute-start | bytes 2162696 | tf_op jit(solution)/shard_map/ppermute | solution.py:581
  63.9 9.3 %collective-permute-start.8 = (bf16[512,512]{1,0:T(8,128)(2,1)S(1)}, bf16[512,512]{1,0:T(8,128)(2,1)}, u32[]{:S(2)}, u32[]{:S(2)}) collective-permute-start(bf16[512,512]{1,0:T(8,128)(2,1)S(1)} %get-tuple-element.55.refs_1_), channel_id=1, source_target_pairs={{0,1},{1,0},{2,3},{3,2},{4,5},{5,4},{6,7},{7,6},{8,9},{9,8},{10,11... | collective-permute-start | bytes 1572872 | tf_op jit(solution)/shard_map/ppermute | solution.py:581
  64.5 8.8 %collective-permute-start.9 = (bf16[512,512]{1,0:T(8,128)(2,1)}, bf16[512,512]{1,0:T(8,128)(2,1)}, u32[]{:S(2)}, u32[]{:S(2)}) collective-permute-start(bf16[512,512]{1,0:T(8,128)(2,1)} %get-tuple-element.56.refs_2_), channel_id=1, source_target_pairs={{0,1},{1,0},{2,3},{3,2},{4,5},{5,4},{6,7},{7,6},{8,9},{9,8},{10,11... | collective-permute-start | bytes 1572872 | tf_op jit(solution)/shard_map/ppermute | solution.py:581
  72.7 33.0 %collective-permute-start.13 = (bf16[1408,256]{1,0:T(8,128)(2,1)}, bf16[1408,256]{1,0:T(8,128)(2,1)}, u32[]{:S(2)}, u32[]{:S(2)}) collective-permute-start(bf16[1408,256]{1,0:T(8,128)(2,1)} %get-tuple-element.86), channel_id=1, source_target_pairs={{0,16},{8,24},{16,0},{24,8},{1,17},{9,25},{17,1},{25,9},{2,18},{10... | collective-permute-start | bytes 2162696 | tf_op jit(solution)/shard_map/ppermute | solution.py:581
  72.9 32.8 %collective-permute-start.14 = (bf16[1408,256]{1,0:T(8,128)(2,1)}, bf16[1408,256]{1,0:T(8,128)(2,1)}, u32[]{:S(2)}, u32[]{:S(2)}) collective-permute-start(bf16[1408,256]{1,0:T(8,128)(2,1)} %get-tuple-element.75), channel_id=1, source_target_pairs={{0,8},{8,0},{16,24},{24,16},{1,9},{9,1},{17,25},{25,17},{2,10},{10... | collective-permute-start | bytes 2162696 | tf_op jit(solution)/shard_map/ppermute | solution.py:581
  73.2 34.1 %collective-permute-start.15 = (bf16[256,1408]{1,0:T(8,128)(2,1)}, bf16[256,1408]{1,0:T(8,128)(2,1)}, u32[]{:S(2)}, u32[]{:S(2)}) collective-permute-start(bf16[256,1408]{1,0:T(8,128)(2,1)} %collective-permute-done.6.refs_7_), channel_id=1, source_target_pairs={{0,2},{2,0},{4,6},{6,4},{1,3},{3,1},{5,7},{7,5},{8,10},{10,8},{12,... | collective-permute-start | bytes 2162696 | tf_op jit(solution)/shard_map/ppermute | solution.py:581
  87.5 19.9 %collective-permute-start.16 = (bf16[256,1408]{1,0:T(8,128)(2,1)}, bf16[256,1408]{1,0:T(8,128)(2,1)S(1)}, u32[]{:S(2)}, u32[]{:S(2)}) collective-permute-start(bf16[256,1408]{1,0:T(8,128)(2,1)} %collective-permute-done.11.refs_8_), channel_id=1, source_target_pairs={{0,2},{2,0},{4,6},{6,4},{1,3},{3,1},{5,7},{7,5},{8,10},{10,8},{12,... | collective-permute-start | bytes 2162696 | tf_op jit(solution)/shard_map/ppermute | solution.py:581
  89.0 23.8 %collective-permute-start.17 = (bf16[1408,256]{1,0:T(8,128)(2,1)}, bf16[1408,256]{1,0:T(8,128)(2,1)S(1)}, u32[]{:S(2)}, u32[]{:S(2)}) collective-permute-start(bf16[1408,256]{1,0:T(8,128)(2,1)} %get-tuple-element.75), channel_id=1, source_target_pairs={{0,16},{8,24},{16,0},{24,8},{1,17},{9,25},{17,1},{25,9},{2,18},{10... | collective-permute-start | bytes 2162696 | tf_op jit(solution)/shard_map/ppermute | solution.py:581
  105.8 16.0 %collective-permute-start.19 = (bf16[1408,256]{1,0:T(8,128)(2,1)}, bf16[1408,256]{1,0:T(8,128)(2,1)S(1)}, u32[]{:S(2)}, u32[]{:S(2)}) collective-permute-start(bf16[1408,256]{1,0:T(8,128)(2,1)} %collective-permute-done.13.refs_2_), channel_id=1, source_target_pairs={{0,8},{8,0},{16,24},{24,16},{1,9},{9,1},{17,25},{25,17},{2,10},{10... | collective-permute-start | bytes 2162696 | tf_op jit(solution)/shard_map/ppermute | solution.py:581
  107.1 15.7 %collective-permute-start.20 = (bf16[1408,256]{1,0:T(8,128)(2,1)}, bf16[1408,256]{1,0:T(8,128)(2,1)S(1)}, u32[]{:S(2)}, u32[]{:S(2)}) collective-permute-start(bf16[1408,256]{1,0:T(8,128)(2,1)} %collective-permute-done.14.refs_1_), channel_id=1, source_target_pairs={{0,16},{8,24},{16,0},{24,8},{1,17},{9,25},{17,1},{25,9},{2,18},{10... | collective-permute-start | bytes 2162696 | tf_op jit(solution)/shard_map/ppermute | solution.py:581
  107.3 15.4 %collective-permute-start.21 = (bf16[1408,256]{1,0:T(8,128)(2,1)}, bf16[1408,256]{1,0:T(8,128)(2,1)S(1)}, u32[]{:S(2)}, u32[]{:S(2)}) collective-permute-start(bf16[1408,256]{1,0:T(8,128)(2,1)} %collective-permute-done.14.refs_1_), channel_id=1, source_target_pairs={{0,2},{2,0},{4,6},{6,4},{1,3},{3,1},{5,7},{7,5},{8,10},{10,8},{12,... | collective-permute-start | bytes 2162696 | tf_op jit(solution)/shard_map/ppermute | solution.py:581
  118.7 12.6 %collective-permute-start.18 = (bf16[512,1280]{1,0:T(8,128)(2,1)S(1)}, bf16[512,1280]{1,0:T(8,128)(2,1)S(1)}, u32[]{:S(2)}, u32[]{:S(2)}) collective-permute-start(bf16[512,1280]{1,0:T(8,128)(2,1)S(1)} %get-tuple-element.77), channel_id=1, source_target_pairs={{0,1},{1,0},{2,3},{3,2},{4,5},{5,4},{6,7},{7,6},{8,9},{9,8},{10,11... | collective-permute-start | bytes 3932168 | tf_op jit(solution)/shard_map/ppermute | solution.py:581
  127.1 5.3 %collective-permute-start.22 = (bf16[512,768]{1,0:T(8,128)(2,1)S(1)}, bf16[512,768]{1,0:T(8,128)(2,1)S(1)}, u32[]{:S(2)}, u32[]{:S(2)}) collective-permute-start(bf16[512,768]{1,0:T(8,128)(2,1)S(1)} %get-tuple-element.79), channel_id=1, source_target_pairs={{0,1},{1,0},{2,3},{3,2},{4,5},{5,4},{6,7},{7,6},{8,9},{9,8},{10,11... | collective-permute-start | bytes 2359304 | tf_op jit(solution)/shard_map/ppermute | solution.py:581
  (16 other events, 77.5 us)

commit v8 on v7

--- a/solution.py
+++ b/solution.py
@@ -39,6 +39,10 @@
     return pl.BlockSpec(
         shape, lambda *_: (0,) * len(shape), pipeline_mode=pl.Buffered(1)
     )
+
+
+def held(array):
+    return pltpu.with_memory_space_constraint(array, pltpu.HBM)
 
 
 def whole_smem():
@@ -231,9 +235,9 @@
             pltpu.VMEM((tile + RIM, width), BF16), pltpu.VMEM((8, HK + HV), F32),
             pltpu.VMEM((HK, HV), F32), pltpu.VMEM((8, HK), F32), pltpu.VMEM((tile, HK), BF16),
         ],
-        compiler_params=params(44),
+        compiler_params=params(24),
         cost_estimate=cost(1000, 1000),
-    )(*prompts, tokens, rim, gain, project, project, project, down, up, bias, conv)
+    )(*prompts, held(tokens), rim, gain, *[held(project)] * 3, held(down), held(up), held(bias), held(conv))
 
 
 def query_kernel(
@@ -289,7 +293,7 @@
         scratch_shapes=[pltpu.VMEM((RIM, width), BF16), pltpu.VMEM((8, HK), F32)],
         compiler_params=params(20),
         cost_estimate=cost(2 * count * width * (HK + HV), 2 * count * width),
-    )(*prompts, normed, rim, gain, project, gate, conv, sums)
+    )(*prompts, normed, rim, gain, held(project), held(gate), held(conv), sums)
 
 
 def composed(later, earlier):
@@ -387,17 +391,46 @@
 
 
 def mix_kernel(
-    tokens_ref, low_ref, high_ref, other_low_ref, other_high_ref, own_weight_ref, other_weight_ref,
-    gain_ref, residual_ref, feed_ref, residual,
+    tokens_hbm, low_ref, high_ref, other_low_ref, other_high_ref, own_hbm, other_hbm, gain_ref,
+    residual_ref, feed_ref, tokens, own_weight, other_weight, residual, token_sems, weight_sems,
 ):
-    first = pl.program_id(0) < pl.num_programs(0) // 2
+    step = pl.program_id(0)
+    tile, width = feed_ref.shape
+    first = step < pl.num_programs(0) // 2
+
+    def token_copy(i):
+        rows = pl.ds(pl.multiple_of(i * tile, tile), tile)
+        return pltpu.make_async_copy(tokens_hbm.at[rows, :], tokens.at[rows, :], token_sems.at[i])
+
+    def weight_copies(i):
+        columns = pl.ds(i * WIDE, WIDE)
+        for j, (source, target) in enumerate(((own_hbm, own_weight), (other_hbm, other_weight))):
+            yield pltpu.make_async_copy(source.at[:, columns], target.at[:, columns], weight_sems.at[j, i])
+
+    @pl.when(step == 0)
+    def _():
+        for i in range(width // WIDE):
+            for copy in weight_copies(i):
+                copy.start()
+            if i == 0:
+                token_copy(0).start()
+        for i in range(1, tokens.shape[0] // tile):
+            token_copy(i).start()
+
+    token_copy(step).wait()
     own = jnp.where(first, low_ref[...], high_ref[...])
     other = jnp.where(first, other_low_ref[...], other_high_ref[...])
-    width = tokens_ref.shape[1]
-    for at in range(0, width, WIDE):
-        columns = pl.ds(at, WIDE)
-        mixed = dot(own, own_weight_ref[:, columns]) + dot(other, other_weight_ref[:, columns])
-        residual[:, columns] = (tokens_ref[:, columns].astype(F32) + mixed).astype(BF16)
+    rows = pl.ds(pl.multiple_of(step * tile, tile), tile)
+    for i in range(width // WIDE):
+        columns = pl.ds(i * WIDE, WIDE)
+
+        @pl.when(step == 0)
+        def _():
+            for copy in weight_copies(i):
+                copy.wait()
+
+        mixed = dot(own, own_weight[:, columns]) + dot(other, other_weight[:, columns])
+        residual[:, columns] = (tokens[rows, columns].astype(F32) + mixed).astype(BF16)
 
     @pl.when(first == (lax.axis_index("hid") == 0))
     def _():
@@ -418,6 +451,7 @@
         pl.BlockSpec((tile, HV), lambda i, s: (jnp.minimum(i, half - 1), 0)),
         pl.BlockSpec((tile, HV), lambda i, s: (jnp.maximum(i - half, 0), 0)),
     ]
+    in_hbm = pl.BlockSpec(memory_space=pltpu.HBM)
     mine = pl.BlockSpec((tile, width), lambda i, s: (jnp.clip(i - s[0] * half, 0, half - 1), 0))
     return pl.pallas_call(
         lambda s, *refs: mix_kernel(*refs),
@@ -425,16 +459,20 @@
         grid_spec=pltpu.PrefetchScalarGridSpec(
             num_scalar_prefetch=1,
             grid=(count // tile,),
-            in_specs=[rows, *halves, *halves, fixed((HV, width)), fixed((HV, width)), fixed((1, width))],
+            in_specs=[in_hbm, *halves, *halves, in_hbm, in_hbm, fixed((1, width))],
             out_specs=[mine, rows],
-            scratch_shapes=[pltpu.VMEM((tile, width), BF16)],
+            scratch_shapes=[
+                pltpu.VMEM((count, width), BF16), pltpu.VMEM((HV, width), BF16),
+                pltpu.VMEM((HV, width), BF16), pltpu.VMEM((tile, width), BF16),
+                pltpu.SemaphoreType.DMA((count // tile,)), pltpu.SemaphoreType.DMA((2, width // WIDE)),
+            ],
         ),
         out_shape=[
             jax.ShapeDtypeStruct((count // 2, width), BF16), jax.ShapeDtypeStruct((count, width), BF16),
         ],
-        compiler_params=params(20),
+        compiler_params=params(24),
         cost_estimate=cost(1000, 1000),
-    )(hid_index, tokens, *own, *others, own_weight, other_weight, gain)
+    )(hid_index, held(tokens), *own, *others, held(own_weight), other_weight, gain)
 
 
 def widen_sums(places, pieces, feed_ref, rows):
@@ -643,16 +681,16 @@
         at = lambda flip: lambda: (lax.axis_index("req") ^ flip) * depth
         own = lambda flip: lambda: at(flip)() + lax.rem(lax.axis_index("seq"), 2) * half
         far = lambda flip: lambda: at(flip)() + (1 - lax.rem(lax.axis_index("seq"), 2)) * half
-        gate_list = [(gate_weight, at(0)), (gate_a, at(1)), (gate_b, at(2)), (gate_c, at(3))]
+        gate_list = [(held(gate_weight), at(0)), (gate_a, at(1)), (gate_b, at(2)), (gate_c, at(3))]
         up_list = [
-            (up_weight, at(0)), (up_a, own(1)), (far_a, far(1)), (up_b, own(2)), (up_c, own(3)),
+            (held(up_weight), at(0)), (up_a, own(1)), (far_a, far(1)), (up_b, own(2)), (up_c, own(3)),
         ]
         sums = widen(feed, (gate_list, up_list))
         sums, down_b_rest, down_a = tied((sums, down_b_rest, down_a))
         down_c_rest, down_c, down_a_far = x(down_b_rest), y(down_a), z(down_a)
         hidden = finish(feed, sums, [(far_b, far(2)), (far_c, far(3))])
         down_lists = [
-            [(down_weight, at(0)), (down_a, own(1)), (down_b_rest, far(2)), (down_b, own(2))],
+            [(held(down_weight), at(0)), (down_a, own(1)), (down_b_rest, far(2)), (down_b, own(2))],
             [(down_c_rest, far(3)), (down_c, own(3)), (down_a_far, far(1))],
         ]
     else:

time: 135 us -> 137 us (1.015)
  the two profiles are of different devices: /device:TPU:27 before, /device:TPU:0 now
where the time goes in v8:
time: 137 us; the launch traced here: 136 us
  Pallas kernels  81.7 us (60%)
  starting transfers between devices  33.4 us (24%)
  waiting for transfers between devices  13.5 us (10%)
  local copies, waits for them, and re-layouts  6.8 us (5%)
    pallas_call x2, Pallas kernels, widen_call(): pl.pallas_call(functools.partial(kernel, places), name=name, grid=(pl.cdi...  20.8 us
    ppermute x20, starting transfers between devices, swapped(): return lax.ppermute(value, axis, [(i, i ^ flip) for i in range(count)])  19.3 us
    pallas_call x1, Pallas kernels, mix(): pl.pallas_call(lambda s, *refs: mix_kernel(*refs), name='mix', grid_spec=...  19.1 us
    pallas_call x1, Pallas kernels, front(): pl.pallas_call(front_kernel, name='front', grid=(count // tile,), in_spec...  14.9 us
    ppermute x3, starting transfers between devices, shifted(): lax.ppermute(value, 'seq', [(i, i + steps) for i in range(count - steps)])  14.1 us
    pallas_call x2, Pallas kernels, narrow(): pl.pallas_call(functools.partial(narrow_kernel, block), name='narrow', in...  11 us
    ppermute x20, waiting for transfers between devices, swapped(): return lax.ppermute(value, axis, [(i, i ^ flip) for i in range(count)])  8.7 us
    pallas_call x1, Pallas kernels, query(): pl.pallas_call(query_kernel, name='query', grid=(count // tile,), in_spec...  7 us
  transfers between devices with their start and end apart: 23, of which 9 were waited for; matrix products, arithmetic and copies ran while one was open for 4% of the time, Pallas kernels for 59%

profile of v8, /device:TPU:0, one launch (start us, length us, event | category | flops | bytes accessed | tf_op | source)
XLA Modules:
  0.0 136.3 jit_solution(11825723927538218582)
XLA Ops:
  1.1 2.6 %collective-permute-start.2 = (bf16[512,1408]{1,0:T(8,128)(2,1)}, bf16[512,1408]{1,0:T(8,128)(2,1)S(1)}, u32[]{:S(2)}, u32[]{:S(2)}) collective-permute-start(bf16[512,1408]{1,0:T(8,128)(2,1)} %refs_0_.4), channel_id=1, source_target_pairs={{0,8},{8,0},{16,24},{24,16},{1,9},{9,1},{17,25},{25,17},{2,10},{10... | collective-permute-start | bytes 4325384 | tf_op jit(solution)/shard_map/ppermute | solution.py:619
  3.7 1.5 %collective-permute-start.3 = (bf16[512,1408]{1,0:T(8,128)(2,1)}, bf16[512,1408]{1,0:T(8,128)(2,1)}, u32[]{:S(2)}, u32[]{:S(2)}) collective-permute-start(bf16[512,1408]{1,0:T(8,128)(2,1)} %refs_0_.4), channel_id=1, source_target_pairs={{0,16},{8,24},{16,0},{24,8},{1,17},{9,25},{17,1},{25,9},{2,18},{10... | collective-permute-start | bytes 4325384 | tf_op jit(solution)/shard_map/ppermute | solution.py:619
  5.2 1.5 %slice.3 = bf16[16,2048]{1,0:T(8,128)(2,1)} slice(bf16[1024,2048]{1,0:T(8,128)(2,1)} %refs_0_.3), slice={[1008:1024], [0:2048]} | slice | bytes 131072 | tf_op jit(solution)/shard_map/slice | solution.py:646
  6.7 4.1 %collective-permute-start = (bf16[16,2048]{1,0:T(8,128)(2,1)}, bf16[16,2048]{1,0:T(8,128)(2,1)}, u32[]{:S(2)}, u32[]{:S(2)}) collective-permute-start(bf16[16,2048]{1,0:T(8,128)(2,1)} %slice.3), channel_id=1, source_target_pairs={{0,2},{2,4},{4,6},{1,3},{3,5},{5,7},{8,10},{10,12},{12,14},{9,11},... | collective-permute-start | bytes 196616 | tf_op jit(solution)/shard_map/ppermute | solution.py:614
  13.7 14.9 %front.1 = (bf16[1024,2048]{1,0:T(8,128)(2,1)S(1)}, f32[1024,256]{1,0:T(8,128)S(1)}, bf16[1024,256]{1,0:T(8,128)(2,1)S(1)}, bf16[1024,256]{1,0:T(8,128)(2,1)S(1)...) custom-call(s32[1,16]{1,0:T(1,128)S(1)} %copy-done.4, ...), custom_call_target="tpu_custom_call" | custom-call | flops 1000 | bytes 1000 | tf_op jit(solution)/shard_map/front/pallas_call | solution.py:214
  28.6 4.4 %collective-permute-start.4 = (bf16[272,512]{1,0:T(8,128)(2,1)S(1)}, bf16[272,512]{1,0:T(8,128)(2,1)S(1)}, u32[]{:S(2)}, u32[]{:S(2)}) collective-permute-start(bf16[272,512]{1,0:T(8,128)(2,1)S(1)} %get-tuple-element.45.later_ref), channel_id=1, source_target_pairs={{0,2},{2,4},{4,6},{1,3},{3,5},{5,7},{8,10},{10,12},{12,14},{9,11},... | collective-permute-start | bytes 835592 | tf_op jit(solution)/shard_map/ppermute | solution.py:614
  34.3 3.9 %collective-permute-done.4.earlier_ref.one_ref = bf16[272,512]{1,0:T(8,128)(2,1)S(1)} collective-permute-done((bf16[272,512]{1,0:T(8,128)(2,1)S(1)}, bf16[272,512]{1,0:T(8,128)(2,1)S(1)}, u32[]{:S(2)}, u32[]{:S(2)}) %collective-permute-start.4) | collective-permute-done | bytes 278560 | tf_op jit(solution)/shard_map/ppermute | solution.py:614
  39.0 5.6 %collective-permute-start.7 = (bf16[272,512]{1,0:T(8,128)(2,1)S(1)}, bf16[272,512]{1,0:T(8,128)(2,1)S(1)}, u32[]{:S(2)}, u32[]{:S(2)}) collective-permute-start(bf16[272,512]{1,0:T(8,128)(2,1)S(1)} %joined.1), channel_id=1, source_target_pairs={{0,4},{2,6},{1,5},{3,7},{8,12},{10,14},{9,13},{11,15},{16,20},{18,... | collective-permute-start | bytes 835592 | tf_op jit(solution)/shard_map/ppermute | solution.py:614
  44.6 7.0 %query.1 = (bf16[1024,256]{1,0:T(8,128)(2,1)S(1)}, bf16[16,3,256]{2,1,0:T(4,128)(2,1)S(1)}, bf16[1024,512]{1,0:T(8,128)(2,1)S(1)}) custom-call(s32[1,16]{1,0:T(1,128)S(1)} %copy-done.5, s32[1,16]{1,0:T(1,128)S(1)} %copy-done.7, bf16[1024,2048]{1,0:T(8,128)(2,1)S(1)} %get-tuple-element.46.normed_ref, bf16[16,2048]{1,0:T(8,128)(2,1)} %collective-permute-done.rim_ref, ...), custom_call_target="tpu_custom_call" | custom-call | flops 3221225472 | bytes 4194304 | tf_op jit(solution)/shard_map/query/pallas_call | solution.py:279
  53.1 1.6 %collective-permute-start.10 = (bf16[256,1408]{1,0:T(8,128)(2,1)}, bf16[256,1408]{1,0:T(8,128)(2,1)}, u32[]{:S(2)}, u32[]{:S(2)}) collective-permute-start(bf16[256,1408]{1,0:T(8,128)(2,1)} %collective-permute-done.5.refs_5_), channel_id=1, source_target_pairs={{0,2},{2,0},{4,6},{6,4},{1,3},{3,1},{5,7},{7,5},{8,10},{10,8},{12,... | collective-permute-start | bytes 2162696 | tf_op jit(solution)/shard_map/ppermute | solution.py:619
  54.7 1.5 %collective-permute-start.11 = (bf16[256,1408]{1,0:T(8,128)(2,1)}, bf16[256,1408]{1,0:T(8,128)(2,1)}, u32[]{:S(2)}, u32[]{:S(2)}) collective-permute-start(bf16[256,1408]{1,0:T(8,128)(2,1)} %collective-permute-done.5.refs_5_), channel_id=1, source_target_pairs={{0,16},{8,24},{16,0},{24,8},{1,17},{9,25},{17,1},{25,9},{2,18},{10... | collective-permute-start | bytes 2162696 | tf_op jit(solution)/shard_map/ppermute | solution.py:619
  56.2 6.9 %pages.1 = (bf16[16,1,256,512]{3,2,1,0:T(8,128)(2,1)}, bf16[512,512]{1,0:T(8,128)(2,1)}, bf16[512,512]{1,0:T(8,128)(2,1)}) custom-call(s32[1,16]{1,0:T(1,128)S(1)} %copy-done.5, s32[1,16]{1,0:T(1,128)S(1)} %copy-done.7, bf16[1024,256]{1,0:T(8,128)(2,1)S(1)} %get-tuple-element.49.raised_ref, bf16[1024,256]{1,0:T(8,128)(2,1)S(1)} %get-tuple-element.50.lowered_ref, ...), custom_call_target="tpu_custom_call" | custom-call | flops 1000 | bytes 1000 | tf_op jit(solution)/shard_map/pages/pallas_call | solution.py:370
  63.7 2.5 %constant_dynamic-slice_fusion = (bf16[1408,256]{1,0:T(8,128)(2,1)}, bf16[1408,256]{1,0:T(8,128)(2,1)}) fusion(bf16[1408,512]{1,0:T(8,128)(2,1)} %refs_0_.5, s32[]{:T(128)S(6)} %select_n.8, s32[]{:T(128)S(6)} %select_n.7), kind=kLoop, calls=%fused_computation.1 | loop fusion | bytes 2883592 | tf_op jit(solution)/shard_map/dynamic_slice | solution.py:658
  66.2 4.6 %collective-permute-done.10.refs_6_ = bf16[256,1408]{1,0:T(8,128)(2,1)} collective-permute-done((bf16[256,1408]{1,0:T(8,128)(2,1)}, bf16[256,1408]{1,0:T(8,128)(2,1)}, u32[]{:S(2)}, u32[]{:S(2)}) %collective-permute-start.10) | collective-permute-done | bytes 720928 | tf_op jit(solution)/shard_map/ppermute | solution.py:619
  70.8 1.5 %collective-permute-start.13 = (bf16[1408,256]{1,0:T(8,128)(2,1)}, bf16[1408,256]{1,0:T(8,128)(2,1)}, u32[]{:S(2)}, u32[]{:S(2)}) collective-permute-start(bf16[1408,256]{1,0:T(8,128)(2,1)} %get-tuple-element.86), channel_id=1, source_target_pairs={{0,16},{8,24},{16,0},{24,8},{1,17},{9,25},{17,1},{25,9},{2,18},{10... | collective-permute-start | bytes 2162696 | tf_op jit(solution)/shard_map/ppermute | solution.py:619
  73.0 1.6 %collective-permute-start.15 = (bf16[256,1408]{1,0:T(8,128)(2,1)}, bf16[256,1408]{1,0:T(8,128)(2,1)}, u32[]{:S(2)}, u32[]{:S(2)}) collective-permute-start(bf16[256,1408]{1,0:T(8,128)(2,1)} %collective-permute-done.6.refs_7_), channel_id=1, source_target_pairs={{0,2},{2,0},{4,6},{6,4},{1,3},{3,1},{5,7},{7,5},{8,10},{10,8},{12,... | collective-permute-start | bytes 2162696 | tf_op jit(solution)/shard_map/ppermute | solution.py:619
  74.6 19.1 %mix.1 = (bf16[512,2048]{1,0:T(8,128)(2,1)S(1)}, bf16[1024,2048]{1,0:T(8,128)(2,1)S(1)}) custom-call(s32[1]{0:T(128)} %bitcast.s, bf16[1024,2048]{1,0:T(8,128)(2,1)} %refs_0_.3, bf16[512,512]{1,0:T(8,128)(2,1)} %get-tuple-element.55.refs_1_, bf16[512,512]{1,0:T(8,128)(2,1)} %get-tuple-element.56.refs_2_, bf16[512,512]{1,0:T(8,128)(2,1)} %collective-permute-done.8.refs_3_, ...), custom_call_target="tpu_custom_call" | custom-call | flops 1000 | bytes 1000 | tf_op jit(solution)/shard_map/mix/pallas_call | solution.py:456
  95.5 15.5 %widen.1 = (bf16[1024,1408]{1,0:T(8,128)(2,1)S(1)}, f32[1024,1408]{1,0:T(8,128)S(1)}) custom-call(bf16[1024,2048]{1,0:T(8,128)(2,1)S(1)} %get-tuple-element.63.feed_ref, bf16[512,1408]{1,0:T(8,128)(2,1)} %refs_0_.4, bf16[512,1408]{1,0:T(8,128)(2,1)S(1)} %collective-permute-done.2.refs_1_, bf16[512,1408]{1,0:T(8,128)(2,1)} %collective-permute-done.3.refs_2_, ...), custom_call_target="tpu_custom_call" | custom-call | flops 1000 | bytes 1000 | tf_op jit(solution)/shard_map/widen/pallas_call | solution.py:512
  113.1 1.6 %collective-permute-start.21 = (bf16[1408,256]{1,0:T(8,128)(2,1)}, bf16[1408,256]{1,0:T(8,128)(2,1)S(1)}, u32[]{:S(2)}, u32[]{:S(2)}) collective-permute-start(bf16[1408,256]{1,0:T(8,128)(2,1)} %collective-permute-done.14.refs_1_), channel_id=1, source_target_pairs={{0,2},{2,0},{4,6},{6,4},{1,3},{3,1},{5,7},{7,5},{8,10},{10,8},{12,... | collective-permute-start | bytes 2162696 | tf_op jit(solution)/shard_map/ppermute | solution.py:619
  114.7 5.4 %finish.1.hidden_hbm = bf16[1024,1408]{1,0:T(8,128)(2,1)S(1)} custom-call(bf16[1024,2048]{1,0:T(8,128)(2,1)S(1)} %get-tuple-element.63.feed_ref, bf16[1024,1408]{1,0:T(8,128)(2,1)S(1)} %get-tuple-element.71.gate_ref, f32[1024,1408]{1,0:T(8,128)S(1)} %get-tuple-element.72.up_ref, bf16[256,1408]{1,0:T(8,128)(2,1)} %collective-permute-done.15.refs_0_, ...), custom_call_target="tpu_custom_call" | custom-call | flops 1000 | bytes 1000 | tf_op jit(solution)/shard_map/finish/pallas_call | solution.py:512
  120.1 6.7 %narrow.2 = (bf16[512,1280]{1,0:T(8,128)(2,1)S(1)}, bf16[512,1280]{1,0:T(8,128)(2,1)S(1)}) custom-call(bf16[1024,1408]{1,0:T(8,128)(2,1)S(1)} %finish.1.hidden_hbm, bf16[1408,512]{1,0:T(8,128)(2,1)} %refs_0_.5, bf16[1408,256]{1,0:T(8,128)(2,1)} %collective-permute-done.14.refs_1_, bf16[1408,256]{1,0:T(8,128)(2,1)} %collective-permute-done.13.refs_2_, ...), custom_call_target="tpu_custom_call" | custom-call | flops 1000 | bytes 1000 | tf_op jit(solution)/shard_map/narrow/pallas_call | solution.py:571
  127.8 4.4 %narrow.3 = (bf16[512,768]{1,0:T(8,128)(2,1)S(1)}, bf16[512,768]{1,0:T(8,128)(2,1)S(1)}) custom-call(bf16[1024,1408]{1,0:T(8,128)(2,1)S(1)} %finish.1.hidden_hbm, bf16[1408,256]{1,0:T(8,128)(2,1)S(1)} %collective-permute-done.19.refs_0_, bf16[1408,256]{1,0:T(8,128)(2,1)S(1)} %collective-permute-done.20.refs_1_, ...), custom_call_target="tpu_custom_call" | custom-call | flops 1000 | bytes 1000 | tf_op jit(solution)/shard_map/narrow/pallas_call | solution.py:571
  133.1 1.5 %collective-permute-done.22.refs_3_ = bf16[512,768]{1,0:T(8,128)(2,1)S(1)} collective-permute-done((bf16[512,768]{1,0:T(8,128)(2,1)S(1)}, bf16[512,768]{1,0:T(8,128)(2,1)S(1)}, u32[]{:S(2)}, u32[]{:S(2)}) %collective-permute-start.22) | collective-permute-done | bytes 786464 | tf_op jit(solution)/shard_map/ppermute | solution.py:619
  134.6 1.8 %close.1 = bf16[512,2048]{1,0:T(8,128)(2,1)} custom-call(bf16[512,2048]{1,0:T(8,128)(2,1)S(1)} %get-tuple-element.61.residual_ref, bf16[512,1280]{1,0:T(8,128)(2,1)S(1)} %get-tuple-element.76.refs_0_, bf16[512,1280]{1,0:T(8,128)(2,1)S(1)} %collective-permute-done.18.refs_1_, bf16[512,768]{1,0:T(8,128)(2,1)S(1)} %get-tuple-element.78.refs_2_, ...), custom_call_target="tpu_custom_call" | custom-call | flops 1000 | bytes 1000 | tf_op jit(solution)/shard_map/close/pallas_call | solution.py:600
  (62 shorter events, 14.0 us)
Async XLA Ops:
  0.6 11.8 %collective-permute-start.1 = (bf16[512,2048]{1,0:T(8,128)(2,1)}, bf16[512,2048]{1,0:T(8,128)(2,1)S(1)}, u32[]{:S(2)}, u32[]{:S(2)}) collective-permute-start(bf16[512,2048]{1,0:T(8,128)(2,1)} %refs_5_.1), channel_id=1, source_target_pairs={{0,1},{1,0},{2,3},{3,2},{4,5},{5,4},{6,7},{7,6},{8,9},{9,8},{10,11... | collective-permute-start | bytes 6291464 | tf_op jit(solution)/shard_map/ppermute | solution.py:619
  1.1 37.2 %collective-permute-start.2 = (bf16[512,1408]{1,0:T(8,128)(2,1)}, bf16[512,1408]{1,0:T(8,128)(2,1)S(1)}, u32[]{:S(2)}, u32[]{:S(2)}) collective-permute-start(bf16[512,1408]{1,0:T(8,128)(2,1)} %refs_0_.4), channel_id=1, source_target_pairs={{0,8},{8,0},{16,24},{24,16},{1,9},{9,1},{17,25},{25,17},{2,10},{10... | collective-permute-start | bytes 4325384 | tf_op jit(solution)/shard_map/ppermute | solution.py:619
  3.7 34.7 %collective-permute-start.3 = (bf16[512,1408]{1,0:T(8,128)(2,1)}, bf16[512,1408]{1,0:T(8,128)(2,1)}, u32[]{:S(2)}, u32[]{:S(2)}) collective-permute-start(bf16[512,1408]{1,0:T(8,128)(2,1)} %refs_0_.4), channel_id=1, source_target_pairs={{0,16},{8,24},{16,0},{24,8},{1,17},{9,25},{17,1},{25,9},{2,18},{10... | collective-permute-start | bytes 4325384 | tf_op jit(solution)/shard_map/ppermute | solution.py:619
  6.7 5.7 %collective-permute-start = (bf16[16,2048]{1,0:T(8,128)(2,1)}, bf16[16,2048]{1,0:T(8,128)(2,1)}, u32[]{:S(2)}, u32[]{:S(2)}) collective-permute-start(bf16[16,2048]{1,0:T(8,128)(2,1)} %slice.3), channel_id=1, source_target_pairs={{0,2},{2,4},{4,6},{1,3},{3,5},{5,7},{8,10},{10,12},{12,14},{9,11},... | collective-permute-start | bytes 196616 | tf_op jit(solution)/shard_map/ppermute | solution.py:614
  28.6 23.0 %copy-start = (bf16[16,3,768]{2,1,0:T(4,128)(2,1)}, bf16[16,3,768]{2,1,0:T(4,128)(2,1)S(1)}, u32[]{:S(2)}) copy-start(bf16[16,3,768]{2,1,0:T(4,128)(2,1)S(1)} %get-tuple-element.82) | copy-start | bytes 221188
  28.6 9.5 %collective-permute-start.4 = (bf16[272,512]{1,0:T(8,128)(2,1)S(1)}, bf16[272,512]{1,0:T(8,128)(2,1)S(1)}, u32[]{:S(2)}, u32[]{:S(2)}) collective-permute-start(bf16[272,512]{1,0:T(8,128)(2,1)S(1)} %get-tuple-element.45.later_ref), channel_id=1, source_target_pairs={{0,2},{2,4},{4,6},{1,3},{3,5},{5,7},{8,10},{10,12},{12,14},{9,11},... | collective-permute-start | bytes 835592 | tf_op jit(solution)/shard_map/ppermute | solution.py:614
  33.1 19.2 %collective-permute-start.5 = (bf16[256,1408]{1,0:T(8,128)(2,1)S(1)}, bf16[256,1408]{1,0:T(8,128)(2,1)}, u32[]{:S(2)}, u32[]{:S(2)}) collective-permute-start(bf16[256,1408]{1,0:T(8,128)(2,1)S(1)} %constant_dynamic-slice_fusion.2), channel_id=1, source_target_pairs={{0,8},{8,0},{16,24},{24,16},{1,9},{9,1},{17,25},{25,17},{2,10},{10... | collective-permute-start | bytes 2162696 | tf_op jit(solution)/shard_map/ppermute | solution.py:619
  33.8 19.4 %collective-permute-start.6 = (bf16[256,1408]{1,0:T(8,128)(2,1)S(1)}, bf16[256,1408]{1,0:T(8,128)(2,1)}, u32[]{:S(2)}, u32[]{:S(2)}) collective-permute-start(bf16[256,1408]{1,0:T(8,128)(2,1)S(1)} %constant_dynamic-slice_fusion.2), channel_id=1, source_target_pairs={{0,16},{8,24},{16,0},{24,8},{1,17},{9,25},{17,1},{25,9},{2,18},{10... | collective-permute-start | bytes 2162696 | tf_op jit(solution)/shard_map/ppermute | solution.py:619
  38.5 55.7 %collective-permute-start.12 = (bf16[512,1408]{1,0:T(8,128)(2,1)}, bf16[512,1408]{1,0:T(8,128)(2,1)}, u32[]{:S(2)}, u32[]{:S(2)}) collective-permute-start(bf16[512,1408]{1,0:T(8,128)(2,1)} %collective-permute-done.3.refs_2_), channel_id=1, source_target_pairs={{0,8},{8,0},{16,24},{24,16},{1,9},{9,1},{17,25},{25,17},{2,10},{10... | collective-permute-start | bytes 4325384 | tf_op jit(solution)/shard_map/ppermute | solution.py:619
  39.0 17.2 %collective-permute-start.7 = (bf16[272,512]{1,0:T(8,128)(2,1)S(1)}, bf16[272,512]{1,0:T(8,128)(2,1)S(1)}, u32[]{:S(2)}, u32[]{:S(2)}) collective-permute-start(bf16[272,512]{1,0:T(8,128)(2,1)S(1)} %joined.1), channel_id=1, source_target_pairs={{0,4},{2,6},{1,5},{3,7},{8,12},{10,14},{9,13},{11,15},{16,20},{18,... | collective-permute-start | bytes 835592 | tf_op jit(solution)/shard_map/ppermute | solution.py:614
  53.1 17.7 %collective-permute-start.10 = (bf16[256,1408]{1,0:T(8,128)(2,1)}, bf16[256,1408]{1,0:T(8,128)(2,1)}, u32[]{:S(2)}, u32[]{:S(2)}) collective-permute-start(bf16[256,1408]{1,0:T(8,128)(2,1)} %collective-permute-done.5.refs_5_), channel_id=1, source_target_pairs={{0,2},{2,0},{4,6},{6,4},{1,3},{3,1},{5,7},{7,5},{8,10},{10,8},{12,... | collective-permute-start | bytes 2162696 | tf_op jit(solution)/shard_map/ppermute | solution.py:619
  54.7 17.6 %collective-permute-start.11 = (bf16[256,1408]{1,0:T(8,128)(2,1)}, bf16[256,1408]{1,0:T(8,128)(2,1)}, u32[]{:S(2)}, u32[]{:S(2)}) collective-permute-start(bf16[256,1408]{1,0:T(8,128)(2,1)} %collective-permute-done.5.refs_5_), channel_id=1, source_target_pairs={{0,16},{8,24},{16,0},{24,8},{1,17},{9,25},{17,1},{25,9},{2,18},{10... | collective-permute-start | bytes 2162696 | tf_op jit(solution)/shard_map/ppermute | solution.py:619
  63.1 9.9 %collective-permute-start.8 = (bf16[512,512]{1,0:T(8,128)(2,1)}, bf16[512,512]{1,0:T(8,128)(2,1)}, u32[]{:S(2)}, u32[]{:S(2)}) collective-permute-start(bf16[512,512]{1,0:T(8,128)(2,1)} %get-tuple-element.55.refs_1_), channel_id=1, source_target_pairs={{0,1},{1,0},{2,3},{3,2},{4,5},{5,4},{6,7},{7,6},{8,9},{9,8},{10,11... | collective-permute-start | bytes 1572872 | tf_op jit(solution)/shard_map/ppermute | solution.py:619
  63.2 11.4 %collective-permute-start.9 = (bf16[512,512]{1,0:T(8,128)(2,1)}, bf16[512,512]{1,0:T(8,128)(2,1)}, u32[]{:S(2)}, u32[]{:S(2)}) collective-permute-start(bf16[512,512]{1,0:T(8,128)(2,1)} %get-tuple-element.56.refs_2_), channel_id=1, source_target_pairs={{0,1},{1,0},{2,3},{3,2},{4,5},{5,4},{6,7},{7,6},{8,9},{9,8},{10,11... | collective-permute-start | bytes 1572872 | tf_op jit(solution)/shard_map/ppermute | solution.py:619
  70.8 40.1 %collective-permute-start.13 = (bf16[1408,256]{1,0:T(8,128)(2,1)}, bf16[1408,256]{1,0:T(8,128)(2,1)}, u32[]{:S(2)}, u32[]{:S(2)}) collective-permute-start(bf16[1408,256]{1,0:T(8,128)(2,1)} %get-tuple-element.86), channel_id=1, source_target_pairs={{0,16},{8,24},{16,0},{24,8},{1,17},{9,25},{17,1},{25,9},{2,18},{10... | collective-permute-start | bytes 2162696 | tf_op jit(solution)/shard_map/ppermute | solution.py:619
  72.4 38.6 %collective-permute-start.14 = (bf16[1408,256]{1,0:T(8,128)(2,1)}, bf16[1408,256]{1,0:T(8,128)(2,1)}, u32[]{:S(2)}, u32[]{:S(2)}) collective-permute-start(bf16[1408,256]{1,0:T(8,128)(2,1)} %get-tuple-element.75), channel_id=1, source_target_pairs={{0,8},{8,0},{16,24},{24,16},{1,9},{9,1},{17,25},{25,17},{2,10},{10... | collective-permute-start | bytes 2162696 | tf_op jit(solution)/shard_map/ppermute | solution.py:619
  73.0 40.2 %collective-permute-start.15 = (bf16[256,1408]{1,0:T(8,128)(2,1)}, bf16[256,1408]{1,0:T(8,128)(2,1)}, u32[]{:S(2)}, u32[]{:S(2)}) collective-permute-start(bf16[256,1408]{1,0:T(8,128)(2,1)} %collective-permute-done.6.refs_7_), channel_id=1, source_target_pairs={{0,2},{2,0},{4,6},{6,4},{1,3},{3,1},{5,7},{7,5},{8,10},{10,8},{12,... | collective-permute-start | bytes 2162696 | tf_op jit(solution)/shard_map/ppermute | solution.py:619
  93.6 21.1 %collective-permute-start.16 = (bf16[256,1408]{1,0:T(8,128)(2,1)}, bf16[256,1408]{1,0:T(8,128)(2,1)S(1)}, u32[]{:S(2)}, u32[]{:S(2)}) collective-permute-start(bf16[256,1408]{1,0:T(8,128)(2,1)} %collective-permute-done.11.refs_8_), channel_id=1, source_target_pairs={{0,2},{2,0},{4,6},{6,4},{1,3},{3,1},{5,7},{7,5},{8,10},{10,8},{12,... | collective-permute-start | bytes 2162696 | tf_op jit(solution)/shard_map/ppermute | solution.py:619
  94.1 25.9 %collective-permute-start.17 = (bf16[1408,256]{1,0:T(8,128)(2,1)}, bf16[1408,256]{1,0:T(8,128)(2,1)S(1)}, u32[]{:S(2)}, u32[]{:S(2)}) collective-permute-start(bf16[1408,256]{1,0:T(8,128)(2,1)} %get-tuple-element.75), channel_id=1, source_target_pairs={{0,16},{8,24},{16,0},{24,8},{1,17},{9,25},{17,1},{25,9},{2,18},{10... | collective-permute-start | bytes 2162696 | tf_op jit(solution)/shard_map/ppermute | solution.py:619
  111.0 15.9 %collective-permute-start.19 = (bf16[1408,256]{1,0:T(8,128)(2,1)}, bf16[1408,256]{1,0:T(8,128)(2,1)S(1)}, u32[]{:S(2)}, u32[]{:S(2)}) collective-permute-start(bf16[1408,256]{1,0:T(8,128)(2,1)} %collective-permute-done.13.refs_2_), channel_id=1, source_target_pairs={{0,8},{8,0},{16,24},{24,16},{1,9},{9,1},{17,25},{25,17},{2,10},{10... | collective-permute-start | bytes 2162696 | tf_op jit(solution)/shard_map/ppermute | solution.py:619
  112.4 15.0 %collective-permute-start.20 = (bf16[1408,256]{1,0:T(8,128)(2,1)}, bf16[1408,256]{1,0:T(8,128)(2,1)S(1)}, u32[]{:S(2)}, u32[]{:S(2)}) collective-permute-start(bf16[1408,256]{1,0:T(8,128)(2,1)} %collective-permute-done.14.refs_1_), channel_id=1, source_target_pairs={{0,16},{8,24},{16,0},{24,8},{1,17},{9,25},{17,1},{25,9},{2,18},{10... | collective-permute-start | bytes 2162696 | tf_op jit(solution)/shard_map/ppermute | solution.py:619
  113.1 14.7 %collective-permute-start.21 = (bf16[1408,256]{1,0:T(8,128)(2,1)}, bf16[1408,256]{1,0:T(8,128)(2,1)S(1)}, u32[]{:S(2)}, u32[]{:S(2)}) collective-permute-start(bf16[1408,256]{1,0:T(8,128)(2,1)} %collective-permute-done.14.refs_1_), channel_id=1, source_target_pairs={{0,2},{2,0},{4,6},{6,4},{1,3},{3,1},{5,7},{7,5},{8,10},{10,8},{12,... | collective-permute-start | bytes 2162696 | tf_op jit(solution)/shard_map/ppermute | solution.py:619
  126.8 6.3 %collective-permute-start.18 = (bf16[512,1280]{1,0:T(8,128)(2,1)S(1)}, bf16[512,1280]{1,0:T(8,128)(2,1)S(1)}, u32[]{:S(2)}, u32[]{:S(2)}) collective-permute-start(bf16[512,1280]{1,0:T(8,128)(2,1)S(1)} %get-tuple-element.77), channel_id=1, source_target_pairs={{0,1},{1,0},{2,3},{3,2},{4,5},{5,4},{6,7},{7,6},{8,9},{9,8},{10,11... | collective-permute-start | bytes 3932168 | tf_op jit(solution)/shard_map/ppermute | solution.py:619
  132.2 2.4 %collective-permute-start.22 = (bf16[512,768]{1,0:T(8,128)(2,1)S(1)}, bf16[512,768]{1,0:T(8,128)(2,1)S(1)}, u32[]{:S(2)}, u32[]{:S(2)}) collective-permute-start(bf16[512,768]{1,0:T(8,128)(2,1)S(1)} %get-tuple-element.79), channel_id=1, source_target_pairs={{0,1},{1,0},{2,3},{3,2},{4,5},{5,4},{6,7},{7,6},{8,9},{9,8},{10,11... | collective-permute-start | bytes 2359304 | tf_op jit(solution)/shard_map/ppermute | solution.py:619
  (10 other events, 98.2 us)

commit v9 on v7

--- a/solution.py
+++ b/solution.py
@@ -39,6 +39,10 @@
     return pl.BlockSpec(
         shape, lambda *_: (0,) * len(shape), pipeline_mode=pl.Buffered(1)
     )
+
+
+def held(array):
+    return pltpu.with_memory_space_constraint(array, pltpu.HBM)
 
 
 def whole_smem():
@@ -231,9 +235,9 @@
             pltpu.VMEM((tile + RIM, width), BF16), pltpu.VMEM((8, HK + HV), F32),
             pltpu.VMEM((HK, HV), F32), pltpu.VMEM((8, HK), F32), pltpu.VMEM((tile, HK), BF16),
         ],
-        compiler_params=params(44),
+        compiler_params=params(24),
         cost_estimate=cost(1000, 1000),
-    )(*prompts, tokens, rim, gain, project, project, project, down, up, bias, conv)
+    )(*prompts, held(tokens), rim, gain, *[held(project)] * 3, held(down), held(up), held(bias), held(conv))
 
 
 def query_kernel(
@@ -289,7 +293,7 @@
         scratch_shapes=[pltpu.VMEM((RIM, width), BF16), pltpu.VMEM((8, HK), F32)],
         compiler_params=params(20),
         cost_estimate=cost(2 * count * width * (HK + HV), 2 * count * width),
-    )(*prompts, normed, rim, gain, project, gate, conv, sums)
+    )(*prompts, normed, rim, gain, held(project), held(gate), held(conv), sums)
 
 
 def composed(later, earlier):
@@ -434,7 +438,7 @@
         ],
         compiler_params=params(20),
         cost_estimate=cost(1000, 1000),
-    )(hid_index, tokens, *own, *others, own_weight, other_weight, gain)
+    )(hid_index, held(tokens), *own, *others, held(own_weight), other_weight, gain)
 
 
 def widen_sums(places, pieces, feed_ref, rows):
@@ -643,16 +647,16 @@
         at = lambda flip: lambda: (lax.axis_index("req") ^ flip) * depth
         own = lambda flip: lambda: at(flip)() + lax.rem(lax.axis_index("seq"), 2) * half
         far = lambda flip: lambda: at(flip)() + (1 - lax.rem(lax.axis_index("seq"), 2)) * half
-        gate_list = [(gate_weight, at(0)), (gate_a, at(1)), (gate_b, at(2)), (gate_c, at(3))]
+        gate_list = [(held(gate_weight), at(0)), (gate_a, at(1)), (gate_b, at(2)), (gate_c, at(3))]
         up_list = [
-            (up_weight, at(0)), (up_a, own(1)), (far_a, far(1)), (up_b, own(2)), (up_c, own(3)),
+            (held(up_weight), at(0)), (up_a, own(1)), (far_a, far(1)), (up_b, own(2)), (up_c, own(3)),
         ]
         sums = widen(feed, (gate_list, up_list))
         sums, down_b_rest, down_a = tied((sums, down_b_rest, down_a))
         down_c_rest, down_c, down_a_far = x(down_b_rest), y(down_a), z(down_a)
         hidden = finish(feed, sums, [(far_b, far(2)), (far_c, far(3))])
         down_lists = [
-            [(down_weight, at(0)), (down_a, own(1)), (down_b_rest, far(2)), (down_b, own(2))],
+            [(held(down_weight), at(0)), (down_a, own(1)), (down_b_rest, far(2)), (down_b, own(2))],
             [(down_c_rest, far(3)), (down_c, own(3)), (down_a_far, far(1))],
         ]
     else:

time: 135 us -> 129 us (0.956)
  the two profiles are of different devices: /device:TPU:27 before, /device:TPU:0 now
where the time goes in v9:
time: 129 us; the launch traced here: 128 us
  Pallas kernels  72.6 us (56%)
  starting transfers between devices  33.4 us (26%)
  waiting for transfers between devices  14.6 us (11%)
  local copies, waits for them, and re-layouts  6.8 us (5%)
    pallas_call x2, Pallas kernels, widen_call(): pl.pallas_call(functools.partial(kernel, places), name=name, grid=(pl.cdi...  20.9 us
    ppermute x20, starting transfers between devices, swapped(): return lax.ppermute(value, axis, [(i, i ^ flip) for i in range(count)])  19.3 us
    pallas_call x1, Pallas kernels, front(): pl.pallas_call(front_kernel, name='front', grid=(count // tile,), in_spec...  14.9 us
    ppermute x3, starting transfers between devices, shifted(): lax.ppermute(value, 'seq', [(i, i + steps) for i in range(count - steps)])  14.1 us
    pallas_call x2, Pallas kernels, narrow(): pl.pallas_call(functools.partial(narrow_kernel, block), name='narrow', in...  11 us
    pallas_call x1, Pallas kernels, mix(): pl.pallas_call(lambda s, *refs: mix_kernel(*refs), name='mix', grid_spec=...  9.98 us
    ppermute x20, waiting for transfers between devices, swapped(): return lax.ppermute(value, axis, [(i, i ^ flip) for i in range(count)])  9.77 us
    pallas_call x1, Pallas kernels, query(): pl.pallas_call(query_kernel, name='query', grid=(count // tile,), in_spec...  7 us
  transfers between devices with their start and end apart: 23, of which 9 were waited for; matrix products, arithmetic and copies ran while one was open for 4% of the time, Pallas kernels for 55%

profile of v9, /device:TPU:0, one launch (start us, length us, event | category | flops | bytes accessed | tf_op | source)
XLA Modules:
  0.0 128.3 jit_solution(18010447426844829385)
XLA Ops:
  1.1 2.6 %collective-permute-start.2 = (bf16[512,1408]{1,0:T(8,128)(2,1)}, bf16[512,1408]{1,0:T(8,128)(2,1)S(1)}, u32[]{:S(2)}, u32[]{:S(2)}) collective-permute-start(bf16[512,1408]{1,0:T(8,128)(2,1)} %refs_0_.4), channel_id=1, source_target_pairs={{0,8},{8,0},{16,24},{24,16},{1,9},{9,1},{17,25},{25,17},{2,10},{10... | collective-permute-start | bytes 4325384 | tf_op jit(solution)/shard_map/ppermute | solution.py:585
  3.7 1.5 %collective-permute-start.3 = (bf16[512,1408]{1,0:T(8,128)(2,1)}, bf16[512,1408]{1,0:T(8,128)(2,1)}, u32[]{:S(2)}, u32[]{:S(2)}) collective-permute-start(bf16[512,1408]{1,0:T(8,128)(2,1)} %refs_0_.4), channel_id=1, source_target_pairs={{0,16},{8,24},{16,0},{24,8},{1,17},{9,25},{17,1},{25,9},{2,18},{10... | collective-permute-start | bytes 4325384 | tf_op jit(solution)/shard_map/ppermute | solution.py:585
  5.2 1.5 %slice.3 = bf16[16,2048]{1,0:T(8,128)(2,1)} slice(bf16[1024,2048]{1,0:T(8,128)(2,1)} %refs_0_.3), slice={[1008:1024], [0:2048]} | slice | bytes 131072 | tf_op jit(solution)/shard_map/slice | solution.py:612
  6.7 4.1 %collective-permute-start = (bf16[16,2048]{1,0:T(8,128)(2,1)}, bf16[16,2048]{1,0:T(8,128)(2,1)}, u32[]{:S(2)}, u32[]{:S(2)}) collective-permute-start(bf16[16,2048]{1,0:T(8,128)(2,1)} %slice.3), channel_id=1, source_target_pairs={{0,2},{2,4},{4,6},{1,3},{3,5},{5,7},{8,10},{10,12},{12,14},{9,11},... | collective-permute-start | bytes 196616 | tf_op jit(solution)/shard_map/ppermute | solution.py:580
  13.7 14.9 %front.1 = (bf16[1024,2048]{1,0:T(8,128)(2,1)S(1)}, f32[1024,256]{1,0:T(8,128)S(1)}, bf16[1024,256]{1,0:T(8,128)(2,1)S(1)}, bf16[1024,256]{1,0:T(8,128)(2,1)S(1)...) custom-call(s32[1,16]{1,0:T(1,128)S(1)} %copy-done.4, ...), custom_call_target="tpu_custom_call" | custom-call | flops 1000 | bytes 1000 | tf_op jit(solution)/shard_map/front/pallas_call | solution.py:214
  28.6 4.4 %collective-permute-start.4 = (bf16[272,512]{1,0:T(8,128)(2,1)S(1)}, bf16[272,512]{1,0:T(8,128)(2,1)S(1)}, u32[]{:S(2)}, u32[]{:S(2)}) collective-permute-start(bf16[272,512]{1,0:T(8,128)(2,1)S(1)} %get-tuple-element.45.later_ref), channel_id=1, source_target_pairs={{0,2},{2,4},{4,6},{1,3},{3,5},{5,7},{8,10},{10,12},{12,14},{9,11},... | collective-permute-start | bytes 835592 | tf_op jit(solution)/shard_map/ppermute | solution.py:580
  34.3 3.9 %collective-permute-done.4.earlier_ref.one_ref = bf16[272,512]{1,0:T(8,128)(2,1)S(1)} collective-permute-done((bf16[272,512]{1,0:T(8,128)(2,1)S(1)}, bf16[272,512]{1,0:T(8,128)(2,1)S(1)}, u32[]{:S(2)}, u32[]{:S(2)}) %collective-permute-start.4) | collective-permute-done | bytes 278560 | tf_op jit(solution)/shard_map/ppermute | solution.py:580
  39.0 5.6 %collective-permute-start.7 = (bf16[272,512]{1,0:T(8,128)(2,1)S(1)}, bf16[272,512]{1,0:T(8,128)(2,1)S(1)}, u32[]{:S(2)}, u32[]{:S(2)}) collective-permute-start(bf16[272,512]{1,0:T(8,128)(2,1)S(1)} %joined.1), channel_id=1, source_target_pairs={{0,4},{2,6},{1,5},{3,7},{8,12},{10,14},{9,13},{11,15},{16,20},{18,... | collective-permute-start | bytes 835592 | tf_op jit(solution)/shard_map/ppermute | solution.py:580
  44.6 7.0 %query.1 = (bf16[1024,256]{1,0:T(8,128)(2,1)S(1)}, bf16[16,3,256]{2,1,0:T(4,128)(2,1)S(1)}, bf16[1024,512]{1,0:T(8,128)(2,1)S(1)}) custom-call(s32[1,16]{1,0:T(1,128)S(1)} %copy-done.5, s32[1,16]{1,0:T(1,128)S(1)} %copy-done.7, bf16[1024,2048]{1,0:T(8,128)(2,1)S(1)} %get-tuple-element.46.normed_ref, bf16[16,2048]{1,0:T(8,128)(2,1)} %collective-permute-done.rim_ref, ...), custom_call_target="tpu_custom_call" | custom-call | flops 3221225472 | bytes 4194304 | tf_op jit(solution)/shard_map/query/pallas_call | solution.py:279
  53.1 1.6 %collective-permute-start.10 = (bf16[256,1408]{1,0:T(8,128)(2,1)}, bf16[256,1408]{1,0:T(8,128)(2,1)}, u32[]{:S(2)}, u32[]{:S(2)}) collective-permute-start(bf16[256,1408]{1,0:T(8,128)(2,1)} %collective-permute-done.5.refs_5_), channel_id=1, source_target_pairs={{0,2},{2,0},{4,6},{6,4},{1,3},{3,1},{5,7},{7,5},{8,10},{10,8},{12,... | collective-permute-start | bytes 2162696 | tf_op jit(solution)/shard_map/ppermute | solution.py:585
  54.7 1.5 %collective-permute-start.11 = (bf16[256,1408]{1,0:T(8,128)(2,1)}, bf16[256,1408]{1,0:T(8,128)(2,1)}, u32[]{:S(2)}, u32[]{:S(2)}) collective-permute-start(bf16[256,1408]{1,0:T(8,128)(2,1)} %collective-permute-done.5.refs_5_), channel_id=1, source_target_pairs={{0,16},{8,24},{16,0},{24,8},{1,17},{9,25},{17,1},{25,9},{2,18},{10... | collective-permute-start | bytes 2162696 | tf_op jit(solution)/shard_map/ppermute | solution.py:585
  56.2 6.9 %pages.1 = (bf16[16,1,256,512]{3,2,1,0:T(8,128)(2,1)}, bf16[512,512]{1,0:T(8,128)(2,1)}, bf16[512,512]{1,0:T(8,128)(2,1)}) custom-call(s32[1,16]{1,0:T(1,128)S(1)} %copy-done.5, s32[1,16]{1,0:T(1,128)S(1)} %copy-done.7, bf16[1024,256]{1,0:T(8,128)(2,1)S(1)} %get-tuple-element.49.raised_ref, bf16[1024,256]{1,0:T(8,128)(2,1)S(1)} %get-tuple-element.50.lowered_ref, ...), custom_call_target="tpu_custom_call" | custom-call | flops 1000 | bytes 1000 | tf_op jit(solution)/shard_map/pages/pallas_call | solution.py:370
  63.7 2.5 %constant_dynamic-slice_fusion = (bf16[1408,256]{1,0:T(8,128)(2,1)}, bf16[1408,256]{1,0:T(8,128)(2,1)}) fusion(bf16[1408,512]{1,0:T(8,128)(2,1)} %refs_0_.5, s32[]{:T(128)S(6)} %select_n.8, s32[]{:T(128)S(6)} %select_n.7), kind=kLoop, calls=%fused_computation.1 | loop fusion | bytes 2883592 | tf_op jit(solution)/shard_map/dynamic_slice | solution.py:624
  66.2 4.6 %collective-permute-done.10.refs_6_ = bf16[256,1408]{1,0:T(8,128)(2,1)} collective-permute-done((bf16[256,1408]{1,0:T(8,128)(2,1)}, bf16[256,1408]{1,0:T(8,128)(2,1)}, u32[]{:S(2)}, u32[]{:S(2)}) %collective-permute-start.10) | collective-permute-done | bytes 720928 | tf_op jit(solution)/shard_map/ppermute | solution.py:585
  70.8 1.5 %collective-permute-start.13 = (bf16[1408,256]{1,0:T(8,128)(2,1)}, bf16[1408,256]{1,0:T(8,128)(2,1)}, u32[]{:S(2)}, u32[]{:S(2)}) collective-permute-start(bf16[1408,256]{1,0:T(8,128)(2,1)} %get-tuple-element.86), channel_id=1, source_target_pairs={{0,16},{8,24},{16,0},{24,8},{1,17},{9,25},{17,1},{25,9},{2,18},{10... | collective-permute-start | bytes 2162696 | tf_op jit(solution)/shard_map/ppermute | solution.py:585
  73.0 1.6 %collective-permute-start.15 = (bf16[256,1408]{1,0:T(8,128)(2,1)}, bf16[256,1408]{1,0:T(8,128)(2,1)}, u32[]{:S(2)}, u32[]{:S(2)}) collective-permute-start(bf16[256,1408]{1,0:T(8,128)(2,1)} %collective-permute-done.6.refs_7_), channel_id=1, source_target_pairs={{0,2},{2,0},{4,6},{6,4},{1,3},{3,1},{5,7},{7,5},{8,10},{10,8},{12,... | collective-permute-start | bytes 2162696 | tf_op jit(solution)/shard_map/ppermute | solution.py:585
  74.6 10.0 %mix.1 = (bf16[512,2048]{1,0:T(8,128)(2,1)S(1)}, bf16[1024,2048]{1,0:T(8,128)(2,1)S(1)}) custom-call(s32[1]{0:T(128)} %bitcast.s, bf16[1024,2048]{1,0:T(8,128)(2,1)} %refs_0_.3, bf16[512,512]{1,0:T(8,128)(2,1)} %get-tuple-element.55.refs_1_, bf16[512,512]{1,0:T(8,128)(2,1)} %get-tuple-element.56.refs_2_, bf16[512,512]{1,0:T(8,128)(2,1)} %collective-permute-done.8.refs_3_, ...), custom_call_target="tpu_custom_call" | custom-call | flops 1000 | bytes 1000 | tf_op jit(solution)/shard_map/mix/pallas_call | solution.py:426
  86.4 15.5 %widen.1 = (bf16[1024,1408]{1,0:T(8,128)(2,1)S(1)}, f32[1024,1408]{1,0:T(8,128)S(1)}) custom-call(bf16[1024,2048]{1,0:T(8,128)(2,1)S(1)} %get-tuple-element.63.feed_ref, bf16[512,1408]{1,0:T(8,128)(2,1)} %refs_0_.4, bf16[512,1408]{1,0:T(8,128)(2,1)S(1)} %collective-permute-done.2.refs_1_, bf16[512,1408]{1,0:T(8,128)(2,1)} %collective-permute-done.3.refs_2_, ...), custom_call_target="tpu_custom_call" | custom-call | flops 1000 | bytes 1000 | tf_op jit(solution)/shard_map/widen/pallas_call | solution.py:478
  104.0 1.6 %collective-permute-start.21 = (bf16[1408,256]{1,0:T(8,128)(2,1)}, bf16[1408,256]{1,0:T(8,128)(2,1)S(1)}, u32[]{:S(2)}, u32[]{:S(2)}) collective-permute-start(bf16[1408,256]{1,0:T(8,128)(2,1)} %collective-permute-done.14.refs_1_), channel_id=1, source_target_pairs={{0,2},{2,0},{4,6},{6,4},{1,3},{3,1},{5,7},{7,5},{8,10},{10,8},{12,... | collective-permute-start | bytes 2162696 | tf_op jit(solution)/shard_map/ppermute | solution.py:585
  105.6 5.4 %finish.1.hidden_hbm = bf16[1024,1408]{1,0:T(8,128)(2,1)S(1)} custom-call(bf16[1024,2048]{1,0:T(8,128)(2,1)S(1)} %get-tuple-element.63.feed_ref, bf16[1024,1408]{1,0:T(8,128)(2,1)S(1)} %get-tuple-element.71.gate_ref, f32[1024,1408]{1,0:T(8,128)S(1)} %get-tuple-element.72.up_ref, bf16[256,1408]{1,0:T(8,128)(2,1)} %collective-permute-done.15.refs_0_, ...), custom_call_target="tpu_custom_call" | custom-call | flops 1000 | bytes 1000 | tf_op jit(solution)/shard_map/finish/pallas_call | solution.py:478
  111.0 6.7 %narrow.2 = (bf16[512,1280]{1,0:T(8,128)(2,1)S(1)}, bf16[512,1280]{1,0:T(8,128)(2,1)S(1)}) custom-call(bf16[1024,1408]{1,0:T(8,128)(2,1)S(1)} %finish.1.hidden_hbm, bf16[1408,512]{1,0:T(8,128)(2,1)} %refs_0_.5, bf16[1408,256]{1,0:T(8,128)(2,1)} %collective-permute-done.14.refs_1_, bf16[1408,256]{1,0:T(8,128)(2,1)} %collective-permute-done.13.refs_2_, ...), custom_call_target="tpu_custom_call" | custom-call | flops 1000 | bytes 1000 | tf_op jit(solution)/shard_map/narrow/pallas_call | solution.py:537
  119.8 4.4 %narrow.3 = (bf16[512,768]{1,0:T(8,128)(2,1)S(1)}, bf16[512,768]{1,0:T(8,128)(2,1)S(1)}) custom-call(bf16[1024,1408]{1,0:T(8,128)(2,1)S(1)} %finish.1.hidden_hbm, bf16[1408,256]{1,0:T(8,128)(2,1)S(1)} %collective-permute-done.19.refs_0_, bf16[1408,256]{1,0:T(8,128)(2,1)S(1)} %collective-permute-done.20.refs_1_, ...), custom_call_target="tpu_custom_call" | custom-call | flops 1000 | bytes 1000 | tf_op jit(solution)/shard_map/narrow/pallas_call | solution.py:537
  125.1 1.5 %collective-permute-done.22.refs_3_ = bf16[512,768]{1,0:T(8,128)(2,1)S(1)} collective-permute-done((bf16[512,768]{1,0:T(8,128)(2,1)S(1)}, bf16[512,768]{1,0:T(8,128)(2,1)S(1)}, u32[]{:S(2)}, u32[]{:S(2)}) %collective-permute-start.22) | collective-permute-done | bytes 786464 | tf_op jit(solution)/shard_map/ppermute | solution.py:585
  126.6 1.8 %close.1 = bf16[512,2048]{1,0:T(8,128)(2,1)} custom-call(bf16[512,2048]{1,0:T(8,128)(2,1)S(1)} %get-tuple-element.61.residual_ref, bf16[512,1280]{1,0:T(8,128)(2,1)S(1)} %get-tuple-element.76.refs_0_, bf16[512,1280]{1,0:T(8,128)(2,1)S(1)} %collective-permute-done.18.refs_1_, bf16[512,768]{1,0:T(8,128)(2,1)S(1)} %get-tuple-element.78.refs_2_, ...), custom_call_target="tpu_custom_call" | custom-call | flops 1000 | bytes 1000 | tf_op jit(solution)/shard_map/close/pallas_call | solution.py:566
  (62 shorter events, 15.1 us)
Async XLA Ops:
  0.6 11.8 %collective-permute-start.1 = (bf16[512,2048]{1,0:T(8,128)(2,1)}, bf16[512,2048]{1,0:T(8,128)(2,1)S(1)}, u32[]{:S(2)}, u32[]{:S(2)}) collective-permute-start(bf16[512,2048]{1,0:T(8,128)(2,1)} %refs_5_.1), channel_id=1, source_target_pairs={{0,1},{1,0},{2,3},{3,2},{4,5},{5,4},{6,7},{7,6},{8,9},{9,8},{10,11... | collective-permute-start | bytes 6291464 | tf_op jit(solution)/shard_map/ppermute | solution.py:585
  1.1 37.2 %collective-permute-start.2 = (bf16[512,1408]{1,0:T(8,128)(2,1)}, bf16[512,1408]{1,0:T(8,128)(2,1)S(1)}, u32[]{:S(2)}, u32[]{:S(2)}) collective-permute-start(bf16[512,1408]{1,0:T(8,128)(2,1)} %refs_0_.4), channel_id=1, source_target_pairs={{0,8},{8,0},{16,24},{24,16},{1,9},{9,1},{17,25},{25,17},{2,10},{10... | collective-permute-start | bytes 4325384 | tf_op jit(solution)/shard_map/ppermute | solution.py:585
  3.7 34.7 %collective-permute-start.3 = (bf16[512,1408]{1,0:T(8,128)(2,1)}, bf16[512,1408]{1,0:T(8,128)(2,1)}, u32[]{:S(2)}, u32[]{:S(2)}) collective-permute-start(bf16[512,1408]{1,0:T(8,128)(2,1)} %refs_0_.4), channel_id=1, source_target_pairs={{0,16},{8,24},{16,0},{24,8},{1,17},{9,25},{17,1},{25,9},{2,18},{10... | collective-permute-start | bytes 4325384 | tf_op jit(solution)/shard_map/ppermute | solution.py:585
  6.7 5.7 %collective-permute-start = (bf16[16,2048]{1,0:T(8,128)(2,1)}, bf16[16,2048]{1,0:T(8,128)(2,1)}, u32[]{:S(2)}, u32[]{:S(2)}) collective-permute-start(bf16[16,2048]{1,0:T(8,128)(2,1)} %slice.3), channel_id=1, source_target_pairs={{0,2},{2,4},{4,6},{1,3},{3,5},{5,7},{8,10},{10,12},{12,14},{9,11},... | collective-permute-start | bytes 196616 | tf_op jit(solution)/shard_map/ppermute | solution.py:580
  28.6 23.0 %copy-start = (bf16[16,3,768]{2,1,0:T(4,128)(2,1)}, bf16[16,3,768]{2,1,0:T(4,128)(2,1)S(1)}, u32[]{:S(2)}) copy-start(bf16[16,3,768]{2,1,0:T(4,128)(2,1)S(1)} %get-tuple-element.82) | copy-start | bytes 221188
  28.6 9.5 %collective-permute-start.4 = (bf16[272,512]{1,0:T(8,128)(2,1)S(1)}, bf16[272,512]{1,0:T(8,128)(2,1)S(1)}, u32[]{:S(2)}, u32[]{:S(2)}) collective-permute-start(bf16[272,512]{1,0:T(8,128)(2,1)S(1)} %get-tuple-element.45.later_ref), channel_id=1, source_target_pairs={{0,2},{2,4},{4,6},{1,3},{3,5},{5,7},{8,10},{10,12},{12,14},{9,11},... | collective-permute-start | bytes 835592 | tf_op jit(solution)/shard_map/ppermute | solution.py:580
  33.1 19.2 %collective-permute-start.5 = (bf16[256,1408]{1,0:T(8,128)(2,1)S(1)}, bf16[256,1408]{1,0:T(8,128)(2,1)}, u32[]{:S(2)}, u32[]{:S(2)}) collective-permute-start(bf16[256,1408]{1,0:T(8,128)(2,1)S(1)} %constant_dynamic-slice_fusion.2), channel_id=1, source_target_pairs={{0,8},{8,0},{16,24},{24,16},{1,9},{9,1},{17,25},{25,17},{2,10},{10... | collective-permute-start | bytes 2162696 | tf_op jit(solution)/shard_map/ppermute | solution.py:585
  33.8 19.4 %collective-permute-start.6 = (bf16[256,1408]{1,0:T(8,128)(2,1)S(1)}, bf16[256,1408]{1,0:T(8,128)(2,1)}, u32[]{:S(2)}, u32[]{:S(2)}) collective-permute-start(bf16[256,1408]{1,0:T(8,128)(2,1)S(1)} %constant_dynamic-slice_fusion.2), channel_id=1, source_target_pairs={{0,16},{8,24},{16,0},{24,8},{1,17},{9,25},{17,1},{25,9},{2,18},{10... | collective-permute-start | bytes 2162696 | tf_op jit(solution)/shard_map/ppermute | solution.py:585
  38.5 46.6 %collective-permute-start.12 = (bf16[512,1408]{1,0:T(8,128)(2,1)}, bf16[512,1408]{1,0:T(8,128)(2,1)}, u32[]{:S(2)}, u32[]{:S(2)}) collective-permute-start(bf16[512,1408]{1,0:T(8,128)(2,1)} %collective-permute-done.3.refs_2_), channel_id=1, source_target_pairs={{0,8},{8,0},{16,24},{24,16},{1,9},{9,1},{17,25},{25,17},{2,10},{10... | collective-permute-start | bytes 4325384 | tf_op jit(solution)/shard_map/ppermute | solution.py:585
  39.0 17.2 %collective-permute-start.7 = (bf16[272,512]{1,0:T(8,128)(2,1)S(1)}, bf16[272,512]{1,0:T(8,128)(2,1)S(1)}, u32[]{:S(2)}, u32[]{:S(2)}) collective-permute-start(bf16[272,512]{1,0:T(8,128)(2,1)S(1)} %joined.1), channel_id=1, source_target_pairs={{0,4},{2,6},{1,5},{3,7},{8,12},{10,14},{9,13},{11,15},{16,20},{18,... | collective-permute-start | bytes 835592 | tf_op jit(solution)/shard_map/ppermute | solution.py:580
  53.1 17.7 %collective-permute-start.10 = (bf16[256,1408]{1,0:T(8,128)(2,1)}, bf16[256,1408]{1,0:T(8,128)(2,1)}, u32[]{:S(2)}, u32[]{:S(2)}) collective-permute-start(bf16[256,1408]{1,0:T(8,128)(2,1)} %collective-permute-done.5.refs_5_), channel_id=1, source_target_pairs={{0,2},{2,0},{4,6},{6,4},{1,3},{3,1},{5,7},{7,5},{8,10},{10,8},{12,... | collective-permute-start | bytes 2162696 | tf_op jit(solution)/shard_map/ppermute | solution.py:585
  54.7 17.6 %collective-permute-start.11 = (bf16[256,1408]{1,0:T(8,128)(2,1)}, bf16[256,1408]{1,0:T(8,128)(2,1)}, u32[]{:S(2)}, u32[]{:S(2)}) collective-permute-start(bf16[256,1408]{1,0:T(8,128)(2,1)} %collective-permute-done.5.refs_5_), channel_id=1, source_target_pairs={{0,16},{8,24},{16,0},{24,8},{1,17},{9,25},{17,1},{25,9},{2,18},{10... | collective-permute-start | bytes 2162696 | tf_op jit(solution)/shard_map/ppermute | solution.py:585
  63.1 9.9 %collective-permute-start.8 = (bf16[512,512]{1,0:T(8,128)(2,1)}, bf16[512,512]{1,0:T(8,128)(2,1)}, u32[]{:S(2)}, u32[]{:S(2)}) collective-permute-start(bf16[512,512]{1,0:T(8,128)(2,1)} %get-tuple-element.55.refs_1_), channel_id=1, source_target_pairs={{0,1},{1,0},{2,3},{3,2},{4,5},{5,4},{6,7},{7,6},{8,9},{9,8},{10,11... | collective-permute-start | bytes 1572872 | tf_op jit(solution)/shard_map/ppermute | solution.py:585
  63.2 11.4 %collective-permute-start.9 = (bf16[512,512]{1,0:T(8,128)(2,1)}, bf16[512,512]{1,0:T(8,128)(2,1)}, u32[]{:S(2)}, u32[]{:S(2)}) collective-permute-start(bf16[512,512]{1,0:T(8,128)(2,1)} %get-tuple-element.56.refs_2_), channel_id=1, source_target_pairs={{0,1},{1,0},{2,3},{3,2},{4,5},{5,4},{6,7},{7,6},{8,9},{9,8},{10,11... | collective-permute-start | bytes 1572872 | tf_op jit(solution)/shard_map/ppermute | solution.py:585
  70.8 31.0 %collective-permute-start.13 = (bf16[1408,256]{1,0:T(8,128)(2,1)}, bf16[1408,256]{1,0:T(8,128)(2,1)}, u32[]{:S(2)}, u32[]{:S(2)}) collective-permute-start(bf16[1408,256]{1,0:T(8,128)(2,1)} %get-tuple-element.86), channel_id=1, source_target_pairs={{0,16},{8,24},{16,0},{24,8},{1,17},{9,25},{17,1},{25,9},{2,18},{10... | collective-permute-start | bytes 2162696 | tf_op jit(solution)/shard_map/ppermute | solution.py:585
  72.4 29.5 %collective-permute-start.14 = (bf16[1408,256]{1,0:T(8,128)(2,1)}, bf16[1408,256]{1,0:T(8,128)(2,1)}, u32[]{:S(2)}, u32[]{:S(2)}) collective-permute-start(bf16[1408,256]{1,0:T(8,128)(2,1)} %get-tuple-element.75), channel_id=1, source_target_pairs={{0,8},{8,0},{16,24},{24,16},{1,9},{9,1},{17,25},{25,17},{2,10},{10... | collective-permute-start | bytes 2162696 | tf_op jit(solution)/shard_map/ppermute | solution.py:585
  73.0 31.1 %collective-permute-start.15 = (bf16[256,1408]{1,0:T(8,128)(2,1)}, bf16[256,1408]{1,0:T(8,128)(2,1)}, u32[]{:S(2)}, u32[]{:S(2)}) collective-permute-start(bf16[256,1408]{1,0:T(8,128)(2,1)} %collective-permute-done.6.refs_7_), channel_id=1, source_target_pairs={{0,2},{2,0},{4,6},{6,4},{1,3},{3,1},{5,7},{7,5},{8,10},{10,8},{12,... | collective-permute-start | bytes 2162696 | tf_op jit(solution)/shard_map/ppermute | solution.py:585
  84.6 21.1 %collective-permute-start.16 = (bf16[256,1408]{1,0:T(8,128)(2,1)}, bf16[256,1408]{1,0:T(8,128)(2,1)S(1)}, u32[]{:S(2)}, u32[]{:S(2)}) collective-permute-start(bf16[256,1408]{1,0:T(8,128)(2,1)} %collective-permute-done.11.refs_8_), channel_id=1, source_target_pairs={{0,2},{2,0},{4,6},{6,4},{1,3},{3,1},{5,7},{7,5},{8,10},{10,8},{12,... | collective-permute-start | bytes 2162696 | tf_op jit(solution)/shard_map/ppermute | solution.py:585
  85.1 26.0 %collective-permute-start.17 = (bf16[1408,256]{1,0:T(8,128)(2,1)}, bf16[1408,256]{1,0:T(8,128)(2,1)S(1)}, u32[]{:S(2)}, u32[]{:S(2)}) collective-permute-start(bf16[1408,256]{1,0:T(8,128)(2,1)} %get-tuple-element.75), channel_id=1, source_target_pairs={{0,16},{8,24},{16,0},{24,8},{1,17},{9,25},{17,1},{25,9},{2,18},{10... | collective-permute-start | bytes 2162696 | tf_op jit(solution)/shard_map/ppermute | solution.py:585
  101.9 15.9 %collective-permute-start.19 = (bf16[1408,256]{1,0:T(8,128)(2,1)}, bf16[1408,256]{1,0:T(8,128)(2,1)S(1)}, u32[]{:S(2)}, u32[]{:S(2)}) collective-permute-start(bf16[1408,256]{1,0:T(8,128)(2,1)} %collective-permute-done.13.refs_2_), channel_id=1, source_target_pairs={{0,8},{8,0},{16,24},{24,16},{1,9},{9,1},{17,25},{25,17},{2,10},{10... | collective-permute-start | bytes 2162696 | tf_op jit(solution)/shard_map/ppermute | solution.py:585
  103.3 15.4 %collective-permute-start.20 = (bf16[1408,256]{1,0:T(8,128)(2,1)}, bf16[1408,256]{1,0:T(8,128)(2,1)S(1)}, u32[]{:S(2)}, u32[]{:S(2)}) collective-permute-start(bf16[1408,256]{1,0:T(8,128)(2,1)} %collective-permute-done.14.refs_1_), channel_id=1, source_target_pairs={{0,16},{8,24},{16,0},{24,8},{1,17},{9,25},{17,1},{25,9},{2,18},{10... | collective-permute-start | bytes 2162696 | tf_op jit(solution)/shard_map/ppermute | solution.py:585
  104.0 15.8 %collective-permute-start.21 = (bf16[1408,256]{1,0:T(8,128)(2,1)}, bf16[1408,256]{1,0:T(8,128)(2,1)S(1)}, u32[]{:S(2)}, u32[]{:S(2)}) collective-permute-start(bf16[1408,256]{1,0:T(8,128)(2,1)} %collective-permute-done.14.refs_1_), channel_id=1, source_target_pairs={{0,2},{2,0},{4,6},{6,4},{1,3},{3,1},{5,7},{7,5},{8,10},{10,8},{12,... | collective-permute-start | bytes 2162696 | tf_op jit(solution)/shard_map/ppermute | solution.py:585
  117.7 7.3 %collective-permute-start.18 = (bf16[512,1280]{1,0:T(8,128)(2,1)S(1)}, bf16[512,1280]{1,0:T(8,128)(2,1)S(1)}, u32[]{:S(2)}, u32[]{:S(2)}) collective-permute-start(bf16[512,1280]{1,0:T(8,128)(2,1)S(1)} %get-tuple-element.77), channel_id=1, source_target_pairs={{0,1},{1,0},{2,3},{3,2},{4,5},{5,4},{6,7},{7,6},{8,9},{9,8},{10,11... | collective-permute-start | bytes 3932168 | tf_op jit(solution)/shard_map/ppermute | solution.py:585
  124.2 2.4 %collective-permute-start.22 = (bf16[512,768]{1,0:T(8,128)(2,1)S(1)}, bf16[512,768]{1,0:T(8,128)(2,1)S(1)}, u32[]{:S(2)}, u32[]{:S(2)}) collective-permute-start(bf16[512,768]{1,0:T(8,128)(2,1)S(1)} %get-tuple-element.79), channel_id=1, source_target_pairs={{0,1},{1,0},{2,3},{3,2},{4,5},{5,4},{6,7},{7,6},{8,9},{9,8},{10,11... | collective-permute-start | bytes 2359304 | tf_op jit(solution)/shard_map/ppermute | solution.py:585
  (10 other events, 100.3 us)

commit v10 on v9

--- a/solution.py
+++ b/solution.py
@@ -456,14 +456,14 @@
         rows = pl.ds(first, ROWS)
         sums = widen_sums(places, pieces, feed_ref, rows)
         gate_ref[rows, :] = silu(sums[0]).astype(BF16)
-        up_ref[rows, :] = sums[1]
+        up_ref[rows, :] = sums[1].astype(BF16)
 
 
 def finish_kernel(places, feed_ref, gate_ref, up_ref, *refs):
     pieces, out_ref = refs[:-1], refs[-1]
     for first in range(0, feed_ref.shape[0], ROWS):
         rows = pl.ds(first, ROWS)
-        total = up_ref[rows, :]
+        total = up_ref[rows, :].astype(F32)
         if pieces:
             total = total + widen_sums(places, pieces, feed_ref, rows)[1]
         out_ref[rows, :] = (gate_ref[rows, :].astype(F32) * total).astype(BF16)
@@ -489,7 +489,7 @@
 
 
 def widen(feed, matrices):
-    return widen_call(widen_kernel, "widen", WIDEN_VMEM, (BF16, F32), feed, (), matrices)
+    return widen_call(widen_kernel, "widen", WIDEN_VMEM, (BF16, BF16), feed, (), matrices)
 
 
 def finish(feed, wholes, pieces):

time: 129 us -> 129 us (level)
  no operation moved by 1% of the time
where the time goes in v10:
time: 129 us; the launch traced here: 128 us
  Pallas kernels  72.5 us (56%)
  starting transfers between devices  33.4 us (26%)
  waiting for transfers between devices  14.7 us (11%)
  local copies, waits for them, and re-layouts  6.8 us (5%)
    pallas_call x2, Pallas kernels, widen_call(): pl.pallas_call(functools.partial(kernel, places), name=name, grid=(pl.cdi...  20.8 us
    ppermute x20, starting transfers between devices, swapped(): return lax.ppermute(value, axis, [(i, i ^ flip) for i in range(count)])  19.3 us
    pallas_call x1, Pallas kernels, front(): pl.pallas_call(front_kernel, name='front', grid=(count // tile,), in_spec...  14.9 us
    ppermute x3, starting transfers between devices, shifted(): lax.ppermute(value, 'seq', [(i, i + steps) for i in range(count - steps)])  14.1 us
    pallas_call x2, Pallas kernels, narrow(): pl.pallas_call(functools.partial(narrow_kernel, block), name='narrow', in...  11 us
    pallas_call x1, Pallas kernels, mix(): pl.pallas_call(lambda s, *refs: mix_kernel(*refs), name='mix', grid_spec=...  9.98 us
    ppermute x20, waiting for transfers between devices, swapped(): return lax.ppermute(value, axis, [(i, i ^ flip) for i in range(count)])  9.87 us
    pallas_call x1, Pallas kernels, query(): pl.pallas_call(query_kernel, name='query', grid=(count // tile,), in_spec...  7 us
  transfers between devices with their start and end apart: 23, of which 9 were waited for; matrix products, arithmetic and copies ran while one was open for 4% of the time, Pallas kernels for 55%

profile of v10, /device:TPU:0, one launch (start us, length us, event | category | flops | bytes accessed | tf_op | source)
XLA Modules:
  0.0 128.3 jit_solution(17200673484608060056)
XLA Ops:
  1.1 2.6 %collective-permute-start.2 = (bf16[512,1408]{1,0:T(8,128)(2,1)}, bf16[512,1408]{1,0:T(8,128)(2,1)S(1)}, u32[]{:S(2)}, u32[]{:S(2)}) collective-permute-start(bf16[512,1408]{1,0:T(8,128)(2,1)} %refs_0_.4), channel_id=1, source_target_pairs={{0,8},{8,0},{16,24},{24,16},{1,9},{9,1},{17,25},{25,17},{2,10},{10... | collective-permute-start | bytes 4325384 | tf_op jit(solution)/shard_map/ppermute | solution.py:585
  3.7 1.5 %collective-permute-start.3 = (bf16[512,1408]{1,0:T(8,128)(2,1)}, bf16[512,1408]{1,0:T(8,128)(2,1)}, u32[]{:S(2)}, u32[]{:S(2)}) collective-permute-start(bf16[512,1408]{1,0:T(8,128)(2,1)} %refs_0_.4), channel_id=1, source_target_pairs={{0,16},{8,24},{16,0},{24,8},{1,17},{9,25},{17,1},{25,9},{2,18},{10... | collective-permute-start | bytes 4325384 | tf_op jit(solution)/shard_map/ppermute | solution.py:585
  5.2 1.5 %slice.3 = bf16[16,2048]{1,0:T(8,128)(2,1)} slice(bf16[1024,2048]{1,0:T(8,128)(2,1)} %refs_0_.3), slice={[1008:1024], [0:2048]} | slice | bytes 131072 | tf_op jit(solution)/shard_map/slice | solution.py:612
  6.7 4.1 %collective-permute-start = (bf16[16,2048]{1,0:T(8,128)(2,1)}, bf16[16,2048]{1,0:T(8,128)(2,1)}, u32[]{:S(2)}, u32[]{:S(2)}) collective-permute-start(bf16[16,2048]{1,0:T(8,128)(2,1)} %slice.3), channel_id=1, source_target_pairs={{0,2},{2,4},{4,6},{1,3},{3,5},{5,7},{8,10},{10,12},{12,14},{9,11},... | collective-permute-start | bytes 196616 | tf_op jit(solution)/shard_map/ppermute | solution.py:580
  13.7 14.9 %front.1 = (bf16[1024,2048]{1,0:T(8,128)(2,1)S(1)}, f32[1024,256]{1,0:T(8,128)S(1)}, bf16[1024,256]{1,0:T(8,128)(2,1)S(1)}, bf16[1024,256]{1,0:T(8,128)(2,1)S(1)...) custom-call(s32[1,16]{1,0:T(1,128)S(1)} %copy-done.4, ...), custom_call_target="tpu_custom_call" | custom-call | flops 1000 | bytes 1000 | tf_op jit(solution)/shard_map/front/pallas_call | solution.py:214
  28.6 4.4 %collective-permute-start.4 = (bf16[272,512]{1,0:T(8,128)(2,1)S(1)}, bf16[272,512]{1,0:T(8,128)(2,1)S(1)}, u32[]{:S(2)}, u32[]{:S(2)}) collective-permute-start(bf16[272,512]{1,0:T(8,128)(2,1)S(1)} %get-tuple-element.45.later_ref), channel_id=1, source_target_pairs={{0,2},{2,4},{4,6},{1,3},{3,5},{5,7},{8,10},{10,12},{12,14},{9,11},... | collective-permute-start | bytes 835592 | tf_op jit(solution)/shard_map/ppermute | solution.py:580
  34.3 3.9 %collective-permute-done.4.earlier_ref.one_ref = bf16[272,512]{1,0:T(8,128)(2,1)S(1)} collective-permute-done((bf16[272,512]{1,0:T(8,128)(2,1)S(1)}, bf16[272,512]{1,0:T(8,128)(2,1)S(1)}, u32[]{:S(2)}, u32[]{:S(2)}) %collective-permute-start.4) | collective-permute-done | bytes 278560 | tf_op jit(solution)/shard_map/ppermute | solution.py:580
  39.0 5.6 %collective-permute-start.7 = (bf16[272,512]{1,0:T(8,128)(2,1)S(1)}, bf16[272,512]{1,0:T(8,128)(2,1)S(1)}, u32[]{:S(2)}, u32[]{:S(2)}) collective-permute-start(bf16[272,512]{1,0:T(8,128)(2,1)S(1)} %joined.1), channel_id=1, source_target_pairs={{0,4},{2,6},{1,5},{3,7},{8,12},{10,14},{9,13},{11,15},{16,20},{18,... | collective-permute-start | bytes 835592 | tf_op jit(solution)/shard_map/ppermute | solution.py:580
  44.6 7.0 %query.1 = (bf16[1024,256]{1,0:T(8,128)(2,1)S(1)}, bf16[16,3,256]{2,1,0:T(4,128)(2,1)S(1)}, bf16[1024,512]{1,0:T(8,128)(2,1)S(1)}) custom-call(s32[1,16]{1,0:T(1,128)S(1)} %copy-done.5, s32[1,16]{1,0:T(1,128)S(1)} %copy-done.7, bf16[1024,2048]{1,0:T(8,128)(2,1)S(1)} %get-tuple-element.46.normed_ref, bf16[16,2048]{1,0:T(8,128)(2,1)} %collective-permute-done.rim_ref, ...), custom_call_target="tpu_custom_call" | custom-call | flops 3221225472 | bytes 4194304 | tf_op jit(solution)/shard_map/query/pallas_call | solution.py:279
  53.1 1.6 %collective-permute-start.10 = (bf16[256,1408]{1,0:T(8,128)(2,1)}, bf16[256,1408]{1,0:T(8,128)(2,1)}, u32[]{:S(2)}, u32[]{:S(2)}) collective-permute-start(bf16[256,1408]{1,0:T(8,128)(2,1)} %collective-permute-done.5.refs_5_), channel_id=1, source_target_pairs={{0,2},{2,0},{4,6},{6,4},{1,3},{3,1},{5,7},{7,5},{8,10},{10,8},{12,... | collective-permute-start | bytes 2162696 | tf_op jit(solution)/shard_map/ppermute | solution.py:585
  54.7 1.5 %collective-permute-start.11 = (bf16[256,1408]{1,0:T(8,128)(2,1)}, bf16[256,1408]{1,0:T(8,128)(2,1)}, u32[]{:S(2)}, u32[]{:S(2)}) collective-permute-start(bf16[256,1408]{1,0:T(8,128)(2,1)} %collective-permute-done.5.refs_5_), channel_id=1, source_target_pairs={{0,16},{8,24},{16,0},{24,8},{1,17},{9,25},{17,1},{25,9},{2,18},{10... | collective-permute-start | bytes 2162696 | tf_op jit(solution)/shard_map/ppermute | solution.py:585
  56.2 6.9 %pages.1 = (bf16[16,1,256,512]{3,2,1,0:T(8,128)(2,1)}, bf16[512,512]{1,0:T(8,128)(2,1)}, bf16[512,512]{1,0:T(8,128)(2,1)}) custom-call(s32[1,16]{1,0:T(1,128)S(1)} %copy-done.5, s32[1,16]{1,0:T(1,128)S(1)} %copy-done.7, bf16[1024,256]{1,0:T(8,128)(2,1)S(1)} %get-tuple-element.49.raised_ref, bf16[1024,256]{1,0:T(8,128)(2,1)S(1)} %get-tuple-element.50.lowered_ref, ...), custom_call_target="tpu_custom_call" | custom-call | flops 1000 | bytes 1000 | tf_op jit(solution)/shard_map/pages/pallas_call | solution.py:370
  63.7 2.5 %constant_dynamic-slice_fusion = (bf16[1408,256]{1,0:T(8,128)(2,1)}, bf16[1408,256]{1,0:T(8,128)(2,1)}) fusion(bf16[1408,512]{1,0:T(8,128)(2,1)} %refs_0_.5, s32[]{:T(128)S(6)} %select_n.8, s32[]{:T(128)S(6)} %select_n.7), kind=kLoop, calls=%fused_computation.1 | loop fusion | bytes 2883592 | tf_op jit(solution)/shard_map/dynamic_slice | solution.py:624
  66.2 4.6 %collective-permute-done.10.refs_6_ = bf16[256,1408]{1,0:T(8,128)(2,1)} collective-permute-done((bf16[256,1408]{1,0:T(8,128)(2,1)}, bf16[256,1408]{1,0:T(8,128)(2,1)}, u32[]{:S(2)}, u32[]{:S(2)}) %collective-permute-start.10) | collective-permute-done | bytes 720928 | tf_op jit(solution)/shard_map/ppermute | solution.py:585
  70.8 1.5 %collective-permute-start.13 = (bf16[1408,256]{1,0:T(8,128)(2,1)}, bf16[1408,256]{1,0:T(8,128)(2,1)}, u32[]{:S(2)}, u32[]{:S(2)}) collective-permute-start(bf16[1408,256]{1,0:T(8,128)(2,1)} %get-tuple-element.86), channel_id=1, source_target_pairs={{0,16},{8,24},{16,0},{24,8},{1,17},{9,25},{17,1},{25,9},{2,18},{10... | collective-permute-start | bytes 2162696 | tf_op jit(solution)/shard_map/ppermute | solution.py:585
  73.0 1.6 %collective-permute-start.15 = (bf16[256,1408]{1,0:T(8,128)(2,1)}, bf16[256,1408]{1,0:T(8,128)(2,1)}, u32[]{:S(2)}, u32[]{:S(2)}) collective-permute-start(bf16[256,1408]{1,0:T(8,128)(2,1)} %collective-permute-done.6.refs_7_), channel_id=1, source_target_pairs={{0,2},{2,0},{4,6},{6,4},{1,3},{3,1},{5,7},{7,5},{8,10},{10,8},{12,... | collective-permute-start | bytes 2162696 | tf_op jit(solution)/shard_map/ppermute | solution.py:585
  74.6 10.0 %mix.1 = (bf16[512,2048]{1,0:T(8,128)(2,1)S(1)}, bf16[1024,2048]{1,0:T(8,128)(2,1)S(1)}) custom-call(s32[1]{0:T(128)} %bitcast.s, bf16[1024,2048]{1,0:T(8,128)(2,1)} %refs_0_.3, bf16[512,512]{1,0:T(8,128)(2,1)} %get-tuple-element.55.refs_1_, bf16[512,512]{1,0:T(8,128)(2,1)} %get-tuple-element.56.refs_2_, bf16[512,512]{1,0:T(8,128)(2,1)} %collective-permute-done.8.refs_3_, ...), custom_call_target="tpu_custom_call" | custom-call | flops 1000 | bytes 1000 | tf_op jit(solution)/shard_map/mix/pallas_call | solution.py:426
  86.4 15.4 %widen.1 = (bf16[1024,1408]{1,0:T(8,128)(2,1)S(1)}, bf16[1024,1408]{1,0:T(8,128)(2,1)S(1)}) custom-call(bf16[1024,2048]{1,0:T(8,128)(2,1)S(1)} %get-tuple-element.63.feed_ref, bf16[512,1408]{1,0:T(8,128)(2,1)} %refs_0_.4, bf16[512,1408]{1,0:T(8,128)(2,1)S(1)} %collective-permute-done.2.refs_1_, bf16[512,1408]{1,0:T(8,128)(2,1)} %collective-permute-done.3.refs_2_, ...), custom_call_target="tpu_custom_call" | custom-call | flops 1000 | bytes 1000 | tf_op jit(solution)/shard_map/widen/pallas_call | solution.py:478
  103.9 1.6 %collective-permute-start.21 = (bf16[1408,256]{1,0:T(8,128)(2,1)}, bf16[1408,256]{1,0:T(8,128)(2,1)S(1)}, u32[]{:S(2)}, u32[]{:S(2)}) collective-permute-start(bf16[1408,256]{1,0:T(8,128)(2,1)} %collective-permute-done.14.refs_1_), channel_id=1, source_target_pairs={{0,2},{2,0},{4,6},{6,4},{1,3},{3,1},{5,7},{7,5},{8,10},{10,8},{12,... | collective-permute-start | bytes 2162696 | tf_op jit(solution)/shard_map/ppermute | solution.py:585
  105.5 5.4 %finish.1.hidden_hbm = bf16[1024,1408]{1,0:T(8,128)(2,1)S(1)} custom-call(bf16[1024,2048]{1,0:T(8,128)(2,1)S(1)} %get-tuple-element.63.feed_ref, bf16[1024,1408]{1,0:T(8,128)(2,1)S(1)} %get-tuple-element.71.gate_ref, bf16[1024,1408]{1,0:T(8,128)(2,1)S(1)} %get-tuple-element.72.up_ref, bf16[256,1408]{1,0:T(8,128)(2,1)} %collective-permute-done.15.refs_0_, ...), custom_call_target="tpu_custom_call" | custom-call | flops 1000 | bytes 1000 | tf_op jit(solution)/shard_map/finish/pallas_call | solution.py:478
  110.9 6.7 %narrow.2 = (bf16[512,1280]{1,0:T(8,128)(2,1)S(1)}, bf16[512,1280]{1,0:T(8,128)(2,1)S(1)}) custom-call(bf16[1024,1408]{1,0:T(8,128)(2,1)S(1)} %finish.1.hidden_hbm, bf16[1408,512]{1,0:T(8,128)(2,1)} %refs_0_.5, bf16[1408,256]{1,0:T(8,128)(2,1)} %collective-permute-done.14.refs_1_, bf16[1408,256]{1,0:T(8,128)(2,1)} %collective-permute-done.13.refs_2_, ...), custom_call_target="tpu_custom_call" | custom-call | flops 1000 | bytes 1000 | tf_op jit(solution)/shard_map/narrow/pallas_call | solution.py:537
  119.8 4.4 %narrow.3 = (bf16[512,768]{1,0:T(8,128)(2,1)S(1)}, bf16[512,768]{1,0:T(8,128)(2,1)S(1)}) custom-call(bf16[1024,1408]{1,0:T(8,128)(2,1)S(1)} %finish.1.hidden_hbm, bf16[1408,256]{1,0:T(8,128)(2,1)S(1)} %collective-permute-done.19.refs_0_, bf16[1408,256]{1,0:T(8,128)(2,1)S(1)} %collective-permute-done.20.refs_1_, ...), custom_call_target="tpu_custom_call" | custom-call | flops 1000 | bytes 1000 | tf_op jit(solution)/shard_map/narrow/pallas_call | solution.py:537
  125.1 1.5 %collective-permute-done.22.refs_3_ = bf16[512,768]{1,0:T(8,128)(2,1)S(1)} collective-permute-done((bf16[512,768]{1,0:T(8,128)(2,1)S(1)}, bf16[512,768]{1,0:T(8,128)(2,1)S(1)}, u32[]{:S(2)}, u32[]{:S(2)}) %collective-permute-start.22) | collective-permute-done | bytes 786464 | tf_op jit(solution)/shard_map/ppermute | solution.py:585
  126.6 1.8 %close.1 = bf16[512,2048]{1,0:T(8,128)(2,1)} custom-call(bf16[512,2048]{1,0:T(8,128)(2,1)S(1)} %get-tuple-element.61.residual_ref, bf16[512,1280]{1,0:T(8,128)(2,1)S(1)} %get-tuple-element.76.refs_0_, bf16[512,1280]{1,0:T(8,128)(2,1)S(1)} %collective-permute-done.18.refs_1_, bf16[512,768]{1,0:T(8,128)(2,1)S(1)} %get-tuple-element.78.refs_2_, ...), custom_call_target="tpu_custom_call" | custom-call | flops 1000 | bytes 1000 | tf_op jit(solution)/shard_map/close/pallas_call | solution.py:566
  (62 shorter events, 15.1 us)
Async XLA Ops:
  0.6 11.8 %collective-permute-start.1 = (bf16[512,2048]{1,0:T(8,128)(2,1)}, bf16[512,2048]{1,0:T(8,128)(2,1)S(1)}, u32[]{:S(2)}, u32[]{:S(2)}) collective-permute-start(bf16[512,2048]{1,0:T(8,128)(2,1)} %refs_5_.1), channel_id=1, source_target_pairs={{0,1},{1,0},{2,3},{3,2},{4,5},{5,4},{6,7},{7,6},{8,9},{9,8},{10,11... | collective-permute-start | bytes 6291464 | tf_op jit(solution)/shard_map/ppermute | solution.py:585
  1.1 37.2 %collective-permute-start.2 = (bf16[512,1408]{1,0:T(8,128)(2,1)}, bf16[512,1408]{1,0:T(8,128)(2,1)S(1)}, u32[]{:S(2)}, u32[]{:S(2)}) collective-permute-start(bf16[512,1408]{1,0:T(8,128)(2,1)} %refs_0_.4), channel_id=1, source_target_pairs={{0,8},{8,0},{16,24},{24,16},{1,9},{9,1},{17,25},{25,17},{2,10},{10... | collective-permute-start | bytes 4325384 | tf_op jit(solution)/shard_map/ppermute | solution.py:585
  3.7 34.7 %collective-permute-start.3 = (bf16[512,1408]{1,0:T(8,128)(2,1)}, bf16[512,1408]{1,0:T(8,128)(2,1)}, u32[]{:S(2)}, u32[]{:S(2)}) collective-permute-start(bf16[512,1408]{1,0:T(8,128)(2,1)} %refs_0_.4), channel_id=1, source_target_pairs={{0,16},{8,24},{16,0},{24,8},{1,17},{9,25},{17,1},{25,9},{2,18},{10... | collective-permute-start | bytes 4325384 | tf_op jit(solution)/shard_map/ppermute | solution.py:585
  6.7 5.7 %collective-permute-start = (bf16[16,2048]{1,0:T(8,128)(2,1)}, bf16[16,2048]{1,0:T(8,128)(2,1)}, u32[]{:S(2)}, u32[]{:S(2)}) collective-permute-start(bf16[16,2048]{1,0:T(8,128)(2,1)} %slice.3), channel_id=1, source_target_pairs={{0,2},{2,4},{4,6},{1,3},{3,5},{5,7},{8,10},{10,12},{12,14},{9,11},... | collective-permute-start | bytes 196616 | tf_op jit(solution)/shard_map/ppermute | solution.py:580
  28.6 23.0 %copy-start = (bf16[16,3,768]{2,1,0:T(4,128)(2,1)}, bf16[16,3,768]{2,1,0:T(4,128)(2,1)S(1)}, u32[]{:S(2)}) copy-start(bf16[16,3,768]{2,1,0:T(4,128)(2,1)S(1)} %get-tuple-element.82) | copy-start | bytes 221188
  28.6 9.5 %collective-permute-start.4 = (bf16[272,512]{1,0:T(8,128)(2,1)S(1)}, bf16[272,512]{1,0:T(8,128)(2,1)S(1)}, u32[]{:S(2)}, u32[]{:S(2)}) collective-permute-start(bf16[272,512]{1,0:T(8,128)(2,1)S(1)} %get-tuple-element.45.later_ref), channel_id=1, source_target_pairs={{0,2},{2,4},{4,6},{1,3},{3,5},{5,7},{8,10},{10,12},{12,14},{9,11},... | collective-permute-start | bytes 835592 | tf_op jit(solution)/shard_map/ppermute | solution.py:580
  33.1 19.2 %collective-permute-start.5 = (bf16[256,1408]{1,0:T(8,128)(2,1)S(1)}, bf16[256,1408]{1,0:T(8,128)(2,1)}, u32[]{:S(2)}, u32[]{:S(2)}) collective-permute-start(bf16[256,1408]{1,0:T(8,128)(2,1)S(1)} %constant_dynamic-slice_fusion.2), channel_id=1, source_target_pairs={{0,8},{8,0},{16,24},{24,16},{1,9},{9,1},{17,25},{25,17},{2,10},{10... | collective-permute-start | bytes 2162696 | tf_op jit(solution)/shard_map/ppermute | solution.py:585
  33.8 19.4 %collective-permute-start.6 = (bf16[256,1408]{1,0:T(8,128)(2,1)S(1)}, bf16[256,1408]{1,0:T(8,128)(2,1)}, u32[]{:S(2)}, u32[]{:S(2)}) collective-permute-start(bf16[256,1408]{1,0:T(8,128)(2,1)S(1)} %constant_dynamic-slice_fusion.2), channel_id=1, source_target_pairs={{0,16},{8,24},{16,0},{24,8},{1,17},{9,25},{17,1},{25,9},{2,18},{10... | collective-permute-start | bytes 2162696 | tf_op jit(solution)/shard_map/ppermute | solution.py:585
  38.5 46.6 %collective-permute-start.12 = (bf16[512,1408]{1,0:T(8,128)(2,1)}, bf16[512,1408]{1,0:T(8,128)(2,1)}, u32[]{:S(2)}, u32[]{:S(2)}) collective-permute-start(bf16[512,1408]{1,0:T(8,128)(2,1)} %collective-permute-done.3.refs_2_), channel_id=1, source_target_pairs={{0,8},{8,0},{16,24},{24,16},{1,9},{9,1},{17,25},{25,17},{2,10},{10... | collective-permute-start | bytes 4325384 | tf_op jit(solution)/shard_map/ppermute | solution.py:585
  39.0 17.2 %collective-permute-start.7 = (bf16[272,512]{1,0:T(8,128)(2,1)S(1)}, bf16[272,512]{1,0:T(8,128)(2,1)S(1)}, u32[]{:S(2)}, u32[]{:S(2)}) collective-permute-start(bf16[272,512]{1,0:T(8,128)(2,1)S(1)} %joined.1), channel_id=1, source_target_pairs={{0,4},{2,6},{1,5},{3,7},{8,12},{10,14},{9,13},{11,15},{16,20},{18,... | collective-permute-start | bytes 835592 | tf_op jit(solution)/shard_map/ppermute | solution.py:580
  53.1 17.7 %collective-permute-start.10 = (bf16[256,1408]{1,0:T(8,128)(2,1)}, bf16[256,1408]{1,0:T(8,128)(2,1)}, u32[]{:S(2)}, u32[]{:S(2)}) collective-permute-start(bf16[256,1408]{1,0:T(8,128)(2,1)} %collective-permute-done.5.refs_5_), channel_id=1, source_target_pairs={{0,2},{2,0},{4,6},{6,4},{1,3},{3,1},{5,7},{7,5},{8,10},{10,8},{12,... | collective-permute-start | bytes 2162696 | tf_op jit(solution)/shard_map/ppermute | solution.py:585
  54.7 17.6 %collective-permute-start.11 = (bf16[256,1408]{1,0:T(8,128)(2,1)}, bf16[256,1408]{1,0:T(8,128)(2,1)}, u32[]{:S(2)}, u32[]{:S(2)}) collective-permute-start(bf16[256,1408]{1,0:T(8,128)(2,1)} %collective-permute-done.5.refs_5_), channel_id=1, source_target_pairs={{0,16},{8,24},{16,0},{24,8},{1,17},{9,25},{17,1},{25,9},{2,18},{10... | collective-permute-start | bytes 2162696 | tf_op jit(solution)/shard_map/ppermute | solution.py:585
  63.1 9.9 %collective-permute-start.8 = (bf16[512,512]{1,0:T(8,128)(2,1)}, bf16[512,512]{1,0:T(8,128)(2,1)}, u32[]{:S(2)}, u32[]{:S(2)}) collective-permute-start(bf16[512,512]{1,0:T(8,128)(2,1)} %get-tuple-element.55.refs_1_), channel_id=1, source_target_pairs={{0,1},{1,0},{2,3},{3,2},{4,5},{5,4},{6,7},{7,6},{8,9},{9,8},{10,11... | collective-permute-start | bytes 1572872 | tf_op jit(solution)/shard_map/ppermute | solution.py:585
  63.2 11.4 %collective-permute-start.9 = (bf16[512,512]{1,0:T(8,128)(2,1)}, bf16[512,512]{1,0:T(8,128)(2,1)}, u32[]{:S(2)}, u32[]{:S(2)}) collective-permute-start(bf16[512,512]{1,0:T(8,128)(2,1)} %get-tuple-element.56.refs_2_), channel_id=1, source_target_pairs={{0,1},{1,0},{2,3},{3,2},{4,5},{5,4},{6,7},{7,6},{8,9},{9,8},{10,11... | collective-permute-start | bytes 1572872 | tf_op jit(solution)/shard_map/ppermute | solution.py:585
  70.8 30.9 %collective-permute-start.13 = (bf16[1408,256]{1,0:T(8,128)(2,1)}, bf16[1408,256]{1,0:T(8,128)(2,1)}, u32[]{:S(2)}, u32[]{:S(2)}) collective-permute-start(bf16[1408,256]{1,0:T(8,128)(2,1)} %get-tuple-element.86), channel_id=1, source_target_pairs={{0,16},{8,24},{16,0},{24,8},{1,17},{9,25},{17,1},{25,9},{2,18},{10... | collective-permute-start | bytes 2162696 | tf_op jit(solution)/shard_map/ppermute | solution.py:585
  72.4 29.4 %collective-permute-start.14 = (bf16[1408,256]{1,0:T(8,128)(2,1)}, bf16[1408,256]{1,0:T(8,128)(2,1)}, u32[]{:S(2)}, u32[]{:S(2)}) collective-permute-start(bf16[1408,256]{1,0:T(8,128)(2,1)} %get-tuple-element.75), channel_id=1, source_target_pairs={{0,8},{8,0},{16,24},{24,16},{1,9},{9,1},{17,25},{25,17},{2,10},{10... | collective-permute-start | bytes 2162696 | tf_op jit(solution)/shard_map/ppermute | solution.py:585
  73.0 31.0 %collective-permute-start.15 = (bf16[256,1408]{1,0:T(8,128)(2,1)}, bf16[256,1408]{1,0:T(8,128)(2,1)}, u32[]{:S(2)}, u32[]{:S(2)}) collective-permute-start(bf16[256,1408]{1,0:T(8,128)(2,1)} %collective-permute-done.6.refs_7_), channel_id=1, source_target_pairs={{0,2},{2,0},{4,6},{6,4},{1,3},{3,1},{5,7},{7,5},{8,10},{10,8},{12,... | collective-permute-start | bytes 2162696 | tf_op jit(solution)/shard_map/ppermute | solution.py:585
  84.6 21.0 %collective-permute-start.16 = (bf16[256,1408]{1,0:T(8,128)(2,1)}, bf16[256,1408]{1,0:T(8,128)(2,1)S(1)}, u32[]{:S(2)}, u32[]{:S(2)}) collective-permute-start(bf16[256,1408]{1,0:T(8,128)(2,1)} %collective-permute-done.11.refs_8_), channel_id=1, source_target_pairs={{0,2},{2,0},{4,6},{6,4},{1,3},{3,1},{5,7},{7,5},{8,10},{10,8},{12,... | collective-permute-start | bytes 2162696 | tf_op jit(solution)/shard_map/ppermute | solution.py:585
  85.1 25.9 %collective-permute-start.17 = (bf16[1408,256]{1,0:T(8,128)(2,1)}, bf16[1408,256]{1,0:T(8,128)(2,1)S(1)}, u32[]{:S(2)}, u32[]{:S(2)}) collective-permute-start(bf16[1408,256]{1,0:T(8,128)(2,1)} %get-tuple-element.75), channel_id=1, source_target_pairs={{0,16},{8,24},{16,0},{24,8},{1,17},{9,25},{17,1},{25,9},{2,18},{10... | collective-permute-start | bytes 2162696 | tf_op jit(solution)/shard_map/ppermute | solution.py:585
  101.8 15.9 %collective-permute-start.19 = (bf16[1408,256]{1,0:T(8,128)(2,1)}, bf16[1408,256]{1,0:T(8,128)(2,1)S(1)}, u32[]{:S(2)}, u32[]{:S(2)}) collective-permute-start(bf16[1408,256]{1,0:T(8,128)(2,1)} %collective-permute-done.13.refs_2_), channel_id=1, source_target_pairs={{0,8},{8,0},{16,24},{24,16},{1,9},{9,1},{17,25},{25,17},{2,10},{10... | collective-permute-start | bytes 2162696 | tf_op jit(solution)/shard_map/ppermute | solution.py:585
  103.2 15.4 %collective-permute-start.20 = (bf16[1408,256]{1,0:T(8,128)(2,1)}, bf16[1408,256]{1,0:T(8,128)(2,1)S(1)}, u32[]{:S(2)}, u32[]{:S(2)}) collective-permute-start(bf16[1408,256]{1,0:T(8,128)(2,1)} %collective-permute-done.14.refs_1_), channel_id=1, source_target_pairs={{0,16},{8,24},{16,0},{24,8},{1,17},{9,25},{17,1},{25,9},{2,18},{10... | collective-permute-start | bytes 2162696 | tf_op jit(solution)/shard_map/ppermute | solution.py:585
  103.9 15.9 %collective-permute-start.21 = (bf16[1408,256]{1,0:T(8,128)(2,1)}, bf16[1408,256]{1,0:T(8,128)(2,1)S(1)}, u32[]{:S(2)}, u32[]{:S(2)}) collective-permute-start(bf16[1408,256]{1,0:T(8,128)(2,1)} %collective-permute-done.14.refs_1_), channel_id=1, source_target_pairs={{0,2},{2,0},{4,6},{6,4},{1,3},{3,1},{5,7},{7,5},{8,10},{10,8},{12,... | collective-permute-start | bytes 2162696 | tf_op jit(solution)/shard_map/ppermute | solution.py:585
  117.6 7.4 %collective-permute-start.18 = (bf16[512,1280]{1,0:T(8,128)(2,1)S(1)}, bf16[512,1280]{1,0:T(8,128)(2,1)S(1)}, u32[]{:S(2)}, u32[]{:S(2)}) collective-permute-start(bf16[512,1280]{1,0:T(8,128)(2,1)S(1)} %get-tuple-element.77), channel_id=1, source_target_pairs={{0,1},{1,0},{2,3},{3,2},{4,5},{5,4},{6,7},{7,6},{8,9},{9,8},{10,11... | collective-permute-start | bytes 3932168 | tf_op jit(solution)/shard_map/ppermute | solution.py:585
  124.2 2.4 %collective-permute-start.22 = (bf16[512,768]{1,0:T(8,128)(2,1)S(1)}, bf16[512,768]{1,0:T(8,128)(2,1)S(1)}, u32[]{:S(2)}, u32[]{:S(2)}) collective-permute-start(bf16[512,768]{1,0:T(8,128)(2,1)S(1)} %get-tuple-element.79), channel_id=1, source_target_pairs={{0,1},{1,0},{2,3},{3,2},{4,5},{5,4},{6,7},{7,6},{8,9},{9,8},{10,11... | collective-permute-start | bytes 2359304 | tf_op jit(solution)/shard_map/ppermute | solution.py:585
  (10 other events, 100.5 us)

commit v11 on v9

--- a/solution.py
+++ b/solution.py
@@ -668,7 +668,7 @@
 
     groups = []
     for pieces in down_lists:
-        theirs, mine = narrow(hidden, [piece for piece, _ in pieces], ROWS)
+        theirs, mine = narrow(hidden, [piece for piece, _ in pieces], ROWS // 2)
         received = swapped(theirs, "hid", 1)
         groups.append((mine, received, [(piece.shape[1], place) for piece, place in pieces]))
     result = close(residual, groups)

time: 129 us -> 129 us (level)
  no operation moved by 1% of the time
where the time goes in v11:
time: 129 us; the launch traced here: 128 us
  Pallas kernels  72.6 us (56%)
  starting transfers between devices  33.4 us (26%)
  waiting for transfers between devices  14.6 us (11%)
  local copies, waits for them, and re-layouts  6.8 us (5%)
    pallas_call x2, Pallas kernels, widen_call(): pl.pallas_call(functools.partial(kernel, places), name=name, grid=(pl.cdi...  20.9 us
    ppermute x20, starting transfers between devices, swapped(): return lax.ppermute(value, axis, [(i, i ^ flip) for i in range(count)])  19.3 us
    pallas_call x1, Pallas kernels, front(): pl.pallas_call(front_kernel, name='front', grid=(count // tile,), in_spec...  14.9 us
    ppermute x3, starting transfers between devices, shifted(): lax.ppermute(value, 'seq', [(i, i + steps) for i in range(count - steps)])  14.1 us
    pallas_call x2, Pallas kernels, narrow(): pl.pallas_call(functools.partial(narrow_kernel, block), name='narrow', in...  11 us
    pallas_call x1, Pallas kernels, mix(): pl.pallas_call(lambda s, *refs: mix_kernel(*refs), name='mix', grid_spec=...  9.98 us
    ppermute x20, waiting for transfers between devices, swapped(): return lax.ppermute(value, axis, [(i, i ^ flip) for i in range(count)])  9.77 us
    pallas_call x1, Pallas kernels, query(): pl.pallas_call(query_kernel, name='query', grid=(count // tile,), in_spec...  7 us
  transfers between devices with their start and end apart: 23, of which 9 were waited for; matrix products, arithmetic and copies ran while one was open for 4% of the time, Pallas kernels for 55%

profile of v11, /device:TPU:0, one launch (start us, length us, event | category | flops | bytes accessed | tf_op | source)
XLA Modules:
  0.0 128.3 jit_solution(18192701171367821386)
XLA Ops:
  1.1 2.6 %collective-permute-start.2 = (bf16[512,1408]{1,0:T(8,128)(2,1)}, bf16[512,1408]{1,0:T(8,128)(2,1)S(1)}, u32[]{:S(2)}, u32[]{:S(2)}) collective-permute-start(bf16[512,1408]{1,0:T(8,128)(2,1)} %refs_0_.4), channel_id=1, source_target_pairs={{0,8},{8,0},{16,24},{24,16},{1,9},{9,1},{17,25},{25,17},{2,10},{10... | collective-permute-start | bytes 4325384 | tf_op jit(solution)/shard_map/ppermute | solution.py:585
  3.7 1.5 %collective-permute-start.3 = (bf16[512,1408]{1,0:T(8,128)(2,1)}, bf16[512,1408]{1,0:T(8,128)(2,1)}, u32[]{:S(2)}, u32[]{:S(2)}) collective-permute-start(bf16[512,1408]{1,0:T(8,128)(2,1)} %refs_0_.4), channel_id=1, source_target_pairs={{0,16},{8,24},{16,0},{24,8},{1,17},{9,25},{17,1},{25,9},{2,18},{10... | collective-permute-start | bytes 4325384 | tf_op jit(solution)/shard_map/ppermute | solution.py:585
  5.2 1.5 %slice.3 = bf16[16,2048]{1,0:T(8,128)(2,1)} slice(bf16[1024,2048]{1,0:T(8,128)(2,1)} %refs_0_.3), slice={[1008:1024], [0:2048]} | slice | bytes 131072 | tf_op jit(solution)/shard_map/slice | solution.py:612
  6.7 4.1 %collective-permute-start = (bf16[16,2048]{1,0:T(8,128)(2,1)}, bf16[16,2048]{1,0:T(8,128)(2,1)}, u32[]{:S(2)}, u32[]{:S(2)}) collective-permute-start(bf16[16,2048]{1,0:T(8,128)(2,1)} %slice.3), channel_id=1, source_target_pairs={{0,2},{2,4},{4,6},{1,3},{3,5},{5,7},{8,10},{10,12},{12,14},{9,11},... | collective-permute-start | bytes 196616 | tf_op jit(solution)/shard_map/ppermute | solution.py:580
  13.7 14.9 %front.1 = (bf16[1024,2048]{1,0:T(8,128)(2,1)S(1)}, f32[1024,256]{1,0:T(8,128)S(1)}, bf16[1024,256]{1,0:T(8,128)(2,1)S(1)}, bf16[1024,256]{1,0:T(8,128)(2,1)S(1)...) custom-call(s32[1,16]{1,0:T(1,128)S(1)} %copy-done.4, ...), custom_call_target="tpu_custom_call" | custom-call | flops 1000 | bytes 1000 | tf_op jit(solution)/shard_map/front/pallas_call | solution.py:214
  28.6 4.4 %collective-permute-start.4 = (bf16[272,512]{1,0:T(8,128)(2,1)S(1)}, bf16[272,512]{1,0:T(8,128)(2,1)S(1)}, u32[]{:S(2)}, u32[]{:S(2)}) collective-permute-start(bf16[272,512]{1,0:T(8,128)(2,1)S(1)} %get-tuple-element.45.later_ref), channel_id=1, source_target_pairs={{0,2},{2,4},{4,6},{1,3},{3,5},{5,7},{8,10},{10,12},{12,14},{9,11},... | collective-permute-start | bytes 835592 | tf_op jit(solution)/shard_map/ppermute | solution.py:580
  34.3 3.9 %collective-permute-done.4.earlier_ref.one_ref = bf16[272,512]{1,0:T(8,128)(2,1)S(1)} collective-permute-done((bf16[272,512]{1,0:T(8,128)(2,1)S(1)}, bf16[272,512]{1,0:T(8,128)(2,1)S(1)}, u32[]{:S(2)}, u32[]{:S(2)}) %collective-permute-start.4) | collective-permute-done | bytes 278560 | tf_op jit(solution)/shard_map/ppermute | solution.py:580
  39.0 5.6 %collective-permute-start.7 = (bf16[272,512]{1,0:T(8,128)(2,1)S(1)}, bf16[272,512]{1,0:T(8,128)(2,1)S(1)}, u32[]{:S(2)}, u32[]{:S(2)}) collective-permute-start(bf16[272,512]{1,0:T(8,128)(2,1)S(1)} %joined.1), channel_id=1, source_target_pairs={{0,4},{2,6},{1,5},{3,7},{8,12},{10,14},{9,13},{11,15},{16,20},{18,... | collective-permute-start | bytes 835592 | tf_op jit(solution)/shard_map/ppermute | solution.py:580
  44.6 7.0 %query.1 = (bf16[1024,256]{1,0:T(8,128)(2,1)S(1)}, bf16[16,3,256]{2,1,0:T(4,128)(2,1)S(1)}, bf16[1024,512]{1,0:T(8,128)(2,1)S(1)}) custom-call(s32[1,16]{1,0:T(1,128)S(1)} %copy-done.5, s32[1,16]{1,0:T(1,128)S(1)} %copy-done.7, bf16[1024,2048]{1,0:T(8,128)(2,1)S(1)} %get-tuple-element.46.normed_ref, bf16[16,2048]{1,0:T(8,128)(2,1)} %collective-permute-done.rim_ref, ...), custom_call_target="tpu_custom_call" | custom-call | flops 3221225472 | bytes 4194304 | tf_op jit(solution)/shard_map/query/pallas_call | solution.py:279
  53.1 1.6 %collective-permute-start.10 = (bf16[256,1408]{1,0:T(8,128)(2,1)}, bf16[256,1408]{1,0:T(8,128)(2,1)}, u32[]{:S(2)}, u32[]{:S(2)}) collective-permute-start(bf16[256,1408]{1,0:T(8,128)(2,1)} %collective-permute-done.5.refs_5_), channel_id=1, source_target_pairs={{0,2},{2,0},{4,6},{6,4},{1,3},{3,1},{5,7},{7,5},{8,10},{10,8},{12,... | collective-permute-start | bytes 2162696 | tf_op jit(solution)/shard_map/ppermute | solution.py:585
  54.7 1.5 %collective-permute-start.11 = (bf16[256,1408]{1,0:T(8,128)(2,1)}, bf16[256,1408]{1,0:T(8,128)(2,1)}, u32[]{:S(2)}, u32[]{:S(2)}) collective-permute-start(bf16[256,1408]{1,0:T(8,128)(2,1)} %collective-permute-done.5.refs_5_), channel_id=1, source_target_pairs={{0,16},{8,24},{16,0},{24,8},{1,17},{9,25},{17,1},{25,9},{2,18},{10... | collective-permute-start | bytes 2162696 | tf_op jit(solution)/shard_map/ppermute | solution.py:585
  56.2 6.9 %pages.1 = (bf16[16,1,256,512]{3,2,1,0:T(8,128)(2,1)}, bf16[512,512]{1,0:T(8,128)(2,1)}, bf16[512,512]{1,0:T(8,128)(2,1)}) custom-call(s32[1,16]{1,0:T(1,128)S(1)} %copy-done.5, s32[1,16]{1,0:T(1,128)S(1)} %copy-done.7, bf16[1024,256]{1,0:T(8,128)(2,1)S(1)} %get-tuple-element.49.raised_ref, bf16[1024,256]{1,0:T(8,128)(2,1)S(1)} %get-tuple-element.50.lowered_ref, ...), custom_call_target="tpu_custom_call" | custom-call | flops 1000 | bytes 1000 | tf_op jit(solution)/shard_map/pages/pallas_call | solution.py:370
  63.7 2.5 %constant_dynamic-slice_fusion = (bf16[1408,256]{1,0:T(8,128)(2,1)}, bf16[1408,256]{1,0:T(8,128)(2,1)}) fusion(bf16[1408,512]{1,0:T(8,128)(2,1)} %refs_0_.5, s32[]{:T(128)S(6)} %select_n.8, s32[]{:T(128)S(6)} %select_n.7), kind=kLoop, calls=%fused_computation.1 | loop fusion | bytes 2883592 | tf_op jit(solution)/shard_map/dynamic_slice | solution.py:624
  66.2 4.6 %collective-permute-done.10.refs_6_ = bf16[256,1408]{1,0:T(8,128)(2,1)} collective-permute-done((bf16[256,1408]{1,0:T(8,128)(2,1)}, bf16[256,1408]{1,0:T(8,128)(2,1)}, u32[]{:S(2)}, u32[]{:S(2)}) %collective-permute-start.10) | collective-permute-done | bytes 720928 | tf_op jit(solution)/shard_map/ppermute | solution.py:585
  70.8 1.5 %collective-permute-start.13 = (bf16[1408,256]{1,0:T(8,128)(2,1)}, bf16[1408,256]{1,0:T(8,128)(2,1)}, u32[]{:S(2)}, u32[]{:S(2)}) collective-permute-start(bf16[1408,256]{1,0:T(8,128)(2,1)} %get-tuple-element.86), channel_id=1, source_target_pairs={{0,16},{8,24},{16,0},{24,8},{1,17},{9,25},{17,1},{25,9},{2,18},{10... | collective-permute-start | bytes 2162696 | tf_op jit(solution)/shard_map/ppermute | solution.py:585
  73.0 1.6 %collective-permute-start.15 = (bf16[256,1408]{1,0:T(8,128)(2,1)}, bf16[256,1408]{1,0:T(8,128)(2,1)}, u32[]{:S(2)}, u32[]{:S(2)}) collective-permute-start(bf16[256,1408]{1,0:T(8,128)(2,1)} %collective-permute-done.6.refs_7_), channel_id=1, source_target_pairs={{0,2},{2,0},{4,6},{6,4},{1,3},{3,1},{5,7},{7,5},{8,10},{10,8},{12,... | collective-permute-start | bytes 2162696 | tf_op jit(solution)/shard_map/ppermute | solution.py:585
  74.6 10.0 %mix.1 = (bf16[512,2048]{1,0:T(8,128)(2,1)S(1)}, bf16[1024,2048]{1,0:T(8,128)(2,1)S(1)}) custom-call(s32[1]{0:T(128)} %bitcast.s, bf16[1024,2048]{1,0:T(8,128)(2,1)} %refs_0_.3, bf16[512,512]{1,0:T(8,128)(2,1)} %get-tuple-element.55.refs_1_, bf16[512,512]{1,0:T(8,128)(2,1)} %get-tuple-element.56.refs_2_, bf16[512,512]{1,0:T(8,128)(2,1)} %collective-permute-done.8.refs_3_, ...), custom_call_target="tpu_custom_call" | custom-call | flops 1000 | bytes 1000 | tf_op jit(solution)/shard_map/mix/pallas_call | solution.py:426
  86.4 15.5 %widen.1 = (bf16[1024,1408]{1,0:T(8,128)(2,1)S(1)}, f32[1024,1408]{1,0:T(8,128)S(1)}) custom-call(bf16[1024,2048]{1,0:T(8,128)(2,1)S(1)} %get-tuple-element.63.feed_ref, bf16[512,1408]{1,0:T(8,128)(2,1)} %refs_0_.4, bf16[512,1408]{1,0:T(8,128)(2,1)S(1)} %collective-permute-done.2.refs_1_, bf16[512,1408]{1,0:T(8,128)(2,1)} %collective-permute-done.3.refs_2_, ...), custom_call_target="tpu_custom_call" | custom-call | flops 1000 | bytes 1000 | tf_op jit(solution)/shard_map/widen/pallas_call | solution.py:478
  104.0 1.6 %collective-permute-start.21 = (bf16[1408,256]{1,0:T(8,128)(2,1)}, bf16[1408,256]{1,0:T(8,128)(2,1)S(1)}, u32[]{:S(2)}, u32[]{:S(2)}) collective-permute-start(bf16[1408,256]{1,0:T(8,128)(2,1)} %collective-permute-done.14.refs_1_), channel_id=1, source_target_pairs={{0,2},{2,0},{4,6},{6,4},{1,3},{3,1},{5,7},{7,5},{8,10},{10,8},{12,... | collective-permute-start | bytes 2162696 | tf_op jit(solution)/shard_map/ppermute | solution.py:585
  105.6 5.4 %finish.1.hidden_hbm = bf16[1024,1408]{1,0:T(8,128)(2,1)S(1)} custom-call(bf16[1024,2048]{1,0:T(8,128)(2,1)S(1)} %get-tuple-element.63.feed_ref, bf16[1024,1408]{1,0:T(8,128)(2,1)S(1)} %get-tuple-element.71.gate_ref, f32[1024,1408]{1,0:T(8,128)S(1)} %get-tuple-element.72.up_ref, bf16[256,1408]{1,0:T(8,128)(2,1)} %collective-permute-done.15.refs_0_, ...), custom_call_target="tpu_custom_call" | custom-call | flops 1000 | bytes 1000 | tf_op jit(solution)/shard_map/finish/pallas_call | solution.py:478
  111.0 6.7 %narrow.2 = (bf16[512,1280]{1,0:T(8,128)(2,1)S(1)}, bf16[512,1280]{1,0:T(8,128)(2,1)S(1)}) custom-call(bf16[1024,1408]{1,0:T(8,128)(2,1)S(1)} %finish.1.hidden_hbm, bf16[1408,512]{1,0:T(8,128)(2,1)} %refs_0_.5, bf16[1408,256]{1,0:T(8,128)(2,1)} %collective-permute-done.14.refs_1_, bf16[1408,256]{1,0:T(8,128)(2,1)} %collective-permute-done.13.refs_2_, ...), custom_call_target="tpu_custom_call" | custom-call | flops 1000 | bytes 1000 | tf_op jit(solution)/shard_map/narrow/pallas_call | solution.py:537
  119.8 4.4 %narrow.3 = (bf16[512,768]{1,0:T(8,128)(2,1)S(1)}, bf16[512,768]{1,0:T(8,128)(2,1)S(1)}) custom-call(bf16[1024,1408]{1,0:T(8,128)(2,1)S(1)} %finish.1.hidden_hbm, bf16[1408,256]{1,0:T(8,128)(2,1)S(1)} %collective-permute-done.19.refs_0_, bf16[1408,256]{1,0:T(8,128)(2,1)S(1)} %collective-permute-done.20.refs_1_, ...), custom_call_target="tpu_custom_call" | custom-call | flops 1000 | bytes 1000 | tf_op jit(solution)/shard_map/narrow/pallas_call | solution.py:537
  125.1 1.5 %collective-permute-done.22.refs_3_ = bf16[512,768]{1,0:T(8,128)(2,1)S(1)} collective-permute-done((bf16[512,768]{1,0:T(8,128)(2,1)S(1)}, bf16[512,768]{1,0:T(8,128)(2,1)S(1)}, u32[]{:S(2)}, u32[]{:S(2)}) %collective-permute-start.22) | collective-permute-done | bytes 786464 | tf_op jit(solution)/shard_map/ppermute | solution.py:585
  126.6 1.8 %close.1 = bf16[512,2048]{1,0:T(8,128)(2,1)} custom-call(bf16[512,2048]{1,0:T(8,128)(2,1)S(1)} %get-tuple-element.61.residual_ref, bf16[512,1280]{1,0:T(8,128)(2,1)S(1)} %get-tuple-element.76.refs_0_, bf16[512,1280]{1,0:T(8,128)(2,1)S(1)} %collective-permute-done.18.refs_1_, bf16[512,768]{1,0:T(8,128)(2,1)S(1)} %get-tuple-element.78.refs_2_, ...), custom_call_target="tpu_custom_call" | custom-call | flops 1000 | bytes 1000 | tf_op jit(solution)/shard_map/close/pallas_call | solution.py:566
  (62 shorter events, 15.1 us)
Async XLA Ops:
  0.6 11.8 %collective-permute-start.1 = (bf16[512,2048]{1,0:T(8,128)(2,1)}, bf16[512,2048]{1,0:T(8,128)(2,1)S(1)}, u32[]{:S(2)}, u32[]{:S(2)}) collective-permute-start(bf16[512,2048]{1,0:T(8,128)(2,1)} %refs_5_.1), channel_id=1, source_target_pairs={{0,1},{1,0},{2,3},{3,2},{4,5},{5,4},{6,7},{7,6},{8,9},{9,8},{10,11... | collective-permute-start | bytes 6291464 | tf_op jit(solution)/shard_map/ppermute | solution.py:585
  1.1 37.2 %collective-permute-start.2 = (bf16[512,1408]{1,0:T(8,128)(2,1)}, bf16[512,1408]{1,0:T(8,128)(2,1)S(1)}, u32[]{:S(2)}, u32[]{:S(2)}) collective-permute-start(bf16[512,1408]{1,0:T(8,128)(2,1)} %refs_0_.4), channel_id=1, source_target_pairs={{0,8},{8,0},{16,24},{24,16},{1,9},{9,1},{17,25},{25,17},{2,10},{10... | collective-permute-start | bytes 4325384 | tf_op jit(solution)/shard_map/ppermute | solution.py:585
  3.7 34.7 %collective-permute-start.3 = (bf16[512,1408]{1,0:T(8,128)(2,1)}, bf16[512,1408]{1,0:T(8,128)(2,1)}, u32[]{:S(2)}, u32[]{:S(2)}) collective-permute-start(bf16[512,1408]{1,0:T(8,128)(2,1)} %refs_0_.4), channel_id=1, source_target_pairs={{0,16},{8,24},{16,0},{24,8},{1,17},{9,25},{17,1},{25,9},{2,18},{10... | collective-permute-start | bytes 4325384 | tf_op jit(solution)/shard_map/ppermute | solution.py:585
  6.7 5.7 %collective-permute-start = (bf16[16,2048]{1,0:T(8,128)(2,1)}, bf16[16,2048]{1,0:T(8,128)(2,1)}, u32[]{:S(2)}, u32[]{:S(2)}) collective-permute-start(bf16[16,2048]{1,0:T(8,128)(2,1)} %slice.3), channel_id=1, source_target_pairs={{0,2},{2,4},{4,6},{1,3},{3,5},{5,7},{8,10},{10,12},{12,14},{9,11},... | collective-permute-start | bytes 196616 | tf_op jit(solution)/shard_map/ppermute | solution.py:580
  28.6 23.0 %copy-start = (bf16[16,3,768]{2,1,0:T(4,128)(2,1)}, bf16[16,3,768]{2,1,0:T(4,128)(2,1)S(1)}, u32[]{:S(2)}) copy-start(bf16[16,3,768]{2,1,0:T(4,128)(2,1)S(1)} %get-tuple-element.82) | copy-start | bytes 221188
  28.6 9.5 %collective-permute-start.4 = (bf16[272,512]{1,0:T(8,128)(2,1)S(1)}, bf16[272,512]{1,0:T(8,128)(2,1)S(1)}, u32[]{:S(2)}, u32[]{:S(2)}) collective-permute-start(bf16[272,512]{1,0:T(8,128)(2,1)S(1)} %get-tuple-element.45.later_ref), channel_id=1, source_target_pairs={{0,2},{2,4},{4,6},{1,3},{3,5},{5,7},{8,10},{10,12},{12,14},{9,11},... | collective-permute-start | bytes 835592 | tf_op jit(solution)/shard_map/ppermute | solution.py:580
  33.1 19.2 %collective-permute-start.5 = (bf16[256,1408]{1,0:T(8,128)(2,1)S(1)}, bf16[256,1408]{1,0:T(8,128)(2,1)}, u32[]{:S(2)}, u32[]{:S(2)}) collective-permute-start(bf16[256,1408]{1,0:T(8,128)(2,1)S(1)} %constant_dynamic-slice_fusion.2), channel_id=1, source_target_pairs={{0,8},{8,0},{16,24},{24,16},{1,9},{9,1},{17,25},{25,17},{2,10},{10... | collective-permute-start | bytes 2162696 | tf_op jit(solution)/shard_map/ppermute | solution.py:585
  33.8 19.4 %collective-permute-start.6 = (bf16[256,1408]{1,0:T(8,128)(2,1)S(1)}, bf16[256,1408]{1,0:T(8,128)(2,1)}, u32[]{:S(2)}, u32[]{:S(2)}) collective-permute-start(bf16[256,1408]{1,0:T(8,128)(2,1)S(1)} %constant_dynamic-slice_fusion.2), channel_id=1, source_target_pairs={{0,16},{8,24},{16,0},{24,8},{1,17},{9,25},{17,1},{25,9},{2,18},{10... | collective-permute-start | bytes 2162696 | tf_op jit(solution)/shard_map/ppermute | solution.py:585
  38.5 46.6 %collective-permute-start.12 = (bf16[512,1408]{1,0:T(8,128)(2,1)}, bf16[512,1408]{1,0:T(8,128)(2,1)}, u32[]{:S(2)}, u32[]{:S(2)}) collective-permute-start(bf16[512,1408]{1,0:T(8,128)(2,1)} %collective-permute-done.3.refs_2_), channel_id=1, source_target_pairs={{0,8},{8,0},{16,24},{24,16},{1,9},{9,1},{17,25},{25,17},{2,10},{10... | collective-permute-start | bytes 4325384 | tf_op jit(solution)/shard_map/ppermute | solution.py:585
  39.0 17.2 %collective-permute-start.7 = (bf16[272,512]{1,0:T(8,128)(2,1)S(1)}, bf16[272,512]{1,0:T(8,128)(2,1)S(1)}, u32[]{:S(2)}, u32[]{:S(2)}) collective-permute-start(bf16[272,512]{1,0:T(8,128)(2,1)S(1)} %joined.1), channel_id=1, source_target_pairs={{0,4},{2,6},{1,5},{3,7},{8,12},{10,14},{9,13},{11,15},{16,20},{18,... | collective-permute-start | bytes 835592 | tf_op jit(solution)/shard_map/ppermute | solution.py:580
  53.1 17.7 %collective-permute-start.10 = (bf16[256,1408]{1,0:T(8,128)(2,1)}, bf16[256,1408]{1,0:T(8,128)(2,1)}, u32[]{:S(2)}, u32[]{:S(2)}) collective-permute-start(bf16[256,1408]{1,0:T(8,128)(2,1)} %collective-permute-done.5.refs_5_), channel_id=1, source_target_pairs={{0,2},{2,0},{4,6},{6,4},{1,3},{3,1},{5,7},{7,5},{8,10},{10,8},{12,... | collective-permute-start | bytes 2162696 | tf_op jit(solution)/shard_map/ppermute | solution.py:585
  54.7 17.6 %collective-permute-start.11 = (bf16[256,1408]{1,0:T(8,128)(2,1)}, bf16[256,1408]{1,0:T(8,128)(2,1)}, u32[]{:S(2)}, u32[]{:S(2)}) collective-permute-start(bf16[256,1408]{1,0:T(8,128)(2,1)} %collective-permute-done.5.refs_5_), channel_id=1, source_target_pairs={{0,16},{8,24},{16,0},{24,8},{1,17},{9,25},{17,1},{25,9},{2,18},{10... | collective-permute-start | bytes 2162696 | tf_op jit(solution)/shard_map/ppermute | solution.py:585
  63.1 9.9 %collective-permute-start.8 = (bf16[512,512]{1,0:T(8,128)(2,1)}, bf16[512,512]{1,0:T(8,128)(2,1)}, u32[]{:S(2)}, u32[]{:S(2)}) collective-permute-start(bf16[512,512]{1,0:T(8,128)(2,1)} %get-tuple-element.55.refs_1_), channel_id=1, source_target_pairs={{0,1},{1,0},{2,3},{3,2},{4,5},{5,4},{6,7},{7,6},{8,9},{9,8},{10,11... | collective-permute-start | bytes 1572872 | tf_op jit(solution)/shard_map/ppermute | solution.py:585
  63.2 11.4 %collective-permute-start.9 = (bf16[512,512]{1,0:T(8,128)(2,1)}, bf16[512,512]{1,0:T(8,128)(2,1)}, u32[]{:S(2)}, u32[]{:S(2)}) collective-permute-start(bf16[512,512]{1,0:T(8,128)(2,1)} %get-tuple-element.56.refs_2_), channel_id=1, source_target_pairs={{0,1},{1,0},{2,3},{3,2},{4,5},{5,4},{6,7},{7,6},{8,9},{9,8},{10,11... | collective-permute-start | bytes 1572872 | tf_op jit(solution)/shard_map/ppermute | solution.py:585
  70.8 31.0 %collective-permute-start.13 = (bf16[1408,256]{1,0:T(8,128)(2,1)}, bf16[1408,256]{1,0:T(8,128)(2,1)}, u32[]{:S(2)}, u32[]{:S(2)}) collective-permute-start(bf16[1408,256]{1,0:T(8,128)(2,1)} %get-tuple-element.86), channel_id=1, source_target_pairs={{0,16},{8,24},{16,0},{24,8},{1,17},{9,25},{17,1},{25,9},{2,18},{10... | collective-permute-start | bytes 2162696 | tf_op jit(solution)/shard_map/ppermute | solution.py:585
  72.4 29.5 %collective-permute-start.14 = (bf16[1408,256]{1,0:T(8,128)(2,1)}, bf16[1408,256]{1,0:T(8,128)(2,1)}, u32[]{:S(2)}, u32[]{:S(2)}) collective-permute-start(bf16[1408,256]{1,0:T(8,128)(2,1)} %get-tuple-element.75), channel_id=1, source_target_pairs={{0,8},{8,0},{16,24},{24,16},{1,9},{9,1},{17,25},{25,17},{2,10},{10... | collective-permute-start | bytes 2162696 | tf_op jit(solution)/shard_map/ppermute | solution.py:585
  73.0 31.1 %collective-permute-start.15 = (bf16[256,1408]{1,0:T(8,128)(2,1)}, bf16[256,1408]{1,0:T(8,128)(2,1)}, u32[]{:S(2)}, u32[]{:S(2)}) collective-permute-start(bf16[256,1408]{1,0:T(8,128)(2,1)} %collective-permute-done.6.refs_7_), channel_id=1, source_target_pairs={{0,2},{2,0},{4,6},{6,4},{1,3},{3,1},{5,7},{7,5},{8,10},{10,8},{12,... | collective-permute-start | bytes 2162696 | tf_op jit(solution)/shard_map/ppermute | solution.py:585
  84.6 21.1 %collective-permute-start.16 = (bf16[256,1408]{1,0:T(8,128)(2,1)}, bf16[256,1408]{1,0:T(8,128)(2,1)S(1)}, u32[]{:S(2)}, u32[]{:S(2)}) collective-permute-start(bf16[256,1408]{1,0:T(8,128)(2,1)} %collective-permute-done.11.refs_8_), channel_id=1, source_target_pairs={{0,2},{2,0},{4,6},{6,4},{1,3},{3,1},{5,7},{7,5},{8,10},{10,8},{12,... | collective-permute-start | bytes 2162696 | tf_op jit(solution)/shard_map/ppermute | solution.py:585
  85.1 26.0 %collective-permute-start.17 = (bf16[1408,256]{1,0:T(8,128)(2,1)}, bf16[1408,256]{1,0:T(8,128)(2,1)S(1)}, u32[]{:S(2)}, u32[]{:S(2)}) collective-permute-start(bf16[1408,256]{1,0:T(8,128)(2,1)} %get-tuple-element.75), channel_id=1, source_target_pairs={{0,16},{8,24},{16,0},{24,8},{1,17},{9,25},{17,1},{25,9},{2,18},{10... | collective-permute-start | bytes 2162696 | tf_op jit(solution)/shard_map/ppermute | solution.py:585
  101.9 15.9 %collective-permute-start.19 = (bf16[1408,256]{1,0:T(8,128)(2,1)}, bf16[1408,256]{1,0:T(8,128)(2,1)S(1)}, u32[]{:S(2)}, u32[]{:S(2)}) collective-permute-start(bf16[1408,256]{1,0:T(8,128)(2,1)} %collective-permute-done.13.refs_2_), channel_id=1, source_target_pairs={{0,8},{8,0},{16,24},{24,16},{1,9},{9,1},{17,25},{25,17},{2,10},{10... | collective-permute-start | bytes 2162696 | tf_op jit(solution)/shard_map/ppermute | solution.py:585
  103.3 15.4 %collective-permute-start.20 = (bf16[1408,256]{1,0:T(8,128)(2,1)}, bf16[1408,256]{1,0:T(8,128)(2,1)S(1)}, u32[]{:S(2)}, u32[]{:S(2)}) collective-permute-start(bf16[1408,256]{1,0:T(8,128)(2,1)} %collective-permute-done.14.refs_1_), channel_id=1, source_target_pairs={{0,16},{8,24},{16,0},{24,8},{1,17},{9,25},{17,1},{25,9},{2,18},{10... | collective-permute-start | bytes 2162696 | tf_op jit(solution)/shard_map/ppermute | solution.py:585
  104.0 15.8 %collective-permute-start.21 = (bf16[1408,256]{1,0:T(8,128)(2,1)}, bf16[1408,256]{1,0:T(8,128)(2,1)S(1)}, u32[]{:S(2)}, u32[]{:S(2)}) collective-permute-start(bf16[1408,256]{1,0:T(8,128)(2,1)} %collective-permute-done.14.refs_1_), channel_id=1, source_target_pairs={{0,2},{2,0},{4,6},{6,4},{1,3},{3,1},{5,7},{7,5},{8,10},{10,8},{12,... | collective-permute-start | bytes 2162696 | tf_op jit(solution)/shard_map/ppermute | solution.py:585
  117.7 7.3 %collective-permute-start.18 = (bf16[512,1280]{1,0:T(8,128)(2,1)S(1)}, bf16[512,1280]{1,0:T(8,128)(2,1)S(1)}, u32[]{:S(2)}, u32[]{:S(2)}) collective-permute-start(bf16[512,1280]{1,0:T(8,128)(2,1)S(1)} %get-tuple-element.77), channel_id=1, source_target_pairs={{0,1},{1,0},{2,3},{3,2},{4,5},{5,4},{6,7},{7,6},{8,9},{9,8},{10,11... | collective-permute-start | bytes 3932168 | tf_op jit(solution)/shard_map/ppermute | solution.py:585
  124.2 2.4 %collective-permute-start.22 = (bf16[512,768]{1,0:T(8,128)(2,1)S(1)}, bf16[512,768]{1,0:T(8,128)(2,1)S(1)}, u32[]{:S(2)}, u32[]{:S(2)}) collective-permute-start(bf16[512,768]{1,0:T(8,128)(2,1)S(1)} %get-tuple-element.79), channel_id=1, source_target_pairs={{0,1},{1,0},{2,3},{3,2},{4,5},{5,4},{6,7},{7,6},{8,9},{9,8},{10,11... | collective-permute-start | bytes 2359304 | tf_op jit(solution)/shard_map/ppermute | solution.py:585
  (10 other events, 100.3 us)

commit v12 on v9

--- a/solution.py
+++ b/solution.py
@@ -459,17 +459,33 @@
         up_ref[rows, :] = sums[1]
 
 
-def finish_kernel(places, feed_ref, gate_ref, up_ref, *refs):
-    pieces, out_ref = refs[:-1], refs[-1]
-    for first in range(0, feed_ref.shape[0], ROWS):
+def finish_kernel(places, feed_any, gate_ref, up_ref, *refs):
+    pieces, (out_ref, feed, sems) = refs[:-3], refs[-3:]
+
+    @pl.when(pl.program_id(0) == 0)
+    def _():
+        copies = []
+        for j, ((_, place), ref) in enumerate(zip(places, pieces)):
+            size = ref.shape[0]
+            columns = pl.ds(pl.multiple_of(place(), 128), size)
+            copies.append(
+                pltpu.make_async_copy(feed_any.at[:, columns], feed.at[:, pl.ds(j * size, size)], sems.at[j])
+            )
+        for copy in copies:
+            copy.start()
+        for copy in copies:
+            copy.wait()
+
+    for first in range(0, feed.shape[0], ROWS):
         rows = pl.ds(first, ROWS)
         total = up_ref[rows, :]
-        if pieces:
-            total = total + widen_sums(places, pieces, feed_ref, rows)[1]
+        for j, ref in enumerate(pieces):
+            size = ref.shape[0]
+            total = total + dot(feed[rows, pl.ds(j * size, size)], ref[...])
         out_ref[rows, :] = (gate_ref[rows, :].astype(F32) * total).astype(BF16)
 
 
-def widen_call(kernel, name, limit, kinds, feed, wholes, matrices):
+def widen_call(kernel, name, limit, kinds, feed, wholes, matrices, feed_spec, scratch=()):
     count, width = feed.shape
     pieces = [piece for matrix in matrices for piece, _ in matrix]
     places = [(i, place) for i, matrix in enumerate(matrices) for _, place in matrix]
@@ -479,21 +495,32 @@
         functools.partial(kernel, places),
         name=name,
         grid=(pl.cdiv(hidden, WIDE),),
-        in_specs=[fixed((count, width))] + [block] * len(wholes)
+        in_specs=[feed_spec] + [block] * len(wholes)
         + [pl.BlockSpec((piece.shape[0], WIDE), lambda i: (0, i)) for piece in pieces],
         out_specs=[block] * len(kinds),
         out_shape=[jax.ShapeDtypeStruct((count, hidden), kind) for kind in kinds],
+        scratch_shapes=list(scratch),
         compiler_params=params(limit),
         cost_estimate=cost(1000, 1000),
     )(feed, *wholes, *pieces)
 
 
 def widen(feed, matrices):
-    return widen_call(widen_kernel, "widen", WIDEN_VMEM, (BF16, F32), feed, (), matrices)
+    return widen_call(
+        widen_kernel, "widen", WIDEN_VMEM, (BF16, F32), feed, (), matrices, fixed(feed.shape)
+    )
 
 
 def finish(feed, wholes, pieces):
-    return widen_call(finish_kernel, "finish", FINISH_VMEM, (BF16,), feed, wholes, ([], pieces))[0]
+    depth = sum(piece.shape[0] for piece, _ in pieces)
+    scratch = (
+        pltpu.VMEM((feed.shape[0], max(depth, 128)), BF16),
+        pltpu.SemaphoreType.DMA((max(len(pieces), 1),)),
+    )
+    return widen_call(
+        finish_kernel, "finish", FINISH_VMEM, (BF16,), feed, wholes, ([], pieces),
+        pl.BlockSpec(memory_space=pl.ANY), scratch,
+    )[0]
 
 
 def narrow_kernel(block, hidden_hbm, *refs):

time: 129 us -> 129 us (level)
  no operation moved by 1% of the time
where the time goes in v12:
time: 129 us; the launch traced here: 128 us
  Pallas kernels  72.8 us (56%)
  starting transfers between devices  33.4 us (26%)
  waiting for transfers between devices  14.4 us (11%)
  local copies, waits for them, and re-layouts  6.8 us (5%)
    pallas_call x2, Pallas kernels, widen_call(): pl.pallas_call(functools.partial(kernel, places), name=name, grid=(pl.cdi...  21 us
    ppermute x20, starting transfers between devices, swapped(): return lax.ppermute(value, axis, [(i, i ^ flip) for i in range(count)])  19.3 us
    pallas_call x1, Pallas kernels, front(): pl.pallas_call(front_kernel, name='front', grid=(count // tile,), in_spec...  14.9 us
    ppermute x3, starting transfers between devices, shifted(): lax.ppermute(value, 'seq', [(i, i + steps) for i in range(count - steps)])  14.1 us
    pallas_call x2, Pallas kernels, narrow(): pl.pallas_call(functools.partial(narrow_kernel, block), name='narrow', in...  11 us
    pallas_call x1, Pallas kernels, mix(): pl.pallas_call(lambda s, *refs: mix_kernel(*refs), name='mix', grid_spec=...  9.98 us
    ppermute x20, waiting for transfers between devices, swapped(): return lax.ppermute(value, axis, [(i, i ^ flip) for i in range(count)])  9.62 us
    pallas_call x1, Pallas kernels, query(): pl.pallas_call(query_kernel, name='query', grid=(count // tile,), in_spec...  7 us
  transfers between devices with their start and end apart: 23, of which 9 were waited for; matrix products, arithmetic and copies ran while one was open for 4% of the time, Pallas kernels for 55%

profile of v12, /device:TPU:0, one launch (start us, length us, event | category | flops | bytes accessed | tf_op | source)
XLA Modules:
  0.0 128.3 jit_solution(16590438548252254344)
XLA Ops:
  1.1 2.6 %collective-permute-start.2 = (bf16[512,1408]{1,0:T(8,128)(2,1)}, bf16[512,1408]{1,0:T(8,128)(2,1)S(1)}, u32[]{:S(2)}, u32[]{:S(2)}) collective-permute-start(bf16[512,1408]{1,0:T(8,128)(2,1)} %refs_0_.4), channel_id=1, source_target_pairs={{0,8},{8,0},{16,24},{24,16},{1,9},{9,1},{17,25},{25,17},{2,10},{10... | collective-permute-start | bytes 4325384 | tf_op jit(solution)/shard_map/ppermute | solution.py:612
  3.7 1.5 %collective-permute-start.3 = (bf16[512,1408]{1,0:T(8,128)(2,1)}, bf16[512,1408]{1,0:T(8,128)(2,1)}, u32[]{:S(2)}, u32[]{:S(2)}) collective-permute-start(bf16[512,1408]{1,0:T(8,128)(2,1)} %refs_0_.4), channel_id=1, source_target_pairs={{0,16},{8,24},{16,0},{24,8},{1,17},{9,25},{17,1},{25,9},{2,18},{10... | collective-permute-start | bytes 4325384 | tf_op jit(solution)/shard_map/ppermute | solution.py:612
  5.2 1.5 %slice.3 = bf16[16,2048]{1,0:T(8,128)(2,1)} slice(bf16[1024,2048]{1,0:T(8,128)(2,1)} %refs_0_.3), slice={[1008:1024], [0:2048]} | slice | bytes 131072 | tf_op jit(solution)/shard_map/slice | solution.py:639
  6.7 4.1 %collective-permute-start = (bf16[16,2048]{1,0:T(8,128)(2,1)}, bf16[16,2048]{1,0:T(8,128)(2,1)}, u32[]{:S(2)}, u32[]{:S(2)}) collective-permute-start(bf16[16,2048]{1,0:T(8,128)(2,1)} %slice.3), channel_id=1, source_target_pairs={{0,2},{2,4},{4,6},{1,3},{3,5},{5,7},{8,10},{10,12},{12,14},{9,11},... | collective-permute-start | bytes 196616 | tf_op jit(solution)/shard_map/ppermute | solution.py:607
  13.7 14.9 %front.1 = (bf16[1024,2048]{1,0:T(8,128)(2,1)S(1)}, f32[1024,256]{1,0:T(8,128)S(1)}, bf16[1024,256]{1,0:T(8,128)(2,1)S(1)}, bf16[1024,256]{1,0:T(8,128)(2,1)S(1)...) custom-call(s32[1,16]{1,0:T(1,128)S(1)} %copy-done.4, ...), custom_call_target="tpu_custom_call" | custom-call | flops 1000 | bytes 1000 | tf_op jit(solution)/shard_map/front/pallas_call | solution.py:214
  28.6 4.4 %collective-permute-start.4 = (bf16[272,512]{1,0:T(8,128)(2,1)S(1)}, bf16[272,512]{1,0:T(8,128)(2,1)S(1)}, u32[]{:S(2)}, u32[]{:S(2)}) collective-permute-start(bf16[272,512]{1,0:T(8,128)(2,1)S(1)} %get-tuple-element.45.later_ref), channel_id=1, source_target_pairs={{0,2},{2,4},{4,6},{1,3},{3,5},{5,7},{8,10},{10,12},{12,14},{9,11},... | collective-permute-start | bytes 835592 | tf_op jit(solution)/shard_map/ppermute | solution.py:607
  34.3 3.9 %collective-permute-done.4.earlier_ref.one_ref = bf16[272,512]{1,0:T(8,128)(2,1)S(1)} collective-permute-done((bf16[272,512]{1,0:T(8,128)(2,1)S(1)}, bf16[272,512]{1,0:T(8,128)(2,1)S(1)}, u32[]{:S(2)}, u32[]{:S(2)}) %collective-permute-start.4) | collective-permute-done | bytes 278560 | tf_op jit(solution)/shard_map/ppermute | solution.py:607
  39.0 5.6 %collective-permute-start.7 = (bf16[272,512]{1,0:T(8,128)(2,1)S(1)}, bf16[272,512]{1,0:T(8,128)(2,1)S(1)}, u32[]{:S(2)}, u32[]{:S(2)}) collective-permute-start(bf16[272,512]{1,0:T(8,128)(2,1)S(1)} %joined.1), channel_id=1, source_target_pairs={{0,4},{2,6},{1,5},{3,7},{8,12},{10,14},{9,13},{11,15},{16,20},{18,... | collective-permute-start | bytes 835592 | tf_op jit(solution)/shard_map/ppermute | solution.py:607
  44.6 7.0 %query.1 = (bf16[1024,256]{1,0:T(8,128)(2,1)S(1)}, bf16[16,3,256]{2,1,0:T(4,128)(2,1)S(1)}, bf16[1024,512]{1,0:T(8,128)(2,1)S(1)}) custom-call(s32[1,16]{1,0:T(1,128)S(1)} %copy-done.5, s32[1,16]{1,0:T(1,128)S(1)} %copy-done.7, bf16[1024,2048]{1,0:T(8,128)(2,1)S(1)} %get-tuple-element.46.normed_ref, bf16[16,2048]{1,0:T(8,128)(2,1)} %collective-permute-done.rim_ref, ...), custom_call_target="tpu_custom_call" | custom-call | flops 3221225472 | bytes 4194304 | tf_op jit(solution)/shard_map/query/pallas_call | solution.py:279
  53.1 1.6 %collective-permute-start.10 = (bf16[256,1408]{1,0:T(8,128)(2,1)}, bf16[256,1408]{1,0:T(8,128)(2,1)}, u32[]{:S(2)}, u32[]{:S(2)}) collective-permute-start(bf16[256,1408]{1,0:T(8,128)(2,1)} %collective-permute-done.5.refs_5_), channel_id=1, source_target_pairs={{0,2},{2,0},{4,6},{6,4},{1,3},{3,1},{5,7},{7,5},{8,10},{10,8},{12,... | collective-permute-start | bytes 2162696 | tf_op jit(solution)/shard_map/ppermute | solution.py:612
  54.7 1.5 %collective-permute-start.11 = (bf16[256,1408]{1,0:T(8,128)(2,1)}, bf16[256,1408]{1,0:T(8,128)(2,1)}, u32[]{:S(2)}, u32[]{:S(2)}) collective-permute-start(bf16[256,1408]{1,0:T(8,128)(2,1)} %collective-permute-done.5.refs_5_), channel_id=1, source_target_pairs={{0,16},{8,24},{16,0},{24,8},{1,17},{9,25},{17,1},{25,9},{2,18},{10... | collective-permute-start | bytes 2162696 | tf_op jit(solution)/shard_map/ppermute | solution.py:612
  56.2 6.9 %pages.1 = (bf16[16,1,256,512]{3,2,1,0:T(8,128)(2,1)}, bf16[512,512]{1,0:T(8,128)(2,1)}, bf16[512,512]{1,0:T(8,128)(2,1)}) custom-call(s32[1,16]{1,0:T(1,128)S(1)} %copy-done.5, s32[1,16]{1,0:T(1,128)S(1)} %copy-done.7, bf16[1024,256]{1,0:T(8,128)(2,1)S(1)} %get-tuple-element.49.raised_ref, bf16[1024,256]{1,0:T(8,128)(2,1)S(1)} %get-tuple-element.50.lowered_ref, ...), custom_call_target="tpu_custom_call" | custom-call | flops 1000 | bytes 1000 | tf_op jit(solution)/shard_map/pages/pallas_call | solution.py:370
  63.7 2.5 %constant_dynamic-slice_fusion = (bf16[1408,256]{1,0:T(8,128)(2,1)}, bf16[1408,256]{1,0:T(8,128)(2,1)}) fusion(bf16[1408,512]{1,0:T(8,128)(2,1)} %refs_0_.5, s32[]{:T(128)S(6)} %select_n.8, s32[]{:T(128)S(6)} %select_n.7), kind=kLoop, calls=%fused_computation.1 | loop fusion | bytes 2883592 | tf_op jit(solution)/shard_map/dynamic_slice | solution.py:651
  66.2 4.6 %collective-permute-done.10.refs_6_ = bf16[256,1408]{1,0:T(8,128)(2,1)} collective-permute-done((bf16[256,1408]{1,0:T(8,128)(2,1)}, bf16[256,1408]{1,0:T(8,128)(2,1)}, u32[]{:S(2)}, u32[]{:S(2)}) %collective-permute-start.10) | collective-permute-done | bytes 720928 | tf_op jit(solution)/shard_map/ppermute | solution.py:612
  70.8 1.5 %collective-permute-start.13 = (bf16[1408,256]{1,0:T(8,128)(2,1)}, bf16[1408,256]{1,0:T(8,128)(2,1)}, u32[]{:S(2)}, u32[]{:S(2)}) collective-permute-start(bf16[1408,256]{1,0:T(8,128)(2,1)} %get-tuple-element.86), channel_id=1, source_target_pairs={{0,16},{8,24},{16,0},{24,8},{1,17},{9,25},{17,1},{25,9},{2,18},{10... | collective-permute-start | bytes 2162696 | tf_op jit(solution)/shard_map/ppermute | solution.py:612
  73.0 1.6 %collective-permute-start.15 = (bf16[256,1408]{1,0:T(8,128)(2,1)}, bf16[256,1408]{1,0:T(8,128)(2,1)}, u32[]{:S(2)}, u32[]{:S(2)}) collective-permute-start(bf16[256,1408]{1,0:T(8,128)(2,1)} %collective-permute-done.6.refs_7_), channel_id=1, source_target_pairs={{0,2},{2,0},{4,6},{6,4},{1,3},{3,1},{5,7},{7,5},{8,10},{10,8},{12,... | collective-permute-start | bytes 2162696 | tf_op jit(solution)/shard_map/ppermute | solution.py:612
  74.6 10.0 %mix.1 = (bf16[512,2048]{1,0:T(8,128)(2,1)S(1)}, bf16[1024,2048]{1,0:T(8,128)(2,1)S(1)}) custom-call(s32[1]{0:T(128)} %bitcast.s, bf16[1024,2048]{1,0:T(8,128)(2,1)} %refs_0_.3, bf16[512,512]{1,0:T(8,128)(2,1)} %get-tuple-element.55.refs_1_, bf16[512,512]{1,0:T(8,128)(2,1)} %get-tuple-element.56.refs_2_, bf16[512,512]{1,0:T(8,128)(2,1)} %collective-permute-done.8.refs_3_, ...), custom_call_target="tpu_custom_call" | custom-call | flops 1000 | bytes 1000 | tf_op jit(solution)/shard_map/mix/pallas_call | solution.py:426
  86.4 15.5 %widen.1 = (bf16[1024,1408]{1,0:T(8,128)(2,1)S(1)}, f32[1024,1408]{1,0:T(8,128)S(1)}) custom-call(bf16[1024,2048]{1,0:T(8,128)(2,1)S(1)} %get-tuple-element.63.feed_ref.feed_any, bf16[512,1408]{1,0:T(8,128)(2,1)} %refs_0_.4, bf16[512,1408]{1,0:T(8,128)(2,1)S(1)} %collective-permute-done.2.refs_1_, bf16[512,1408]{1,0:T(8,128)(2,1)} %collective-permute-done.3.refs_2_, ...), custom_call_target="tpu_custom_call" | custom-call | flops 1000 | bytes 1000 | tf_op jit(solution)/shard_map/widen/pallas_call | solution.py:494
  104.0 1.6 %collective-permute-start.21 = (bf16[1408,256]{1,0:T(8,128)(2,1)}, bf16[1408,256]{1,0:T(8,128)(2,1)S(1)}, u32[]{:S(2)}, u32[]{:S(2)}) collective-permute-start(bf16[1408,256]{1,0:T(8,128)(2,1)} %collective-permute-done.14.refs_1_), channel_id=1, source_target_pairs={{0,2},{2,0},{4,6},{6,4},{1,3},{3,1},{5,7},{7,5},{8,10},{10,8},{12,... | collective-permute-start | bytes 2162696 | tf_op jit(solution)/shard_map/ppermute | solution.py:612
  105.6 5.5 %finish.1.hidden_hbm = bf16[1024,1408]{1,0:T(8,128)(2,1)S(1)} custom-call(bf16[1024,2048]{1,0:T(8,128)(2,1)S(1)} %get-tuple-element.63.feed_ref.feed_any, bf16[1024,1408]{1,0:T(8,128)(2,1)S(1)} %get-tuple-element.71.gate_ref, f32[1024,1408]{1,0:T(8,128)S(1)} %get-tuple-element.72.up_ref, bf16[256,1408]{1,0:T(8,128)(2,1)} %collective-permute-done.15.refs_0_, ...), custom_call_target="tpu_custom_call" | custom-call | flops 1000 | bytes 1000 | tf_op jit(solution)/shard_map/finish/pallas_call | solution.py:494
  111.2 6.7 %narrow.2 = (bf16[512,1280]{1,0:T(8,128)(2,1)S(1)}, bf16[512,1280]{1,0:T(8,128)(2,1)S(1)}) custom-call(bf16[1024,1408]{1,0:T(8,128)(2,1)S(1)} %finish.1.hidden_hbm, bf16[1408,512]{1,0:T(8,128)(2,1)} %refs_0_.5, bf16[1408,256]{1,0:T(8,128)(2,1)} %collective-permute-done.14.refs_1_, bf16[1408,256]{1,0:T(8,128)(2,1)} %collective-permute-done.13.refs_2_, ...), custom_call_target="tpu_custom_call" | custom-call | flops 1000 | bytes 1000 | tf_op jit(solution)/shard_map/narrow/pallas_call | solution.py:564
  119.8 4.4 %narrow.3 = (bf16[512,768]{1,0:T(8,128)(2,1)S(1)}, bf16[512,768]{1,0:T(8,128)(2,1)S(1)}) custom-call(bf16[1024,1408]{1,0:T(8,128)(2,1)S(1)} %finish.1.hidden_hbm, bf16[1408,256]{1,0:T(8,128)(2,1)S(1)} %collective-permute-done.19.refs_0_, bf16[1408,256]{1,0:T(8,128)(2,1)S(1)} %collective-permute-done.20.refs_1_, ...), custom_call_target="tpu_custom_call" | custom-call | flops 1000 | bytes 1000 | tf_op jit(solution)/shard_map/narrow/pallas_call | solution.py:564
  125.1 1.5 %collective-permute-done.22.refs_3_ = bf16[512,768]{1,0:T(8,128)(2,1)S(1)} collective-permute-done((bf16[512,768]{1,0:T(8,128)(2,1)S(1)}, bf16[512,768]{1,0:T(8,128)(2,1)S(1)}, u32[]{:S(2)}, u32[]{:S(2)}) %collective-permute-start.22) | collective-permute-done | bytes 786464 | tf_op jit(solution)/shard_map/ppermute | solution.py:612
  126.6 1.8 %close.1 = bf16[512,2048]{1,0:T(8,128)(2,1)} custom-call(bf16[512,2048]{1,0:T(8,128)(2,1)S(1)} %get-tuple-element.61.residual_ref, bf16[512,1280]{1,0:T(8,128)(2,1)S(1)} %get-tuple-element.76.refs_0_, bf16[512,1280]{1,0:T(8,128)(2,1)S(1)} %collective-permute-done.18.refs_1_, bf16[512,768]{1,0:T(8,128)(2,1)S(1)} %get-tuple-element.78.refs_2_, ...), custom_call_target="tpu_custom_call" | custom-call | flops 1000 | bytes 1000 | tf_op jit(solution)/shard_map/close/pallas_call | solution.py:593
  (62 shorter events, 14.9 us)
Async XLA Ops:
  0.6 11.8 %collective-permute-start.1 = (bf16[512,2048]{1,0:T(8,128)(2,1)}, bf16[512,2048]{1,0:T(8,128)(2,1)S(1)}, u32[]{:S(2)}, u32[]{:S(2)}) collective-permute-start(bf16[512,2048]{1,0:T(8,128)(2,1)} %refs_5_.1), channel_id=1, source_target_pairs={{0,1},{1,0},{2,3},{3,2},{4,5},{5,4},{6,7},{7,6},{8,9},{9,8},{10,11... | collective-permute-start | bytes 6291464 | tf_op jit(solution)/shard_map/ppermute | solution.py:612
  1.1 37.2 %collective-permute-start.2 = (bf16[512,1408]{1,0:T(8,128)(2,1)}, bf16[512,1408]{1,0:T(8,128)(2,1)S(1)}, u32[]{:S(2)}, u32[]{:S(2)}) collective-permute-start(bf16[512,1408]{1,0:T(8,128)(2,1)} %refs_0_.4), channel_id=1, source_target_pairs={{0,8},{8,0},{16,24},{24,16},{1,9},{9,1},{17,25},{25,17},{2,10},{10... | collective-permute-start | bytes 4325384 | tf_op jit(solution)/shard_map/ppermute | solution.py:612
  3.7 34.7 %collective-permute-start.3 = (bf16[512,1408]{1,0:T(8,128)(2,1)}, bf16[512,1408]{1,0:T(8,128)(2,1)}, u32[]{:S(2)}, u32[]{:S(2)}) collective-permute-start(bf16[512,1408]{1,0:T(8,128)(2,1)} %refs_0_.4), channel_id=1, source_target_pairs={{0,16},{8,24},{16,0},{24,8},{1,17},{9,25},{17,1},{25,9},{2,18},{10... | collective-permute-start | bytes 4325384 | tf_op jit(solution)/shard_map/ppermute | solution.py:612
  6.7 5.7 %collective-permute-start = (bf16[16,2048]{1,0:T(8,128)(2,1)}, bf16[16,2048]{1,0:T(8,128)(2,1)}, u32[]{:S(2)}, u32[]{:S(2)}) collective-permute-start(bf16[16,2048]{1,0:T(8,128)(2,1)} %slice.3), channel_id=1, source_target_pairs={{0,2},{2,4},{4,6},{1,3},{3,5},{5,7},{8,10},{10,12},{12,14},{9,11},... | collective-permute-start | bytes 196616 | tf_op jit(solution)/shard_map/ppermute | solution.py:607
  28.6 23.0 %copy-start = (bf16[16,3,768]{2,1,0:T(4,128)(2,1)}, bf16[16,3,768]{2,1,0:T(4,128)(2,1)S(1)}, u32[]{:S(2)}) copy-start(bf16[16,3,768]{2,1,0:T(4,128)(2,1)S(1)} %get-tuple-element.82) | copy-start | bytes 221188
  28.6 9.5 %collective-permute-start.4 = (bf16[272,512]{1,0:T(8,128)(2,1)S(1)}, bf16[272,512]{1,0:T(8,128)(2,1)S(1)}, u32[]{:S(2)}, u32[]{:S(2)}) collective-permute-start(bf16[272,512]{1,0:T(8,128)(2,1)S(1)} %get-tuple-element.45.later_ref), channel_id=1, source_target_pairs={{0,2},{2,4},{4,6},{1,3},{3,5},{5,7},{8,10},{10,12},{12,14},{9,11},... | collective-permute-start | bytes 835592 | tf_op jit(solution)/shard_map/ppermute | solution.py:607
  33.1 19.2 %collective-permute-start.5 = (bf16[256,1408]{1,0:T(8,128)(2,1)S(1)}, bf16[256,1408]{1,0:T(8,128)(2,1)}, u32[]{:S(2)}, u32[]{:S(2)}) collective-permute-start(bf16[256,1408]{1,0:T(8,128)(2,1)S(1)} %constant_dynamic-slice_fusion.2), channel_id=1, source_target_pairs={{0,8},{8,0},{16,24},{24,16},{1,9},{9,1},{17,25},{25,17},{2,10},{10... | collective-permute-start | bytes 2162696 | tf_op jit(solution)/shard_map/ppermute | solution.py:612
  33.8 19.4 %collective-permute-start.6 = (bf16[256,1408]{1,0:T(8,128)(2,1)S(1)}, bf16[256,1408]{1,0:T(8,128)(2,1)}, u32[]{:S(2)}, u32[]{:S(2)}) collective-permute-start(bf16[256,1408]{1,0:T(8,128)(2,1)S(1)} %constant_dynamic-slice_fusion.2), channel_id=1, source_target_pairs={{0,16},{8,24},{16,0},{24,8},{1,17},{9,25},{17,1},{25,9},{2,18},{10... | collective-permute-start | bytes 2162696 | tf_op jit(solution)/shard_map/ppermute | solution.py:612
  38.5 46.6 %collective-permute-start.12 = (bf16[512,1408]{1,0:T(8,128)(2,1)}, bf16[512,1408]{1,0:T(8,128)(2,1)}, u32[]{:S(2)}, u32[]{:S(2)}) collective-permute-start(bf16[512,1408]{1,0:T(8,128)(2,1)} %collective-permute-done.3.refs_2_), channel_id=1, source_target_pairs={{0,8},{8,0},{16,24},{24,16},{1,9},{9,1},{17,25},{25,17},{2,10},{10... | collective-permute-start | bytes 4325384 | tf_op jit(solution)/shard_map/ppermute | solution.py:612
  39.0 17.2 %collective-permute-start.7 = (bf16[272,512]{1,0:T(8,128)(2,1)S(1)}, bf16[272,512]{1,0:T(8,128)(2,1)S(1)}, u32[]{:S(2)}, u32[]{:S(2)}) collective-permute-start(bf16[272,512]{1,0:T(8,128)(2,1)S(1)} %joined.1), channel_id=1, source_target_pairs={{0,4},{2,6},{1,5},{3,7},{8,12},{10,14},{9,13},{11,15},{16,20},{18,... | collective-permute-start | bytes 835592 | tf_op jit(solution)/shard_map/ppermute | solution.py:607
  53.1 17.7 %collective-permute-start.10 = (bf16[256,1408]{1,0:T(8,128)(2,1)}, bf16[256,1408]{1,0:T(8,128)(2,1)}, u32[]{:S(2)}, u32[]{:S(2)}) collective-permute-start(bf16[256,1408]{1,0:T(8,128)(2,1)} %collective-permute-done.5.refs_5_), channel_id=1, source_target_pairs={{0,2},{2,0},{4,6},{6,4},{1,3},{3,1},{5,7},{7,5},{8,10},{10,8},{12,... | collective-permute-start | bytes 2162696 | tf_op jit(solution)/shard_map/ppermute | solution.py:612
  54.7 17.6 %collective-permute-start.11 = (bf16[256,1408]{1,0:T(8,128)(2,1)}, bf16[256,1408]{1,0:T(8,128)(2,1)}, u32[]{:S(2)}, u32[]{:S(2)}) collective-permute-start(bf16[256,1408]{1,0:T(8,128)(2,1)} %collective-permute-done.5.refs_5_), channel_id=1, source_target_pairs={{0,16},{8,24},{16,0},{24,8},{1,17},{9,25},{17,1},{25,9},{2,18},{10... | collective-permute-start | bytes 2162696 | tf_op jit(solution)/shard_map/ppermute | solution.py:612
  63.1 9.9 %collective-permute-start.8 = (bf16[512,512]{1,0:T(8,128)(2,1)}, bf16[512,512]{1,0:T(8,128)(2,1)}, u32[]{:S(2)}, u32[]{:S(2)}) collective-permute-start(bf16[512,512]{1,0:T(8,128)(2,1)} %get-tuple-element.55.refs_1_), channel_id=1, source_target_pairs={{0,1},{1,0},{2,3},{3,2},{4,5},{5,4},{6,7},{7,6},{8,9},{9,8},{10,11... | collective-permute-start | bytes 1572872 | tf_op jit(solution)/shard_map/ppermute | solution.py:612
  63.2 11.4 %collective-permute-start.9 = (bf16[512,512]{1,0:T(8,128)(2,1)}, bf16[512,512]{1,0:T(8,128)(2,1)}, u32[]{:S(2)}, u32[]{:S(2)}) collective-permute-start(bf16[512,512]{1,0:T(8,128)(2,1)} %get-tuple-element.56.refs_2_), channel_id=1, source_target_pairs={{0,1},{1,0},{2,3},{3,2},{4,5},{5,4},{6,7},{7,6},{8,9},{9,8},{10,11... | collective-permute-start | bytes 1572872 | tf_op jit(solution)/shard_map/ppermute | solution.py:612
  70.8 31.0 %collective-permute-start.13 = (bf16[1408,256]{1,0:T(8,128)(2,1)}, bf16[1408,256]{1,0:T(8,128)(2,1)}, u32[]{:S(2)}, u32[]{:S(2)}) collective-permute-start(bf16[1408,256]{1,0:T(8,128)(2,1)} %get-tuple-element.86), channel_id=1, source_target_pairs={{0,16},{8,24},{16,0},{24,8},{1,17},{9,25},{17,1},{25,9},{2,18},{10... | collective-permute-start | bytes 2162696 | tf_op jit(solution)/shard_map/ppermute | solution.py:612
  72.4 29.5 %collective-permute-start.14 = (bf16[1408,256]{1,0:T(8,128)(2,1)}, bf16[1408,256]{1,0:T(8,128)(2,1)}, u32[]{:S(2)}, u32[]{:S(2)}) collective-permute-start(bf16[1408,256]{1,0:T(8,128)(2,1)} %get-tuple-element.75), channel_id=1, source_target_pairs={{0,8},{8,0},{16,24},{24,16},{1,9},{9,1},{17,25},{25,17},{2,10},{10... | collective-permute-start | bytes 2162696 | tf_op jit(solution)/shard_map/ppermute | solution.py:612
  73.0 31.1 %collective-permute-start.15 = (bf16[256,1408]{1,0:T(8,128)(2,1)}, bf16[256,1408]{1,0:T(8,128)(2,1)}, u32[]{:S(2)}, u32[]{:S(2)}) collective-permute-start(bf16[256,1408]{1,0:T(8,128)(2,1)} %collective-permute-done.6.refs_7_), channel_id=1, source_target_pairs={{0,2},{2,0},{4,6},{6,4},{1,3},{3,1},{5,7},{7,5},{8,10},{10,8},{12,... | collective-permute-start | bytes 2162696 | tf_op jit(solution)/shard_map/ppermute | solution.py:612
  84.6 21.1 %collective-permute-start.16 = (bf16[256,1408]{1,0:T(8,128)(2,1)}, bf16[256,1408]{1,0:T(8,128)(2,1)S(1)}, u32[]{:S(2)}, u32[]{:S(2)}) collective-permute-start(bf16[256,1408]{1,0:T(8,128)(2,1)} %collective-permute-done.11.refs_8_), channel_id=1, source_target_pairs={{0,2},{2,0},{4,6},{6,4},{1,3},{3,1},{5,7},{7,5},{8,10},{10,8},{12,... | collective-permute-start | bytes 2162696 | tf_op jit(solution)/shard_map/ppermute | solution.py:612
  85.1 26.1 %collective-permute-start.17 = (bf16[1408,256]{1,0:T(8,128)(2,1)}, bf16[1408,256]{1,0:T(8,128)(2,1)S(1)}, u32[]{:S(2)}, u32[]{:S(2)}) collective-permute-start(bf16[1408,256]{1,0:T(8,128)(2,1)} %get-tuple-element.75), channel_id=1, source_target_pairs={{0,16},{8,24},{16,0},{24,8},{1,17},{9,25},{17,1},{25,9},{2,18},{10... | collective-permute-start | bytes 2162696 | tf_op jit(solution)/shard_map/ppermute | solution.py:612
  101.9 16.1 %collective-permute-start.19 = (bf16[1408,256]{1,0:T(8,128)(2,1)}, bf16[1408,256]{1,0:T(8,128)(2,1)S(1)}, u32[]{:S(2)}, u32[]{:S(2)}) collective-permute-start(bf16[1408,256]{1,0:T(8,128)(2,1)} %collective-permute-done.13.refs_2_), channel_id=1, source_target_pairs={{0,8},{8,0},{16,24},{24,16},{1,9},{9,1},{17,25},{25,17},{2,10},{10... | collective-permute-start | bytes 2162696 | tf_op jit(solution)/shard_map/ppermute | solution.py:612
  103.3 15.4 %collective-permute-start.20 = (bf16[1408,256]{1,0:T(8,128)(2,1)}, bf16[1408,256]{1,0:T(8,128)(2,1)S(1)}, u32[]{:S(2)}, u32[]{:S(2)}) collective-permute-start(bf16[1408,256]{1,0:T(8,128)(2,1)} %collective-permute-done.14.refs_1_), channel_id=1, source_target_pairs={{0,16},{8,24},{16,0},{24,8},{1,17},{9,25},{17,1},{25,9},{2,18},{10... | collective-permute-start | bytes 2162696 | tf_op jit(solution)/shard_map/ppermute | solution.py:612
  104.0 15.8 %collective-permute-start.21 = (bf16[1408,256]{1,0:T(8,128)(2,1)}, bf16[1408,256]{1,0:T(8,128)(2,1)S(1)}, u32[]{:S(2)}, u32[]{:S(2)}) collective-permute-start(bf16[1408,256]{1,0:T(8,128)(2,1)} %collective-permute-done.14.refs_1_), channel_id=1, source_target_pairs={{0,2},{2,0},{4,6},{6,4},{1,3},{3,1},{5,7},{7,5},{8,10},{10,8},{12,... | collective-permute-start | bytes 2162696 | tf_op jit(solution)/shard_map/ppermute | solution.py:612
  117.9 7.2 %collective-permute-start.18 = (bf16[512,1280]{1,0:T(8,128)(2,1)S(1)}, bf16[512,1280]{1,0:T(8,128)(2,1)S(1)}, u32[]{:S(2)}, u32[]{:S(2)}) collective-permute-start(bf16[512,1280]{1,0:T(8,128)(2,1)S(1)} %get-tuple-element.77), channel_id=1, source_target_pairs={{0,1},{1,0},{2,3},{3,2},{4,5},{5,4},{6,7},{7,6},{8,9},{9,8},{10,11... | collective-permute-start | bytes 3932168 | tf_op jit(solution)/shard_map/ppermute | solution.py:612
  124.2 2.4 %collective-permute-start.22 = (bf16[512,768]{1,0:T(8,128)(2,1)S(1)}, bf16[512,768]{1,0:T(8,128)(2,1)S(1)}, u32[]{:S(2)}, u32[]{:S(2)}) collective-permute-start(bf16[512,768]{1,0:T(8,128)(2,1)S(1)} %get-tuple-element.79), channel_id=1, source_target_pairs={{0,1},{1,0},{2,3},{3,2},{4,5},{5,4},{6,7},{7,6},{8,9},{9,8},{10,11... | collective-permute-start | bytes 2359304 | tf_op jit(solution)/shard_map/ppermute | solution.py:612
  (10 other events, 100.0 us)
